TPU v7x, 32 devices: a whole 2x2x4 slice. The times are simulated.
32 devices in a mesh: layer: 4 (over x, core), feat: 8 (over z, y).
Axes of the slice: x: 2, y: 2, z: 4, core: 2. Of those that a mesh axis runs over, the one named last changes fastest.
Arguments:
- layer_inputs: bfloat16 [4, 512, 2048], P('layer', 'feat'), may hold values from -6 to 6
- targets: float32 [4, 512, 2048], P('layer', None, 'feat'), may hold values from -5 to 5
- encoder: bfloat16 [4, 2048, 32768], P('layer', None, 'feat'), may hold values from -0.125 to 0.125
- encoder_bias: float32 [4, 32768], P('layer', 'feat'), may hold values from -3 to 3
- decoder: bfloat16 [4, 4, 32768, 2048], P('layer', None, 'feat'), may hold values from -0.03125 to 0.03125
Outputs:
- residual: float32 [4, 512, 2048], P('layer', None, 'feat')
All inputs are finite; a program needn't handle non-finite values.
Results may differ from a plain program's by a relative error of at most 0.0025.
Values may be sent and summed in bfloat16 or wider, within the bound.
No kernel may reach another device: no remote copies, remote signals or barrier semaphores. Data moves between devices by JAX's collectives and lax.ppermute only.
A program may use at most 192 MiB of HBM per device.

v0:
```python
import jax
import jax.numpy as jnp
from jax import lax
from jax.sharding import PartitionSpec as P

L_WIN = 4


def from_partner(array, axis, stride):
    return lax.ppermute(array, axis, [(i, i ^ 1 << stride) for i in range(lax.axis_size(axis))])


def on_device(layer_inputs, targets, encoder, encoder_bias, decoder):
    groups = lax.axis_size("layer") // L_WIN
    depth_bits = groups.bit_length() - 1
    position = lax.axis_index("layer")
    target_layer = position // groups
    group_index = position % groups
    gathered = lax.all_gather(layer_inputs[0], "feat", axis=0, tiled=True)
    for bit_index in range(depth_bits):
        partner = from_partner(gathered, "layer", bit_index)
        upper_bit = position >> bit_index & 1
        gathered = jnp.where(
            upper_bit == 1,
            jnp.concatenate([partner, gathered], 0),
            jnp.concatenate([gathered, partner], 0),
        )
    preact = (
        jnp.dot(gathered, encoder[0], preferred_element_type=jnp.float32) + encoder_bias[0][None, :]
    )
    features = jax.nn.relu(preact).astype(jnp.bfloat16)
    tok_count = features.shape[0]
    every_layer = lax.all_gather(features[None], "layer", axis=0, tiled=True)
    by_layer = every_layer.reshape(L_WIN, groups, tok_count, features.shape[1])
    mine_only = lax.dynamic_index_in_dim(by_layer, group_index, 1, keepdims=False)
    flipped = mine_only[::-1]
    padded = jnp.concatenate([flipped, jnp.zeros_like(flipped)], 0)
    stacked = lax.dynamic_slice_in_dim(padded, L_WIN - 1 - target_layer, L_WIN, 0)
    rebuilt = jnp.einsum("ktf,kfd->td", stacked, decoder[0], preferred_element_type=jnp.float32)
    for bit_index in reversed(range(depth_bits)):
        half_rows = rebuilt.shape[0] // 2
        upper_bit = position >> bit_index & 1
        kept_half = jnp.where(upper_bit == 1, rebuilt[half_rows:], rebuilt[:half_rows])
        sent_half = jnp.where(upper_bit == 1, rebuilt[:half_rows], rebuilt[half_rows:])
        rebuilt = kept_half + from_partner(sent_half, "layer", bit_index)
    summed = lax.psum_scatter(rebuilt, "feat", scatter_dimension=1, tiled=True)
    residual = summed - targets[0]
    return residual[None]


def solution(mesh):
    placed = (
        P("layer", "feat", None),
        P("layer", None, "feat"),
        P("layer", None, "feat"),
        P("layer", "feat"),
        P("layer", None, "feat", None),
    )
    return jax.shard_map(
        on_device, mesh=mesh, in_specs=placed, out_specs=P("layer", None, "feat"), check_vma=False
    )
```

profile of v0, /device:TPU:2, one launch (start us, length us, event | category | flops | bytes accessed | tf_op | source)
XLA Modules:
  0.0 334.1 jit_solution(2689262815551460917)
XLA Ops:
  6.5 0.0 all-gather.5.cloned.1.call-start
  6.5 0.7 all-gather.5.cloned.1.call-update
  7.3 0.0 all-gather.7.cloned.1.call-start
  7.3 52.7 %all-gather.5.cloned.1.call-done = bf16[1,512,2048]{2,1,0:T(8,128)(2,1)} async-done(((bf16[1,64,2048]{2,1,0:T(8,128)(2,1)}), bf16[1,512,2048]{2,1,0:T(8,128)(2,1)}) %all-gather.5.cloned.1.call-update) | async-done | bytes 2097168 | tf_op jit(solution)/shard_map/all_gather | solution.py:19
  60.0 14.4 %maximum_convert_fusion = bf16[512,4096]{1,0:T(8,128)(2,1)} fusion(bf16[1,2048,4096]{2,1,0:T(8,128)(2,1)} %param.7, f32[4096]{0:T(1024)} %bitcast.24, bf16[1,512,2048]{2,1,0:T(8,128)(2,1)} %all-gather.5.cloned.1.call-done), kind=kOutput, calls=%fused_computation.5 | convolution fusion | flops 8596226048 | bytes 23085056 | tf_op jit(solution)/shard_map/dot_general | solution.py:29
  74.4 0.0 all-gather.7.cloned.1.call-update
  74.4 0.0 reduce-scatter.2.cloned.1.call-start
  74.5 103.4 %all-gather.7.cloned.1.call-done = bf16[2048,4096]{1,0:T(8,128)(2,1)} async-done(((bf16[512,4096]{1,0:T(8,128)(2,1)}), bf16[2048,4096]{1,0:T(8,128)(2,1)}) %all-gather.7.cloned.1.call-update) | async-done | bytes 16777232 | tf_op jit(solution)/shard_map/all_gather | solution.py:33
  177.9 14.0 %rev.3 = bf16[4,512,4096]{2,1,0:T(8,128)(2,1)} reverse(bf16[4,512,4096]{2,1,0:T(8,128)(2,1)} %bitcast.23), dimensions={0} | reverse | bytes 33554432 | tf_op jit(solution)/shard_map/rev | solution.py:36
  191.8 0.0 copy-start
  191.8 44.1 %fusion.6 = f32[512,2048]{1,0:T(8,128)} fusion(bf16[1,4,4096,2048]{3,2,1,0:T(8,128)(2,1)} %param.9, s32[]{:T(128)S(6)} %select_n.12, bf16[4,512,4096]{2,1,0:T(8,128)(2,1)} %rev.3), kind=kOutput, calls=%fused_computation.6 | convolution fusion | flops 34359738368 | bytes 88080384 | tf_op jit(solution)/shard_map/ktf,kfd->td/dot_general | solution.py:39
  235.9 0.0 reduce-scatter.2.cloned.1.call-update
  235.9 89.7 %reduce-scatter.2.cloned.1.call-done = f32[512,256]{1,0:T(8,128)} async-done(((f32[512,2048]{1,0:T(8,128)}), f32[512,256]{1,0:T(8,128)}) %reduce-scatter.2.cloned.1.call-update) | async-done | bytes 524304 | tf_op jit(solution)/shard_map/reduce_scatter | solution.py:46
  325.7 0.0 copy-done
  325.7 1.9 fusion.10
Async XLA Ops:
  6.5 53.5 %all-gather.5.cloned.1.call-start = ((), (), s32[]{:S(2)}) async-start(), calls=%async_computation.2 | async-start | bytes 2359296 | tf_op jit(solution)/shard_map/all_gather | solution.py:19
  7.3 170.6 %all-gather.7.cloned.1.call-start = ((), (), s32[]{:S(2)}) async-start(), calls=%async_computation.3 | async-start | bytes 20971520 | tf_op jit(solution)/shard_map/all_gather | solution.py:33
  74.4 251.2 %reduce-scatter.2.cloned.1.call-start = ((), (), s32[]{:S(2)}) async-start(), calls=%async_computation.1 | async-start | bytes 4718592 | tf_op jit(solution)/shard_map/reduce_scatter | solution.py:46
  191.8 133.8 %copy-start = (f32[1,512,256]{2,1,0:T(8,128)S(1)}, f32[1,512,256]{2,1,0:T(8,128)}, u32[]{:S(2)}) copy-start(f32[1,512,256]{2,1,0:T(8,128)} %param.6) | copy-start | bytes 1572868
Sparse Core Ops, SparseCore 0:
  9.5 50.5 all-gather.4
  74.6 103.2 all-gather.6
  236.0 89.5 reduce-scatter.1
where the time goes:
time: 336 us; the launch traced here: 334 us
  waiting for transfers between devices  247 us (74%)
  matrix products  58.5 us (17%)
  local copies, waits for them, and re-layouts  14 us (4%)
  between operations  13.1 us (4%)
    all_gather x1, waiting for transfers between devices, on_device(): every_layer = lax.all_gather(features[None], 'layer', axis=0, tiled=True)  103 us
    reduce_scatter x1, waiting for transfers between devices, on_device(): summed = lax.psum_scatter(rebuilt, 'feat', scatter_dimension=1, tiled=True)  89.7 us
    all_gather x1, waiting for transfers between devices, on_device(): gathered = lax.all_gather(layer_inputs[0], 'feat', axis=0, tiled=True)  52.7 us
    dot_general x1, matrix products, on_device(): jnp.einsum('ktf,kfd->td', stacked, decoder[0], preferred_element_type=jnp...  44.1 us
    dot_general x1, matrix products, on_device(): jnp.dot(gathered, encoder[0], preferred_element_type=jnp.float32)  14.4 us
    rev x1, local copies, waits for them, and re-layouts, on_device(): flipped = mine_only[::-1]  14 us
  transfers between devices with their start and end apart: 3, of which 3 were waited for; matrix products, arithmetic and copies ran while one was open for 0% of the time, Pallas kernels for 0%

commit v1 on v0

--- a/solution.py
+++ b/solution.py
@@ -1,16 +1,296 @@
+import functools
+
 import jax
 import jax.numpy as jnp
 from jax import lax
+from jax.experimental import pallas as pl
+from jax.experimental.pallas import tpu as pltpu
 from jax.sharding import PartitionSpec as P
 
 L_WIN = 4
-
-
-def from_partner(array, axis, stride):
-    return lax.ppermute(array, axis, [(i, i ^ 1 << stride) for i in range(lax.axis_size(axis))])
-
-
-def on_device(layer_inputs, targets, encoder, encoder_bias, decoder):
+VMEM_BYTES = 56 * 1024 * 1024
+
+
+def exchange(array, axis, flip):
+    size = lax.axis_size(axis)
+    return lax.ppermute(array, axis, [(i, i ^ flip) for i in range(size)])
+
+
+def load_rows(parts, dest, sems):
+    copies = []
+    row = 0
+    for i, part in enumerate(parts):
+        rows = part.shape[0]
+        copies.append(pltpu.make_async_copy(part, dest.at[pl.ds(row, rows)], sems.at[i]))
+        row += rows
+    for copy in copies:
+        copy.start()
+    for copy in copies:
+        copy.wait()
+
+
+def encode_kernel(n_in, n_out, *refs):
+    parts, refs = refs[:n_in], refs[n_in:]
+    weight, bias, refs = refs[0], refs[1], refs[3:]
+    outs, (tokens, sems) = refs[:n_out], refs[n_out:]
+
+    @pl.when(pl.program_id(0) == 0)
+    def _():
+        load_rows(parts, tokens, sems)
+
+    preact = jnp.dot(tokens[...], weight[0], preferred_element_type=jnp.float32) + bias[...]
+    acts = jnp.maximum(preact, 0.0).astype(jnp.bfloat16)
+    row = 0
+    for out in outs:
+        out[...] = acts[row : row + out.shape[0]]
+        row += out.shape[0]
+
+
+def encode(parts, out_rows, weight, bias, after):
+    rows = sum(part.shape[0] for part in parts)
+    _, width, features = weight.shape
+    block = min(512, features)
+    anywhere = pl.BlockSpec(memory_space=pl.ANY)
+    return pl.pallas_call(
+        functools.partial(encode_kernel, len(parts), len(out_rows)),
+        grid=(features // block,),
+        in_specs=[anywhere] * len(parts)
+        + [
+            pl.BlockSpec((1, width, block), lambda j: (0, 0, j)),
+            pl.BlockSpec((1, block), lambda j: (0, j)),
+            anywhere,
+        ],
+        out_specs=[pl.BlockSpec((n, block), lambda j: (0, j)) for n in out_rows],
+        out_shape=[jax.ShapeDtypeStruct((n, features), jnp.bfloat16) for n in out_rows],
+        scratch_shapes=[
+            pltpu.VMEM((rows, width), jnp.bfloat16),
+            pltpu.SemaphoreType.DMA((len(parts),)),
+        ],
+        compiler_params=pltpu.CompilerParams(vmem_limit_bytes=VMEM_BYTES),
+        name="encode",
+    )(*parts, weight, bias, after)
+
+
+def own_kernel(n_parts, info, *refs):
+    mine, theirs, refs = refs[:n_parts], refs[n_parts : 2 * n_parts], refs[2 * n_parts :]
+    w_mine, w_theirs, out, a_mine, a_theirs, sems = refs
+    first = pl.program_id(0) == 0
+    has_neighbour = info[1] == 1
+
+    @pl.when(first)
+    def _():
+        load_rows(mine, a_mine, sems)
+
+    @pl.when(first & has_neighbour)
+    def _():
+        load_rows(theirs, a_theirs, sems)
+
+    out[...] = jnp.dot(a_mine[...], w_mine[0, 0], preferred_element_type=jnp.float32)
+
+    @pl.when(has_neighbour)
+    def _():
+        out[...] += jnp.dot(a_theirs[...], w_theirs[0, 0], preferred_element_type=jnp.float32)
+
+
+def decode_own(info, mine, theirs, decoder, shards):
+    rows = sum(part.shape[0] for part in mine)
+    _, _, features, width = decoder.shape
+    cols = width // shards
+    anywhere = pl.BlockSpec(memory_space=pl.ANY)
+    return pl.pallas_call(
+        functools.partial(own_kernel, len(mine)),
+        grid_spec=pltpu.PrefetchScalarGridSpec(
+            num_scalar_prefetch=1,
+            grid=(shards,),
+            in_specs=[anywhere] * (2 * len(mine))
+            + [
+                pl.BlockSpec((1, 1, features, cols), lambda j, info: (0, 0, 0, info[0] ^ j)),
+                pl.BlockSpec(
+                    (1, 1, features, cols), lambda j, info: (0, info[1], 0, info[0] ^ (j * info[1]))
+                ),
+            ],
+            out_specs=pl.BlockSpec((rows, cols), lambda j, info: (0, j)),
+            scratch_shapes=[
+                pltpu.VMEM((rows, features), jnp.bfloat16),
+                pltpu.VMEM((rows, features), jnp.bfloat16),
+                pltpu.SemaphoreType.DMA((len(mine),)),
+            ],
+        ),
+        out_shape=jax.ShapeDtypeStruct((rows, width), jnp.float32),
+        compiler_params=pltpu.CompilerParams(vmem_limit_bytes=VMEM_BYTES),
+        name="decode_own",
+    )(info, *mine, *theirs, decoder, decoder)
+
+
+def crossed_kernel(n_parts, shards, info, *refs):
+    direct, swapped, refs = refs[:n_parts], refs[n_parts : 2 * n_parts], refs[2 * n_parts :]
+    w_direct, w_swapped, base, refs = refs[0], refs[1], refs[2], refs[4:]
+    outs, (a_direct, a_swapped, sems) = refs[:shards], refs[shards:]
+    step = pl.program_id(0)
+    has_crossed = info[2] == 1
+
+    @pl.when((step == 0) & has_crossed)
+    def _():
+        load_rows(direct, a_direct, sems)
+        load_rows(swapped, a_swapped, sems)
+
+    def store(value):
+        for r, out in enumerate(outs):
+
+            @pl.when(step == r)
+            def _():
+                out[...] = value.astype(out.dtype)
+
+    @pl.when(has_crossed)
+    def _():
+        store(
+            base[...]
+            + jnp.dot(a_direct[...], w_direct[0, 0], preferred_element_type=jnp.float32)
+            + jnp.dot(a_swapped[...], w_swapped[0, 0], preferred_element_type=jnp.float32)
+        )
+
+    @pl.when(jnp.logical_not(has_crossed))
+    def _():
+        store(base[...])
+
+
+def decode_crossed(info, direct, swapped, decoder, base, row, shards, after):
+    rows = sum(part.shape[0] for part in direct)
+    _, _, features, width = decoder.shape
+    cols = width // shards
+    at = row // rows
+    anywhere = pl.BlockSpec(memory_space=pl.ANY)
+    return pl.pallas_call(
+        functools.partial(crossed_kernel, len(direct), shards),
+        grid_spec=pltpu.PrefetchScalarGridSpec(
+            num_scalar_prefetch=1,
+            grid=(shards,),
+            in_specs=[anywhere] * (2 * len(direct))
+            + [
+                pl.BlockSpec(
+                    (1, 1, features, cols), lambda j, info: (0, info[3], 0, info[0] ^ (j * info[2]))
+                ),
+                pl.BlockSpec(
+                    (1, 1, features, cols), lambda j, info: (0, info[4], 0, info[0] ^ (j * info[2]))
+                ),
+                pl.BlockSpec((rows, cols), lambda j, info: (at, j)),
+                anywhere,
+            ],
+            out_specs=[pl.BlockSpec((rows, cols), lambda j, info: (0, 0))] * shards,
+            scratch_shapes=[
+                pltpu.VMEM((rows, features), jnp.bfloat16),
+                pltpu.VMEM((rows, features), jnp.bfloat16),
+                pltpu.SemaphoreType.DMA((len(direct),)),
+            ],
+        ),
+        out_shape=[
+            jax.ShapeDtypeStruct((rows, cols), jnp.float32 if r == 0 else jnp.bfloat16)
+            for r in range(shards)
+        ],
+        compiler_params=pltpu.CompilerParams(vmem_limit_bytes=VMEM_BYTES),
+        name="decode_crossed",
+    )(info, *direct, *swapped, decoder, decoder, base, after)
+
+
+def sum_kernel(blocks, sign, info, base, *refs):
+    received, out = refs[:-1], refs[-1]
+    me = info[0]
+    out[...] = sign * base[...]
+    for (source, slot), ref in zip(blocks, received):
+        size = ref.shape[0] // len(slot)
+        for k, s in enumerate(slot):
+            at = pl.ds(pl.multiple_of((me ^ (source ^ s)) * size, size), size)
+            out[at, :] += ref[pl.ds(k * size, size), :].astype(jnp.float32)
+
+
+def add_up(info, base, sign, blocks, received):
+    whole = lambda array: pl.BlockSpec(array.shape, lambda i, info: (0, 0))
+    return pl.pallas_call(
+        functools.partial(sum_kernel, blocks, sign),
+        grid_spec=pltpu.PrefetchScalarGridSpec(
+            num_scalar_prefetch=1,
+            grid=(1,),
+            in_specs=[whole(base)] + [whole(array) for array in received],
+            out_specs=whole(base),
+        ),
+        out_shape=jax.ShapeDtypeStruct(base.shape, base.dtype),
+        compiler_params=pltpu.CompilerParams(vmem_limit_bytes=VMEM_BYTES),
+        name="add_up",
+    )(info, base, *received)
+
+
+def pipelined(layer_inputs, targets, encoder, encoder_bias, decoder):
+    shards = lax.axis_size("feat")
+    layers = lax.axis_size("layer")
+    half = layers // 2
+    layer = lax.axis_index("layer")
+    feat = lax.axis_index("feat")
+    upper = layer >= half
+    source = jnp.where(upper, layer - half, 0)
+    other = jnp.where(upper, (layer ^ 1) - half, 0)
+    info = jnp.stack(
+        [
+            feat,
+            layer & 1,
+            upper.astype(jnp.int32),
+            jnp.where(upper, layer - source, 0),
+            jnp.where(upper, layer - other, 0),
+        ]
+    ).astype(jnp.int32)
+
+    tokens = layer_inputs[0]
+    size = tokens.shape[0]
+    mid = shards // 2
+    groups = [[0], [1], list(range(2, mid)), list(range(mid, shards - 2)), [shards - 2], [shards - 1]]
+    calls = [[0], [1], [2], [3, 4, 5]]
+    waves = [[0, 1, 2], [3], [4], [5]]
+
+    inputs = [tokens] + [exchange(tokens, "feat", s) for s in range(1, shards)]
+    acts = []
+    after = tokens
+    for call in calls:
+        parts = [inputs[s] for g in call for s in groups[g]]
+        rows = [len(groups[g]) * size for g in call]
+        acts += encode(parts, rows, encoder, encoder_bias, after)
+        after = acts[-1]
+
+    up = [(i, i + half) for i in range(half)]
+    across = [(i, i ^ 1) for i in range(half, layers)]
+    beside = [(i, i + 1) for i in range(0, layers, 2)]
+    direct = [lax.ppermute(a, "layer", up) for a in acts]
+    neighbour = [lax.ppermute(a, "layer", beside) for a in acts]
+    swapped = [lax.ppermute(a, "layer", across) for a in direct]
+
+    base = decode_own(info, acts, neighbour, decoder, shards)
+    total = targets[0]
+    sign = -1.0
+    row = 0
+    after = base
+    blocks, received = [], []
+    for number, wave in enumerate(waves):
+        slots = [s for g in wave for s in groups[g]]
+        partial = decode_crossed(
+            info,
+            [direct[g] for g in wave],
+            [swapped[g] for g in wave],
+            decoder,
+            base,
+            row,
+            shards,
+            after,
+        )
+        after = partial[0]
+        row += len(slots) * size
+        if number == len(waves) - 1:
+            total = add_up(info, total, sign, blocks, received)
+            sign, blocks, received = 1.0, [], []
+        for r, part in enumerate(partial):
+            blocks.append((r, slots))
+            received.append(part if r == 0 else exchange(part, "feat", r))
+    return add_up(info, total, sign, blocks, received)[None]
+
+
+def grouped(layer_inputs, targets, encoder, encoder_bias, decoder):
     groups = lax.axis_size("layer") // L_WIN
     depth_bits = groups.bit_length() - 1
     position = lax.axis_index("layer")
@@ -18,7 +298,7 @@
     group_index = position % groups
     gathered = lax.all_gather(layer_inputs[0], "feat", axis=0, tiled=True)
     for bit_index in range(depth_bits):
-        partner = from_partner(gathered, "layer", bit_index)
+        partner = exchange(gathered, "layer", 1 << bit_index)
         upper_bit = position >> bit_index & 1
         gathered = jnp.where(
             upper_bit == 1,
@@ -42,7 +322,7 @@
         upper_bit = position >> bit_index & 1
         kept_half = jnp.where(upper_bit == 1, rebuilt[half_rows:], rebuilt[:half_rows])
         sent_half = jnp.where(upper_bit == 1, rebuilt[:half_rows], rebuilt[half_rows:])
-        rebuilt = kept_half + from_partner(sent_half, "layer", bit_index)
+        rebuilt = kept_half + exchange(sent_half, "layer", 1 << bit_index)
     summed = lax.psum_scatter(rebuilt, "feat", scatter_dimension=1, tiled=True)
     residual = summed - targets[0]
     return residual[None]
@@ -56,6 +336,12 @@
         P("layer", "feat"),
         P("layer", None, "feat", None),
     )
+    shards = mesh.shape["feat"]
+    simple = mesh.shape["layer"] == L_WIN and shards >= 8 and shards & (shards - 1) == 0
     return jax.shard_map(
-        on_device, mesh=mesh, in_specs=placed, out_specs=P("layer", None, "feat"), check_vma=False
+        pipelined if simple else grouped,
+        mesh=mesh,
+        in_specs=placed,
+        out_specs=P("layer", None, "feat"),
+        check_vma=False,
     )

time: 336 us -> 336 us (level); the launches traced: 334 us -> 330 us
  waiting for transfers between devices: 247 us -> 93.1 us
  Pallas kernels: 0 us -> 148 us
  starting transfers between devices: 0.08 us -> 83.6 us
  matrix products: 58.5 us -> 0 us
  between operations: 13.1 us -> 1.12 us
  local copies, waits for them, and re-layouts: 14 us -> 4.13 us
    all_gather x2 -> x0, waiting for transfers between devices: 156 us -> none  [the longest x1 103 us: on_device(): every_layer = lax.all_gather(features[None], 'layer', axis=0, tiled=True)]
    pallas_call x0 -> x11, Pallas kernels: none -> 148 us  [the longest x4 77.1 us: decode_crossed(): pl.pallas_call(functools.partial(crossed_kernel, len(direct), shards), gr...]
    ppermute x0 -> x53, waiting for transfers between devices: none -> 93.1 us  [the longest x6 69.2 us: pipelined(): direct = [lax.ppermute(a, 'layer', up) for a in acts]]
    reduce_scatter x1 -> x0, waiting for transfers between devices: 89.7 us -> none  [on_device(): summed = lax.psum_scatter(rebuilt, 'feat', scatter_dimension=1, tiled=True)]
    ppermute x0 -> x53, starting transfers between devices: none -> 83.6 us  [the longest x35 54.5 us: exchange(): return lax.ppermute(array, axis, [(i, i ^ flip) for i in range(size)])]
    dot_general x2 -> x0, matrix products: 58.5 us -> none  [the longest x1 44.1 us: on_device(): jnp.einsum('ktf,kfd->td', stacked, decoder[0], preferred_element_type=jnp...]
    rev x1 -> x0, local copies, waits for them, and re-layouts: 14 us -> none  [on_device(): flipped = mine_only[::-1]]
    unnamed x2 -> x138, local copies, waits for them, and re-layouts: 0.01 us -> 3.48 us
  transfers between devices with their start and end apart: 3 -> 53, of which waited for: 3 -> 10; matrix products, arithmetic and copies ran while one was open for 0% -> 0% of each run, Pallas kernels for 0% -> 38%
where the time goes in v1:
time: 336 us; the launch traced here: 330 us
  Pallas kernels  148 us (44%)
  waiting for transfers between devices  93.1 us (28%)
  starting transfers between devices  83.6 us (25%)
  local copies, waits for them, and re-layouts  4.13 us (1%)
    pallas_call x4, Pallas kernels, decode_crossed(): pl.pallas_call(functools.partial(crossed_kernel, len(direct), shards), gr...  77.1 us
    ppermute x6, waiting for transfers between devices, pipelined(): direct = [lax.ppermute(a, 'layer', up) for a in acts]  69.2 us
    ppermute x35, starting transfers between devices, exchange(): return lax.ppermute(array, axis, [(i, i ^ flip) for i in range(size)])  54.5 us
    pallas_call x4, Pallas kernels, encode(): pl.pallas_call(functools.partial(encode_kernel, len(parts), len(out_rows)...  46.7 us
    ppermute x35, waiting for transfers between devices, exchange(): return lax.ppermute(array, axis, [(i, i ^ flip) for i in range(size)])  23.9 us
    pallas_call x1, Pallas kernels, decode_own(): pl.pallas_call(functools.partial(own_kernel, len(mine)), grid_spec=pltpu....  18.1 us
    ppermute x6, starting transfers between devices, pipelined(): swapped = [lax.ppermute(a, 'layer', across) for a in direct]  13.2 us
    ppermute x6, starting transfers between devices, pipelined(): neighbour = [lax.ppermute(a, 'layer', beside) for a in acts]  8.11 us
  transfers between devices with their start and end apart: 53, of which 10 were waited for; matrix products, arithmetic and copies ran while one was open for 0% of the time, Pallas kernels for 38%

profile of v1, /device:TPU:2, one launch (start us, length us, event | category | flops | bytes accessed | tf_op | source)
XLA Modules:
  0.0 330.1 jit_solution(15301956639014752957)
XLA Ops:
  3.5 3.5 %collective-permute-start.10 = (bf16[64,2048]{1,0:T(8,128)(2,1)}, bf16[64,2048]{1,0:T(8,128)(2,1)S(1)}, u32[]{:S(2)}, u32[]{:S(2)}) collective-permute-start(bf16[64,2048]{1,0:T(8,128)(2,1)} %bitcast.11), channel_id=1, source_target_pairs={{0,5},{1,4},{2,7},{3,6},{4,1},{5,0},{6,3},{7,2},{8,13},{9,12},{10,... | collective-permute-start | bytes 786440 | tf_op jit(solution)/shard_map/ppermute | solution.py:16
  8.4 5.2 %collective-permute-done.1.refs_0_ = bf16[64,2048]{1,0:T(8,128)(2,1)S(1)} collective-permute-done((bf16[64,2048]{1,0:T(8,128)(2,1)}, bf16[64,2048]{1,0:T(8,128)(2,1)S(1)}, u32[]{:S(2)}, u32[]{:S(2)}) %collective-permute-start.1) | collective-permute-done | bytes 262176 | tf_op jit(solution)/shard_map/ppermute | solution.py:16
  13.6 4.5 %collective-permute-start.12 = (bf16[64,2048]{1,0:T(8,128)(2,1)}, bf16[64,2048]{1,0:T(8,128)(2,1)S(1)}, u32[]{:S(2)}, u32[]{:S(2)}) collective-permute-start(bf16[64,2048]{1,0:T(8,128)(2,1)} %bitcast.13), channel_id=1, source_target_pairs={{0,7},{1,6},{2,5},{3,4},{4,3},{5,2},{6,1},{7,0},{8,15},{9,14},{10,... | collective-permute-start | bytes 786440 | tf_op jit(solution)/shard_map/ppermute | solution.py:16
  18.2 11.3 %encode.4.refs_3_.refs_0_ = bf16[64,4096]{1,0:T(8,128)(2,1)} custom-call(bf16[64,2048]{1,0:T(8,128)(2,1)} %bitcast.15, bf16[1,2048,4096]{2,1,0:T(8,128)(2,1)} %refs_4_.1, f32[1,4096]{1,0:T(1,128)} %refs_5_.1, bf16[64,2048]{1,0:T(8,128)(2,1)} %bitcast.16), custom_call_target="tpu_custom_call" | custom-call | tf_op jit(solution)/shard_map/encode/pallas_call | solution.py:54
  29.5 11.3 %encode.5.refs_4_.refs_1_ = bf16[64,4096]{1,0:T(8,128)(2,1)} custom-call(bf16[64,2048]{1,0:T(8,128)(2,1)} %copy-done.19, bf16[1,2048,4096]{2,1,0:T(8,128)(2,1)} %refs_4_.1, f32[1,4096]{1,0:T(1,128)} %refs_5_.1, bf16[64,4096]{1,0:T(8,128)(2,1)} %encode.4.refs_3_.refs_0_), custom_call_target="tpu_custom_call" | custom-call | tf_op jit(solution)/shard_map/encode/pallas_call | solution.py:54
  42.4 11.4 %encode.6.refs_6_.refs_2_ = bf16[128,4096]{1,0:T(8,128)(2,1)} custom-call(bf16[64,2048]{1,0:T(8,128)(2,1)} %copy-done.16, bf16[64,2048]{1,0:T(8,128)(2,1)} %copy-done.18, bf16[1,2048,4096]{2,1,0:T(8,128)(2,1)} %refs_4_.1, f32[1,4096]{1,0:T(1,128)} %refs_5_.1, bf16[64,4096]{1,0:T(8,128)(2,1)} %encode.5.refs_4_.refs_1_), custom_call_target="tpu_custom_call" | custom-call | tf_op jit(solution)/shard_map/encode/pallas_call | solution.py:54
  56.8 12.8 %encode.7 = (bf16[128,4096]{1,0:T(8,128)(2,1)}, bf16[64,4096]{1,0:T(8,128)(2,1)}, bf16[64,4096]{1,0:T(8,128)(2,1)}) custom-call(bf16[64,2048]{1,0:T(8,128)(2,1)} %copy-done.17, bf16[64,2048]{1,0:T(8,128)(2,1)} %copy-done.13, bf16[64,2048]{1,0:T(8,128)(2,1)} %copy-done.14, bf16[64,2048]{1,0:T(8,128)(2,1)} %copy-done.15, bf16[1,2048,4096]{2,1,0:T(8,128)(2,1)} %refs_4_.1, ...), custom_call_target="tpu_custom_call" | custom-call | tf_op jit(solution)/shard_map/encode/pallas_call | solution.py:54
  80.1 55.3 %collective-permute-done.2.refs_1_ = bf16[64,4096]{1,0:T(8,128)(2,1)} collective-permute-done((bf16[64,4096]{1,0:T(8,128)(2,1)S(1)}, bf16[64,4096]{1,0:T(8,128)(2,1)}, u32[]{:S(2)}, u32[]{:S(2)}) %collective-permute-start.2) | collective-permute-done | bytes 524320 | tf_op jit(solution)/shard_map/ppermute | solution.py:260
  136.7 9.7 %collective-permute-done.35.refs_0_ = bf16[64,4096]{1,0:T(8,128)(2,1)} collective-permute-done((bf16[64,4096]{1,0:T(8,128)(2,1)}, bf16[64,4096]{1,0:T(8,128)(2,1)}, u32[]{:S(2)}, u32[]{:S(2)}) %collective-permute-start.35) | collective-permute-done | bytes 524320 | tf_op jit(solution)/shard_map/ppermute | solution.py:260
  147.8 4.3 %collective-permute-done.44.refs_0_ = bf16[64,4096]{1,0:T(8,128)(2,1)} collective-permute-done((bf16[64,4096]{1,0:T(8,128)(2,1)}, bf16[64,4096]{1,0:T(8,128)(2,1)}, u32[]{:S(2)}, u32[]{:S(2)}) %collective-permute-start.44) | collective-permute-done | bytes 524320 | tf_op jit(solution)/shard_map/ppermute | solution.py:260
  154.0 2.4 collective-permute-start.8
  158.4 2.4 collective-permute-start.7
  162.8 2.6 collective-permute-start.45
  166.1 18.1 %decode_own.1.refs_8_.refs_9_.refs_4_ = f32[512,2048]{1,0:T(8,128)} custom-call(s32[5]{0:T(128)} %stack.27.info, bf16[64,4096]{1,0:T(8,128)(2,1)} %encode.4.refs_3_.refs_0_, bf16[64,4096]{1,0:T(8,128)(2,1)} %encode.5.refs_4_.refs_1_, bf16[128,4096]{1,0:T(8,128)(2,1)} %encode.6.refs_6_.refs_2_, bf16[128,4096]{1,0:T(8,128)(2,1)} %get-tuple-element.40.refs_3_, ...), custom_call_target="tpu_custom_call" | custom-call | tf_op jit(solution)/shard_map/decode_own/pallas_call | solution.py:100
  184.3 21.5 %decode_crossed.4 = (f32[256,256]{1,0:T(8,128)}, bf16[256,256]{1,0:T(8,128)(2,1)}, bf16[256,256]{1,0:T(8,128)(2,1)}, bf16[256,256]{1,0:T(8,128)(2,1)}, bf16[256,...) custom-call(s32[5]{0:T(128)} %stack.27.info, ...), custom_call_target="tpu_custom_call" | custom-call | tf_op jit(solution)/shard_map/decode_crossed/pallas_call | solution.py:163
  206.8 18.5 %decode_crossed.5 = (f32[128,256]{1,0:T(8,128)}, bf16[128,256]{1,0:T(8,128)(2,1)}, bf16[128,256]{1,0:T(8,128)(2,1)}, bf16[128,256]{1,0:T(8,128)(2,1)}, bf16[128,...) custom-call(s32[5]{0:T(128)} %stack.27.info, ...), custom_call_target="tpu_custom_call" | custom-call | tf_op jit(solution)/shard_map/decode_crossed/pallas_call | solution.py:163
  225.3 18.5 %decode_crossed.6 = (f32[64,256]{1,0:T(8,128)}, bf16[64,256]{1,0:T(8,128)(2,1)}, bf16[64,256]{1,0:T(8,128)(2,1)}, bf16[64,256]{1,0:T(8,128)(2,1)}, bf16[64,256]{...) custom-call(s32[5]{0:T(128)} %stack.27.info, ...), custom_call_target="tpu_custom_call" | custom-call | tf_op jit(solution)/shard_map/decode_crossed/pallas_call | solution.py:163
  244.0 18.6 %decode_crossed.7 = (f32[64,256]{1,0:T(8,128)}, bf16[64,256]{1,0:T(8,128)(2,1)}, bf16[64,256]{1,0:T(8,128)(2,1)}, bf16[64,256]{1,0:T(8,128)(2,1)}, bf16[64,256]{...) custom-call(s32[5]{0:T(128)} %stack.27.info, ...), custom_call_target="tpu_custom_call" | custom-call | tf_op jit(solution)/shard_map/decode_crossed/pallas_call | solution.py:163
  263.2 2.9 collective-permute-start.47
  271.6 2.5 collective-permute-start.41
  274.5 4.6 %collective-permute-start.43 = (bf16[64,256]{1,0:T(8,128)(2,1)S(1)}, bf16[64,256]{1,0:T(8,128)(2,1)S(1)}, u32[]{:S(2)}, u32[]{:S(2)}) collective-permute-start(bf16[64,256]{1,0:T(8,128)(2,1)S(1)} %copy-done.62), channel_id=1, source_target_pairs={{0,7},{1,6},{2,5},{3,4},{4,3},{5,2},{6,1},{7,0},{8,15},{9,14},{10,... | collective-permute-start | bytes 98312 | tf_op jit(solution)/shard_map/ppermute | solution.py:16
  283.7 3.3 %collective-permute-start.32 = (bf16[128,256]{1,0:T(8,128)(2,1)S(1)}, bf16[128,256]{1,0:T(8,128)(2,1)S(1)}, u32[]{:S(2)}, u32[]{:S(2)}) collective-permute-start(bf16[128,256]{1,0:T(8,128)(2,1)S(1)} %copy-done.57), channel_id=1, source_target_pairs={{0,5},{1,4},{2,7},{3,6},{4,1},{5,0},{6,3},{7,2},{8,13},{9,12},{10,... | collective-permute-start | bytes 196616 | tf_op jit(solution)/shard_map/ppermute | solution.py:16
  287.8 4.2 %collective-permute-start.34 = (bf16[128,256]{1,0:T(8,128)(2,1)S(1)}, bf16[128,256]{1,0:T(8,128)(2,1)S(1)}, u32[]{:S(2)}, u32[]{:S(2)}) collective-permute-start(bf16[128,256]{1,0:T(8,128)(2,1)S(1)} %copy-done.55), channel_id=1, source_target_pairs={{0,7},{1,6},{2,5},{3,4},{4,3},{5,2},{6,1},{7,0},{8,15},{9,14},{10,... | collective-permute-start | bytes 196616 | tf_op jit(solution)/shard_map/ppermute | solution.py:16
  291.9 2.1 collective-permute-start.21
  297.4 2.4 collective-permute-start.24
  299.8 2.1 collective-permute-start.25
  302.7 6.8 %collective-permute-done.22.refs_4_ = bf16[256,256]{1,0:T(8,128)(2,1)S(1)} collective-permute-done((bf16[256,256]{1,0:T(8,128)(2,1)S(1)}, bf16[256,256]{1,0:T(8,128)(2,1)S(1)}, u32[]{:S(2)}, u32[]{:S(2)}) %collective-permute-start.22) | collective-permute-done | bytes 131104 | tf_op jit(solution)/shard_map/ppermute | solution.py:16
  309.5 6.4 %collective-permute-done.23.refs_5_ = bf16[256,256]{1,0:T(8,128)(2,1)S(1)} collective-permute-done((bf16[256,256]{1,0:T(8,128)(2,1)S(1)}, bf16[256,256]{1,0:T(8,128)(2,1)S(1)}, u32[]{:S(2)}, u32[]{:S(2)}) %collective-permute-start.23) | collective-permute-done | bytes 131104 | tf_op jit(solution)/shard_map/ppermute | solution.py:16
  318.3 3.4 %add_up.2.base = f32[512,256]{1,0:T(8,128)} custom-call(s32[5]{0:T(128)} %stack.27.info, f32[512,256]{1,0:T(8,128)} %bitcast.17, f32[256,256]{1,0:T(8,128)} %get-tuple-element.43.refs_5_.refs_0_, bf16[256,256]{1,0:T(8,128)(2,1)} %copy-done.20, bf16[256,256]{1,0:T(8,128)(2,1)} %copy-done.21, bf16[256,256]{1,0:T(8,128)(2,1)} %copy-done.22, ...), custom_call_target="tpu_custom_call" | custom-call | tf_op jit(solution)/shard_map/add_up/pallas_call | solution.py:208
  321.7 2.6 collective-permute-done.49.refs_4_
  324.3 2.4 collective-permute-done.50.refs_5_
  327.4 2.7 add_up.3
  (224 shorter events, 48.8 us)
Async XLA Ops:
  0.0 13.6 %collective-permute-start.1 = (bf16[64,2048]{1,0:T(8,128)(2,1)}, bf16[64,2048]{1,0:T(8,128)(2,1)S(1)}, u32[]{:S(2)}, u32[]{:S(2)}) collective-permute-start(bf16[64,2048]{1,0:T(8,128)(2,1)} %bitcast.8), channel_id=1, source_target_pairs={{0,1},{1,0},{2,3},{3,2},{4,5},{5,4},{6,7},{7,6},{8,9},{9,8},{10,11... | collective-permute-start | bytes 786440 | tf_op jit(solution)/shard_map/ppermute | solution.py:16
  1.5 16.5 %collective-permute-start.3 = (bf16[64,2048]{1,0:T(8,128)(2,1)}, bf16[64,2048]{1,0:T(8,128)(2,1)S(1)}, u32[]{:S(2)}, u32[]{:S(2)}) collective-permute-start(bf16[64,2048]{1,0:T(8,128)(2,1)} %bitcast.9), channel_id=1, source_target_pairs={{0,2},{1,3},{2,0},{3,1},{4,6},{5,7},{6,4},{7,5},{8,10},{9,11},{10,... | collective-permute-start | bytes 786440 | tf_op jit(solution)/shard_map/ppermute | solution.py:16
  3.1 37.8 %collective-permute-start.4 = (bf16[64,2048]{1,0:T(8,128)(2,1)}, bf16[64,2048]{1,0:T(8,128)(2,1)S(1)}, u32[]{:S(2)}, u32[]{:S(2)}) collective-permute-start(bf16[64,2048]{1,0:T(8,128)(2,1)} %bitcast.10), channel_id=1, source_target_pairs={{0,3},{1,2},{2,1},{3,0},{4,7},{5,6},{6,5},{7,4},{8,11},{9,10},{10,... | collective-permute-start | bytes 786440 | tf_op jit(solution)/shard_map/ppermute | solution.py:16
  3.5 50.3 %collective-permute-start.10 = (bf16[64,2048]{1,0:T(8,128)(2,1)}, bf16[64,2048]{1,0:T(8,128)(2,1)S(1)}, u32[]{:S(2)}, u32[]{:S(2)}) collective-permute-start(bf16[64,2048]{1,0:T(8,128)(2,1)} %bitcast.11), channel_id=1, source_target_pairs={{0,5},{1,4},{2,7},{3,6},{4,1},{5,0},{6,3},{7,2},{8,13},{9,12},{10,... | collective-permute-start | bytes 786440 | tf_op jit(solution)/shard_map/ppermute | solution.py:16
  7.0 48.2 %collective-permute-start.11 = (bf16[64,2048]{1,0:T(8,128)(2,1)}, bf16[64,2048]{1,0:T(8,128)(2,1)S(1)}, u32[]{:S(2)}, u32[]{:S(2)}) collective-permute-start(bf16[64,2048]{1,0:T(8,128)(2,1)} %bitcast.12), channel_id=1, source_target_pairs={{0,6},{1,7},{2,4},{3,5},{4,2},{5,3},{6,0},{7,1},{8,14},{9,15},{10,... | collective-permute-start | bytes 786440 | tf_op jit(solution)/shard_map/ppermute | solution.py:16
  13.6 41.7 %collective-permute-start.12 = (bf16[64,2048]{1,0:T(8,128)(2,1)}, bf16[64,2048]{1,0:T(8,128)(2,1)S(1)}, u32[]{:S(2)}, u32[]{:S(2)}) collective-permute-start(bf16[64,2048]{1,0:T(8,128)(2,1)} %bitcast.13), channel_id=1, source_target_pairs={{0,7},{1,6},{2,5},{3,4},{4,3},{5,2},{6,1},{7,0},{8,15},{9,14},{10,... | collective-permute-start | bytes 786440 | tf_op jit(solution)/shard_map/ppermute | solution.py:16
  18.1 37.2 %collective-permute-start.9 = (bf16[64,2048]{1,0:T(8,128)(2,1)}, bf16[64,2048]{1,0:T(8,128)(2,1)S(1)}, u32[]{:S(2)}, u32[]{:S(2)}) collective-permute-start(bf16[64,2048]{1,0:T(8,128)(2,1)} %bitcast.14), channel_id=1, source_target_pairs={{0,4},{1,5},{2,6},{3,7},{4,0},{5,1},{6,2},{7,3},{8,12},{9,13},{10,... | collective-permute-start | bytes 786440 | tf_op jit(solution)/shard_map/ppermute | solution.py:16
  40.9 32.6 %collective-permute-start.13 = (bf16[64,4096]{1,0:T(8,128)(2,1)S(1)}, bf16[64,4096]{1,0:T(8,128)(2,1)S(1)}, u32[]{:S(2)}, u32[]{:S(2)}) collective-permute-start(bf16[64,4096]{1,0:T(8,128)(2,1)S(1)} %copy-done.1), channel_id=1, source_target_pairs={{0,8},{16,24},{1,9},{17,25},{2,10},{18,26},{3,11},{19,27},{4,12},{... | collective-permute-start | bytes 1572872 | tf_op jit(solution)/shard_map/ppermute | solution.py:261
  53.8 21.0 %collective-permute-start = (bf16[64,4096]{1,0:T(8,128)(2,1)S(1)}, bf16[64,4096]{1,0:T(8,128)(2,1)S(1)}, u32[]{:S(2)}, u32[]{:S(2)}) collective-permute-start(bf16[64,4096]{1,0:T(8,128)(2,1)S(1)} %copy-done.1), channel_id=1, source_target_pairs={{0,16},{8,24},{1,17},{9,25},{2,18},{10,26},{3,19},{11,27},{4,20},{... | collective-permute-start | bytes 1572872 | tf_op jit(solution)/shard_map/ppermute | solution.py:260
  73.6 80.4 %collective-permute-start.5 = (bf16[128,4096]{1,0:T(8,128)(2,1)S(1)}, bf16[128,4096]{1,0:T(8,128)(2,1)}, u32[]{:S(2)}, u32[]{:S(2)}) collective-permute-start(bf16[128,4096]{1,0:T(8,128)(2,1)S(1)} %copy-done), channel_id=1, source_target_pairs={{0,16},{8,24},{1,17},{9,25},{2,18},{10,26},{3,19},{11,27},{4,20},{... | collective-permute-start | bytes 3145736 | tf_op jit(solution)/shard_map/ppermute | solution.py:260
  74.9 81.6 %collective-permute-start.26 = (bf16[128,4096]{1,0:T(8,128)(2,1)}, bf16[128,4096]{1,0:T(8,128)(2,1)S(1)}, u32[]{:S(2)}, u32[]{:S(2)}) collective-permute-start(bf16[128,4096]{1,0:T(8,128)(2,1)} %get-tuple-element.40.refs_3_), channel_id=1, source_target_pairs={{0,16},{8,24},{1,17},{9,25},{2,18},{10,26},{3,19},{11,27},{4,20},{... | collective-permute-start | bytes 3145736 | tf_op jit(solution)/shard_map/ppermute | solution.py:260
  76.2 59.2 %collective-permute-start.2 = (bf16[64,4096]{1,0:T(8,128)(2,1)S(1)}, bf16[64,4096]{1,0:T(8,128)(2,1)}, u32[]{:S(2)}, u32[]{:S(2)}) collective-permute-start(bf16[64,4096]{1,0:T(8,128)(2,1)S(1)} %copy-done.2), channel_id=1, source_target_pairs={{0,16},{8,24},{1,17},{9,25},{2,18},{10,26},{3,19},{11,27},{4,20},{... | collective-permute-start | bytes 1572872 | tf_op jit(solution)/shard_map/ppermute | solution.py:260
  77.5 69.0 %collective-permute-start.35 = (bf16[64,4096]{1,0:T(8,128)(2,1)}, bf16[64,4096]{1,0:T(8,128)(2,1)}, u32[]{:S(2)}, u32[]{:S(2)}) collective-permute-start(bf16[64,4096]{1,0:T(8,128)(2,1)} %get-tuple-element.41.refs_4_), channel_id=1, source_target_pairs={{0,16},{8,24},{1,17},{9,25},{2,18},{10,26},{3,19},{11,27},{4,20},{... | collective-permute-start | bytes 1572872 | tf_op jit(solution)/shard_map/ppermute | solution.py:260
  78.8 73.2 %collective-permute-start.44 = (bf16[64,4096]{1,0:T(8,128)(2,1)}, bf16[64,4096]{1,0:T(8,128)(2,1)}, u32[]{:S(2)}, u32[]{:S(2)}) collective-permute-start(bf16[64,4096]{1,0:T(8,128)(2,1)} %get-tuple-element.42.refs_5_), channel_id=1, source_target_pairs={{0,16},{8,24},{1,17},{9,25},{2,18},{10,26},{3,19},{11,27},{4,20},{... | collective-permute-start | bytes 1572872 | tf_op jit(solution)/shard_map/ppermute | solution.py:260
  135.4 25.4 %collective-permute-start.16 = (bf16[128,4096]{1,0:T(8,128)(2,1)}, bf16[128,4096]{1,0:T(8,128)(2,1)S(1)}, u32[]{:S(2)}, u32[]{:S(2)}) collective-permute-start(bf16[128,4096]{1,0:T(8,128)(2,1)} %get-tuple-element.40.refs_3_), channel_id=1, source_target_pairs={{0,8},{16,24},{1,9},{17,25},{2,10},{18,26},{3,11},{19,27},{4,12},{... | collective-permute-start | bytes 3145736 | tf_op jit(solution)/shard_map/ppermute | solution.py:261
  146.5 16.3 %collective-permute-start.15 = (bf16[128,4096]{1,0:T(8,128)(2,1)S(1)}, bf16[128,4096]{1,0:T(8,128)(2,1)S(1)}, u32[]{:S(2)}, u32[]{:S(2)}) collective-permute-start(bf16[128,4096]{1,0:T(8,128)(2,1)S(1)} %copy-done), channel_id=1, source_target_pairs={{0,8},{16,24},{1,9},{17,25},{2,10},{18,26},{3,11},{19,27},{4,12},{... | collective-permute-start | bytes 3145736 | tf_op jit(solution)/shard_map/ppermute | solution.py:261
  154.0 30.2 %collective-permute-start.8 = (bf16[128,4096]{1,0:T(8,128)(2,1)}, bf16[128,4096]{1,0:T(8,128)(2,1)}, u32[]{:S(2)}, u32[]{:S(2)}) collective-permute-start(bf16[128,4096]{1,0:T(8,128)(2,1)} %collective-permute-done.5.refs_2_), channel_id=1, source_target_pairs={{16,24},{24,16},{17,25},{25,17},{18,26},{26,18},{19,27},{27,19},{2... | collective-permute-start | bytes 3145736 | tf_op jit(solution)/shard_map/ppermute | solution.py:262
  156.4 49.3 %collective-permute-start.27 = (bf16[128,4096]{1,0:T(8,128)(2,1)S(1)}, bf16[128,4096]{1,0:T(8,128)(2,1)S(1)}, u32[]{:S(2)}, u32[]{:S(2)}) collective-permute-start(bf16[128,4096]{1,0:T(8,128)(2,1)S(1)} %collective-permute-done.26.refs_0_), channel_id=1, source_target_pairs={{16,24},{24,16},{17,25},{25,17},{18,26},{26,18},{19,27},{27,19},{2... | collective-permute-start | bytes 3145736 | tf_op jit(solution)/shard_map/ppermute | solution.py:262
  158.4 25.9 %collective-permute-start.7 = (bf16[64,4096]{1,0:T(8,128)(2,1)}, bf16[64,4096]{1,0:T(8,128)(2,1)}, u32[]{:S(2)}, u32[]{:S(2)}) collective-permute-start(bf16[64,4096]{1,0:T(8,128)(2,1)} %collective-permute-done.2.refs_1_), channel_id=1, source_target_pairs={{16,24},{24,16},{17,25},{25,17},{18,26},{26,18},{19,27},{27,19},{2... | collective-permute-start | bytes 1572872 | tf_op jit(solution)/shard_map/ppermute | solution.py:262
  160.8 64.4 %collective-permute-start.36 = (bf16[64,4096]{1,0:T(8,128)(2,1)}, bf16[64,4096]{1,0:T(8,128)(2,1)}, u32[]{:S(2)}, u32[]{:S(2)}) collective-permute-start(bf16[64,4096]{1,0:T(8,128)(2,1)} %collective-permute-done.35.refs_0_), channel_id=1, source_target_pairs={{16,24},{24,16},{17,25},{25,17},{18,26},{26,18},{19,27},{27,19},{2... | collective-permute-start | bytes 1572872 | tf_op jit(solution)/shard_map/ppermute | solution.py:262
  162.8 81.0 %collective-permute-start.45 = (bf16[64,4096]{1,0:T(8,128)(2,1)}, bf16[64,4096]{1,0:T(8,128)(2,1)}, u32[]{:S(2)}, u32[]{:S(2)}) collective-permute-start(bf16[64,4096]{1,0:T(8,128)(2,1)} %collective-permute-done.44.refs_0_), channel_id=1, source_target_pairs={{16,24},{24,16},{17,25},{25,17},{18,26},{26,18},{19,27},{27,19},{2... | collective-permute-start | bytes 1572872 | tf_op jit(solution)/shard_map/ppermute | solution.py:262
  269.6 13.3 %collective-permute-start.28 = (bf16[128,256]{1,0:T(8,128)(2,1)S(1)}, bf16[128,256]{1,0:T(8,128)(2,1)S(1)}, u32[]{:S(2)}, u32[]{:S(2)}) collective-permute-start(bf16[128,256]{1,0:T(8,128)(2,1)S(1)} %copy-done.61), channel_id=1, source_target_pairs={{0,1},{1,0},{2,3},{3,2},{4,5},{5,4},{6,7},{7,6},{8,9},{9,8},{10,11... | collective-permute-start | bytes 196616 | tf_op jit(solution)/shard_map/ppermute | solution.py:16
  281.6 15.8 %collective-permute-start.19 = (bf16[256,256]{1,0:T(8,128)(2,1)S(1)}, bf16[256,256]{1,0:T(8,128)(2,1)S(1)}, u32[]{:S(2)}, u32[]{:S(2)}) collective-permute-start(bf16[256,256]{1,0:T(8,128)(2,1)S(1)} %copy-done.54), channel_id=1, source_target_pairs={{0,1},{1,0},{2,3},{3,2},{4,5},{5,4},{6,7},{7,6},{8,9},{9,8},{10,11... | collective-permute-start | bytes 393224 | tf_op jit(solution)/shard_map/ppermute | solution.py:16
  282.9 16.9 %collective-permute-start.20 = (bf16[256,256]{1,0:T(8,128)(2,1)S(1)}, bf16[256,256]{1,0:T(8,128)(2,1)S(1)}, u32[]{:S(2)}, u32[]{:S(2)}) collective-permute-start(bf16[256,256]{1,0:T(8,128)(2,1)S(1)} %copy-done.53), channel_id=1, source_target_pairs={{0,2},{1,3},{2,0},{3,1},{4,6},{5,7},{6,4},{7,5},{8,10},{9,11},{10,... | collective-permute-start | bytes 393224 | tf_op jit(solution)/shard_map/ppermute | solution.py:16
  294.0 15.5 %collective-permute-start.22 = (bf16[256,256]{1,0:T(8,128)(2,1)S(1)}, bf16[256,256]{1,0:T(8,128)(2,1)S(1)}, u32[]{:S(2)}, u32[]{:S(2)}) collective-permute-start(bf16[256,256]{1,0:T(8,128)(2,1)S(1)} %copy-done.51), channel_id=1, source_target_pairs={{0,4},{1,5},{2,6},{3,7},{4,0},{5,1},{6,2},{7,3},{8,12},{9,13},{10,... | collective-permute-start | bytes 393224 | tf_op jit(solution)/shard_map/ppermute | solution.py:16
  295.4 20.4 %collective-permute-start.23 = (bf16[256,256]{1,0:T(8,128)(2,1)S(1)}, bf16[256,256]{1,0:T(8,128)(2,1)S(1)}, u32[]{:S(2)}, u32[]{:S(2)}) collective-permute-start(bf16[256,256]{1,0:T(8,128)(2,1)S(1)} %copy-done.50), channel_id=1, source_target_pairs={{0,5},{1,4},{2,7},{3,6},{4,1},{5,0},{6,3},{7,2},{8,13},{9,12},{10,... | collective-permute-start | bytes 393224 | tf_op jit(solution)/shard_map/ppermute | solution.py:16
  297.4 18.5 %collective-permute-start.24 = (bf16[256,256]{1,0:T(8,128)(2,1)S(1)}, bf16[256,256]{1,0:T(8,128)(2,1)S(1)}, u32[]{:S(2)}, u32[]{:S(2)}) collective-permute-start(bf16[256,256]{1,0:T(8,128)(2,1)S(1)} %copy-done.49), channel_id=1, source_target_pairs={{0,6},{1,7},{2,4},{3,5},{4,2},{5,3},{6,0},{7,1},{8,14},{9,15},{10,... | collective-permute-start | bytes 393224 | tf_op jit(solution)/shard_map/ppermute | solution.py:16
  299.8 17.8 %collective-permute-start.25 = (bf16[256,256]{1,0:T(8,128)(2,1)S(1)}, bf16[256,256]{1,0:T(8,128)(2,1)S(1)}, u32[]{:S(2)}, u32[]{:S(2)}) collective-permute-start(bf16[256,256]{1,0:T(8,128)(2,1)S(1)} %copy-done.48), channel_id=1, source_target_pairs={{0,7},{1,6},{2,5},{3,4},{4,3},{5,2},{6,1},{7,0},{8,15},{9,14},{10,... | collective-permute-start | bytes 393224 | tf_op jit(solution)/shard_map/ppermute | solution.py:16
  301.9 19.8 %collective-permute-start.48 = (bf16[64,256]{1,0:T(8,128)(2,1)}, bf16[64,256]{1,0:T(8,128)(2,1)S(1)}, u32[]{:S(2)}, u32[]{:S(2)}) collective-permute-start(bf16[64,256]{1,0:T(8,128)(2,1)} %get-tuple-element.70), channel_id=1, source_target_pairs={{0,3},{1,2},{2,1},{3,0},{4,7},{5,6},{6,5},{7,4},{8,11},{9,10},{10,... | collective-permute-start | bytes 98312 | tf_op jit(solution)/shard_map/ppermute | solution.py:16
  309.5 14.8 %collective-permute-start.49 = (bf16[64,256]{1,0:T(8,128)(2,1)}, bf16[64,256]{1,0:T(8,128)(2,1)S(1)}, u32[]{:S(2)}, u32[]{:S(2)}) collective-permute-start(bf16[64,256]{1,0:T(8,128)(2,1)} %get-tuple-element.71), channel_id=1, source_target_pairs={{0,4},{1,5},{2,6},{3,7},{4,0},{5,1},{6,2},{7,3},{8,12},{9,13},{10,... | collective-permute-start | bytes 98312 | tf_op jit(solution)/shard_map/ppermute | solution.py:16
  315.9 10.9 %collective-permute-start.50 = (bf16[64,256]{1,0:T(8,128)(2,1)}, bf16[64,256]{1,0:T(8,128)(2,1)S(1)}, u32[]{:S(2)}, u32[]{:S(2)}) collective-permute-start(bf16[64,256]{1,0:T(8,128)(2,1)} %get-tuple-element.72), channel_id=1, source_target_pairs={{0,5},{1,4},{2,7},{3,6},{4,1},{5,0},{6,3},{7,2},{8,13},{9,12},{10,... | collective-permute-start | bytes 98312 | tf_op jit(solution)/shard_map/ppermute | solution.py:16
  315.9 10.9 %collective-permute-start.51 = (bf16[64,256]{1,0:T(8,128)(2,1)}, bf16[64,256]{1,0:T(8,128)(2,1)S(1)}, u32[]{:S(2)}, u32[]{:S(2)}) collective-permute-start(bf16[64,256]{1,0:T(8,128)(2,1)} %get-tuple-element.73), channel_id=1, source_target_pairs={{0,6},{1,7},{2,4},{3,5},{4,2},{5,3},{6,0},{7,1},{8,14},{9,15},{10,... | collective-permute-start | bytes 98312 | tf_op jit(solution)/shard_map/ppermute | solution.py:16
  (90 other events, 2203.6 us)

commit v2 on v0

--- a/solution.py
+++ b/solution.py
@@ -1,16 +1,273 @@
+import functools
+
 import jax
 import jax.numpy as jnp
 from jax import lax
+from jax.experimental import pallas as pl
+from jax.experimental.pallas import tpu as pltpu
 from jax.sharding import PartitionSpec as P
 
 L_WIN = 4
-
-
-def from_partner(array, axis, stride):
-    return lax.ppermute(array, axis, [(i, i ^ 1 << stride) for i in range(lax.axis_size(axis))])
-
-
-def on_device(layer_inputs, targets, encoder, encoder_bias, decoder):
+MIB = 1024 * 1024
+
+
+def exchange(array, axis, flip):
+    size = lax.axis_size(axis)
+    return lax.ppermute(array, axis, [(i, i ^ flip) for i in range(size)])
+
+
+ENCODE_MIB = 28
+DECODE_MIB = 40
+SLOTS = 4
+ANYWHERE = pl.BlockSpec(memory_space=pl.ANY)
+
+
+def streamed(source, buffer, sems):
+    slots, block = buffer.shape[0], buffer.shape[1]
+    step, steps = pl.program_id(0), pl.num_programs(0)
+
+    def copy(k):
+        slot = lax.rem(k, slots)
+        rows = pl.ds(pl.multiple_of(k * block, block), block)
+        return pltpu.make_async_copy(source.at[rows], buffer.at[slot], sems.at[slot])
+
+    @pl.when(step == 0)
+    def _():
+        for k in range(slots - 1):
+            copy(jnp.int32(k)).start()
+
+    @pl.when(step + slots - 1 < steps)
+    def _():
+        copy(step + slots - 1).start()
+
+    copy(step).wait()
+    return buffer[lax.rem(step, slots)]
+
+
+def stacked(parts):
+    values = [part[...] for part in parts]
+    return values[0] if len(values) == 1 else jnp.concatenate(values, axis=0)
+
+
+def encode_kernel(n_in, n_out, *refs):
+    parts, (weight, bias), refs = refs[:n_in], refs[n_in : n_in + 2], refs[n_in + 2 :]
+    outs, (total, buffer, sems) = refs[-3 - n_out : -3], refs[-3:]
+    step = pl.program_id(0)
+
+    @pl.when(step == 0)
+    def _():
+        total[...] = jnp.broadcast_to(bias[...], total.shape)
+
+    block = streamed(weight.at[0], buffer, sems)
+    total[...] += jnp.dot(stacked(parts), block, preferred_element_type=jnp.float32)
+
+    @pl.when(step == pl.num_programs(0) - 1)
+    def _():
+        row = 0
+        for out in outs:
+            size = out.shape[0]
+            out[...] = jnp.maximum(total[pl.ds(row, size), :], 0.0).astype(out.dtype)
+            row += size
+
+
+def encode(parts, out_rows, weight, bias, after):
+    rows = sum(part.shape[0] for part in parts)
+    _, width, features = weight.shape
+    block = min(256, width)
+    return pl.pallas_call(
+        functools.partial(encode_kernel, len(parts), len(out_rows)),
+        grid=(width // block,),
+        in_specs=[pl.BlockSpec((part.shape[0], block), lambda k: (0, k)) for part in parts]
+        + [
+            ANYWHERE,
+            pl.BlockSpec((1, features), lambda k: (0, 0)),
+        ]
+        + [ANYWHERE] * len(after),
+        out_specs=[pl.BlockSpec((n, features), lambda k: (0, 0)) for n in out_rows],
+        out_shape=[jax.ShapeDtypeStruct((n, features), jnp.bfloat16) for n in out_rows],
+        scratch_shapes=[
+            pltpu.VMEM((rows, features), jnp.float32),
+            pltpu.VMEM((SLOTS, block, features), weight.dtype),
+            pltpu.SemaphoreType.DMA((SLOTS,)),
+        ],
+        compiler_params=pltpu.CompilerParams(vmem_limit_bytes=ENCODE_MIB * MIB),
+        name="encode",
+    )(*parts, weight, bias, *after)
+
+
+def decode_kernel(n, lags, flags, n_base, n_out, info, *refs):
+    first, second, refs = refs[:n], refs[n : 2 * n], refs[2 * n :]
+    weights, base, refs = refs[0], refs[1 : 1 + n_base], refs[1 + n_base :]
+    buffers, sems, refs = refs[-4:-2], refs[-2:], refs[:-4]
+    if n_out:
+        out, total = refs[-2:]
+    else:
+        out = total = refs[-1]
+    step = pl.program_id(0)
+
+    @pl.when(step == 0)
+    def _():
+        total[...] = base[0][...] if n_base else jnp.zeros_like(total)
+
+    def add(parts, lag, buffer, sem):
+        block = streamed(weights.at[0, 0 if lag is None else info[lag]], buffer, sem)
+        total[...] += jnp.dot(stacked(parts), block, preferred_element_type=jnp.float32)
+
+    for flag, *source in zip(flags, (first, second), lags, buffers, sems):
+        if flag is None:
+            add(*source)
+        else:
+            pl.when(info[flag] == 1)(functools.partial(add, *source))
+
+    if n_out:
+
+        @pl.when(step == pl.num_programs(0) - 1)
+        def _():
+            for j in range(n_out):
+                cols = out.shape[2]
+                out[j] = total[:, j * cols : (j + 1) * cols].astype(out.dtype)
+
+
+def decode(info, first, second, decoder, lags, flags, base, row, shards, after):
+    n = len(first)
+    rows = sum(part.shape[0] for part in first)
+    _, _, features, width = decoder.shape
+    block = min(512, features)
+
+    def masked(k, info, flag):
+        return k if flag is None else k * info[flag]
+
+    def acts(part, flag):
+        return pl.BlockSpec((part.shape[0], block), lambda k, info: (0, masked(k, info, flag)))
+
+    in_specs = [acts(part, flags[0]) for part in first] + [acts(part, flags[1]) for part in second]
+    in_specs.append(ANYWHERE)
+    operands = [*first, *second, decoder]
+    if base is not None:
+        at = row // rows
+        in_specs.append(
+            pl.BlockSpec((rows, width), lambda k, info: (at, 0), pipeline_mode=pl.Buffered(1))
+        )
+        operands.append(base)
+        shape, dtype = (shards, rows, width // shards), jnp.bfloat16
+    else:
+        shape, dtype = (rows, width), jnp.float32
+    return pl.pallas_call(
+        functools.partial(
+            decode_kernel, n, lags, flags, int(base is not None), 0 if base is None else shards
+        ),
+        grid_spec=pltpu.PrefetchScalarGridSpec(
+            num_scalar_prefetch=1,
+            grid=(features // block,),
+            in_specs=in_specs + [ANYWHERE] * len(after),
+            out_specs=pl.BlockSpec(shape, lambda k, info: (0,) * len(shape)),
+            scratch_shapes=([] if base is None else [pltpu.VMEM((rows, width), jnp.float32)])
+            + [pltpu.VMEM((SLOTS, block, width), decoder.dtype)] * 2
+            + [pltpu.SemaphoreType.DMA((SLOTS,))] * 2,
+        ),
+        out_shape=jax.ShapeDtypeStruct(shape, dtype),
+        compiler_params=pltpu.CompilerParams(vmem_limit_bytes=DECODE_MIB * MIB),
+        name="decode_own" if base is None else "decode_crossed",
+    )(info, *operands, *after)
+
+
+def sum_kernel(sign, slots, base, *refs):
+    received, out = refs[: len(slots)], refs[-1]
+    out[...] = sign * base[...]
+    for ref, blocks in zip(received, slots):
+        size = ref.shape[1] // len(blocks)
+        for source in range(ref.shape[0]):
+            for k, s in enumerate(blocks):
+                at = pl.ds((source ^ s) * size, size)
+                out[at, :] += ref[source, pl.ds(k * size, size), :].astype(jnp.float32)
+
+
+def add_up(base, sign, slots, received, after):
+    return pl.pallas_call(
+        functools.partial(sum_kernel, sign, slots),
+        in_specs=[pl.BlockSpec(memory_space=pltpu.VMEM)] * (1 + len(received))
+        + [ANYWHERE] * len(after),
+        out_specs=pl.BlockSpec(memory_space=pltpu.VMEM),
+        out_shape=jax.ShapeDtypeStruct(base.shape, base.dtype),
+        compiler_params=pltpu.CompilerParams(vmem_limit_bytes=ENCODE_MIB * MIB),
+        name="add_up",
+    )(base, *received, *after)
+
+
+def pipelined(layer_inputs, targets, encoder, encoder_bias, decoder):
+    shards = lax.axis_size("feat")
+    layers = lax.axis_size("layer")
+    half = layers // 2
+    layer = lax.axis_index("layer")
+    upper = layer >= half
+    info = jnp.stack(
+        [
+            layer & 1,
+            upper.astype(jnp.int32),
+            jnp.full_like(layer, half),
+            jnp.where(upper, layer - ((layer ^ 1) - half), 0),
+        ]
+    ).astype(jnp.int32)
+    odd_, upper_, lag_direct, lag_swapped = range(4)
+
+    def up(a):
+        return lax.ppermute(a, "layer", [(i, i + half) for i in range(half)])
+
+    def across(a):
+        return lax.ppermute(a, "layer", [(i, i ^ 1) for i in range(half, layers)])
+
+    def beside(a):
+        return lax.ppermute(a, "layer", [(i, i + 1) for i in range(0, layers, 2)])
+
+    def scatter(partial):
+        return lax.all_to_all(partial, "feat", 0, 0)
+
+    def run_encode(slots, after):
+        parts = [x[s] for s in slots]
+        return encode(parts, [len(slots) * size], encoder, encoder_bias, after)[0]
+
+    x = {0: layer_inputs[0]}
+    size = x[0].shape[0]
+    for s in range(1, shards):
+        if s == 1 or s % 2 == 0:
+            x[s] = exchange(x[0], "feat", s)
+    for s in range(3, shards, 2):
+        x[s] = exchange(x[s - 1], "feat", 1)
+    slots = [[0], [1, 2], [3] + list(range(4, shards, 2)), list(range(5, shards, 2))]
+
+    a0 = run_encode(slots[0], [])
+    d0, n0 = up(a0), beside(a0)
+    a1 = run_encode(slots[1], [a0])
+    d1, n1 = up(a1), beside(a1)
+    a2 = run_encode(slots[2], [a1, d0])
+    d2, n2 = up(a2), beside(a2)
+    a3 = run_encode(slots[3], [a2, d1])
+    d3, n3 = up(a3), beside(a3)
+    acts = [a0, a1, a2, a3]
+    d0, d1, _ = lax.optimization_barrier((d0, d1, a3))
+    c0, c1 = across(d0), across(d1)
+    base = decode(
+        info, acts, [n0, n1, n2, n3], decoder, (None, odd_), (None, odd_), None, 0, shards, []
+    )
+    lags, flags = (lag_direct, lag_swapped), (upper_, upper_)
+    waves = [slots[0] + slots[1], slots[2], slots[3]]
+    p0 = decode(info, [d0, d1], [c0, c1], decoder, lags, flags, base, 0, shards, [])
+    r0 = scatter(p0)
+    d2, _ = lax.optimization_barrier((d2, p0))
+    c2 = across(d2)
+    row = size * len(waves[0])
+    p1 = decode(info, [d2], [c2], decoder, lags, flags, base, row, shards, [p0])
+    r1 = scatter(p1)
+    d3, _ = lax.optimization_barrier((d3, p1))
+    c3 = across(d3)
+    row += size * len(waves[1])
+    p2 = decode(info, [d3], [c3], decoder, lags, flags, base, row, shards, [p1])
+    r2 = scatter(p2)
+    total = add_up(targets[0], -1.0, waves[:2], [r0, r1], [p2])
+    return add_up(total, 1.0, waves[2:], [r2], [])[None]
+
+
+def grouped(layer_inputs, targets, encoder, encoder_bias, decoder):
     groups = lax.axis_size("layer") // L_WIN
     depth_bits = groups.bit_length() - 1
     position = lax.axis_index("layer")
@@ -18,7 +275,7 @@
     group_index = position % groups
     gathered = lax.all_gather(layer_inputs[0], "feat", axis=0, tiled=True)
     for bit_index in range(depth_bits):
-        partner = from_partner(gathered, "layer", bit_index)
+        partner = exchange(gathered, "layer", 1 << bit_index)
         upper_bit = position >> bit_index & 1
         gathered = jnp.where(
             upper_bit == 1,
@@ -42,7 +299,7 @@
         upper_bit = position >> bit_index & 1
         kept_half = jnp.where(upper_bit == 1, rebuilt[half_rows:], rebuilt[:half_rows])
         sent_half = jnp.where(upper_bit == 1, rebuilt[:half_rows], rebuilt[half_rows:])
-        rebuilt = kept_half + from_partner(sent_half, "layer", bit_index)
+        rebuilt = kept_half + exchange(sent_half, "layer", 1 << bit_index)
     summed = lax.psum_scatter(rebuilt, "feat", scatter_dimension=1, tiled=True)
     residual = summed - targets[0]
     return residual[None]
@@ -56,6 +313,12 @@
         P("layer", "feat"),
         P("layer", None, "feat", None),
     )
+    shards = mesh.shape["feat"]
+    simple = mesh.shape["layer"] == L_WIN and shards >= 8 and shards & (shards - 1) == 0
     return jax.shard_map(
-        on_device, mesh=mesh, in_specs=placed, out_specs=P("layer", None, "feat"), check_vma=False
+        pipelined if simple else grouped,
+        mesh=mesh,
+        in_specs=placed,
+        out_specs=P("layer", None, "feat"),
+        check_vma=False,
     )

time: 336 us -> 207 us (0.62)
  waiting for transfers between devices: 247 us -> 33.9 us
  Pallas kernels: 0 us -> 91.3 us
  starting transfers between devices: 0.08 us -> 61.1 us
  matrix products: 58.5 us -> 0 us
  between operations: 13.1 us -> 0.44 us
  local copies, waits for them, and re-layouts: 14 us -> 18.6 us
    all_gather x2 -> x0, waiting for transfers between devices: 156 us -> none  [the longest x1 103 us: on_device(): every_layer = lax.all_gather(features[None], 'layer', axis=0, tiled=True)]
    pallas_call x0 -> x10, Pallas kernels: none -> 91.3 us  [the longest x4 62.9 us: decode(): pl.pallas_call(functools.partial(decode_kernel, n, lags, flags, int(base...]
    reduce_scatter x1 -> x0, waiting for transfers between devices: 89.7 us -> none  [on_device(): summed = lax.psum_scatter(rebuilt, 'feat', scatter_dimension=1, tiled=True)]
    dot_general x2 -> x0, matrix products: 58.5 us -> none  [the longest x1 44.1 us: on_device(): jnp.einsum('ktf,kfd->td', stacked, decoder[0], preferred_element_type=jnp...]
    ppermute x0 -> x19, starting transfers between devices: none -> 41.7 us  [the longest x4 20.1 us: across(): return lax.ppermute(a, 'layer', [(i, i ^ 1) for i in range(half, layers)])]
    ppermute x0 -> x19, waiting for transfers between devices: none -> 20 us  [the longest x7 16.4 us: exchange(): return lax.ppermute(array, axis, [(i, i ^ flip) for i in range(size)])]
    all_to_all x0 -> x3, starting transfers between devices: none -> 19.4 us  [scatter(): return lax.all_to_all(partial, 'feat', 0, 0)]
    unnamed x2 -> x44, local copies, waits for them, and re-layouts: 0.01 us -> 18.6 us
  transfers between devices with their start and end apart: 3 -> 22, of which waited for: 3 -> 5; matrix products, arithmetic and copies ran while one was open for 0% -> 0% of each run, Pallas kernels for 0% -> 44%
where the time goes in v2:
time: 207 us; the launch traced here: 205 us
  Pallas kernels  91.3 us (44%)
  starting transfers between devices  61.1 us (30%)
  waiting for transfers between devices  33.9 us (16%)
  local copies, waits for them, and re-layouts  18.6 us (9%)
    pallas_call x4, Pallas kernels, decode(): pl.pallas_call(functools.partial(decode_kernel, n, lags, flags, int(base...  62.9 us
    pallas_call x4, Pallas kernels, encode(): pl.pallas_call(functools.partial(encode_kernel, len(parts), len(out_rows)...  27.2 us
    ppermute x4, starting transfers between devices, across(): return lax.ppermute(a, 'layer', [(i, i ^ 1) for i in range(half, layers)])  20.1 us
    all_to_all x3, starting transfers between devices, scatter(): return lax.all_to_all(partial, 'feat', 0, 0)  19.4 us
    unnamed x44, local copies, waits for them, and re-layouts  18.6 us
    ppermute x7, waiting for transfers between devices, exchange(): return lax.ppermute(array, axis, [(i, i ^ flip) for i in range(size)])  16.4 us
    all_to_all x3, waiting for transfers between devices, scatter(): return lax.all_to_all(partial, 'feat', 0, 0)  13.9 us
    ppermute x7, starting transfers between devices, exchange(): return lax.ppermute(array, axis, [(i, i ^ flip) for i in range(size)])  8.51 us
  transfers between devices with their start and end apart: 22, of which 5 were waited for; matrix products, arithmetic and copies ran while one was open for 0% of the time, Pallas kernels for 44%

profile of v2, /device:TPU:2, one launch (start us, length us, event | category | flops | bytes accessed | tf_op | source)
XLA Modules:
  0.0 205.3 jit_solution(1645266715210120097)
XLA Ops:
  0.0 1.6 collective-permute-start.2
  1.6 1.5 collective-permute-start.1
  3.1 5.8 %copy-done = bf16[1,2048,4096]{2,1,0:T(8,128)(2,1)S(1)} copy-done((bf16[1,2048,4096]{2,1,0:T(8,128)(2,1)S(1)}, bf16[1,2048,4096]{2,1,0:T(8,128)(2,1)}, u32[]{:S(2)}) %copy-start) | copy-done | bytes 16777240
  10.5 5.4 %encode.4.refs_4_.refs_0_ = bf16[64,4096]{1,0:T(8,128)(2,1)S(1)} custom-call(bf16[64,2048]{1,0:T(8,128)(2,1)S(1)} %bitcast.11, bf16[1,2048,4096]{2,1,0:T(8,128)(2,1)S(1)} %copy-done, f32[1,4096]{1,0:T(1,128)S(1)} %copy-done.16), custom_call_target="tpu_custom_call" | custom-call | tf_op jit(solution)/shard_map/encode/pallas_call | solution.py:77
  15.9 1.4 collective-permute-start
  17.4 6.4 %encode.5.refs_5_.refs_1_ = bf16[128,4096]{1,0:T(8,128)(2,1)} custom-call(bf16[64,2048]{1,0:T(8,128)(2,1)S(1)} %collective-permute-done.1.refs_0_, bf16[64,2048]{1,0:T(8,128)(2,1)S(1)} %collective-permute-done.2.refs_1_, bf16[1,2048,4096]{2,1,0:T(8,128)(2,1)S(1)} %copy-done.1, f32[1,4096]{1,0:T(1,128)S(1)} %copy-done.17, ...), custom_call_target="tpu_custom_call" | custom-call | tf_op jit(solution)/shard_map/encode/pallas_call | solution.py:77
  23.9 1.6 collective-permute-start.3
  25.4 2.7 %collective-permute-start.4 = (bf16[64,2048]{1,0:T(8,128)(2,1)S(1)}, bf16[64,2048]{1,0:T(8,128)(2,1)}, u32[]{:S(2)}, u32[]{:S(2)}) collective-permute-start(bf16[64,2048]{1,0:T(8,128)(2,1)S(1)} %bitcast.12), channel_id=1, source_target_pairs={{0,4},{1,5},{2,6},{3,7},{4,0},{5,1},{6,2},{7,3},{8,12},{9,13},{10,... | collective-permute-start | bytes 786440 | tf_op jit(solution)/shard_map/ppermute | solution.py:16
  28.8 16.4 %collective-permute-done.4.refs_1_ = bf16[64,2048]{1,0:T(8,128)(2,1)} collective-permute-done((bf16[64,2048]{1,0:T(8,128)(2,1)S(1)}, bf16[64,2048]{1,0:T(8,128)(2,1)}, u32[]{:S(2)}, u32[]{:S(2)}) %collective-permute-start.4) | collective-permute-done | bytes 262176 | tf_op jit(solution)/shard_map/ppermute | solution.py:16
  45.7 1.5 collective-permute-start.7
  50.7 8.8 %encode.6.refs_4_.refs_2_ = bf16[192,4096]{1,0:T(8,128)(2,1)} custom-call(bf16[64,2048]{1,0:T(8,128)(2,1)S(1)} %copy-done.15, bf16[64,2048]{1,0:T(8,128)(2,1)} %collective-permute-done.4.refs_1_, bf16[64,2048]{1,0:T(8,128)(2,1)} %collective-permute-done.6.refs_2_, bf16[1,2048,4096]{2,1,0:T(8,128)(2,1)S(1)} %copy-done.1, f32[1,4096]{1,0:T(1,128)S(1)} %copy-done.17, ...), custom_call_target="tpu_custom_call" | custom-call | tf_op jit(solution)/shard_map/encode/pallas_call | solution.py:77
  59.5 2.6 %collective-permute-start.13 = (bf16[192,4096]{1,0:T(8,128)(2,1)}, bf16[192,4096]{1,0:T(8,128)(2,1)}, u32[]{:S(2)}, u32[]{:S(2)}) collective-permute-start(bf16[192,4096]{1,0:T(8,128)(2,1)} %encode.6.refs_4_.refs_2_), channel_id=1, source_target_pairs={{0,8},{16,24},{1,9},{17,25},{2,10},{18,26},{3,11},{19,27},{4,12},{... | collective-permute-start | bytes 4718600 | tf_op jit(solution)/shard_map/ppermute | solution.py:220
  62.1 1.3 collective-permute-start.12
  63.5 1.3 collective-permute-start.11
  64.8 1.3 collective-permute-start.15
  66.2 6.6 %encode.7.refs_3_ = bf16[128,4096]{1,0:T(8,128)(2,1)S(1)} custom-call(bf16[64,2048]{1,0:T(8,128)(2,1)} %collective-permute-done.5.refs_0_, bf16[64,2048]{1,0:T(8,128)(2,1)} %collective-permute-done.7.refs_1_, bf16[1,2048,4096]{2,1,0:T(8,128)(2,1)S(1)} %bitcast.7, f32[1,4096]{1,0:T(1,128)S(1)} %copy-done.17, bf16[192,4096]{1,0:T(8,128)(2,1)} %encode.6.refs_4_.refs_2_, ...), custom_call_target="tpu_custom_call" | custom-call | tf_op jit(solution)/shard_map/encode/pallas_call | solution.py:77
  72.9 2.3 %collective-permute-start.14 = (bf16[128,4096]{1,0:T(8,128)(2,1)S(1)}, bf16[128,4096]{1,0:T(8,128)(2,1)}, u32[]{:S(2)}, u32[]{:S(2)}) collective-permute-start(bf16[128,4096]{1,0:T(8,128)(2,1)S(1)} %encode.7.refs_3_), channel_id=1, source_target_pairs={{0,8},{16,24},{1,9},{17,25},{2,10},{18,26},{3,11},{19,27},{4,12},{... | collective-permute-start | bytes 3145736 | tf_op jit(solution)/shard_map/ppermute | solution.py:220
  75.2 1.9 collective-permute-start.10
  78.1 2.4 %collective-permute-start.9 = (bf16[64,4096]{1,0:T(8,128)(2,1)S(1)}, bf16[64,4096]{1,0:T(8,128)(2,1)}, u32[]{:S(2)}, u32[]{:S(2)}) collective-permute-start(bf16[64,4096]{1,0:T(8,128)(2,1)S(1)} %copy-done.8), channel_id=1, source_target_pairs={{16,24},{24,16},{17,25},{25,17},{18,26},{26,18},{19,27},{27,19},{2... | collective-permute-start | bytes 1572872 | tf_op jit(solution)/shard_map/ppermute | solution.py:217
  81.8 14.2 %decode_own.1.refs_5_.refs_3_ = f32[512,2048]{1,0:T(8,128)S(1)} custom-call(s32[4]{0:T(128)S(1)} %pad_add_fusion.info, bf16[64,4096]{1,0:T(8,128)(2,1)S(1)} %copy-done.6, bf16[128,4096]{1,0:T(8,128)(2,1)} %encode.5.refs_5_.refs_1_, bf16[192,4096]{1,0:T(8,128)(2,1)} %encode.6.refs_4_.refs_2_, bf16[128,4096]{1,0:T(8,128)(2,1)S(1)} %encode.7.refs_3_, ...), custom_call_target="tpu_custom_call" | custom-call | tf_op jit(solution)/shard_map/decode_own/pallas_call | solution.py:155
  96.0 17.0 %decode_crossed.3.refs_4_ = bf16[8,192,256]{2,1,0:T(8,128)(2,1)} custom-call(s32[4]{0:T(128)S(1)} %pad_add_fusion.info, bf16[64,4096]{1,0:T(8,128)(2,1)S(1)} %copy-done.8, bf16[128,4096]{1,0:T(8,128)(2,1)} %collective-permute-done.3.refs_5_.refs_1_, bf16[64,4096]{1,0:T(8,128)(2,1)} %collective-permute-done.9.refs_2_, ...), custom_call_target="tpu_custom_call" | custom-call | tf_op jit(solution)/shard_map/decode_crossed/pallas_call | solution.py:155
  113.1 13.9 %collective-permute-start.16 = (bf16[192,4096]{1,0:T(8,128)(2,1)}, bf16[192,4096]{1,0:T(8,128)(2,1)}, u32[]{:S(2)}, u32[]{:S(2)}) collective-permute-start(bf16[192,4096]{1,0:T(8,128)(2,1)} %collective-permute-done.15.refs_0_), channel_id=1, source_target_pairs={{16,24},{24,16},{17,25},{25,17},{18,26},{26,18},{19,27},{27,19},{2... | collective-permute-start | bytes 4718600 | tf_op jit(solution)/shard_map/ppermute | solution.py:217
  126.9 8.0 %all-to-all-start = ((bf16[8,192,256]{2,1,0:T(8,128)(2,1)}), bf16[8,192,256]{2,1,0:T(8,128)(2,1)S(1)}, u32[]{:S(2)}, u32[]{:S(2)}) async-start(bf16[8,192,256]{2,1,0:T(8,128)(2,1)} %decode_crossed.3.refs_4_), calls=%async_computation | async-start | bytes 1572864 | tf_op jit(solution)/shard_map/all_to_all | solution.py:223
  136.2 2.2 %copy-done.3 = f32[512,2048]{1,0:T(8,128)S(1)} copy-done((f32[512,2048]{1,0:T(8,128)S(1)}, f32[512,2048]{1,0:T(8,128)}, u32[]{:S(2)}) %copy-start.3) | copy-done | bytes 4194328
  138.4 16.5 %decode_crossed.4.refs_4_ = bf16[8,192,256]{2,1,0:T(8,128)(2,1)} custom-call(s32[4]{0:T(128)S(1)} %pad_add_fusion.info, bf16[192,4096]{1,0:T(8,128)(2,1)} %collective-permute-done.15.refs_0_, bf16[192,4096]{1,0:T(8,128)(2,1)} %collective-permute-done.16.refs_1_, bf16[1,4,4096,2048]{3,2,1,0:T(8,128)(2,1)} %refs_2_.9, f32[512,2048]{1,0:T(8,128)S(1)} %copy-done.3, ...), custom_call_target="tpu_custom_call" | custom-call | tf_op jit(solution)/shard_map/decode_crossed/pallas_call | solution.py:155
  155.3 5.6 %all-to-all-start.1 = ((bf16[8,192,256]{2,1,0:T(8,128)(2,1)}), bf16[8,192,256]{2,1,0:T(8,128)(2,1)S(1)}, u32[]{:S(2)}, u32[]{:S(2)}) async-start(bf16[8,192,256]{2,1,0:T(8,128)(2,1)} %decode_crossed.4.refs_4_), calls=%async_computation.1 | async-start | bytes 1572864 | tf_op jit(solution)/shard_map/all_to_all | solution.py:223
  161.7 1.9 collective-permute-start.18
  163.6 2.8 %collective-permute-done.18.refs_1_ = bf16[128,4096]{1,0:T(8,128)(2,1)S(1)} collective-permute-done((bf16[128,4096]{1,0:T(8,128)(2,1)}, bf16[128,4096]{1,0:T(8,128)(2,1)S(1)}, u32[]{:S(2)}, u32[]{:S(2)}) %collective-permute-start.18) | collective-permute-done | bytes 1048608 | tf_op jit(solution)/shard_map/ppermute | solution.py:217
  166.4 2.2 %copy-done.4 = f32[512,2048]{1,0:T(8,128)S(1)} copy-done((f32[512,2048]{1,0:T(8,128)S(1)}, f32[512,2048]{1,0:T(8,128)}, u32[]{:S(2)}) %copy-start.4) | copy-done | bytes 4194328
  168.6 15.2 %decode_crossed.5.refs_2_ = bf16[8,128,256]{2,1,0:T(8,128)(2,1)} custom-call(s32[4]{0:T(128)S(1)} %pad_add_fusion.info, bf16[128,4096]{1,0:T(8,128)(2,1)} %collective-permute-done.17.refs_0_, bf16[128,4096]{1,0:T(8,128)(2,1)S(1)} %collective-permute-done.18.refs_1_, bf16[1,4,4096,2048]{3,2,1,0:T(8,128)(2,1)} %refs_2_.9, f32[512,2048]{1,0:T(8,128)S(1)} %copy-done.4, ...), custom_call_target="tpu_custom_call" | custom-call | tf_op jit(solution)/shard_map/decode_crossed/pallas_call | solution.py:155
  183.9 5.7 %all-to-all-start.2 = ((bf16[8,128,256]{2,1,0:T(8,128)(2,1)}), bf16[8,128,256]{2,1,0:T(8,128)(2,1)S(1)}, u32[]{:S(2)}, u32[]{:S(2)}) async-start(bf16[8,128,256]{2,1,0:T(8,128)(2,1)} %decode_crossed.5.refs_2_), calls=%async_computation.2 | async-start | bytes 1048576 | tf_op jit(solution)/shard_map/all_to_all | solution.py:223
  190.9 13.5 %all-to-all-done.2.refs_0_ = bf16[8,128,256]{2,1,0:T(8,128)(2,1)S(1)} async-done(((bf16[8,128,256]{2,1,0:T(8,128)(2,1)}), bf16[8,128,256]{2,1,0:T(8,128)(2,1)S(1)}, u32[]{:S(2)}, u32[]{:S(2)}) %all-to-all-start.2) | async-done | bytes 524320 | tf_op jit(solution)/shard_map/all_to_all | solution.py:223
  (68 shorter events, 13.3 us)
Async XLA Ops:
  0.0 17.4 %collective-permute-start.2 = (bf16[64,2048]{1,0:T(8,128)(2,1)}, bf16[64,2048]{1,0:T(8,128)(2,1)S(1)}, u32[]{:S(2)}, u32[]{:S(2)}) collective-permute-start(bf16[64,2048]{1,0:T(8,128)(2,1)} %bitcast.9), channel_id=1, source_target_pairs={{0,2},{1,3},{2,0},{3,1},{4,6},{5,7},{6,4},{7,5},{8,10},{9,11},{10,... | collective-permute-start | bytes 786440 | tf_op jit(solution)/shard_map/ppermute | solution.py:16
  1.6 15.8 %collective-permute-start.1 = (bf16[64,2048]{1,0:T(8,128)(2,1)}, bf16[64,2048]{1,0:T(8,128)(2,1)S(1)}, u32[]{:S(2)}, u32[]{:S(2)}) collective-permute-start(bf16[64,2048]{1,0:T(8,128)(2,1)} %bitcast.10), channel_id=1, source_target_pairs={{0,1},{1,0},{2,3},{3,2},{4,5},{5,4},{6,7},{7,6},{8,9},{9,8},{10,11... | collective-permute-start | bytes 786440 | tf_op jit(solution)/shard_map/ppermute | solution.py:16
  10.5 6.9 %copy-start.1 = (bf16[1,2048,4096]{2,1,0:T(8,128)(2,1)S(1)}, bf16[1,2048,4096]{2,1,0:T(8,128)(2,1)}, u32[]{:S(2)}) copy-start(bf16[1,2048,4096]{2,1,0:T(8,128)(2,1)} %refs_2_.7) | copy-start | bytes 50331652
  10.5 6.9 %copy-start.17 = (f32[1,4096]{1,0:T(1,128)S(1)}, f32[1,4096]{1,0:T(1,128)}, u32[]{:S(2)}) copy-start(f32[1,4096]{1,0:T(1,128)} %refs_3_.5) | copy-start | bytes 49156
  15.9 7.9 %copy-start.5 = (bf16[64,4096]{1,0:T(8,128)(2,1)}, bf16[64,4096]{1,0:T(8,128)(2,1)S(1)}, u32[]{:S(2)}) copy-start(bf16[64,4096]{1,0:T(8,128)(2,1)S(1)} %encode.4.refs_4_.refs_0_) | copy-start | bytes 1572868
  15.9 9.5 %copy-start.13 = (bf16[1,64,2048]{2,1,0:T(8,128)(2,1)S(1)}, bf16[1,64,2048]{2,1,0:T(8,128)(2,1)}, u32[]{:S(2)}) copy-start(bf16[1,64,2048]{2,1,0:T(8,128)(2,1)} %param.5) | copy-start | bytes 786436
  15.9 31.3 %collective-permute-start = (bf16[64,4096]{1,0:T(8,128)(2,1)S(1)}, bf16[64,4096]{1,0:T(8,128)(2,1)S(1)}, u32[]{:S(2)}, u32[]{:S(2)}) collective-permute-start(bf16[64,4096]{1,0:T(8,128)(2,1)S(1)} %encode.4.refs_4_.refs_0_), channel_id=1, source_target_pairs={{0,16},{8,24},{1,17},{9,25},{2,18},{10,26},{3,19},{11,27},{4,20},{... | collective-permute-start | bytes 1572872 | tf_op jit(solution)/shard_map/ppermute | solution.py:214
  17.4 48.7 %slice-start = ((s8[16777216]{0:T(1024)(128)(4,1)}), s8[4194304]{0:T(1024)(128)(4,1)S(1)}, s32[]{:S(2)}) async-start(s8[16777216]{0:T(1024)(128)(4,1)} %bitcast.6), calls=%async_computation.3 | async-start | bytes 8388608
  17.4 48.7 %slice-start.1 = ((s8[16777216]{0:T(1024)(128)(4,1)}), s8[4194304]{0:T(1024)(128)(4,1)S(1)}, s32[]{:S(2)}) async-start(s8[16777216]{0:T(1024)(128)(4,1)} %bitcast.6), calls=%async_computation.4 | async-start | bytes 8388608
  23.8 42.3 %slice-start.2 = ((s8[16777216]{0:T(1024)(128)(4,1)}), s8[4194304]{0:T(1024)(128)(4,1)S(1)}, s32[]{:S(2)}) async-start(s8[16777216]{0:T(1024)(128)(4,1)} %bitcast.6), calls=%async_computation.5 | async-start | bytes 8388608
  23.9 42.3 %slice-start.3 = ((s8[16777216]{0:T(1024)(128)(4,1)}), s8[4194304]{0:T(1024)(128)(4,1)S(1)}, s32[]{:S(2)}) async-start(s8[16777216]{0:T(1024)(128)(4,1)} %bitcast.6), calls=%async_computation.6 | async-start | bytes 8388608
  23.9 42.3 %collective-permute-start.3 = (bf16[128,4096]{1,0:T(8,128)(2,1)}, bf16[128,4096]{1,0:T(8,128)(2,1)}, u32[]{:S(2)}, u32[]{:S(2)}) collective-permute-start(bf16[128,4096]{1,0:T(8,128)(2,1)} %encode.5.refs_5_.refs_1_), channel_id=1, source_target_pairs={{0,16},{8,24},{1,17},{9,25},{2,18},{10,26},{3,19},{11,27},{4,20},{... | collective-permute-start | bytes 3145736 | tf_op jit(solution)/shard_map/ppermute | solution.py:214
  25.4 19.8 %collective-permute-start.4 = (bf16[64,2048]{1,0:T(8,128)(2,1)S(1)}, bf16[64,2048]{1,0:T(8,128)(2,1)}, u32[]{:S(2)}, u32[]{:S(2)}) collective-permute-start(bf16[64,2048]{1,0:T(8,128)(2,1)S(1)} %bitcast.12), channel_id=1, source_target_pairs={{0,4},{1,5},{2,6},{3,7},{4,0},{5,1},{6,2},{7,3},{8,12},{9,13},{10,... | collective-permute-start | bytes 786440 | tf_op jit(solution)/shard_map/ppermute | solution.py:16
  28.1 17.6 %collective-permute-start.6 = (bf16[64,2048]{1,0:T(8,128)(2,1)S(1)}, bf16[64,2048]{1,0:T(8,128)(2,1)}, u32[]{:S(2)}, u32[]{:S(2)}) collective-permute-start(bf16[64,2048]{1,0:T(8,128)(2,1)S(1)} %bitcast.13), channel_id=1, source_target_pairs={{0,6},{1,7},{2,4},{3,5},{4,2},{5,3},{6,0},{7,1},{8,14},{9,15},{10,... | collective-permute-start | bytes 786440 | tf_op jit(solution)/shard_map/ppermute | solution.py:16
  28.3 19.7 %collective-permute-start.8 = (bf16[64,2048]{1,0:T(8,128)(2,1)S(1)}, bf16[64,2048]{1,0:T(8,128)(2,1)S(1)}, u32[]{:S(2)}, u32[]{:S(2)}) collective-permute-start(bf16[64,2048]{1,0:T(8,128)(2,1)S(1)} %collective-permute-done.2.refs_1_), channel_id=1, source_target_pairs={{0,1},{1,0},{2,3},{3,2},{4,5},{5,4},{6,7},{7,6},{8,9},{9,8},{10,11... | collective-permute-start | bytes 786440 | tf_op jit(solution)/shard_map/ppermute | solution.py:16
  45.2 18.3 %collective-permute-start.5 = (bf16[64,2048]{1,0:T(8,128)(2,1)}, bf16[64,2048]{1,0:T(8,128)(2,1)}, u32[]{:S(2)}, u32[]{:S(2)}) collective-permute-start(bf16[64,2048]{1,0:T(8,128)(2,1)} %collective-permute-done.4.refs_1_), channel_id=1, source_target_pairs={{0,1},{1,0},{2,3},{3,2},{4,5},{5,4},{6,7},{7,6},{8,9},{9,8},{10,11... | collective-permute-start | bytes 786440 | tf_op jit(solution)/shard_map/ppermute | solution.py:16
  45.7 19.1 %collective-permute-start.7 = (bf16[64,2048]{1,0:T(8,128)(2,1)}, bf16[64,2048]{1,0:T(8,128)(2,1)}, u32[]{:S(2)}, u32[]{:S(2)}) collective-permute-start(bf16[64,2048]{1,0:T(8,128)(2,1)} %collective-permute-done.6.refs_2_), channel_id=1, source_target_pairs={{0,1},{1,0},{2,3},{3,2},{4,5},{5,4},{6,7},{7,6},{8,9},{9,8},{10,11... | collective-permute-start | bytes 786440 | tf_op jit(solution)/shard_map/ppermute | solution.py:16
  59.5 21.0 %copy-start.6 = (bf16[64,4096]{1,0:T(8,128)(2,1)S(1)}, bf16[64,4096]{1,0:T(8,128)(2,1)}, u32[]{:S(2)}) copy-start(bf16[64,4096]{1,0:T(8,128)(2,1)} %copy-done.5) | copy-start | bytes 1572868
  59.5 21.0 %collective-permute-start.13 = (bf16[192,4096]{1,0:T(8,128)(2,1)}, bf16[192,4096]{1,0:T(8,128)(2,1)}, u32[]{:S(2)}, u32[]{:S(2)}) collective-permute-start(bf16[192,4096]{1,0:T(8,128)(2,1)} %encode.6.refs_4_.refs_2_), channel_id=1, source_target_pairs={{0,8},{16,24},{1,9},{17,25},{2,10},{18,26},{3,11},{19,27},{4,12},{... | collective-permute-start | bytes 4718600 | tf_op jit(solution)/shard_map/ppermute | solution.py:220
  62.1 14.9 %collective-permute-start.12 = (bf16[128,4096]{1,0:T(8,128)(2,1)}, bf16[128,4096]{1,0:T(8,128)(2,1)S(1)}, u32[]{:S(2)}, u32[]{:S(2)}) collective-permute-start(bf16[128,4096]{1,0:T(8,128)(2,1)} %encode.5.refs_5_.refs_1_), channel_id=1, source_target_pairs={{0,8},{16,24},{1,9},{17,25},{2,10},{18,26},{3,11},{19,27},{4,12},{... | collective-permute-start | bytes 3145736 | tf_op jit(solution)/shard_map/ppermute | solution.py:220
  63.5 11.7 %collective-permute-start.11 = (bf16[64,4096]{1,0:T(8,128)(2,1)}, bf16[64,4096]{1,0:T(8,128)(2,1)S(1)}, u32[]{:S(2)}, u32[]{:S(2)}) collective-permute-start(bf16[64,4096]{1,0:T(8,128)(2,1)} %copy-done.5), channel_id=1, source_target_pairs={{0,8},{16,24},{1,9},{17,25},{2,10},{18,26},{3,11},{19,27},{4,12},{... | collective-permute-start | bytes 1572872 | tf_op jit(solution)/shard_map/ppermute | solution.py:220
  64.8 48.2 %collective-permute-start.15 = (bf16[192,4096]{1,0:T(8,128)(2,1)}, bf16[192,4096]{1,0:T(8,128)(2,1)}, u32[]{:S(2)}, u32[]{:S(2)}) collective-permute-start(bf16[192,4096]{1,0:T(8,128)(2,1)} %encode.6.refs_4_.refs_2_), channel_id=1, source_target_pairs={{0,16},{8,24},{1,17},{9,25},{2,18},{10,26},{3,19},{11,27},{4,20},{... | collective-permute-start | bytes 4718600 | tf_op jit(solution)/shard_map/ppermute | solution.py:214
  72.9 7.7 %collective-permute-start.14 = (bf16[128,4096]{1,0:T(8,128)(2,1)S(1)}, bf16[128,4096]{1,0:T(8,128)(2,1)}, u32[]{:S(2)}, u32[]{:S(2)}) collective-permute-start(bf16[128,4096]{1,0:T(8,128)(2,1)S(1)} %encode.7.refs_3_), channel_id=1, source_target_pairs={{0,8},{16,24},{1,9},{17,25},{2,10},{18,26},{3,11},{19,27},{4,12},{... | collective-permute-start | bytes 3145736 | tf_op jit(solution)/shard_map/ppermute | solution.py:220
  75.2 20.9 %collective-permute-start.10 = (bf16[128,4096]{1,0:T(8,128)(2,1)}, bf16[128,4096]{1,0:T(8,128)(2,1)}, u32[]{:S(2)}, u32[]{:S(2)}) collective-permute-start(bf16[128,4096]{1,0:T(8,128)(2,1)} %collective-permute-done.3.refs_5_.refs_1_), channel_id=1, source_target_pairs={{16,24},{24,16},{17,25},{25,17},{18,26},{26,18},{19,27},{27,19},{2... | collective-permute-start | bytes 3145736 | tf_op jit(solution)/shard_map/ppermute | solution.py:217
  78.1 18.0 %collective-permute-start.9 = (bf16[64,4096]{1,0:T(8,128)(2,1)S(1)}, bf16[64,4096]{1,0:T(8,128)(2,1)}, u32[]{:S(2)}, u32[]{:S(2)}) collective-permute-start(bf16[64,4096]{1,0:T(8,128)(2,1)S(1)} %copy-done.8), channel_id=1, source_target_pairs={{16,24},{24,16},{17,25},{25,17},{18,26},{26,18},{19,27},{27,19},{2... | collective-permute-start | bytes 1572872 | tf_op jit(solution)/shard_map/ppermute | solution.py:217
  96.0 17.0 %copy-start.2 = (f32[512,2048]{1,0:T(8,128)}, f32[512,2048]{1,0:T(8,128)S(1)}, u32[]{:S(2)}) copy-start(f32[512,2048]{1,0:T(8,128)S(1)} %decode_own.1.refs_5_.refs_3_) | copy-start | bytes 12582916
  113.1 23.1 %collective-permute-start.16 = (bf16[192,4096]{1,0:T(8,128)(2,1)}, bf16[192,4096]{1,0:T(8,128)(2,1)}, u32[]{:S(2)}, u32[]{:S(2)}) collective-permute-start(bf16[192,4096]{1,0:T(8,128)(2,1)} %collective-permute-done.15.refs_0_), channel_id=1, source_target_pairs={{16,24},{24,16},{17,25},{25,17},{18,26},{26,18},{19,27},{27,19},{2... | collective-permute-start | bytes 4718600 | tf_op jit(solution)/shard_map/ppermute | solution.py:217
  126.9 28.4 %all-to-all-start = ((bf16[8,192,256]{2,1,0:T(8,128)(2,1)}), bf16[8,192,256]{2,1,0:T(8,128)(2,1)S(1)}, u32[]{:S(2)}, u32[]{:S(2)}) async-start(bf16[8,192,256]{2,1,0:T(8,128)(2,1)} %decode_crossed.3.refs_4_), calls=%async_computation | async-start | bytes 1572864 | tf_op jit(solution)/shard_map/all_to_all | solution.py:223
  134.9 26.8 %collective-permute-start.17 = (bf16[128,4096]{1,0:T(8,128)(2,1)S(1)}, bf16[128,4096]{1,0:T(8,128)(2,1)}, u32[]{:S(2)}, u32[]{:S(2)}) collective-permute-start(bf16[128,4096]{1,0:T(8,128)(2,1)S(1)} %encode.7.refs_3_), channel_id=1, source_target_pairs={{0,16},{8,24},{1,17},{9,25},{2,18},{10,26},{3,19},{11,27},{4,20},{... | collective-permute-start | bytes 3145736 | tf_op jit(solution)/shard_map/ppermute | solution.py:214
  155.3 28.6 %all-to-all-start.1 = ((bf16[8,192,256]{2,1,0:T(8,128)(2,1)}), bf16[8,192,256]{2,1,0:T(8,128)(2,1)S(1)}, u32[]{:S(2)}, u32[]{:S(2)}) async-start(bf16[8,192,256]{2,1,0:T(8,128)(2,1)} %decode_crossed.4.refs_4_), calls=%async_computation.1 | async-start | bytes 1572864 | tf_op jit(solution)/shard_map/all_to_all | solution.py:223
  161.7 4.8 %collective-permute-start.18 = (bf16[128,4096]{1,0:T(8,128)(2,1)}, bf16[128,4096]{1,0:T(8,128)(2,1)S(1)}, u32[]{:S(2)}, u32[]{:S(2)}) collective-permute-start(bf16[128,4096]{1,0:T(8,128)(2,1)} %collective-permute-done.17.refs_0_), channel_id=1, source_target_pairs={{16,24},{24,16},{17,25},{25,17},{18,26},{26,18},{19,27},{27,19},{2... | collective-permute-start | bytes 3145736 | tf_op jit(solution)/shard_map/ppermute | solution.py:217
  183.9 20.5 %all-to-all-start.2 = ((bf16[8,128,256]{2,1,0:T(8,128)(2,1)}), bf16[8,128,256]{2,1,0:T(8,128)(2,1)S(1)}, u32[]{:S(2)}, u32[]{:S(2)}) async-start(bf16[8,128,256]{2,1,0:T(8,128)(2,1)} %decode_crossed.5.refs_2_), calls=%async_computation.2 | async-start | bytes 1048576 | tf_op jit(solution)/shard_map/all_to_all | solution.py:223
  (12 other events, 18.5 us)

commit v3 on v0

--- a/solution.py
+++ b/solution.py
@@ -1,16 +1,336 @@
+import functools
+
 import jax
 import jax.numpy as jnp
 from jax import lax
+from jax.experimental import pallas as pl
+from jax.experimental.pallas import tpu as pltpu
 from jax.sharding import PartitionSpec as P
 
 L_WIN = 4
-
-
-def from_partner(array, axis, stride):
-    return lax.ppermute(array, axis, [(i, i ^ 1 << stride) for i in range(lax.axis_size(axis))])
-
-
-def on_device(layer_inputs, targets, encoder, encoder_bias, decoder):
+MIB = 1024 * 1024
+
+
+def exchange(array, axis, flip):
+    size = lax.axis_size(axis)
+    return lax.ppermute(array, axis, [(i, i ^ flip) for i in range(size)])
+
+
+ANYWHERE = pl.BlockSpec(memory_space=pl.ANY)
+WHOLE = pl.BlockSpec(memory_space=pltpu.VMEM)
+SLOTS = 3
+ENCODE_MIB = 12
+FIRST_MIB = 46
+LATER_MIB = 26
+
+
+def encode_kernel(n_in, n_out, *refs):
+    parts, (weight, bias), refs = refs[:n_in], refs[n_in : n_in + 2], refs[n_in + 2 :]
+    outs, tokens = refs[-1 - n_out : -1], refs[-1]
+    row = 0
+    for part in parts:
+        size = part.shape[0]
+        tokens[pl.ds(row, size), :] = part[...]
+        row += size
+    features = weight.shape[2]
+    block = min(512, features)
+
+    @pl.loop(0, features // block)
+    def _(j):
+        cols = pl.ds(pl.multiple_of(j * block, block), block)
+        preact = jnp.dot(tokens[...], weight[0, :, cols], preferred_element_type=jnp.float32)
+        acts = jnp.maximum(preact + bias[:, cols], 0.0).astype(jnp.bfloat16)
+        row = 0
+        for out in outs:
+            size = out.shape[0]
+            out[:, cols] = acts[row : row + size]
+            row += size
+
+
+def first_kernel(*refs):
+    *parts, weight, bias, out, keep, tokens, sems = refs
+    row = 0
+    features = weight.shape[2]
+    block = features // sems.shape[0]
+
+    def fetch(j):
+        cols = pl.ds(pl.multiple_of(j * block, block), block)
+        return pltpu.make_async_copy(weight.at[0, :, cols], keep.at[0, :, cols], sems.at[j])
+
+    for j in range(sems.shape[0]):
+        fetch(jnp.int32(j)).start()
+    for part in parts:
+        size = part.shape[0]
+        tokens[pl.ds(row, size), :] = part[...]
+        row += size
+
+    @pl.loop(0, sems.shape[0])
+    def _(j):
+        fetch(j).wait()
+        cols = pl.ds(pl.multiple_of(j * block, block), block)
+        preact = jnp.dot(tokens[...], keep[0, :, cols], preferred_element_type=jnp.float32)
+        out[:, cols] = jnp.maximum(preact + bias[:, cols], 0.0).astype(out.dtype)
+
+
+def encode_first(parts, weight, bias):
+    rows = sum(part.shape[0] for part in parts)
+    _, width, features = weight.shape
+    steps = max(1, features // 512)
+    return pl.pallas_call(
+        first_kernel,
+        in_specs=[WHOLE] * len(parts) + [ANYWHERE, WHOLE],
+        out_specs=[WHOLE, WHOLE],
+        out_shape=[
+            jax.ShapeDtypeStruct((rows, features), jnp.bfloat16),
+            pltpu.VMEM(weight.shape, weight.dtype),
+        ],
+        scratch_shapes=[pltpu.VMEM((rows, width), jnp.bfloat16), pltpu.SemaphoreType.DMA((steps,))],
+        compiler_params=pltpu.CompilerParams(vmem_limit_bytes=ENCODE_MIB * MIB),
+        name="encode_first",
+    )(*parts, weight, bias)
+
+
+def encode(parts, out_rows, weight, bias, after):
+    rows = sum(part.shape[0] for part in parts)
+    _, width, features = weight.shape
+    return pl.pallas_call(
+        functools.partial(encode_kernel, len(parts), len(out_rows)),
+        in_specs=[WHOLE] * (len(parts) + 2) + [ANYWHERE] * len(after),
+        out_specs=[WHOLE] * len(out_rows),
+        out_shape=[jax.ShapeDtypeStruct((n, features), jnp.bfloat16) for n in out_rows],
+        scratch_shapes=[pltpu.VMEM((rows, width), jnp.bfloat16)],
+        compiler_params=pltpu.CompilerParams(vmem_limit_bytes=ENCODE_MIB * MIB),
+        name="encode",
+    )(*parts, weight, bias, *after)
+
+
+def wave_kernel(pairs, base_row, n_base, keep_total, n_parts, info, *refs):
+    parts, refs = refs[:n_parts], refs[n_parts:]
+    weights, base, refs = refs[0], refs[1 : 1 + n_base], refs[1 + n_base :]
+    n_rings = 2 * len(pairs)
+    rings, sems, refs = refs[-2 * n_rings : -n_rings], refs[-n_rings:], refs[: -2 * n_rings]
+    out, total = refs[-2:]
+    step, steps = pl.program_id(0), pl.num_programs(0)
+    slots, block = rings[0].shape[0], rings[0].shape[1]
+
+    def on(flag, action):
+        if flag is None:
+            action()
+        else:
+            pl.when(info[flag] == 1)(action)
+
+    def fetch(i, lag, k):
+        slot = lax.rem(k, slots)
+        rows = pl.ds(pl.multiple_of(k * block, block), block)
+        source = weights.at[0, 0 if lag is None else info[lag], rows]
+        return pltpu.make_async_copy(source, rings[i].at[slot], sems[i].at[slot])
+
+    def fetch_all(k):
+        for i, (_, lag, flag) in enumerate(s for _, _, *pair in pairs for s in pair):
+            on(flag, lambda: fetch(i, lag, k).start())
+
+    @pl.when(step == 0)
+    def _():
+        for k in range(slots - 1):
+            fetch_all(jnp.int32(k))
+
+    pl.when(step + slots - 1 < steps)(lambda: fetch_all(step + slots - 1))
+
+    @pl.when(step == 0)
+    def _():
+        total[...] = base[0][pl.ds(base_row, total.shape[0]), :] if n_base else jnp.zeros_like(total)
+
+    def product(i, source):
+        places, lag, _ = source
+        fetch(i, lag, step).wait()
+        values = [parts[p][...] for p in places]
+        acts = values[0] if len(values) == 1 else jnp.concatenate(values, axis=0)
+        return jnp.dot(acts, rings[i][lax.rem(step, slots)], preferred_element_type=jnp.float32)
+
+    for number, (row, size, first, second) in enumerate(pairs):
+        at = pl.ds(row, size)
+        i = 2 * number
+
+        def both():
+            total[at, :] += product(i, first) + product(i + 1, second)
+
+        def one():
+            total[at, :] += product(i, first)
+
+        if first[2] is None:
+            pl.when(info[second[2]] == 0)(one)
+        pl.when(info[second[2]] == 1)(both)
+
+    @pl.when(step == steps - 1)
+    def _():
+        cols = out.shape[2]
+        for j in range(out.shape[0]):
+            out[j] = total[: out.shape[1], j * cols : (j + 1) * cols].astype(out.dtype)
+
+
+def decode_wave(info, pairs, decoder, base, base_row, done_rows, keep_total, shards, after, limit):
+    _, _, features, width = decoder.shape
+    block = min(512, features)
+    rows = max(row + size for row, size, _, _ in pairs)
+    operands, in_specs, numbered = [], [], []
+    for row, size, *pair in pairs:
+        placed = []
+        for parts, lag, flag in pair:
+            places = []
+            for part in parts:
+                places.append(len(operands))
+                operands.append(part)
+                in_specs.append(
+                    pl.BlockSpec(
+                        (part.shape[0], block),
+                        lambda k, info, flag=flag: (0, k if flag is None else k * info[flag]),
+                    )
+                )
+            placed.append((tuple(places), lag, flag))
+        numbered.append((row, size, *placed))
+    n_parts = len(operands)
+    operands.append(decoder)
+    in_specs.append(ANYWHERE)
+    if base is not None:
+        operands.append(base)
+        in_specs.append(
+            pl.BlockSpec(base.shape, lambda k, info: (0, 0), pipeline_mode=pl.Buffered(1))
+        )
+    total_shape = jax.ShapeDtypeStruct((rows, width), jnp.float32)
+    out_shape = jax.ShapeDtypeStruct((shards, done_rows, width // shards), jnp.bfloat16)
+    out_spec = pl.BlockSpec(out_shape.shape, lambda k, info: (0, 0, 0))
+    total_spec = pl.BlockSpec(total_shape.shape, lambda k, info: (0, 0))
+    return pl.pallas_call(
+        functools.partial(
+            wave_kernel, numbered, base_row, int(base is not None), keep_total, n_parts
+        ),
+        grid_spec=pltpu.PrefetchScalarGridSpec(
+            num_scalar_prefetch=1,
+            grid=(features // block,),
+            in_specs=in_specs + [ANYWHERE] * len(after),
+            out_specs=[out_spec, total_spec] if keep_total else [out_spec],
+            scratch_shapes=([] if keep_total else [pltpu.VMEM(total_shape.shape, jnp.float32)])
+            + [pltpu.VMEM((SLOTS, block, width), decoder.dtype)] * (2 * len(pairs))
+            + [pltpu.SemaphoreType.DMA((SLOTS,))] * (2 * len(pairs)),
+        ),
+        out_shape=[out_shape, total_shape] if keep_total else [out_shape],
+        compiler_params=pltpu.CompilerParams(vmem_limit_bytes=limit * MIB),
+        name="decode_wave",
+    )(info, *operands, *after)
+
+
+def sum_kernel(sign, slots, base, *refs):
+    received, out = refs[: len(slots)], refs[-1]
+    out[...] = sign * base[...]
+    for ref, blocks in zip(received, slots):
+        size = ref.shape[1] // len(blocks)
+        for source in range(ref.shape[0]):
+            for k, s in enumerate(blocks):
+                at = pl.ds((source ^ s) * size, size)
+                out[at, :] += ref[source, pl.ds(k * size, size), :].astype(jnp.float32)
+
+
+def add_up(base, sign, slots, received, after):
+    return pl.pallas_call(
+        functools.partial(sum_kernel, sign, slots),
+        in_specs=[WHOLE] * (1 + len(received)) + [ANYWHERE] * len(after),
+        out_specs=WHOLE,
+        out_shape=jax.ShapeDtypeStruct(base.shape, base.dtype),
+        compiler_params=pltpu.CompilerParams(vmem_limit_bytes=ENCODE_MIB * MIB),
+        name="add_up",
+    )(base, *received, *after)
+
+
+def pipelined(layer_inputs, targets, encoder, encoder_bias, decoder):
+    shards = lax.axis_size("feat")
+    layers = lax.axis_size("layer")
+    half = layers // 2
+    layer = lax.axis_index("layer")
+    upper = layer >= half
+    info = jnp.stack(
+        [
+            layer & 1,
+            upper.astype(jnp.int32),
+            jnp.full_like(layer, half),
+            jnp.where(upper, layer - ((layer ^ 1) - half), 0),
+        ]
+    ).astype(jnp.int32)
+
+    def up(a):
+        return lax.ppermute(a, "layer", [(i, i + half) for i in range(half)])
+
+    def across(a):
+        return lax.ppermute(a, "layer", [(i, i ^ 1) for i in range(half, layers)])
+
+    def beside(a):
+        return lax.ppermute(a, "layer", [(i, i + 1) for i in range(0, layers, 2)])
+
+    def scatter(partial):
+        return lax.all_to_all(partial, "feat", 0, 0)
+
+    def after(value, *earlier):
+        return lax.optimization_barrier((value, *earlier))[0]
+
+    tokens = layer_inputs[0]
+    size = tokens.shape[0]
+    near = exchange(tokens, "feat", 1)
+    far = [exchange(tokens, "feat", s) for s in range(2, shards, 2)]
+    a0, kept = encode_first([tokens, near], pltpu.with_memory_space_constraint(encoder, pltpu.HBM), encoder_bias)
+    weight = pltpu.with_memory_space_constraint(kept, pltpu.VMEM)
+    def run_encode(parts, earlier):
+        return encode(parts, [sum(p.shape[0] for p in parts)], weight, encoder_bias, earlier)[0]
+
+    d0, n0 = up(a0), beside(a0)
+    rest = exchange(jnp.concatenate(far, axis=0), "feat", 1)
+    a1 = run_encode(far, [a0])
+    d1, n1 = up(a1), beside(a1)
+    a2 = run_encode([rest], [a1, d0])
+    d2, n2 = up(a2), beside(a2)
+    slots = [[0, 1], list(range(2, shards, 2)), list(range(3, shards, 2))]
+
+    odd_, upper_, lag_direct, lag_swapped = range(4)
+    c0 = across(after(d0, a2))
+    held = 2 * size
+    wave, base = decode_wave(
+        info,
+        [
+            (0, shards * size, ([a0, a1, a2], None, None), ([n0, n1, n2], odd_, odd_)),
+            (0, held, ([d0], lag_direct, upper_), ([c0], lag_swapped, upper_)),
+        ],
+        decoder,
+        None,
+        0,
+        held,
+        True,
+        shards,
+        [],
+        FIRST_MIB,
+    )
+    received = [scatter(wave)]
+    row = held
+    for blocks, d in zip(slots[1:], (d1, d2)):
+        d = after(d, wave)
+        rows = size * len(blocks)
+        c = across(d)
+        (wave,) = decode_wave(
+            info,
+            [(0, rows, ([d], lag_direct, upper_), ([c], lag_swapped, upper_))],
+            decoder,
+            base,
+            row,
+            rows,
+            False,
+            shards,
+            [wave],
+            LATER_MIB,
+        )
+        received.append(scatter(wave))
+        row += rows
+    total = add_up(targets[0], -1.0, slots[:2], received[:2], [wave])
+    return add_up(total, 1.0, slots[2:], received[2:], [])[None]
+
+
+def grouped(layer_inputs, targets, encoder, encoder_bias, decoder):
     groups = lax.axis_size("layer") // L_WIN
     depth_bits = groups.bit_length() - 1
     position = lax.axis_index("layer")
@@ -18,7 +338,7 @@
     group_index = position % groups
     gathered = lax.all_gather(layer_inputs[0], "feat", axis=0, tiled=True)
     for bit_index in range(depth_bits):
-        partner = from_partner(gathered, "layer", bit_index)
+        partner = exchange(gathered, "layer", 1 << bit_index)
         upper_bit = position >> bit_index & 1
         gathered = jnp.where(
             upper_bit == 1,
@@ -42,7 +362,7 @@
         upper_bit = position >> bit_index & 1
         kept_half = jnp.where(upper_bit == 1, rebuilt[half_rows:], rebuilt[:half_rows])
         sent_half = jnp.where(upper_bit == 1, rebuilt[:half_rows], rebuilt[half_rows:])
-        rebuilt = kept_half + from_partner(sent_half, "layer", bit_index)
+        rebuilt = kept_half + exchange(sent_half, "layer", 1 << bit_index)
     summed = lax.psum_scatter(rebuilt, "feat", scatter_dimension=1, tiled=True)
     residual = summed - targets[0]
     return residual[None]
@@ -56,6 +376,12 @@
         P("layer", "feat"),
         P("layer", None, "feat", None),
     )
+    shards = mesh.shape["feat"]
+    simple = mesh.shape["layer"] == L_WIN and shards >= 8 and shards & (shards - 1) == 0
     return jax.shard_map(
-        on_device, mesh=mesh, in_specs=placed, out_specs=P("layer", None, "feat"), check_vma=False
+        pipelined if simple else grouped,
+        mesh=mesh,
+        in_specs=placed,
+        out_specs=P("layer", None, "feat"),
+        check_vma=False,
     )

time: 336 us -> 192 us (0.57)
  waiting for transfers between devices: 247 us -> 58.4 us
  Pallas kernels: 0 us -> 74.9 us
  matrix products: 58.5 us -> 0 us
  starting transfers between devices: 0.08 us -> 49.4 us
  between operations: 13.1 us -> 0.2 us
  local copies, waits for them, and re-layouts: 14 us -> 7.87 us
    all_gather x2 -> x0, waiting for transfers between devices: 156 us -> none  [the longest x1 103 us: on_device(): every_layer = lax.all_gather(features[None], 'layer', axis=0, tiled=True)]
    reduce_scatter x1 -> x0, waiting for transfers between devices: 89.7 us -> none  [on_device(): summed = lax.psum_scatter(rebuilt, 'feat', scatter_dimension=1, tiled=True)]
    pallas_call x0 -> x8, Pallas kernels: none -> 74.9 us  [the longest x3 56.7 us: decode_wave(): pl.pallas_call(functools.partial(wave_kernel, numbered, base_row, int(bas...]
    dot_general x2 -> x0, matrix products: 58.5 us -> none  [the longest x1 44.1 us: on_device(): jnp.einsum('ktf,kfd->td', stacked, decoder[0], preferred_element_type=jnp...]
    ppermute x0 -> x14, waiting for transfers between devices: none -> 34.9 us  [the longest x5 16.7 us: exchange(): return lax.ppermute(array, axis, [(i, i ^ flip) for i in range(size)])]
    ppermute x0 -> x14, starting transfers between devices: none -> 34 us  [the longest x3 16.4 us: across(): return lax.ppermute(a, 'layer', [(i, i ^ 1) for i in range(half, layers)])]
    all_to_all x0 -> x3, waiting for transfers between devices: none -> 23.5 us  [scatter(): return lax.all_to_all(partial, 'feat', 0, 0)]
    all_to_all x0 -> x3, starting transfers between devices: none -> 15.4 us  [scatter(): return lax.all_to_all(partial, 'feat', 0, 0)]
  transfers between devices with their start and end apart: 3 -> 17, of which waited for: 3 -> 8; matrix products, arithmetic and copies ran while one was open for 0% -> 0% of each run, Pallas kernels for 0% -> 39%
where the time goes in v3:
time: 192 us; the launch traced here: 191 us
  Pallas kernels  74.9 us (39%)
  waiting for transfers between devices  58.4 us (30%)
  starting transfers between devices  49.4 us (26%)
  local copies, waits for them, and re-layouts  7.87 us (4%)
    pallas_call x3, Pallas kernels, decode_wave(): pl.pallas_call(functools.partial(wave_kernel, numbered, base_row, int(bas...  56.7 us
    all_to_all x3, waiting for transfers between devices, scatter(): return lax.all_to_all(partial, 'feat', 0, 0)  23.5 us
    ppermute x5, waiting for transfers between devices, exchange(): return lax.ppermute(array, axis, [(i, i ^ flip) for i in range(size)])  16.7 us
    ppermute x3, starting transfers between devices, across(): return lax.ppermute(a, 'layer', [(i, i ^ 1) for i in range(half, layers)])  16.4 us
    all_to_all x3, starting transfers between devices, scatter(): return lax.all_to_all(partial, 'feat', 0, 0)  15.4 us
    ppermute x3, waiting for transfers between devices, up(): return lax.ppermute(a, 'layer', [(i, i + half) for i in range(half)])  15.3 us
    pallas_call x2, Pallas kernels, encode(): pl.pallas_call(functools.partial(encode_kernel, len(parts), len(out_rows)...  9.65 us
    unnamed x16, local copies, waits for them, and re-layouts  7.87 us
  transfers between devices with their start and end apart: 17, of which 8 were waited for; matrix products, arithmetic and copies ran while one was open for 0% of the time, Pallas kernels for 39%

profile of v3, /device:TPU:2, one launch (start us, length us, event | category | flops | bytes accessed | tf_op | source)
XLA Modules:
  0.0 191.0 jit_solution(13273679478928331144)
XLA Ops:
  0.0 1.5 collective-permute-start
  1.5 1.6 collective-permute-start.1
  3.1 2.6 %collective-permute-start.2 = (bf16[64,2048]{1,0:T(8,128)(2,1)}, bf16[64,2048]{1,0:T(8,128)(2,1)S(1)}, u32[]{:S(2)}, u32[]{:S(2)}) collective-permute-start(bf16[64,2048]{1,0:T(8,128)(2,1)} %bitcast.9), channel_id=1, source_target_pairs={{0,4},{1,5},{2,6},{3,7},{4,0},{5,1},{6,2},{7,3},{8,12},{9,13},{10,... | collective-permute-start | bytes 786440 | tf_op jit(solution)/shard_map/ppermute | solution.py:16
  5.9 2.3 %collective-permute-done.refs_1_ = bf16[64,2048]{1,0:T(8,128)(2,1)S(1)} collective-permute-done((bf16[64,2048]{1,0:T(8,128)(2,1)}, bf16[64,2048]{1,0:T(8,128)(2,1)S(1)}, u32[]{:S(2)}, u32[]{:S(2)}) %collective-permute-start) | collective-permute-done | bytes 262176 | tf_op jit(solution)/shard_map/ppermute | solution.py:16
  9.9 7.5 %encode_first.1 = (bf16[128,4096]{1,0:T(8,128)(2,1)}, bf16[1,2048,4096]{2,1,0:T(8,128)(2,1)S(1)}) custom-call(bf16[64,2048]{1,0:T(8,128)(2,1)S(1)} %bitcast.11, bf16[64,2048]{1,0:T(8,128)(2,1)S(1)} %collective-permute-done.refs_1_, bf16[1,2048,4096]{2,1,0:T(8,128)(2,1)} %refs_2_.4, f32[1,4096]{1,0:T(1,128)S(1)} %copy-done.6), custom_call_target="tpu_custom_call" | custom-call | tf_op jit(solution)/shard_map/encode_first/pallas_call | solution.py:79
  17.4 1.3 collective-permute-start.5
  18.7 6.0 %collective-permute-done.2.refs_1_ = bf16[64,2048]{1,0:T(8,128)(2,1)S(1)} collective-permute-done((bf16[64,2048]{1,0:T(8,128)(2,1)}, bf16[64,2048]{1,0:T(8,128)(2,1)S(1)}, u32[]{:S(2)}, u32[]{:S(2)}) %collective-permute-start.2) | collective-permute-done | bytes 262176 | tf_op jit(solution)/shard_map/ppermute | solution.py:16
  25.3 4.8 %encode.2.refs_3_.refs_1_ = bf16[192,4096]{1,0:T(8,128)(2,1)S(1)} custom-call(bf16[64,2048]{1,0:T(8,128)(2,1)S(1)} %collective-permute-done.1.refs_0_, bf16[64,2048]{1,0:T(8,128)(2,1)S(1)} %collective-permute-done.2.refs_1_, bf16[64,2048]{1,0:T(8,128)(2,1)S(1)} %collective-permute-done.3.refs_2_, ...), custom_call_target="tpu_custom_call" | custom-call | tf_op jit(solution)/shard_map/encode/pallas_call | solution.py:96
  30.2 2.5 %collective-permute-start.7 = (bf16[192,4096]{1,0:T(8,128)(2,1)S(1)}, bf16[192,4096]{1,0:T(8,128)(2,1)}, u32[]{:S(2)}, u32[]{:S(2)}) collective-permute-start(bf16[192,4096]{1,0:T(8,128)(2,1)S(1)} %encode.2.refs_3_.refs_1_), channel_id=1, source_target_pairs={{0,8},{16,24},{1,9},{17,25},{2,10},{18,26},{3,11},{19,27},{4,12},{... | collective-permute-start | bytes 4718600 | tf_op jit(solution)/shard_map/ppermute | solution.py:266
  32.6 8.4 %collective-permute-done.4.refs_0_ = bf16[192,2048]{1,0:T(8,128)(2,1)S(1)} collective-permute-done((bf16[192,2048]{1,0:T(8,128)(2,1)S(1)}, bf16[192,2048]{1,0:T(8,128)(2,1)S(1)}, u32[]{:S(2)}, u32[]{:S(2)}) %collective-permute-start.4) | collective-permute-done | bytes 786464 | tf_op jit(solution)/shard_map/ppermute | solution.py:16
  41.0 2.6 %collective-permute-done.5.refs_4_.refs_6_ = bf16[128,4096]{1,0:T(8,128)(2,1)} collective-permute-done((bf16[128,4096]{1,0:T(8,128)(2,1)}, bf16[128,4096]{1,0:T(8,128)(2,1)}, u32[]{:S(2)}, u32[]{:S(2)}) %collective-permute-start.5) | collective-permute-done | bytes 1048608 | tf_op jit(solution)/shard_map/ppermute | solution.py:260
  43.7 4.8 %encode.3.refs_2_ = bf16[192,4096]{1,0:T(8,128)(2,1)S(1)} custom-call(bf16[192,2048]{1,0:T(8,128)(2,1)S(1)} %collective-permute-done.4.refs_0_, bf16[1,2048,4096]{2,1,0:T(8,128)(2,1)S(1)} %get-tuple-element.13.refs_3_.refs_1_, f32[1,4096]{1,0:T(1,128)S(1)} %copy-done.7, bf16[192,4096]{1,0:T(8,128)(2,1)S(1)} %encode.2.refs_3_.refs_1_, ...), custom_call_target="tpu_custom_call" | custom-call | tf_op jit(solution)/shard_map/encode/pallas_call | solution.py:96
  48.5 2.5 %collective-permute-start.8 = (bf16[192,4096]{1,0:T(8,128)(2,1)S(1)}, bf16[192,4096]{1,0:T(8,128)(2,1)}, u32[]{:S(2)}, u32[]{:S(2)}) collective-permute-start(bf16[192,4096]{1,0:T(8,128)(2,1)S(1)} %encode.3.refs_2_), channel_id=1, source_target_pairs={{0,8},{16,24},{1,9},{17,25},{2,10},{18,26},{3,11},{19,27},{4,12},{... | collective-permute-start | bytes 4718600 | tf_op jit(solution)/shard_map/ppermute | solution.py:266
  51.0 1.3 collective-permute-start.10
  52.3 2.3 %collective-permute-start.6 = (bf16[128,4096]{1,0:T(8,128)(2,1)}, bf16[128,4096]{1,0:T(8,128)(2,1)}, u32[]{:S(2)}, u32[]{:S(2)}) collective-permute-start(bf16[128,4096]{1,0:T(8,128)(2,1)} %get-tuple-element.12.refs_5_.refs_0_), channel_id=1, source_target_pairs={{0,8},{16,24},{1,9},{17,25},{2,10},{18,26},{3,11},{19,27},{4,12},{... | collective-permute-start | bytes 3145736 | tf_op jit(solution)/shard_map/ppermute | solution.py:266
  54.6 1.9 collective-permute-start.9
  56.6 2.9 %collective-permute-done.9.refs_7_ = bf16[128,4096]{1,0:T(8,128)(2,1)} collective-permute-done((bf16[128,4096]{1,0:T(8,128)(2,1)}, bf16[128,4096]{1,0:T(8,128)(2,1)}, u32[]{:S(2)}, u32[]{:S(2)}) %collective-permute-start.9) | collective-permute-done | bytes 1048608 | tf_op jit(solution)/shard_map/ppermute | solution.py:263
  59.5 26.2 %decode_wave.3 = (bf16[8,128,256]{2,1,0:T(8,128)(2,1)S(1)}, f32[512,2048]{1,0:T(8,128)}) custom-call(s32[4]{0:T(128)S(1)} %pad_add_fusion.info, bf16[128,4096]{1,0:T(8,128)(2,1)} %get-tuple-element.12.refs_5_.refs_0_, bf16[192,4096]{1,0:T(8,128)(2,1)S(1)} %encode.2.refs_3_.refs_1_, bf16[192,4096]{1,0:T(8,128)(2,1)S(1)} %encode.3.refs_2_, ...), custom_call_target="tpu_custom_call" | custom-call | tf_op jit(solution)/shard_map/decode_wave/pallas_call | solution.py:203
  86.5 12.6 %collective-permute-start.11 = (bf16[192,4096]{1,0:T(8,128)(2,1)}, bf16[192,4096]{1,0:T(8,128)(2,1)}, u32[]{:S(2)}, u32[]{:S(2)}) collective-permute-start(bf16[192,4096]{1,0:T(8,128)(2,1)} %collective-permute-done.10.refs_0_), channel_id=1, source_target_pairs={{16,24},{24,16},{17,25},{25,17},{18,26},{26,18},{19,27},{27,19},{2... | collective-permute-start | bytes 4718600 | tf_op jit(solution)/shard_map/ppermute | solution.py:263
  99.1 1.3 collective-permute-start.12
  100.4 5.9 %all-to-all-start = ((bf16[8,128,256]{2,1,0:T(8,128)(2,1)}), bf16[8,128,256]{2,1,0:T(8,128)(2,1)S(1)}, u32[]{:S(2)}, u32[]{:S(2)}) async-start(bf16[8,128,256]{2,1,0:T(8,128)(2,1)} %copy-done.2), calls=%async_computation | async-start | bytes 1048576 | tf_op jit(solution)/shard_map/all_to_all | solution.py:269
  106.3 2.2 %copy-done = f32[512,2048]{1,0:T(8,128)S(1)} copy-done((f32[512,2048]{1,0:T(8,128)S(1)}, f32[512,2048]{1,0:T(8,128)}, u32[]{:S(2)}) %copy-start) | copy-done | bytes 4194328
  108.5 1.0 copy-done.3
  109.5 15.2 %decode_wave.4.refs_4_ = bf16[8,192,256]{2,1,0:T(8,128)(2,1)} custom-call(s32[4]{0:T(128)S(1)} %pad_add_fusion.info, bf16[192,4096]{1,0:T(8,128)(2,1)} %collective-permute-done.10.refs_0_, bf16[192,4096]{1,0:T(8,128)(2,1)} %collective-permute-done.11.refs_1_, bf16[1,4,4096,2048]{3,2,1,0:T(8,128)(2,1)} %refs_2_.7, f32[512,2048]{1,0:T(8,128)S(1)} %copy-done, ...), custom_call_target="tpu_custom_call" | custom-call | tf_op jit(solution)/shard_map/decode_wave/pallas_call | solution.py:203
  124.7 12.6 %collective-permute-done.12.refs_0_ = bf16[192,4096]{1,0:T(8,128)(2,1)} collective-permute-done((bf16[192,4096]{1,0:T(8,128)(2,1)S(1)}, bf16[192,4096]{1,0:T(8,128)(2,1)}, u32[]{:S(2)}, u32[]{:S(2)}) %collective-permute-start.12) | collective-permute-done | bytes 1572896 | tf_op jit(solution)/shard_map/ppermute | solution.py:260
  137.4 1.9 %collective-permute-start.13 = (bf16[192,4096]{1,0:T(8,128)(2,1)}, bf16[192,4096]{1,0:T(8,128)(2,1)}, u32[]{:S(2)}, u32[]{:S(2)}) collective-permute-start(bf16[192,4096]{1,0:T(8,128)(2,1)} %collective-permute-done.12.refs_0_), channel_id=1, source_target_pairs={{16,24},{24,16},{17,25},{25,17},{18,26},{26,18},{19,27},{27,19},{2... | collective-permute-start | bytes 4718600 | tf_op jit(solution)/shard_map/ppermute | solution.py:263
  139.3 5.9 %all-to-all-start.1 = ((bf16[8,192,256]{2,1,0:T(8,128)(2,1)}), bf16[8,192,256]{2,1,0:T(8,128)(2,1)S(1)}, u32[]{:S(2)}, u32[]{:S(2)}) async-start(bf16[8,192,256]{2,1,0:T(8,128)(2,1)} %decode_wave.4.refs_4_), calls=%async_computation.1 | async-start | bytes 1572864 | tf_op jit(solution)/shard_map/all_to_all | solution.py:269
  145.2 2.2 %copy-done.1 = f32[512,2048]{1,0:T(8,128)S(1)} copy-done((f32[512,2048]{1,0:T(8,128)S(1)}, f32[512,2048]{1,0:T(8,128)}, u32[]{:S(2)}) %copy-start.1) | copy-done | bytes 4194328
  147.4 15.3 %decode_wave.5.refs_2_ = bf16[8,192,256]{2,1,0:T(8,128)(2,1)} custom-call(s32[4]{0:T(128)S(1)} %pad_add_fusion.info, bf16[192,4096]{1,0:T(8,128)(2,1)} %collective-permute-done.12.refs_0_, bf16[192,4096]{1,0:T(8,128)(2,1)} %collective-permute-done.13.refs_1_, bf16[1,4,4096,2048]{3,2,1,0:T(8,128)(2,1)} %refs_2_.7, f32[512,2048]{1,0:T(8,128)S(1)} %copy-done.1, ...), custom_call_target="tpu_custom_call" | custom-call | tf_op jit(solution)/shard_map/decode_wave/pallas_call | solution.py:203
  162.7 3.3 %all-to-all-done.1.refs_1_ = bf16[8,192,256]{2,1,0:T(8,128)(2,1)S(1)} async-done(((bf16[8,192,256]{2,1,0:T(8,128)(2,1)}), bf16[8,192,256]{2,1,0:T(8,128)(2,1)S(1)}, u32[]{:S(2)}, u32[]{:S(2)}) %all-to-all-start.1) | async-done | bytes 786464 | tf_op jit(solution)/shard_map/all_to_all | solution.py:269
  166.0 3.6 %all-to-all-start.2 = ((bf16[8,192,256]{2,1,0:T(8,128)(2,1)}), bf16[8,192,256]{2,1,0:T(8,128)(2,1)S(1)}, u32[]{:S(2)}, u32[]{:S(2)}) async-start(bf16[8,192,256]{2,1,0:T(8,128)(2,1)} %decode_wave.5.refs_2_), calls=%async_computation.2 | async-start | bytes 1572864 | tf_op jit(solution)/shard_map/all_to_all | solution.py:269
  169.9 20.2 %all-to-all-done.2.refs_0_ = bf16[8,192,256]{2,1,0:T(8,128)(2,1)S(1)} async-done(((bf16[8,192,256]{2,1,0:T(8,128)(2,1)}), bf16[8,192,256]{2,1,0:T(8,128)(2,1)S(1)}, u32[]{:S(2)}, u32[]{:S(2)}) %all-to-all-start.2) | async-done | bytes 786464 | tf_op jit(solution)/shard_map/all_to_all | solution.py:269
  (28 shorter events, 4.6 us)
Async XLA Ops:
  0.0 8.3 %collective-permute-start = (bf16[64,2048]{1,0:T(8,128)(2,1)}, bf16[64,2048]{1,0:T(8,128)(2,1)S(1)}, u32[]{:S(2)}, u32[]{:S(2)}) collective-permute-start(bf16[64,2048]{1,0:T(8,128)(2,1)} %bitcast.7), channel_id=1, source_target_pairs={{0,1},{1,0},{2,3},{3,2},{4,5},{5,4},{6,7},{7,6},{8,9},{9,8},{10,11... | collective-permute-start | bytes 786440 | tf_op jit(solution)/shard_map/ppermute | solution.py:16
  1.5 17.2 %collective-permute-start.1 = (bf16[64,2048]{1,0:T(8,128)(2,1)}, bf16[64,2048]{1,0:T(8,128)(2,1)S(1)}, u32[]{:S(2)}, u32[]{:S(2)}) collective-permute-start(bf16[64,2048]{1,0:T(8,128)(2,1)} %bitcast.8), channel_id=1, source_target_pairs={{0,2},{1,3},{2,0},{3,1},{4,6},{5,7},{6,4},{7,5},{8,10},{9,11},{10,... | collective-permute-start | bytes 786440 | tf_op jit(solution)/shard_map/ppermute | solution.py:16
  3.1 21.6 %collective-permute-start.2 = (bf16[64,2048]{1,0:T(8,128)(2,1)}, bf16[64,2048]{1,0:T(8,128)(2,1)S(1)}, u32[]{:S(2)}, u32[]{:S(2)}) collective-permute-start(bf16[64,2048]{1,0:T(8,128)(2,1)} %bitcast.9), channel_id=1, source_target_pairs={{0,4},{1,5},{2,6},{3,7},{4,0},{5,1},{6,2},{7,3},{8,12},{9,13},{10,... | collective-permute-start | bytes 786440 | tf_op jit(solution)/shard_map/ppermute | solution.py:16
  5.7 19.0 %collective-permute-start.3 = (bf16[64,2048]{1,0:T(8,128)(2,1)}, bf16[64,2048]{1,0:T(8,128)(2,1)S(1)}, u32[]{:S(2)}, u32[]{:S(2)}) collective-permute-start(bf16[64,2048]{1,0:T(8,128)(2,1)} %bitcast.10), channel_id=1, source_target_pairs={{0,6},{1,7},{2,4},{3,5},{4,2},{5,3},{6,0},{7,1},{8,14},{9,15},{10,... | collective-permute-start | bytes 786440 | tf_op jit(solution)/shard_map/ppermute | solution.py:16
  8.3 1.0 copy-start.5
  9.2 0.7 copy-start.6
  17.4 7.9 %copy-start.7 = (f32[1,4096]{1,0:T(1,128)S(1)}, f32[1,4096]{1,0:T(1,128)}, u32[]{:S(2)}) copy-start(f32[1,4096]{1,0:T(1,128)} %refs_2_.5) | copy-start | bytes 49156
  17.4 26.2 %collective-permute-start.5 = (bf16[128,4096]{1,0:T(8,128)(2,1)}, bf16[128,4096]{1,0:T(8,128)(2,1)}, u32[]{:S(2)}, u32[]{:S(2)}) collective-permute-start(bf16[128,4096]{1,0:T(8,128)(2,1)} %get-tuple-element.12.refs_5_.refs_0_), channel_id=1, source_target_pairs={{0,16},{8,24},{1,17},{9,25},{2,18},{10,26},{3,19},{11,27},{4,20},{... | collective-permute-start | bytes 3145736 | tf_op jit(solution)/shard_map/ppermute | solution.py:260
  24.7 16.3 %collective-permute-start.4 = (bf16[192,2048]{1,0:T(8,128)(2,1)S(1)}, bf16[192,2048]{1,0:T(8,128)(2,1)S(1)}, u32[]{:S(2)}, u32[]{:S(2)}) collective-permute-start(bf16[192,2048]{1,0:T(8,128)(2,1)S(1)} %pad_maximum_fusion), channel_id=1, source_target_pairs={{0,1},{1,0},{2,3},{3,2},{4,5},{5,4},{6,7},{7,6},{8,9},{9,8},{10,11... | collective-permute-start | bytes 2359304 | tf_op jit(solution)/shard_map/ppermute | solution.py:16
  30.2 26.4 %collective-permute-start.7 = (bf16[192,4096]{1,0:T(8,128)(2,1)S(1)}, bf16[192,4096]{1,0:T(8,128)(2,1)}, u32[]{:S(2)}, u32[]{:S(2)}) collective-permute-start(bf16[192,4096]{1,0:T(8,128)(2,1)S(1)} %encode.2.refs_3_.refs_1_), channel_id=1, source_target_pairs={{0,8},{16,24},{1,9},{17,25},{2,10},{18,26},{3,11},{19,27},{4,12},{... | collective-permute-start | bytes 4718600 | tf_op jit(solution)/shard_map/ppermute | solution.py:266
  48.5 11.0 %collective-permute-start.8 = (bf16[192,4096]{1,0:T(8,128)(2,1)S(1)}, bf16[192,4096]{1,0:T(8,128)(2,1)}, u32[]{:S(2)}, u32[]{:S(2)}) collective-permute-start(bf16[192,4096]{1,0:T(8,128)(2,1)S(1)} %encode.3.refs_2_), channel_id=1, source_target_pairs={{0,8},{16,24},{1,9},{17,25},{2,10},{18,26},{3,11},{19,27},{4,12},{... | collective-permute-start | bytes 4718600 | tf_op jit(solution)/shard_map/ppermute | solution.py:266
  51.0 35.5 %collective-permute-start.10 = (bf16[192,4096]{1,0:T(8,128)(2,1)S(1)}, bf16[192,4096]{1,0:T(8,128)(2,1)}, u32[]{:S(2)}, u32[]{:S(2)}) collective-permute-start(bf16[192,4096]{1,0:T(8,128)(2,1)S(1)} %encode.2.refs_3_.refs_1_), channel_id=1, source_target_pairs={{0,16},{8,24},{1,17},{9,25},{2,18},{10,26},{3,19},{11,27},{4,20},{... | collective-permute-start | bytes 4718600 | tf_op jit(solution)/shard_map/ppermute | solution.py:260
  52.3 4.3 %collective-permute-start.6 = (bf16[128,4096]{1,0:T(8,128)(2,1)}, bf16[128,4096]{1,0:T(8,128)(2,1)}, u32[]{:S(2)}, u32[]{:S(2)}) collective-permute-start(bf16[128,4096]{1,0:T(8,128)(2,1)} %get-tuple-element.12.refs_5_.refs_0_), channel_id=1, source_target_pairs={{0,8},{16,24},{1,9},{17,25},{2,10},{18,26},{3,11},{19,27},{4,12},{... | collective-permute-start | bytes 3145736 | tf_op jit(solution)/shard_map/ppermute | solution.py:266
  54.6 4.9 %collective-permute-start.9 = (bf16[128,4096]{1,0:T(8,128)(2,1)}, bf16[128,4096]{1,0:T(8,128)(2,1)}, u32[]{:S(2)}, u32[]{:S(2)}) collective-permute-start(bf16[128,4096]{1,0:T(8,128)(2,1)} %collective-permute-done.5.refs_4_.refs_6_), channel_id=1, source_target_pairs={{16,24},{24,16},{17,25},{25,17},{18,26},{26,18},{19,27},{27,19},{2... | collective-permute-start | bytes 3145736 | tf_op jit(solution)/shard_map/ppermute | solution.py:263
  85.7 0.8 copy-start.2
  86.5 19.8 %collective-permute-start.11 = (bf16[192,4096]{1,0:T(8,128)(2,1)}, bf16[192,4096]{1,0:T(8,128)(2,1)}, u32[]{:S(2)}, u32[]{:S(2)}) collective-permute-start(bf16[192,4096]{1,0:T(8,128)(2,1)} %collective-permute-done.10.refs_0_), channel_id=1, source_target_pairs={{16,24},{24,16},{17,25},{25,17},{18,26},{26,18},{19,27},{27,19},{2... | collective-permute-start | bytes 4718600 | tf_op jit(solution)/shard_map/ppermute | solution.py:263
  99.1 38.3 %collective-permute-start.12 = (bf16[192,4096]{1,0:T(8,128)(2,1)S(1)}, bf16[192,4096]{1,0:T(8,128)(2,1)}, u32[]{:S(2)}, u32[]{:S(2)}) collective-permute-start(bf16[192,4096]{1,0:T(8,128)(2,1)S(1)} %encode.3.refs_2_), channel_id=1, source_target_pairs={{0,16},{8,24},{1,17},{9,25},{2,18},{10,26},{3,19},{11,27},{4,20},{... | collective-permute-start | bytes 4718600 | tf_op jit(solution)/shard_map/ppermute | solution.py:260
  100.4 38.9 %all-to-all-start = ((bf16[8,128,256]{2,1,0:T(8,128)(2,1)}), bf16[8,128,256]{2,1,0:T(8,128)(2,1)S(1)}, u32[]{:S(2)}, u32[]{:S(2)}) async-start(bf16[8,128,256]{2,1,0:T(8,128)(2,1)} %copy-done.2), calls=%async_computation | async-start | bytes 1048576 | tf_op jit(solution)/shard_map/all_to_all | solution.py:269
  106.3 2.2 %copy-start = (f32[512,2048]{1,0:T(8,128)S(1)}, f32[512,2048]{1,0:T(8,128)}, u32[]{:S(2)}) copy-start(f32[512,2048]{1,0:T(8,128)} %get-tuple-element.17.refs_3_) | copy-start | bytes 12582916
  108.5 1.0 copy-start.3
  137.4 7.8 %collective-permute-start.13 = (bf16[192,4096]{1,0:T(8,128)(2,1)}, bf16[192,4096]{1,0:T(8,128)(2,1)}, u32[]{:S(2)}, u32[]{:S(2)}) collective-permute-start(bf16[192,4096]{1,0:T(8,128)(2,1)} %collective-permute-done.12.refs_0_), channel_id=1, source_target_pairs={{16,24},{24,16},{17,25},{25,17},{18,26},{26,18},{19,27},{27,19},{2... | collective-permute-start | bytes 4718600 | tf_op jit(solution)/shard_map/ppermute | solution.py:263
  139.3 26.7 %all-to-all-start.1 = ((bf16[8,192,256]{2,1,0:T(8,128)(2,1)}), bf16[8,192,256]{2,1,0:T(8,128)(2,1)S(1)}, u32[]{:S(2)}, u32[]{:S(2)}) async-start(bf16[8,192,256]{2,1,0:T(8,128)(2,1)} %decode_wave.4.refs_4_), calls=%async_computation.1 | async-start | bytes 1572864 | tf_op jit(solution)/shard_map/all_to_all | solution.py:269
  145.2 2.2 %copy-start.1 = (f32[512,2048]{1,0:T(8,128)S(1)}, f32[512,2048]{1,0:T(8,128)}, u32[]{:S(2)}) copy-start(f32[512,2048]{1,0:T(8,128)} %get-tuple-element.17.refs_3_) | copy-start | bytes 12582916
  162.6 7.0 %copy-start.4 = (f32[1,512,256]{2,1,0:T(8,128)S(1)}, f32[1,512,256]{2,1,0:T(8,128)}, u32[]{:S(2)}) copy-start(f32[1,512,256]{2,1,0:T(8,128)} %param.6) | copy-start | bytes 1572868
  166.0 24.0 %all-to-all-start.2 = ((bf16[8,192,256]{2,1,0:T(8,128)(2,1)}), bf16[8,192,256]{2,1,0:T(8,128)(2,1)S(1)}, u32[]{:S(2)}, u32[]{:S(2)}) async-start(bf16[8,192,256]{2,1,0:T(8,128)(2,1)} %decode_wave.5.refs_2_), calls=%async_computation.2 | async-start | bytes 1572864 | tf_op jit(solution)/shard_map/all_to_all | solution.py:269

commit v4 on v0

--- a/solution.py
+++ b/solution.py
@@ -1,16 +1,393 @@
+import functools
+
 import jax
 import jax.numpy as jnp
 from jax import lax
+from jax.experimental import pallas as pl
+from jax.experimental.pallas import tpu as pltpu
 from jax.sharding import PartitionSpec as P
 
 L_WIN = 4
-
-
-def from_partner(array, axis, stride):
-    return lax.ppermute(array, axis, [(i, i ^ 1 << stride) for i in range(lax.axis_size(axis))])
-
-
-def on_device(layer_inputs, targets, encoder, encoder_bias, decoder):
+MIB = 1024 * 1024
+
+
+def exchange(array, axis, flip):
+    size = lax.axis_size(axis)
+    return lax.ppermute(array, axis, [(i, i ^ flip) for i in range(size)])
+
+
+ANYWHERE = pl.BlockSpec(memory_space=pl.ANY)
+WHOLE = pl.BlockSpec(memory_space=pltpu.VMEM)
+SLOTS = 3
+ENCODE_MIB = 12
+DECODE_MIB = 26
+
+
+def fill(order, parts, rows_of):
+    at = 0
+    for part, row, size in order:
+        rows_of[pl.ds(at, size), :] = parts[part][pl.ds(row, size), :]
+        at += size
+
+
+def encode_kernel(order, pieces, n_in, n_after, stream, *refs):
+    parts, weight, bias, refs = refs[:n_in], refs[n_in], refs[n_in + 1], refs[n_in + 2 + n_after :]
+    outs, refs = refs[: len(pieces)], refs[len(pieces) :]
+    features = weight.shape[2]
+    if stream:
+        kept, tokens, sems = refs
+        block = features // sems.shape[0]
+    else:
+        kept, (tokens,) = weight, refs
+        block = min(512, features)
+
+    def fetch(j):
+        cols = pl.ds(pl.multiple_of(j * block, block), block)
+        return pltpu.make_async_copy(weight.at[0, :, cols], kept.at[0, :, cols], sems.at[j])
+
+    if stream:
+        for j in range(features // block):
+            fetch(jnp.int32(j)).start()
+    fill(order, parts, tokens)
+
+    @pl.loop(0, features // block)
+    def _(j):
+        if stream:
+            fetch(j).wait()
+        cols = pl.ds(pl.multiple_of(j * block, block), block)
+        preact = jnp.dot(tokens[...], kept[0, :, cols], preferred_element_type=jnp.float32)
+        acts = jnp.maximum(preact + bias[:, cols], 0.0).astype(jnp.bfloat16)
+        for out, (row, size) in zip(outs, pieces):
+            out[:, cols] = acts[row : row + size]
+
+
+def encode(parts, order, pieces, weight, bias, after, stream=False):
+    rows = sum(size for _, _, size in order)
+    _, width, features = weight.shape
+    out_shape = [jax.ShapeDtypeStruct((size, features), jnp.bfloat16) for _, size in pieces]
+    scratch = [pltpu.VMEM((rows, width), jnp.bfloat16)]
+    if stream:
+        out_shape.append(pltpu.VMEM(weight.shape, weight.dtype))
+        scratch.append(pltpu.SemaphoreType.DMA((max(1, features // 512),)))
+        weight = pltpu.with_memory_space_constraint(weight, pltpu.HBM)
+    else:
+        weight = pltpu.with_memory_space_constraint(weight, pltpu.VMEM)
+    return pl.pallas_call(
+        functools.partial(encode_kernel, order, pieces, len(parts), len(after), stream),
+        in_specs=[WHOLE] * len(parts) + [ANYWHERE if stream else WHOLE, WHOLE] + [ANYWHERE] * len(after),
+        out_specs=[WHOLE] * len(out_shape),
+        out_shape=out_shape,
+        scratch_shapes=scratch,
+        compiler_params=pltpu.CompilerParams(vmem_limit_bytes=ENCODE_MIB * MIB),
+        name="encode",
+    )(*parts, weight, bias, *after)
+
+
+def first_wave_kernel(counts, info, *refs):
+    groups = []
+    for count in counts:
+        groups.append(refs[:count])
+        refs = refs[count:]
+    mine, theirs, direct, swapped = groups
+    weights, out, total, *kept = refs[:5]
+    rings, ring_sems, kept_sems = refs[-3:]
+    step, steps = pl.program_id(0), pl.num_programs(0)
+    slots, block = rings.shape[1], rings.shape[2]
+    odd, upper = info[0] == 1, info[1] == 1
+
+    def rows(k):
+        return pl.ds(pl.multiple_of(k * block, block), block)
+
+    def fetch(source, k):
+        slot = lax.rem(k, slots)
+        return pltpu.make_async_copy(
+            weights.at[0, source, rows(k)], rings.at[source, slot], ring_sems.at[source, slot]
+        )
+
+    def keep(source, k):
+        return pltpu.make_async_copy(
+            weights.at[0, info[2 + source], rows(k)],
+            kept[source].at[rows(k)],
+            kept_sems.at[source, k],
+        )
+
+    def fetch_all(k):
+        fetch(0, k).start()
+        pl.when(odd)(lambda: fetch(1, k).start())
+
+        @pl.when(upper)
+        def _():
+            keep(0, k).start()
+            keep(1, k).start()
+
+    @pl.when(step == 0)
+    def _():
+        for k in range(slots - 1):
+            fetch_all(jnp.int32(k))
+        total[...] = jnp.zeros_like(total)
+
+    pl.when(step + slots - 1 < steps)(lambda: fetch_all(step + slots - 1))
+
+    def product(parts, weight):
+        values = [part[...] for part in parts]
+        acts = values[0] if len(values) == 1 else jnp.concatenate(values, axis=0)
+        return jnp.dot(acts, weight, preferred_element_type=jnp.float32)
+
+    slot = lax.rem(step, slots)
+    fetch(0, step).wait()
+
+    @pl.when(jnp.logical_not(odd))
+    def _():
+        total[...] += product(mine, rings[0, slot])
+
+    @pl.when(odd)
+    def _():
+        fetch(1, step).wait()
+        total[...] += product(mine, rings[0, slot]) + product(theirs, rings[1, slot])
+
+    done = out.shape[1]
+
+    @pl.when(upper)
+    def _():
+        keep(0, step).wait()
+        keep(1, step).wait()
+        total[:done, :] += product(direct, kept[0][rows(step), :]) + product(
+            swapped, kept[1][rows(step), :]
+        )
+
+    @pl.when(step == steps - 1)
+    def _():
+        cols = out.shape[2]
+        for j in range(out.shape[0]):
+            out[j] = total[:done, j * cols : (j + 1) * cols].astype(out.dtype)
+
+
+def decode_first(info, mine, theirs, direct, swapped, decoder, shards, after):
+    _, _, features, width = decoder.shape
+    block = min(512, features)
+    steps = features // block
+    rows = sum(part.shape[0] for part in mine)
+    done = sum(part.shape[0] for part in direct)
+
+    def acts(part, flag):
+        return pl.BlockSpec(
+            (part.shape[0], block), lambda k, info: (0, k if flag is None else k * info[flag])
+        )
+
+    groups = (mine, theirs, direct, swapped)
+    in_specs = [acts(p, flag) for parts, flag in zip(groups, (None, 0, 1, 1)) for p in parts]
+    return pl.pallas_call(
+        functools.partial(first_wave_kernel, [len(parts) for parts in groups]),
+        grid_spec=pltpu.PrefetchScalarGridSpec(
+            num_scalar_prefetch=1,
+            grid=(steps,),
+            in_specs=in_specs + [ANYWHERE] * (1 + len(after)),
+            out_specs=[
+                pl.BlockSpec((shards, done, width // shards), lambda k, info: (0, 0, 0)),
+                pl.BlockSpec((rows, width), lambda k, info: (0, 0)),
+                WHOLE,
+                WHOLE,
+            ],
+            scratch_shapes=[
+                pltpu.VMEM((2, SLOTS, block, width), decoder.dtype),
+                pltpu.SemaphoreType.DMA((2, SLOTS)),
+                pltpu.SemaphoreType.DMA((2, steps)),
+            ],
+        ),
+        out_shape=[
+            jax.ShapeDtypeStruct((shards, done, width // shards), jnp.bfloat16),
+            pltpu.HBM((rows, width), jnp.float32),
+            pltpu.VMEM((features, width), decoder.dtype),
+            pltpu.VMEM((features, width), decoder.dtype),
+        ],
+        compiler_params=pltpu.CompilerParams(vmem_limit_bytes=DECODE_MIB * MIB),
+        name="decode_first",
+    )(info, *sum(groups, []), decoder, *after)
+
+
+def later_wave_kernel(order, row, n, info, *refs):
+    direct, swapped, (base, *kept) = refs[:n], refs[n : 2 * n], refs[2 * n : 2 * n + 3]
+    out, first, second, start, sem = refs[-5:]
+    rows = out.shape[1]
+    shards, cols = out.shape[0], out.shape[2]
+    span = 2 if shards % 2 == 0 else 1
+    copy = pltpu.make_async_copy(base.at[pl.ds(row, rows)], start, sem)
+    copy.start()
+    fill(order, direct, first)
+    fill(order, swapped, second)
+    copy.wait()
+
+    @pl.loop(0, shards // span)
+    def _(j):
+        at = pl.ds(pl.multiple_of(j * span * cols, span * cols), span * cols)
+
+        def store(value):
+            for i in range(span):
+                out[j * span + i] = value[:, i * cols : (i + 1) * cols].astype(out.dtype)
+
+        @pl.when(info[1] == 1)
+        def _():
+            store(
+                start[:, at]
+                + jnp.dot(first[...], kept[0][:, at], preferred_element_type=jnp.float32)
+                + jnp.dot(second[...], kept[1][:, at], preferred_element_type=jnp.float32)
+            )
+
+        @pl.when(info[1] == 0)
+        def _():
+            store(start[:, at])
+
+
+def decode_later(info, direct, swapped, order, base, kept, row, shards, after):
+    rows = sum(size for _, _, size in order)
+    features, width = kept[0].shape
+    kept = [pltpu.with_memory_space_constraint(weight, pltpu.VMEM) for weight in kept]
+    return pl.pallas_call(
+        functools.partial(later_wave_kernel, order, row, len(direct)),
+        in_specs=[pl.BlockSpec(memory_space=pltpu.SMEM)]
+        + [WHOLE] * (2 * len(direct))
+        + [ANYWHERE, WHOLE, WHOLE]
+        + [ANYWHERE] * len(after),
+        out_specs=WHOLE,
+        out_shape=jax.ShapeDtypeStruct((shards, rows, width // shards), jnp.bfloat16),
+        scratch_shapes=[
+            pltpu.VMEM((rows, features), jnp.bfloat16),
+            pltpu.VMEM((rows, features), jnp.bfloat16),
+            pltpu.VMEM((rows, width), jnp.float32),
+            pltpu.SemaphoreType.DMA,
+        ],
+        compiler_params=pltpu.CompilerParams(vmem_limit_bytes=DECODE_MIB * MIB),
+        name="decode_later",
+    )(info, *direct, *swapped, base, *kept, *after)
+
+
+def sum_kernel(sign, slots, base, *refs):
+    received, out = refs[: len(slots)], refs[-1]
+    out[...] = sign * base[...]
+    for ref, blocks in zip(received, slots):
+        size = ref.shape[1] // len(blocks)
+        for source in range(ref.shape[0]):
+            for k, s in enumerate(blocks):
+                at = pl.ds((source ^ s) * size, size)
+                out[at, :] += ref[source, pl.ds(k * size, size), :].astype(jnp.float32)
+
+
+def add_up(base, sign, slots, received, after):
+    return pl.pallas_call(
+        functools.partial(sum_kernel, sign, slots),
+        in_specs=[WHOLE] * (1 + len(received)) + [ANYWHERE] * len(after),
+        out_specs=WHOLE,
+        out_shape=jax.ShapeDtypeStruct(base.shape, base.dtype),
+        compiler_params=pltpu.CompilerParams(vmem_limit_bytes=ENCODE_MIB * MIB),
+        name="add_up",
+    )(base, *received, *after)
+
+
+def pipelined(layer_inputs, targets, encoder, encoder_bias, decoder):
+    shards = lax.axis_size("feat")
+    layers = lax.axis_size("layer")
+    half = layers // 2
+    layer = lax.axis_index("layer")
+    upper = layer >= half
+    info = jnp.stack(
+        [
+            layer & 1,
+            upper.astype(jnp.int32),
+            jnp.full_like(layer, half),
+            jnp.where(upper, layer - ((layer ^ 1) - half), 0),
+        ]
+    ).astype(jnp.int32)
+
+    def up(a):
+        return lax.ppermute(a, "layer", [(i, i + half) for i in range(half)])
+
+    def across(a):
+        return lax.ppermute(a, "layer", [(i, i ^ 1) for i in range(half, layers)])
+
+    def beside(a):
+        return lax.ppermute(a, "layer", [(i, i + 1) for i in range(0, layers, 2)])
+
+    def scatter(partial):
+        return lax.all_to_all(partial, "feat", 0, 0)
+
+    def after(value, *earlier):
+        return lax.optimization_barrier((value, *earlier))[0]
+
+    tokens = layer_inputs[0]
+    size = tokens.shape[0]
+    near = exchange(tokens, "feat", 1)
+    far = [exchange(tokens, "feat", s) for s in range(2, shards, 2)]
+    three = exchange(near, "feat", 2)
+
+    a0, a0a, a0b, encoder_kept = encode(
+        [tokens, near],
+        [(0, 0, size), (1, 0, size)],
+        [(0, 2 * size), (0, size), (size, size)],
+        encoder,
+        encoder_bias,
+        [],
+        stream=True,
+    )
+    d0a, d0b, n0 = up(a0a), up(a0b), beside(a0)
+    rest = exchange(after(jnp.concatenate(far[1:], axis=0), far[0], three), "feat", 1)
+    (a1,) = encode(
+        [far[0], three],
+        [(0, 0, size), (1, 0, size)],
+        [(0, 2 * size)],
+        encoder_kept,
+        encoder_bias,
+        [a0],
+    )
+    d1, n1 = up(a1), beside(a1)
+    others = shards - 4
+    order = []
+    for k in range(others // 2):
+        order += [(k, 0, size), (others // 2, k * size, size)]
+    a2, a2a, a2b = encode(
+        far[1:] + [rest],
+        order,
+        [(0, others * size), (0, (others - 1) * size), ((others - 1) * size, size)],
+        encoder_kept,
+        encoder_bias,
+        [a1, d0a],
+    )
+    d2, d3, n2 = up(a2a), up(a2b), beside(after(a2, d0b))
+
+    c0a, c0b = across(after(d0a, a2)), across(d0b)
+    wave, base, *kept = decode_first(
+        info, [a0, a1, a2], [n0, n1, n2], [d0a, d0b], [c0a, c0b], decoder, shards, []
+    )
+    received = [scatter(wave)]
+    c1 = across(after(d1, wave))
+    wave = decode_later(
+        info, [d1], [c1], [(0, 0, 2 * size)], base, kept, 2 * size, shards, [wave]
+    )
+    received.append(scatter(wave))
+    c2 = across(after(d2, wave))
+    early = (others - 2) * size
+    wave = decode_later(
+        info, [d2], [c2], [(0, 0, early)], base, kept, 4 * size, shards, [wave]
+    )
+    received.append(scatter(wave))
+    c3 = across(after(d3, wave))
+    wave = decode_later(
+        info,
+        [d2, d3],
+        [c2, c3],
+        [(0, early, size), (1, 0, size)],
+        base,
+        kept,
+        4 * size + early,
+        shards,
+        [wave],
+    )
+    received.append(scatter(wave))
+    slots = [[0, 1], [2, 3], list(range(4, shards - 2)), [shards - 2, shards - 1]]
+    total = add_up(targets[0], -1.0, slots[:3], received[:3], [wave])
+    return add_up(total, 1.0, slots[3:], received[3:], [])[None]
+
+
+def grouped(layer_inputs, targets, encoder, encoder_bias, decoder):
     groups = lax.axis_size("layer") // L_WIN
     depth_bits = groups.bit_length() - 1
     position = lax.axis_index("layer")
@@ -18,7 +395,7 @@
     group_index = position % groups
     gathered = lax.all_gather(layer_inputs[0], "feat", axis=0, tiled=True)
     for bit_index in range(depth_bits):
-        partner = from_partner(gathered, "layer", bit_index)
+        partner = exchange(gathered, "layer", 1 << bit_index)
         upper_bit = position >> bit_index & 1
         gathered = jnp.where(
             upper_bit == 1,
@@ -42,7 +419,7 @@
         upper_bit = position >> bit_index & 1
         kept_half = jnp.where(upper_bit == 1, rebuilt[half_rows:], rebuilt[:half_rows])
         sent_half = jnp.where(upper_bit == 1, rebuilt[:half_rows], rebuilt[half_rows:])
-        rebuilt = kept_half + from_partner(sent_half, "layer", bit_index)
+        rebuilt = kept_half + exchange(sent_half, "layer", 1 << bit_index)
     summed = lax.psum_scatter(rebuilt, "feat", scatter_dimension=1, tiled=True)
     residual = summed - targets[0]
     return residual[None]
@@ -56,6 +433,12 @@
         P("layer", "feat"),
         P("layer", None, "feat", None),
     )
+    shards = mesh.shape["feat"]
+    simple = mesh.shape["layer"] == L_WIN and shards >= 8 and shards & (shards - 1) == 0
     return jax.shard_map(
-        on_device, mesh=mesh, in_specs=placed, out_specs=P("layer", None, "feat"), check_vma=False
-    )
+        pipelined if simple else grouped,
+        mesh=mesh,
+        in_specs=placed,
+        out_specs=P("layer", None, "feat"),
+        check_vma=False,
+    )

time: 336 us -> 221 us (0.66)
  waiting for transfers between devices: 247 us -> 33.5 us
  Pallas kernels: 0 us -> 70.5 us
  starting transfers between devices: 0.08 us -> 63.8 us
  matrix products: 58.5 us -> 0 us
  local copies, waits for them, and re-layouts: 14 us -> 50.7 us
  between operations: 13.1 us -> 0.38 us
    all_gather x2 -> x0, waiting for transfers between devices: 156 us -> none  [the longest x1 103 us: on_device(): every_layer = lax.all_gather(features[None], 'layer', axis=0, tiled=True)]
    reduce_scatter x1 -> x0, waiting for transfers between devices: 89.7 us -> none  [on_device(): summed = lax.psum_scatter(rebuilt, 'feat', scatter_dimension=1, tiled=True)]
    pallas_call x0 -> x9, Pallas kernels: none -> 70.5 us  [the longest x3 27.2 us: decode_later(): pl.pallas_call(functools.partial(later_wave_kernel, order, row, len(direc...]
    dot_general x2 -> x0, matrix products: 58.5 us -> none  [the longest x1 44.1 us: on_device(): jnp.einsum('ktf,kfd->td', stacked, decoder[0], preferred_element_type=jnp...]
    unnamed x2 -> x44, local copies, waits for them, and re-layouts: 0.01 us -> 50.7 us
    ppermute x0 -> x19, starting transfers between devices: none -> 40.7 us  [the longest x5 19.2 us: across(): return lax.ppermute(a, 'layer', [(i, i ^ 1) for i in range(half, layers)])]
    all_to_all x0 -> x4, starting transfers between devices: none -> 23.1 us  [scatter(): return lax.all_to_all(partial, 'feat', 0, 0)]
    ppermute x0 -> x19, waiting for transfers between devices: none -> 20 us  [the longest x6 18.1 us: exchange(): return lax.ppermute(array, axis, [(i, i ^ flip) for i in range(size)])]
  transfers between devices with their start and end apart: 3 -> 23, of which waited for: 3 -> 7; matrix products, arithmetic and copies ran while one was open for 0% -> 0% of each run, Pallas kernels for 0% -> 32%
where the time goes in v4:
time: 221 us; the launch traced here: 220 us
  Pallas kernels  70.5 us (32%)
  starting transfers between devices  63.8 us (29%)
  local copies, waits for them, and re-layouts  50.7 us (23%)
  waiting for transfers between devices  33.5 us (15%)
    unnamed x44, local copies, waits for them, and re-layouts  50.7 us
    pallas_call x3, Pallas kernels, decode_later(): pl.pallas_call(functools.partial(later_wave_kernel, order, row, len(direc...  27.2 us
    pallas_call x1, Pallas kernels, decode_first(): pl.pallas_call(functools.partial(first_wave_kernel, [len(parts) for parts...  24.1 us
    all_to_all x4, starting transfers between devices, scatter(): return lax.all_to_all(partial, 'feat', 0, 0)  23.1 us
    ppermute x5, starting transfers between devices, across(): return lax.ppermute(a, 'layer', [(i, i ^ 1) for i in range(half, layers)])  19.2 us
    pallas_call x3, Pallas kernels, encode(): pl.pallas_call(functools.partial(encode_kernel, order, pieces, len(parts)...  18.1 us
    ppermute x6, waiting for transfers between devices, exchange(): return lax.ppermute(array, axis, [(i, i ^ flip) for i in range(size)])  18.1 us
    all_to_all x4, waiting for transfers between devices, scatter(): return lax.all_to_all(partial, 'feat', 0, 0)  13.5 us
  transfers between devices with their start and end apart: 23, of which 7 were waited for; matrix products, arithmetic and copies ran while one was open for 0% of the time, Pallas kernels for 32%

profile of v4, /device:TPU:2, one launch (start us, length us, event | category | flops | bytes accessed | tf_op | source)
XLA Modules:
  0.0 219.5 jit_solution(9775225319290715167)
XLA Ops:
  1.5 2.6 %collective-permute-start.3 = (bf16[64,2048]{1,0:T(8,128)(2,1)}, bf16[64,2048]{1,0:T(8,128)(2,1)S(1)}, u32[]{:S(2)}, u32[]{:S(2)}) collective-permute-start(bf16[64,2048]{1,0:T(8,128)(2,1)} %bitcast.8), channel_id=1, source_target_pairs={{0,4},{1,5},{2,6},{3,7},{4,0},{5,1},{6,2},{7,3},{8,12},{9,13},{10,... | collective-permute-start | bytes 786440 | tf_op jit(solution)/shard_map/ppermute | solution.py:16
  5.7 2.6 %collective-permute-done.refs_1_ = bf16[64,2048]{1,0:T(8,128)(2,1)S(1)} collective-permute-done((bf16[64,2048]{1,0:T(8,128)(2,1)}, bf16[64,2048]{1,0:T(8,128)(2,1)S(1)}, u32[]{:S(2)}, u32[]{:S(2)}) %collective-permute-start) | collective-permute-done | bytes 262176 | tf_op jit(solution)/shard_map/ppermute | solution.py:16
  11.5 6.5 %encode.3 = (bf16[128,4096]{1,0:T(8,128)(2,1)S(1)}, bf16[64,4096]{1,0:T(8,128)(2,1)S(1)}, bf16[64,4096]{1,0:T(8,128)(2,1)S(1)}, bf16[1,2048,4096]{2,1,0:T(8,128)(2,1)S(1)}) custom-call(bf16[64,2048]{1,0:T(8,128)(2,1)S(1)} %bitcast.11, bf16[64,2048]{1,0:T(8,128)(2,1)S(1)} %collective-permute-done.refs_1_, bf16[1,2048,4096]{2,1,0:T(8,128)(2,1)} %refs_2_.1, ...), custom_call_target="tpu_custom_call" | custom-call | tf_op jit(solution)/shard_map/encode/pallas_call | solution.py:75
  19.3 3.5 %collective-permute-done.3.refs_0_ = bf16[64,2048]{1,0:T(8,128)(2,1)S(1)} collective-permute-done((bf16[64,2048]{1,0:T(8,128)(2,1)}, bf16[64,2048]{1,0:T(8,128)(2,1)S(1)}, u32[]{:S(2)}, u32[]{:S(2)}) %collective-permute-start.3) | collective-permute-done | bytes 262176 | tf_op jit(solution)/shard_map/ppermute | solution.py:16
  22.9 2.1 collective-permute-done.1.refs_0_
  25.0 3.6 %collective-permute-done.2.refs_1_ = bf16[64,2048]{1,0:T(8,128)(2,1)S(1)} collective-permute-done((bf16[64,2048]{1,0:T(8,128)(2,1)S(1)}, bf16[64,2048]{1,0:T(8,128)(2,1)S(1)}, u32[]{:S(2)}, u32[]{:S(2)}) %collective-permute-start.2) | collective-permute-done | bytes 262176 | tf_op jit(solution)/shard_map/ppermute | solution.py:16
  30.4 3.8 %encode.4.refs_5_.refs_1_ = bf16[128,4096]{1,0:T(8,128)(2,1)S(1)} custom-call(bf16[64,2048]{1,0:T(8,128)(2,1)S(1)} %collective-permute-done.1.refs_0_, bf16[64,2048]{1,0:T(8,128)(2,1)S(1)} %collective-permute-done.2.refs_1_, bf16[1,2048,4096]{2,1,0:T(8,128)(2,1)S(1)} %get-tuple-element.23.refs_2_.refs_3_, f32[1,4096]{1,0:T(1,128)S(1)} %copy-done.15, ...), custom_call_target="tpu_custom_call" | custom-call | tf_op jit(solution)/shard_map/encode/pallas_call | solution.py:75
  34.2 6.3 %collective-permute-done.5.refs_2_ = bf16[128,2048]{1,0:T(8,128)(2,1)S(1)} collective-permute-done((bf16[128,2048]{1,0:T(8,128)(2,1)S(1)}, bf16[128,2048]{1,0:T(8,128)(2,1)S(1)}, u32[]{:S(2)}, u32[]{:S(2)}) %collective-permute-start.5) | collective-permute-done | bytes 524320 | tf_op jit(solution)/shard_map/ppermute | solution.py:16
  40.5 7.8 %encode.5 = (bf16[256,4096]{1,0:T(8,128)(2,1)}, bf16[192,4096]{1,0:T(8,128)(2,1)}, bf16[64,4096]{1,0:T(8,128)(2,1)}) custom-call(bf16[64,2048]{1,0:T(8,128)(2,1)S(1)} %collective-permute-done.3.refs_0_, bf16[64,2048]{1,0:T(8,128)(2,1)S(1)} %collective-permute-done.4.refs_1_, bf16[128,2048]{1,0:T(8,128)(2,1)S(1)} %collective-permute-done.5.refs_2_, ...), custom_call_target="tpu_custom_call" | custom-call | tf_op jit(solution)/shard_map/encode/pallas_call | solution.py:75
  48.3 2.6 %collective-permute-start.10 = (bf16[256,4096]{1,0:T(8,128)(2,1)}, bf16[256,4096]{1,0:T(8,128)(2,1)}, u32[]{:S(2)}, u32[]{:S(2)}) collective-permute-start(bf16[256,4096]{1,0:T(8,128)(2,1)} %get-tuple-element.28.refs_2_), channel_id=1, source_target_pairs={{0,8},{16,24},{1,9},{17,25},{2,10},{18,26},{3,11},{19,27},{4,12},{... | collective-permute-start | bytes 6291464 | tf_op jit(solution)/shard_map/ppermute | solution.py:308
  52.3 1.9 collective-permute-start.12
  54.2 3.4 %collective-permute-start.8 = (bf16[128,4096]{1,0:T(8,128)(2,1)S(1)}, bf16[128,4096]{1,0:T(8,128)(2,1)}, u32[]{:S(2)}, u32[]{:S(2)}) collective-permute-start(bf16[128,4096]{1,0:T(8,128)(2,1)S(1)} %encode.4.refs_5_.refs_1_), channel_id=1, source_target_pairs={{0,8},{16,24},{1,9},{17,25},{2,10},{18,26},{3,11},{19,27},{4,12},{... | collective-permute-start | bytes 3145736 | tf_op jit(solution)/shard_map/ppermute | solution.py:308
  59.0 1.9 collective-permute-start.11
  62.9 24.1 %decode_first.1 = (bf16[8,128,256]{2,1,0:T(8,128)(2,1)}, f32[512,2048]{1,0:T(8,128)}, bf16[4096,2048]{1,0:T(8,128)(2,1)S(1)}, bf16[4096,2048]{1,0:T(8,128)(2,1)S(1)}) custom-call(s32[4]{0:T(128)} %pad_add_fusion.info, bf16[128,4096]{1,0:T(8,128)(2,1)} %copy-done.10, bf16[128,4096]{1,0:T(8,128)(2,1)} %copy-done.8, ...), custom_call_target="tpu_custom_call" | custom-call | tf_op jit(solution)/shard_map/decode_first/pallas_call | solution.py:179
  87.0 5.8 %copy-done = bf16[4096,2048]{1,0:T(8,128)(2,1)} copy-done((bf16[4096,2048]{1,0:T(8,128)(2,1)}, bf16[4096,2048]{1,0:T(8,128)(2,1)S(1)}, u32[]{:S(2)}) %copy-start) | copy-done | bytes 16777240
  92.7 5.8 %copy-done.4 = bf16[4096,2048]{1,0:T(8,128)(2,1)} copy-done((bf16[4096,2048]{1,0:T(8,128)(2,1)}, bf16[4096,2048]{1,0:T(8,128)(2,1)S(1)}, u32[]{:S(2)}) %copy-start.4) | copy-done | bytes 16777240
  98.5 11.5 %collective-permute-start.14 = (bf16[128,4096]{1,0:T(8,128)(2,1)}, bf16[128,4096]{1,0:T(8,128)(2,1)S(1)}, u32[]{:S(2)}, u32[]{:S(2)}) collective-permute-start(bf16[128,4096]{1,0:T(8,128)(2,1)} %collective-permute-done.13.refs_0_), channel_id=1, source_target_pairs={{16,24},{24,16},{17,25},{25,17},{18,26},{26,18},{19,27},{27,19},{2... | collective-permute-start | bytes 3145736 | tf_op jit(solution)/shard_map/ppermute | solution.py:305
  110.0 5.0 %all-to-all-start = ((bf16[8,128,256]{2,1,0:T(8,128)(2,1)}), bf16[8,128,256]{2,1,0:T(8,128)(2,1)S(1)}, u32[]{:S(2)}, u32[]{:S(2)}) async-start(bf16[8,128,256]{2,1,0:T(8,128)(2,1)} %get-tuple-element.30.refs_5_), calls=%async_computation | async-start | bytes 1048576 | tf_op jit(solution)/shard_map/all_to_all | solution.py:311
  116.0 5.8 %copy-done.1 = bf16[4096,2048]{1,0:T(8,128)(2,1)S(1)} copy-done((bf16[4096,2048]{1,0:T(8,128)(2,1)S(1)}, bf16[4096,2048]{1,0:T(8,128)(2,1)}, u32[]{:S(2)}) %copy-start.1) | copy-done | bytes 16777240
  121.7 5.8 %copy-done.5 = bf16[4096,2048]{1,0:T(8,128)(2,1)S(1)} copy-done((bf16[4096,2048]{1,0:T(8,128)(2,1)S(1)}, bf16[4096,2048]{1,0:T(8,128)(2,1)}, u32[]{:S(2)}) %copy-start.5) | copy-done | bytes 16777240
  127.5 8.7 %decode_later.3.refs_5_ = bf16[8,128,256]{2,1,0:T(8,128)(2,1)} custom-call(s32[4]{0:T(128)} %pad_add_fusion.info, bf16[128,4096]{1,0:T(8,128)(2,1)} %collective-permute-done.13.refs_0_, bf16[128,4096]{1,0:T(8,128)(2,1)} %copy-done.17, f32[512,2048]{1,0:T(8,128)} %get-tuple-element.32.refs_2_.refs_4_, bf16[4096,2048]{1,0:T(8,128)(2,1)S(1)} %copy-done.1, ...), custom_call_target="tpu_custom_call" | custom-call | tf_op jit(solution)/shard_map/decode_later/pallas_call | solution.py:245
  136.3 1.9 collective-permute-start.16
  138.2 6.0 %all-to-all-start.1 = ((bf16[8,128,256]{2,1,0:T(8,128)(2,1)}), bf16[8,128,256]{2,1,0:T(8,128)(2,1)S(1)}, u32[]{:S(2)}, u32[]{:S(2)}) async-start(bf16[8,128,256]{2,1,0:T(8,128)(2,1)} %decode_later.3.refs_5_), calls=%async_computation.1 | async-start | bytes 1048576 | tf_op jit(solution)/shard_map/all_to_all | solution.py:311
  145.5 5.8 %copy-done.2 = bf16[4096,2048]{1,0:T(8,128)(2,1)S(1)} copy-done((bf16[4096,2048]{1,0:T(8,128)(2,1)S(1)}, bf16[4096,2048]{1,0:T(8,128)(2,1)}, u32[]{:S(2)}) %copy-start.2) | copy-done | bytes 16777240
  151.3 5.8 %copy-done.6 = bf16[4096,2048]{1,0:T(8,128)(2,1)S(1)} copy-done((bf16[4096,2048]{1,0:T(8,128)(2,1)S(1)}, bf16[4096,2048]{1,0:T(8,128)(2,1)}, u32[]{:S(2)}) %copy-start.6) | copy-done | bytes 16777240
  157.0 9.1 %decode_later.4.refs_7_ = bf16[8,128,256]{2,1,0:T(8,128)(2,1)} custom-call(s32[4]{0:T(128)} %pad_add_fusion.info, bf16[192,4096]{1,0:T(8,128)(2,1)} %collective-permute-done.15.refs_0_, bf16[192,4096]{1,0:T(8,128)(2,1)} %collective-permute-done.16.refs_1_.refs_2_, f32[512,2048]{1,0:T(8,128)} %get-tuple-element.32.refs_2_.refs_4_, ...), custom_call_target="tpu_custom_call" | custom-call | tf_op jit(solution)/shard_map/decode_later/pallas_call | solution.py:245
  166.2 6.1 %all-to-all-start.2 = ((bf16[8,128,256]{2,1,0:T(8,128)(2,1)}), bf16[8,128,256]{2,1,0:T(8,128)(2,1)S(1)}, u32[]{:S(2)}, u32[]{:S(2)}) async-start(bf16[8,128,256]{2,1,0:T(8,128)(2,1)} %decode_later.4.refs_7_), calls=%async_computation.2 | async-start | bytes 1048576 | tf_op jit(solution)/shard_map/all_to_all | solution.py:311
  177.0 5.8 %copy-done.3 = bf16[4096,2048]{1,0:T(8,128)(2,1)S(1)} copy-done((bf16[4096,2048]{1,0:T(8,128)(2,1)S(1)}, bf16[4096,2048]{1,0:T(8,128)(2,1)}, u32[]{:S(2)}) %copy-start.3) | copy-done | bytes 16777240
  182.7 5.8 %copy-done.7 = bf16[4096,2048]{1,0:T(8,128)(2,1)S(1)} copy-done((bf16[4096,2048]{1,0:T(8,128)(2,1)S(1)}, bf16[4096,2048]{1,0:T(8,128)(2,1)}, u32[]{:S(2)}) %copy-start.7) | copy-done | bytes 16777240
  188.5 9.4 %decode_later.5.refs_3_ = bf16[8,128,256]{2,1,0:T(8,128)(2,1)} custom-call(s32[4]{0:T(128)} %pad_add_fusion.info, bf16[192,4096]{1,0:T(8,128)(2,1)} %collective-permute-done.15.refs_0_, bf16[64,4096]{1,0:T(8,128)(2,1)} %copy-done.20, bf16[192,4096]{1,0:T(8,128)(2,1)} %collective-permute-done.16.refs_1_.refs_2_, bf16[64,4096]{1,0:T(8,128)(2,1)} %copy-done.21, ...), custom_call_target="tpu_custom_call" | custom-call | tf_op jit(solution)/shard_map/decode_later/pallas_call | solution.py:245
  197.9 6.0 %all-to-all-start.3 = ((bf16[8,128,256]{2,1,0:T(8,128)(2,1)}), bf16[8,128,256]{2,1,0:T(8,128)(2,1)S(1)}, u32[]{:S(2)}, u32[]{:S(2)}) async-start(bf16[8,128,256]{2,1,0:T(8,128)(2,1)} %decode_later.5.refs_3_), calls=%async_computation.3 | async-start | bytes 1048576 | tf_op jit(solution)/shard_map/all_to_all | solution.py:311
  205.2 13.5 %all-to-all-done.3.refs_0_ = bf16[8,128,256]{2,1,0:T(8,128)(2,1)S(1)} async-done(((bf16[8,128,256]{2,1,0:T(8,128)(2,1)}), bf16[8,128,256]{2,1,0:T(8,128)(2,1)S(1)}, u32[]{:S(2)}, u32[]{:S(2)}) %all-to-all-start.3) | async-done | bytes 524320 | tf_op jit(solution)/shard_map/all_to_all | solution.py:311
  (69 shorter events, 23.2 us)
Async XLA Ops:
  0.0 8.3 %collective-permute-start = (bf16[64,2048]{1,0:T(8,128)(2,1)}, bf16[64,2048]{1,0:T(8,128)(2,1)S(1)}, u32[]{:S(2)}, u32[]{:S(2)}) collective-permute-start(bf16[64,2048]{1,0:T(8,128)(2,1)} %bitcast.7), channel_id=1, source_target_pairs={{0,1},{1,0},{2,3},{3,2},{4,5},{5,4},{6,7},{7,6},{8,9},{9,8},{10,11... | collective-permute-start | bytes 786440 | tf_op jit(solution)/shard_map/ppermute | solution.py:16
  1.5 21.3 %collective-permute-start.3 = (bf16[64,2048]{1,0:T(8,128)(2,1)}, bf16[64,2048]{1,0:T(8,128)(2,1)S(1)}, u32[]{:S(2)}, u32[]{:S(2)}) collective-permute-start(bf16[64,2048]{1,0:T(8,128)(2,1)} %bitcast.8), channel_id=1, source_target_pairs={{0,4},{1,5},{2,6},{3,7},{4,0},{5,1},{6,2},{7,3},{8,12},{9,13},{10,... | collective-permute-start | bytes 786440 | tf_op jit(solution)/shard_map/ppermute | solution.py:16
  4.1 18.8 %collective-permute-start.4 = (bf16[64,2048]{1,0:T(8,128)(2,1)}, bf16[64,2048]{1,0:T(8,128)(2,1)S(1)}, u32[]{:S(2)}, u32[]{:S(2)}) collective-permute-start(bf16[64,2048]{1,0:T(8,128)(2,1)} %bitcast.9), channel_id=1, source_target_pairs={{0,6},{1,7},{2,4},{3,5},{4,2},{5,3},{6,0},{7,1},{8,14},{9,15},{10,... | collective-permute-start | bytes 786440 | tf_op jit(solution)/shard_map/ppermute | solution.py:16
  5.5 19.6 %collective-permute-start.1 = (bf16[64,2048]{1,0:T(8,128)(2,1)}, bf16[64,2048]{1,0:T(8,128)(2,1)S(1)}, u32[]{:S(2)}, u32[]{:S(2)}) collective-permute-start(bf16[64,2048]{1,0:T(8,128)(2,1)} %bitcast.10), channel_id=1, source_target_pairs={{0,2},{1,3},{2,0},{3,1},{4,6},{5,7},{6,4},{7,5},{8,10},{9,11},{10,... | collective-permute-start | bytes 786440 | tf_op jit(solution)/shard_map/ppermute | solution.py:16
  8.3 20.4 %collective-permute-start.2 = (bf16[64,2048]{1,0:T(8,128)(2,1)S(1)}, bf16[64,2048]{1,0:T(8,128)(2,1)S(1)}, u32[]{:S(2)}, u32[]{:S(2)}) collective-permute-start(bf16[64,2048]{1,0:T(8,128)(2,1)S(1)} %collective-permute-done.refs_1_), channel_id=1, source_target_pairs={{0,2},{1,3},{2,0},{3,1},{4,6},{5,7},{6,4},{7,5},{8,10},{9,11},{10,... | collective-permute-start | bytes 786440 | tf_op jit(solution)/shard_map/ppermute | solution.py:16
  11.5 18.9 %copy-start.15 = (f32[1,4096]{1,0:T(1,128)S(1)}, f32[1,4096]{1,0:T(1,128)}, u32[]{:S(2)}) copy-start(f32[1,4096]{1,0:T(1,128)} %refs_4_.1) | copy-start | bytes 49156
  18.0 32.9 %copy-start.10 = (bf16[128,4096]{1,0:T(8,128)(2,1)}, bf16[128,4096]{1,0:T(8,128)(2,1)S(1)}, u32[]{:S(2)}) copy-start(bf16[128,4096]{1,0:T(8,128)(2,1)S(1)} %get-tuple-element.22.refs_4_.refs_0_) | copy-start | bytes 3145732
  18.0 16.2 %collective-permute-start.6 = (bf16[64,4096]{1,0:T(8,128)(2,1)S(1)}, bf16[64,4096]{1,0:T(8,128)(2,1)S(1)}, u32[]{:S(2)}, u32[]{:S(2)}) collective-permute-start(bf16[64,4096]{1,0:T(8,128)(2,1)S(1)} %get-tuple-element.25), channel_id=1, source_target_pairs={{0,16},{8,24},{1,17},{9,25},{2,18},{10,26},{3,19},{11,27},{4,20},{... | collective-permute-start | bytes 1572872 | tf_op jit(solution)/shard_map/ppermute | solution.py:302
  28.6 11.9 %collective-permute-start.5 = (bf16[128,2048]{1,0:T(8,128)(2,1)S(1)}, bf16[128,2048]{1,0:T(8,128)(2,1)S(1)}, u32[]{:S(2)}, u32[]{:S(2)}) collective-permute-start(bf16[128,2048]{1,0:T(8,128)(2,1)S(1)} %pad_maximum_fusion), channel_id=1, source_target_pairs={{0,1},{1,0},{2,3},{3,2},{4,5},{5,4},{6,7},{7,6},{8,9},{9,8},{10,11... | collective-permute-start | bytes 1572872 | tf_op jit(solution)/shard_map/ppermute | solution.py:16
  29.1 19.2 %collective-permute-start.9 = (bf16[64,4096]{1,0:T(8,128)(2,1)S(1)}, bf16[64,4096]{1,0:T(8,128)(2,1)S(1)}, u32[]{:S(2)}, u32[]{:S(2)}) collective-permute-start(bf16[64,4096]{1,0:T(8,128)(2,1)S(1)} %get-tuple-element.27), channel_id=1, source_target_pairs={{0,16},{8,24},{1,17},{9,25},{2,18},{10,26},{3,19},{11,27},{4,20},{... | collective-permute-start | bytes 1572872 | tf_op jit(solution)/shard_map/ppermute | solution.py:302
  34.2 23.4 %copy-start.8 = (bf16[128,4096]{1,0:T(8,128)(2,1)}, bf16[128,4096]{1,0:T(8,128)(2,1)S(1)}, u32[]{:S(2)}) copy-start(bf16[128,4096]{1,0:T(8,128)(2,1)S(1)} %encode.4.refs_5_.refs_1_) | copy-start | bytes 3145732
  34.2 24.7 %copy-start.11 = (bf16[64,4096]{1,0:T(8,128)(2,1)}, bf16[64,4096]{1,0:T(8,128)(2,1)S(1)}, u32[]{:S(2)}) copy-start(bf16[64,4096]{1,0:T(8,128)(2,1)S(1)} %collective-permute-done.6.refs_6_) | copy-start | bytes 1572868
  48.3 14.6 %copy-start.18 = (bf16[64,4096]{1,0:T(8,128)(2,1)}, bf16[64,4096]{1,0:T(8,128)(2,1)S(1)}, u32[]{:S(2)}) copy-start(bf16[64,4096]{1,0:T(8,128)(2,1)S(1)} %collective-permute-done.9.refs_7_) | copy-start | bytes 1572868
  48.3 14.6 %collective-permute-start.10 = (bf16[256,4096]{1,0:T(8,128)(2,1)}, bf16[256,4096]{1,0:T(8,128)(2,1)}, u32[]{:S(2)}, u32[]{:S(2)}) collective-permute-start(bf16[256,4096]{1,0:T(8,128)(2,1)} %get-tuple-element.28.refs_2_), channel_id=1, source_target_pairs={{0,8},{16,24},{1,9},{17,25},{2,10},{18,26},{3,11},{19,27},{4,12},{... | collective-permute-start | bytes 6291464 | tf_op jit(solution)/shard_map/ppermute | solution.py:308
  51.0 9.9 %collective-permute-start.7 = (bf16[128,4096]{1,0:T(8,128)(2,1)S(1)}, bf16[128,4096]{1,0:T(8,128)(2,1)S(1)}, u32[]{:S(2)}, u32[]{:S(2)}) collective-permute-start(bf16[128,4096]{1,0:T(8,128)(2,1)S(1)} %get-tuple-element.22.refs_4_.refs_0_), channel_id=1, source_target_pairs={{0,8},{16,24},{1,9},{17,25},{2,10},{18,26},{3,11},{19,27},{4,12},{... | collective-permute-start | bytes 3145736 | tf_op jit(solution)/shard_map/ppermute | solution.py:308
  52.3 6.6 %collective-permute-start.12 = (bf16[64,4096]{1,0:T(8,128)(2,1)S(1)}, bf16[64,4096]{1,0:T(8,128)(2,1)S(1)}, u32[]{:S(2)}, u32[]{:S(2)}) collective-permute-start(bf16[64,4096]{1,0:T(8,128)(2,1)S(1)} %collective-permute-done.9.refs_7_), channel_id=1, source_target_pairs={{16,24},{24,16},{17,25},{25,17},{18,26},{26,18},{19,27},{27,19},{2... | collective-permute-start | bytes 1572872 | tf_op jit(solution)/shard_map/ppermute | solution.py:305
  54.2 8.7 %collective-permute-start.8 = (bf16[128,4096]{1,0:T(8,128)(2,1)S(1)}, bf16[128,4096]{1,0:T(8,128)(2,1)}, u32[]{:S(2)}, u32[]{:S(2)}) collective-permute-start(bf16[128,4096]{1,0:T(8,128)(2,1)S(1)} %encode.4.refs_5_.refs_1_), channel_id=1, source_target_pairs={{0,8},{16,24},{1,9},{17,25},{2,10},{18,26},{3,11},{19,27},{4,12},{... | collective-permute-start | bytes 3145736 | tf_op jit(solution)/shard_map/ppermute | solution.py:308
  57.6 40.9 %collective-permute-start.13 = (bf16[128,4096]{1,0:T(8,128)(2,1)S(1)}, bf16[128,4096]{1,0:T(8,128)(2,1)}, u32[]{:S(2)}, u32[]{:S(2)}) collective-permute-start(bf16[128,4096]{1,0:T(8,128)(2,1)S(1)} %encode.4.refs_5_.refs_1_), channel_id=1, source_target_pairs={{0,16},{8,24},{1,17},{9,25},{2,18},{10,26},{3,19},{11,27},{4,20},{... | collective-permute-start | bytes 3145736 | tf_op jit(solution)/shard_map/ppermute | solution.py:302
  59.0 3.9 %collective-permute-start.11 = (bf16[64,4096]{1,0:T(8,128)(2,1)S(1)}, bf16[64,4096]{1,0:T(8,128)(2,1)}, u32[]{:S(2)}, u32[]{:S(2)}) collective-permute-start(bf16[64,4096]{1,0:T(8,128)(2,1)S(1)} %collective-permute-done.6.refs_6_), channel_id=1, source_target_pairs={{16,24},{24,16},{17,25},{25,17},{18,26},{26,18},{19,27},{27,19},{2... | collective-permute-start | bytes 1572872 | tf_op jit(solution)/shard_map/ppermute | solution.py:305
  60.9 75.3 %collective-permute-start.15 = (bf16[192,4096]{1,0:T(8,128)(2,1)}, bf16[192,4096]{1,0:T(8,128)(2,1)}, u32[]{:S(2)}, u32[]{:S(2)}) collective-permute-start(bf16[192,4096]{1,0:T(8,128)(2,1)} %get-tuple-element.35), channel_id=1, source_target_pairs={{0,16},{8,24},{1,17},{9,25},{2,18},{10,26},{3,19},{11,27},{4,20},{... | collective-permute-start | bytes 4718600 | tf_op jit(solution)/shard_map/ppermute | solution.py:302
  98.5 16.4 %collective-permute-start.14 = (bf16[128,4096]{1,0:T(8,128)(2,1)}, bf16[128,4096]{1,0:T(8,128)(2,1)S(1)}, u32[]{:S(2)}, u32[]{:S(2)}) collective-permute-start(bf16[128,4096]{1,0:T(8,128)(2,1)} %collective-permute-done.13.refs_0_), channel_id=1, source_target_pairs={{16,24},{24,16},{17,25},{25,17},{18,26},{26,18},{19,27},{27,19},{2... | collective-permute-start | bytes 3145736 | tf_op jit(solution)/shard_map/ppermute | solution.py:305
  110.0 28.2 %all-to-all-start = ((bf16[8,128,256]{2,1,0:T(8,128)(2,1)}), bf16[8,128,256]{2,1,0:T(8,128)(2,1)S(1)}, u32[]{:S(2)}, u32[]{:S(2)}) async-start(bf16[8,128,256]{2,1,0:T(8,128)(2,1)} %get-tuple-element.30.refs_5_), calls=%async_computation | async-start | bytes 1048576 | tf_op jit(solution)/shard_map/all_to_all | solution.py:311
  116.0 5.8 %copy-start.1 = (bf16[4096,2048]{1,0:T(8,128)(2,1)S(1)}, bf16[4096,2048]{1,0:T(8,128)(2,1)}, u32[]{:S(2)}) copy-start(bf16[4096,2048]{1,0:T(8,128)(2,1)} %copy-done) | copy-start | bytes 50331652
  121.7 5.8 %copy-start.5 = (bf16[4096,2048]{1,0:T(8,128)(2,1)S(1)}, bf16[4096,2048]{1,0:T(8,128)(2,1)}, u32[]{:S(2)}) copy-start(bf16[4096,2048]{1,0:T(8,128)(2,1)} %copy-done.4) | copy-start | bytes 50331652
  136.3 9.2 %collective-permute-start.16 = (bf16[192,4096]{1,0:T(8,128)(2,1)}, bf16[192,4096]{1,0:T(8,128)(2,1)}, u32[]{:S(2)}, u32[]{:S(2)}) collective-permute-start(bf16[192,4096]{1,0:T(8,128)(2,1)} %collective-permute-done.15.refs_0_), channel_id=1, source_target_pairs={{16,24},{24,16},{17,25},{25,17},{18,26},{26,18},{19,27},{27,19},{2... | collective-permute-start | bytes 4718600 | tf_op jit(solution)/shard_map/ppermute | solution.py:305
  138.2 28.0 %all-to-all-start.1 = ((bf16[8,128,256]{2,1,0:T(8,128)(2,1)}), bf16[8,128,256]{2,1,0:T(8,128)(2,1)S(1)}, u32[]{:S(2)}, u32[]{:S(2)}) async-start(bf16[8,128,256]{2,1,0:T(8,128)(2,1)} %decode_later.3.refs_5_), calls=%async_computation.1 | async-start | bytes 1048576 | tf_op jit(solution)/shard_map/all_to_all | solution.py:311
  144.2 28.1 %collective-permute-start.17 = (bf16[64,4096]{1,0:T(8,128)(2,1)}, bf16[64,4096]{1,0:T(8,128)(2,1)S(1)}, u32[]{:S(2)}, u32[]{:S(2)}) collective-permute-start(bf16[64,4096]{1,0:T(8,128)(2,1)} %get-tuple-element.37), channel_id=1, source_target_pairs={{0,16},{8,24},{1,17},{9,25},{2,18},{10,26},{3,19},{11,27},{4,20},{... | collective-permute-start | bytes 1572872 | tf_op jit(solution)/shard_map/ppermute | solution.py:302
  145.5 5.8 %copy-start.2 = (bf16[4096,2048]{1,0:T(8,128)(2,1)S(1)}, bf16[4096,2048]{1,0:T(8,128)(2,1)}, u32[]{:S(2)}) copy-start(bf16[4096,2048]{1,0:T(8,128)(2,1)} %copy-done) | copy-start | bytes 50331652
  166.2 37.7 %copy-start.12 = (f32[1,512,256]{2,1,0:T(8,128)S(1)}, f32[1,512,256]{2,1,0:T(8,128)}, u32[]{:S(2)}) copy-start(f32[1,512,256]{2,1,0:T(8,128)} %param.6) | copy-start | bytes 1572868
  166.2 31.7 %all-to-all-start.2 = ((bf16[8,128,256]{2,1,0:T(8,128)(2,1)}), bf16[8,128,256]{2,1,0:T(8,128)(2,1)S(1)}, u32[]{:S(2)}, u32[]{:S(2)}) async-start(bf16[8,128,256]{2,1,0:T(8,128)(2,1)} %decode_later.4.refs_7_), calls=%async_computation.2 | async-start | bytes 1048576 | tf_op jit(solution)/shard_map/all_to_all | solution.py:311
  172.3 3.8 %collective-permute-start.18 = (bf16[64,4096]{1,0:T(8,128)(2,1)S(1)}, bf16[64,4096]{1,0:T(8,128)(2,1)S(1)}, u32[]{:S(2)}, u32[]{:S(2)}) collective-permute-start(bf16[64,4096]{1,0:T(8,128)(2,1)S(1)} %collective-permute-done.17.refs_1_), channel_id=1, source_target_pairs={{16,24},{24,16},{17,25},{25,17},{18,26},{26,18},{19,27},{27,19},{2... | collective-permute-start | bytes 1572872 | tf_op jit(solution)/shard_map/ppermute | solution.py:305
  197.9 20.8 %all-to-all-start.3 = ((bf16[8,128,256]{2,1,0:T(8,128)(2,1)}), bf16[8,128,256]{2,1,0:T(8,128)(2,1)S(1)}, u32[]{:S(2)}, u32[]{:S(2)}) async-start(bf16[8,128,256]{2,1,0:T(8,128)(2,1)} %decode_later.5.refs_3_), calls=%async_computation.3 | async-start | bytes 1048576 | tf_op jit(solution)/shard_map/all_to_all | solution.py:311
  (13 other events, 41.1 us)

commit v5 on v4

--- a/solution.py
+++ b/solution.py
@@ -19,8 +19,9 @@
 ANYWHERE = pl.BlockSpec(memory_space=pl.ANY)
 WHOLE = pl.BlockSpec(memory_space=pltpu.VMEM)
 SLOTS = 3
-ENCODE_MIB = 12
-DECODE_MIB = 26
+ENCODE_MIB = 16
+DECODE_MIB = 27
+SUM_MIB = 12
 
 
 def fill(order, parts, rows_of):
@@ -83,13 +84,33 @@
     )(*parts, weight, bias, *after)
 
 
+def split(info, value, out, sent, j):
+    cols = out.shape[2]
+    low, high = value[:, :cols], value[:, cols:]
+
+    @pl.when(info[4] == 0)
+    def _():
+        out[j] = low
+        sent[j] = high.astype(sent.dtype)
+
+    @pl.when(info[4] == 1)
+    def _():
+        out[j] = high
+        sent[j] = low.astype(sent.dtype)
+
+
+def halves(shards, rows, width):
+    shape = (shards // 2, rows, width // shards)
+    return [jax.ShapeDtypeStruct(shape, jnp.float32), jax.ShapeDtypeStruct(shape, jnp.bfloat16)]
+
+
 def first_wave_kernel(counts, info, *refs):
     groups = []
     for count in counts:
         groups.append(refs[:count])
         refs = refs[count:]
     mine, theirs, direct, swapped = groups
-    weights, out, total, *kept = refs[:5]
+    weights, out, sent, total, *kept = refs[:6]
     rings, ring_sems, kept_sems = refs[-3:]
     step, steps = pl.program_id(0), pl.num_programs(0)
     slots, block = rings.shape[1], rings.shape[2]
@@ -159,7 +180,7 @@
     def _():
         cols = out.shape[2]
         for j in range(out.shape[0]):
-            out[j] = total[:done, j * cols : (j + 1) * cols].astype(out.dtype)
+            split(info, total[:done, 2 * j * cols : 2 * (j + 1) * cols], out, sent, j)
 
 
 def decode_first(info, mine, theirs, direct, swapped, decoder, shards, after):
@@ -183,7 +204,7 @@
             grid=(steps,),
             in_specs=in_specs + [ANYWHERE] * (1 + len(after)),
             out_specs=[
-                pl.BlockSpec((shards, done, width // shards), lambda k, info: (0, 0, 0)),
+                *[pl.BlockSpec(h.shape, lambda k, info: (0, 0, 0)) for h in halves(shards, done, width)],
                 pl.BlockSpec((rows, width), lambda k, info: (0, 0)),
                 WHOLE,
                 WHOLE,
@@ -195,7 +216,7 @@
             ],
         ),
         out_shape=[
-            jax.ShapeDtypeStruct((shards, done, width // shards), jnp.bfloat16),
+            *halves(shards, done, width),
             pltpu.HBM((rows, width), jnp.float32),
             pltpu.VMEM((features, width), decoder.dtype),
             pltpu.VMEM((features, width), decoder.dtype),
@@ -207,35 +228,26 @@
 
 def later_wave_kernel(order, row, n, info, *refs):
     direct, swapped, (base, *kept) = refs[:n], refs[n : 2 * n], refs[2 * n : 2 * n + 3]
-    out, first, second, start, sem = refs[-5:]
+    out, sent, first, second, start, sem = refs[-6:]
     rows = out.shape[1]
-    shards, cols = out.shape[0], out.shape[2]
-    span = 2 if shards % 2 == 0 else 1
+    pairs, cols = out.shape[0], out.shape[2]
     copy = pltpu.make_async_copy(base.at[pl.ds(row, rows)], start, sem)
     copy.start()
     fill(order, direct, first)
     fill(order, swapped, second)
     copy.wait()
 
-    @pl.loop(0, shards // span)
+    @pl.loop(0, pairs)
     def _(j):
-        at = pl.ds(pl.multiple_of(j * span * cols, span * cols), span * cols)
-
-        def store(value):
-            for i in range(span):
-                out[j * span + i] = value[:, i * cols : (i + 1) * cols].astype(out.dtype)
+        at = pl.ds(pl.multiple_of(j * 2 * cols, 2 * cols), 2 * cols)
 
         @pl.when(info[1] == 1)
         def _():
-            store(
-                start[:, at]
-                + jnp.dot(first[...], kept[0][:, at], preferred_element_type=jnp.float32)
-                + jnp.dot(second[...], kept[1][:, at], preferred_element_type=jnp.float32)
-            )
-
-        @pl.when(info[1] == 0)
-        def _():
-            store(start[:, at])
+            start[:, at] += jnp.dot(
+                first[...], kept[0][:, at], preferred_element_type=jnp.float32
+            ) + jnp.dot(second[...], kept[1][:, at], preferred_element_type=jnp.float32)
+
+        split(info, start[:, at], out, sent, j)
 
 
 def decode_later(info, direct, swapped, order, base, kept, row, shards, after):
@@ -248,8 +260,8 @@
         + [WHOLE] * (2 * len(direct))
         + [ANYWHERE, WHOLE, WHOLE]
         + [ANYWHERE] * len(after),
-        out_specs=WHOLE,
-        out_shape=jax.ShapeDtypeStruct((shards, rows, width // shards), jnp.bfloat16),
+        out_specs=[WHOLE, WHOLE],
+        out_shape=halves(shards, rows, width),
         scratch_shapes=[
             pltpu.VMEM((rows, features), jnp.bfloat16),
             pltpu.VMEM((rows, features), jnp.bfloat16),
@@ -261,26 +273,56 @@
     )(info, *direct, *swapped, base, *kept, *after)
 
 
-def sum_kernel(sign, slots, base, *refs):
-    received, out = refs[: len(slots)], refs[-1]
+def pair_kernel(size, n_after, info, mine, theirs, *refs):
+    outs = refs[n_after:]
+    z = info[5]
+    rows = mine.shape[1]
+    for q, out in enumerate(outs):
+        for at in range(0, rows, size):
+            partner = at // size ^ 1
+            total = mine[z ^ q, pl.ds(at, size), :] + theirs[
+                z ^ q, pl.ds(partner * size, size), :
+            ].astype(jnp.float32)
+            out[pl.ds(at, size), :] = total.astype(out.dtype)
+
+
+def add_pair(info, mine, theirs, size, after):
+    count, rows, cols = mine.shape
+    return pl.pallas_call(
+        functools.partial(pair_kernel, size, len(after)),
+        in_specs=[pl.BlockSpec(memory_space=pltpu.SMEM), WHOLE, WHOLE] + [ANYWHERE] * len(after),
+        out_specs=[WHOLE] * count,
+        out_shape=[
+            jax.ShapeDtypeStruct((rows, cols), jnp.float32 if q == 0 else jnp.bfloat16)
+            for q in range(count)
+        ],
+        compiler_params=pltpu.CompilerParams(vmem_limit_bytes=SUM_MIB * MIB),
+        name="add_pair",
+    )(info, mine, theirs, *after)
+
+
+def sum_kernel(sign, pieces, info, base, *refs):
+    received, out = refs[: len(pieces)], refs[-1]
+    me = info[6]
     out[...] = sign * base[...]
-    for ref, blocks in zip(received, slots):
-        size = ref.shape[1] // len(blocks)
-        for source in range(ref.shape[0]):
-            for k, s in enumerate(blocks):
-                at = pl.ds((source ^ s) * size, size)
-                out[at, :] += ref[source, pl.ds(k * size, size), :].astype(jnp.float32)
-
-
-def add_up(base, sign, slots, received, after):
+    for ref, (source, blocks) in zip(received, pieces):
+        size = ref.shape[0] // len(blocks)
+        for k, s in enumerate(blocks):
+            at = pl.ds(pl.multiple_of((me ^ (source ^ s)) * size, size), size)
+            out[at, :] += ref[pl.ds(k * size, size), :].astype(jnp.float32)
+
+
+def add_up(info, base, sign, pieces, received, after):
     return pl.pallas_call(
-        functools.partial(sum_kernel, sign, slots),
-        in_specs=[WHOLE] * (1 + len(received)) + [ANYWHERE] * len(after),
+        functools.partial(sum_kernel, sign, pieces),
+        in_specs=[pl.BlockSpec(memory_space=pltpu.SMEM)]
+        + [WHOLE] * (1 + len(received))
+        + [ANYWHERE] * len(after),
         out_specs=WHOLE,
         out_shape=jax.ShapeDtypeStruct(base.shape, base.dtype),
-        compiler_params=pltpu.CompilerParams(vmem_limit_bytes=ENCODE_MIB * MIB),
+        compiler_params=pltpu.CompilerParams(vmem_limit_bytes=SUM_MIB * MIB),
         name="add_up",
-    )(base, *received, *after)
+    )(info, base, *received, *after)
 
 
 def pipelined(layer_inputs, targets, encoder, encoder_bias, decoder):
@@ -288,6 +330,7 @@
     layers = lax.axis_size("layer")
     half = layers // 2
     layer = lax.axis_index("layer")
+    feat = lax.axis_index("feat")
     upper = layer >= half
     info = jnp.stack(
         [
@@ -295,6 +338,9 @@
             upper.astype(jnp.int32),
             jnp.full_like(layer, half),
             jnp.where(upper, layer - ((layer ^ 1) - half), 0),
+            feat & 1,
+            feat >> 1,
+            feat,
         ]
     ).astype(jnp.int32)
 
@@ -306,9 +352,6 @@
 
     def beside(a):
         return lax.ppermute(a, "layer", [(i, i + 1) for i in range(0, layers, 2)])
-
-    def scatter(partial):
-        return lax.all_to_all(partial, "feat", 0, 0)
 
     def after(value, *earlier):
         return lax.optimization_barrier((value, *earlier))[0]
@@ -353,38 +396,41 @@
     )
     d2, d3, n2 = up(a2a), up(a2b), beside(after(a2, d0b))
 
-    c0a, c0b = across(after(d0a, a2)), across(d0b)
-    wave, base, *kept = decode_first(
+    c0a, c0b = across(after(d0a, n2)), across(after(d0b, n2))
+    mine, sent, base, *kept = decode_first(
         info, [a0, a1, a2], [n0, n1, n2], [d0a, d0b], [c0a, c0b], decoder, shards, []
     )
-    received = [scatter(wave)]
-    c1 = across(after(d1, wave))
-    wave = decode_later(
-        info, [d1], [c1], [(0, 0, 2 * size)], base, kept, 2 * size, shards, [wave]
-    )
-    received.append(scatter(wave))
-    c2 = across(after(d2, wave))
+    slots = [[0, 1], [2, 3], list(range(4, shards - 2)), [shards - 2, shards - 1]]
+
+    def meet(mine, sent, *earlier):
+        return add_pair(info, mine, exchange(sent, "feat", 1), size, list(earlier))
+
+    def spread(number, sums):
+        parts = [part if q == 0 else exchange(part, "feat", 2 * q) for q, part in enumerate(sums)]
+        return [(2 * q, slots[number]) for q in range(len(parts))], parts
+
+    def later(number, direct, swapped, order, *earlier):
+        row = slots[number][0] * size
+        return decode_later(info, direct, swapped, order, base, kept, row, shards, list(earlier))
+
+    c1 = across(after(d1, sent))
+    mine1, sent1 = later(1, [d1], [c1], [(0, 0, 2 * size)], sent)
+    met0 = meet(mine, sent, sent1)
+    where0, parts0 = spread(0, met0)
+    met1 = meet(mine1, sent1, met0[0])
+    where1, parts1 = spread(1, met1)
+    c2 = across(after(d2, met1[0]))
     early = (others - 2) * size
-    wave = decode_later(
-        info, [d2], [c2], [(0, 0, early)], base, kept, 4 * size, shards, [wave]
-    )
-    received.append(scatter(wave))
-    c3 = across(after(d3, wave))
-    wave = decode_later(
-        info,
-        [d2, d3],
-        [c2, c3],
-        [(0, early, size), (1, 0, size)],
-        base,
-        kept,
-        4 * size + early,
-        shards,
-        [wave],
-    )
-    received.append(scatter(wave))
-    slots = [[0, 1], [2, 3], list(range(4, shards - 2)), [shards - 2, shards - 1]]
-    total = add_up(targets[0], -1.0, slots[:3], received[:3], [wave])
-    return add_up(total, 1.0, slots[3:], received[3:], [])[None]
+    mine2, sent2 = later(2, [d2], [c2], [(0, 0, early)], met1[0], *parts0)
+    c3 = across(after(d3, sent2))
+    order = [(0, early, size), (1, 0, size)]
+    mine3, sent3 = later(3, [d2, d3], [c2, c3], order, sent2, *parts1)
+    met2 = meet(mine2, sent2, sent3)
+    where2, parts2 = spread(2, met2)
+    total = add_up(info, targets[0], -1.0, where0 + where1, parts0 + parts1, [met2[0]])
+    met3 = meet(mine3, sent3, total)
+    where3, parts3 = spread(3, met3)
+    return add_up(info, total, 1.0, where2 + where3, parts2 + parts3, [])[None]
 
 
 def grouped(layer_inputs, targets, encoder, encoder_bias, decoder):

time: 221 us -> 190 us (0.86)
  local copies, waits for them, and re-layouts: 50.7 us -> 13.7 us
  waiting for transfers between devices: 33.5 us -> 41.5 us
  starting transfers between devices: 63.8 us -> 59.6 us
  Pallas kernels: 70.5 us -> 73.6 us
    unnamed x44 -> x72, local copies, waits for them, and re-layouts: 50.7 us -> 13.1 us
    all_to_all x4 -> x0, starting transfers between devices: 23.1 us -> none  [scatter(): return lax.all_to_all(partial, 'feat', 0, 0)]
    ppermute x6 -> x22, waiting for transfers between devices: 18.1 us -> 39.6 us  [exchange(): return lax.ppermute(array, axis, [(i, i ^ flip) for i in range(size)])]
    ppermute x6 -> x22, starting transfers between devices: 7.77 us -> 28.6 us  [exchange(): return lax.ppermute(array, axis, [(i, i ^ flip) for i in range(size)])]
    all_to_all x4 -> x0, waiting for transfers between devices: 13.5 us -> none  [scatter(): return lax.all_to_all(partial, 'feat', 0, 0)]
    pallas_call x2 -> x6, Pallas kernels: 1.13 us -> 4.53 us  [the longest x4 2.36 us: add_pair(): pl.pallas_call(functools.partial(pair_kernel, size, len(after)), in_specs...]
    ppermute x3, starting transfers between devices: 7.37 us -> 5.06 us  [beside(): return lax.ppermute(a, 'layer', [(i, i + 1) for i in range(0, layers, 2)])]
  transfers between devices with their start and end apart: 23 -> 35, of which waited for: 7 -> 13; matrix products, arithmetic and copies ran while one was open for 0% -> 0% of each run, Pallas kernels for 32% -> 38%
where the time goes in v5:
time: 190 us; the launch traced here: 189 us
  Pallas kernels  73.6 us (39%)
  starting transfers between devices  59.6 us (31%)
  waiting for transfers between devices  41.5 us (22%)
  local copies, waits for them, and re-layouts  13.7 us (7%)
    ppermute x22, waiting for transfers between devices, exchange(): return lax.ppermute(array, axis, [(i, i ^ flip) for i in range(size)])  39.6 us
    ppermute x22, starting transfers between devices, exchange(): return lax.ppermute(array, axis, [(i, i ^ flip) for i in range(size)])  28.6 us
    pallas_call x3, Pallas kernels, decode_later(): pl.pallas_call(functools.partial(later_wave_kernel, order, row, len(direc...  27.8 us
    pallas_call x1, Pallas kernels, decode_first(): pl.pallas_call(functools.partial(first_wave_kernel, [len(parts) for parts...  24 us
    ppermute x5, starting transfers between devices, across(): return lax.ppermute(a, 'layer', [(i, i ^ 1) for i in range(half, layers)])  19.5 us
    pallas_call x3, Pallas kernels, encode(): pl.pallas_call(functools.partial(encode_kernel, order, pieces, len(parts)...  17.2 us
    unnamed x72, local copies, waits for them, and re-layouts  13.1 us
    ppermute x5, starting transfers between devices, up(): return lax.ppermute(a, 'layer', [(i, i + half) for i in range(half)])  6.44 us
  transfers between devices with their start and end apart: 35, of which 13 were waited for; matrix products, arithmetic and copies ran while one was open for 0% of the time, Pallas kernels for 38%

profile of v5, /device:TPU:2, one launch (start us, length us, event | category | flops | bytes accessed | tf_op | source)
XLA Modules:
  0.0 189.0 jit_solution(4891052814996983118)
XLA Ops:
  1.5 2.6 %collective-permute-start.3 = (bf16[64,2048]{1,0:T(8,128)(2,1)}, bf16[64,2048]{1,0:T(8,128)(2,1)S(1)}, u32[]{:S(2)}, u32[]{:S(2)}) collective-permute-start(bf16[64,2048]{1,0:T(8,128)(2,1)} %bitcast.11), channel_id=1, source_target_pairs={{0,4},{1,5},{2,6},{3,7},{4,0},{5,1},{6,2},{7,3},{8,12},{9,13},{10,... | collective-permute-start | bytes 786440 | tf_op jit(solution)/shard_map/ppermute | solution.py:16
  5.7 2.6 %collective-permute-done.refs_1_ = bf16[64,2048]{1,0:T(8,128)(2,1)S(1)} collective-permute-done((bf16[64,2048]{1,0:T(8,128)(2,1)}, bf16[64,2048]{1,0:T(8,128)(2,1)S(1)}, u32[]{:S(2)}, u32[]{:S(2)}) %collective-permute-start) | collective-permute-done | bytes 262176 | tf_op jit(solution)/shard_map/ppermute | solution.py:16
  11.5 6.5 %encode.3 = (bf16[128,4096]{1,0:T(8,128)(2,1)S(1)}, bf16[64,4096]{1,0:T(8,128)(2,1)S(1)}, bf16[64,4096]{1,0:T(8,128)(2,1)S(1)}, bf16[1,2048,4096]{2,1,0:T(8,128)(2,1)S(1)}) custom-call(bf16[64,2048]{1,0:T(8,128)(2,1)S(1)} %bitcast.14, bf16[64,2048]{1,0:T(8,128)(2,1)S(1)} %collective-permute-done.refs_1_, bf16[1,2048,4096]{2,1,0:T(8,128)(2,1)} %refs_2_.1, ...), custom_call_target="tpu_custom_call" | custom-call | tf_op jit(solution)/shard_map/encode/pallas_call | solution.py:76
  19.3 3.5 %collective-permute-done.3.refs_0_ = bf16[64,2048]{1,0:T(8,128)(2,1)S(1)} collective-permute-done((bf16[64,2048]{1,0:T(8,128)(2,1)}, bf16[64,2048]{1,0:T(8,128)(2,1)S(1)}, u32[]{:S(2)}, u32[]{:S(2)}) %collective-permute-start.3) | collective-permute-done | bytes 262176 | tf_op jit(solution)/shard_map/ppermute | solution.py:16
  22.9 2.1 %collective-permute-done.1.refs_0_ = bf16[64,2048]{1,0:T(8,128)(2,1)S(1)} collective-permute-done((bf16[64,2048]{1,0:T(8,128)(2,1)}, bf16[64,2048]{1,0:T(8,128)(2,1)S(1)}, u32[]{:S(2)}, u32[]{:S(2)}) %collective-permute-start.1) | collective-permute-done | bytes 262176 | tf_op jit(solution)/shard_map/ppermute | solution.py:16
  25.0 3.6 %collective-permute-done.2.refs_1_ = bf16[64,2048]{1,0:T(8,128)(2,1)S(1)} collective-permute-done((bf16[64,2048]{1,0:T(8,128)(2,1)S(1)}, bf16[64,2048]{1,0:T(8,128)(2,1)S(1)}, u32[]{:S(2)}, u32[]{:S(2)}) %collective-permute-start.2) | collective-permute-done | bytes 262176 | tf_op jit(solution)/shard_map/ppermute | solution.py:16
  30.4 3.7 %encode.4.refs_5_.refs_1_ = bf16[128,4096]{1,0:T(8,128)(2,1)S(1)} custom-call(bf16[64,2048]{1,0:T(8,128)(2,1)S(1)} %collective-permute-done.1.refs_0_, bf16[64,2048]{1,0:T(8,128)(2,1)S(1)} %collective-permute-done.2.refs_1_, bf16[1,2048,4096]{2,1,0:T(8,128)(2,1)S(1)} %get-tuple-element.47.refs_2_.refs_3_, f32[1,4096]{1,0:T(1,128)S(1)} %copy-done.28, ...), custom_call_target="tpu_custom_call" | custom-call | tf_op jit(solution)/shard_map/encode/pallas_call | solution.py:76
  34.2 6.3 %collective-permute-done.5.refs_2_ = bf16[128,2048]{1,0:T(8,128)(2,1)S(1)} collective-permute-done((bf16[128,2048]{1,0:T(8,128)(2,1)S(1)}, bf16[128,2048]{1,0:T(8,128)(2,1)S(1)}, u32[]{:S(2)}, u32[]{:S(2)}) %collective-permute-start.5) | collective-permute-done | bytes 524320 | tf_op jit(solution)/shard_map/ppermute | solution.py:16
  40.5 7.0 %encode.5 = (bf16[256,4096]{1,0:T(8,128)(2,1)S(1)}, bf16[192,4096]{1,0:T(8,128)(2,1)}, bf16[64,4096]{1,0:T(8,128)(2,1)S(1)}) custom-call(bf16[64,2048]{1,0:T(8,128)(2,1)S(1)} %collective-permute-done.3.refs_0_, bf16[64,2048]{1,0:T(8,128)(2,1)S(1)} %collective-permute-done.4.refs_1_, bf16[128,2048]{1,0:T(8,128)(2,1)S(1)} %collective-permute-done.5.refs_2_, ...), custom_call_target="tpu_custom_call" | custom-call | tf_op jit(solution)/shard_map/encode/pallas_call | solution.py:76
  50.3 2.3 %collective-permute-start.8 = (bf16[128,4096]{1,0:T(8,128)(2,1)S(1)}, bf16[128,4096]{1,0:T(8,128)(2,1)}, u32[]{:S(2)}, u32[]{:S(2)}) collective-permute-start(bf16[128,4096]{1,0:T(8,128)(2,1)S(1)} %encode.4.refs_5_.refs_1_), channel_id=1, source_target_pairs={{0,8},{16,24},{1,9},{17,25},{2,10},{18,26},{3,11},{19,27},{4,12},{... | collective-permute-start | bytes 3145736 | tf_op jit(solution)/shard_map/ppermute | solution.py:354
  53.9 1.9 %collective-permute-start.12 = (bf16[64,4096]{1,0:T(8,128)(2,1)}, bf16[64,4096]{1,0:T(8,128)(2,1)}, u32[]{:S(2)}, u32[]{:S(2)}) collective-permute-start(bf16[64,4096]{1,0:T(8,128)(2,1)} %collective-permute-done.9.refs_7_), channel_id=1, source_target_pairs={{16,24},{24,16},{17,25},{25,17},{18,26},{26,18},{19,27},{27,19},{2... | collective-permute-start | bytes 1572872 | tf_op jit(solution)/shard_map/ppermute | solution.py:351
  55.8 2.4 %collective-permute-start.11 = (bf16[64,4096]{1,0:T(8,128)(2,1)S(1)}, bf16[64,4096]{1,0:T(8,128)(2,1)}, u32[]{:S(2)}, u32[]{:S(2)}) collective-permute-start(bf16[64,4096]{1,0:T(8,128)(2,1)S(1)} %collective-permute-done.6.refs_6_), channel_id=1, source_target_pairs={{16,24},{24,16},{17,25},{25,17},{18,26},{26,18},{19,27},{27,19},{2... | collective-permute-start | bytes 1572872 | tf_op jit(solution)/shard_map/ppermute | solution.py:351
  60.2 24.0 %decode_first.1 = (f32[4,128,256]{2,1,0:T(8,128)}, bf16[4,128,256]{2,1,0:T(8,128)(2,1)}, f32[512,2048]{1,0:T(8,128)}, bf16[4096,2048]{1,0:T(8,128)(2,1)S(1)}, bf16[4096,2048]{1,0:T(8,128)(2,1)S(1)}) custom-call(s32[7]{0:T(128)} %stack.31.info, bf16[128,4096]{1,0:T(8,128)(2,1)} %copy-done.1, bf16[128,4096]{1,0:T(8,128)(2,1)} %copy-done, ...), custom_call_target="tpu_custom_call" | custom-call | tf_op jit(solution)/shard_map/decode_first/pallas_call | solution.py:200
  84.3 11.1 %collective-permute-start.15 = (bf16[128,4096]{1,0:T(8,128)(2,1)}, bf16[128,4096]{1,0:T(8,128)(2,1)S(1)}, u32[]{:S(2)}, u32[]{:S(2)}) collective-permute-start(bf16[128,4096]{1,0:T(8,128)(2,1)} %collective-permute-done.14.refs_0_), channel_id=1, source_target_pairs={{16,24},{24,16},{17,25},{25,17},{18,26},{26,18},{19,27},{27,19},{2... | collective-permute-start | bytes 3145736 | tf_op jit(solution)/shard_map/ppermute | solution.py:351
  96.0 1.9 %collective-permute-done.15.refs_1_ = bf16[128,4096]{1,0:T(8,128)(2,1)S(1)} collective-permute-done((bf16[128,4096]{1,0:T(8,128)(2,1)}, bf16[128,4096]{1,0:T(8,128)(2,1)S(1)}, u32[]{:S(2)}, u32[]{:S(2)}) %collective-permute-start.15) | collective-permute-done | bytes 1048608 | tf_op jit(solution)/shard_map/ppermute | solution.py:351
  98.9 9.0 %decode_later.3 = (f32[4,128,256]{2,1,0:T(8,128)}, bf16[4,128,256]{2,1,0:T(8,128)(2,1)}) custom-call(s32[7]{0:T(128)} %stack.31.info, bf16[128,4096]{1,0:T(8,128)(2,1)} %collective-permute-done.14.refs_0_, bf16[128,4096]{1,0:T(8,128)(2,1)} %copy-done.34, f32[512,2048]{1,0:T(8,128)} %get-tuple-element.58.refs_2_.refs_4_, ...), custom_call_target="tpu_custom_call" | custom-call | tf_op jit(solution)/shard_map/decode_later/pallas_call | solution.py:257
  110.1 6.7 %collective-permute-done.19.theirs = bf16[4,128,256]{2,1,0:T(8,128)(2,1)S(1)} collective-permute-done((bf16[4,128,256]{2,1,0:T(8,128)(2,1)}, bf16[4,128,256]{2,1,0:T(8,128)(2,1)S(1)}, u32[]{:S(2)}, u32[]{:S(2)}) %collective-permute-start.19) | collective-permute-done | bytes 262176 | tf_op jit(solution)/shard_map/ppermute | solution.py:16
  119.1 1.9 %collective-permute-start.24 = (bf16[192,4096]{1,0:T(8,128)(2,1)}, bf16[192,4096]{1,0:T(8,128)(2,1)S(1)}, u32[]{:S(2)}, u32[]{:S(2)}) collective-permute-start(bf16[192,4096]{1,0:T(8,128)(2,1)} %collective-permute-done.23.refs_0_), channel_id=1, source_target_pairs={{16,24},{24,16},{17,25},{25,17},{18,26},{26,18},{19,27},{27,19},{2... | collective-permute-start | bytes 4718600 | tf_op jit(solution)/shard_map/ppermute | solution.py:351
  122.3 1.6 collective-permute-start.16
  123.9 2.5 %collective-permute-start.17 = (bf16[128,256]{1,0:T(8,128)(2,1)S(1)}, bf16[128,256]{1,0:T(8,128)(2,1)S(1)}, u32[]{:S(2)}, u32[]{:S(2)}) collective-permute-start(bf16[128,256]{1,0:T(8,128)(2,1)S(1)} %get-tuple-element.64), channel_id=1, source_target_pairs={{0,4},{1,5},{2,6},{3,7},{4,0},{5,1},{6,2},{7,3},{8,12},{9,13},{10,... | collective-permute-start | bytes 196616 | tf_op jit(solution)/shard_map/ppermute | solution.py:16
  127.2 1.9 collective-permute-done.17.refs_8_.refs_2_
  129.1 3.5 %collective-permute-done.18.refs_9_.refs_3_ = bf16[128,256]{1,0:T(8,128)(2,1)S(1)} collective-permute-done((bf16[128,256]{1,0:T(8,128)(2,1)S(1)}, bf16[128,256]{1,0:T(8,128)(2,1)S(1)}, u32[]{:S(2)}, u32[]{:S(2)}) %collective-permute-start.18) | collective-permute-done | bytes 65568 | tf_op jit(solution)/shard_map/ppermute | solution.py:16
  134.3 9.3 %decode_later.4 = (f32[4,128,256]{2,1,0:T(8,128)}, bf16[4,128,256]{2,1,0:T(8,128)(2,1)}) custom-call(s32[7]{0:T(128)} %stack.31.info, bf16[192,4096]{1,0:T(8,128)(2,1)} %collective-permute-done.23.refs_0_, bf16[192,4096]{1,0:T(8,128)(2,1)} %copy-done.31, f32[512,2048]{1,0:T(8,128)} %get-tuple-element.58.refs_2_.refs_4_, ...), custom_call_target="tpu_custom_call" | custom-call | tf_op jit(solution)/shard_map/decode_later/pallas_call | solution.py:257
  143.6 2.1 %collective-permute-start.27 = (bf16[64,4096]{1,0:T(8,128)(2,1)}, bf16[64,4096]{1,0:T(8,128)(2,1)S(1)}, u32[]{:S(2)}, u32[]{:S(2)}) collective-permute-start(bf16[64,4096]{1,0:T(8,128)(2,1)} %collective-permute-done.26.refs_1_), channel_id=1, source_target_pairs={{16,24},{24,16},{17,25},{25,17},{18,26},{26,18},{19,27},{27,19},{2... | collective-permute-start | bytes 1572872 | tf_op jit(solution)/shard_map/ppermute | solution.py:351
  145.8 1.8 collective-permute-start.20
  147.5 1.7 collective-permute-start.21
  151.1 1.9 %collective-permute-done.21.refs_10_.refs_6_ = bf16[128,256]{1,0:T(8,128)(2,1)S(1)} collective-permute-done((bf16[128,256]{1,0:T(8,128)(2,1)S(1)}, bf16[128,256]{1,0:T(8,128)(2,1)S(1)}, u32[]{:S(2)}, u32[]{:S(2)}) %collective-permute-start.21) | collective-permute-done | bytes 65568 | tf_op jit(solution)/shard_map/ppermute | solution.py:16
  153.0 2.8 %collective-permute-done.22.refs_11_.refs_7_ = bf16[128,256]{1,0:T(8,128)(2,1)S(1)} collective-permute-done((bf16[128,256]{1,0:T(8,128)(2,1)S(1)}, bf16[128,256]{1,0:T(8,128)(2,1)S(1)}, u32[]{:S(2)}, u32[]{:S(2)}) %collective-permute-start.22) | collective-permute-done | bytes 65568 | tf_op jit(solution)/shard_map/ppermute | solution.py:16
  157.2 9.5 %decode_later.5 = (f32[4,128,256]{2,1,0:T(8,128)}, bf16[4,128,256]{2,1,0:T(8,128)(2,1)}) custom-call(s32[7]{0:T(128)} %stack.31.info, bf16[192,4096]{1,0:T(8,128)(2,1)} %collective-permute-done.23.refs_0_, bf16[64,4096]{1,0:T(8,128)(2,1)} %collective-permute-done.26.refs_1_, bf16[192,4096]{1,0:T(8,128)(2,1)} %copy-done.31, bf16[64,4096]{1,0:T(8,128)(2,1)} %copy-done.35, ...), custom_call_target="tpu_custom_call" | custom-call | tf_op jit(solution)/shard_map/decode_later/pallas_call | solution.py:257
  168.9 1.8 collective-permute-start.28
  179.1 2.3 %collective-permute-start.33 = (bf16[128,256]{1,0:T(8,128)(2,1)S(1)}, bf16[128,256]{1,0:T(8,128)(2,1)S(1)}, u32[]{:S(2)}, u32[]{:S(2)}) collective-permute-start(bf16[128,256]{1,0:T(8,128)(2,1)S(1)} %get-tuple-element.85), channel_id=1, source_target_pairs={{0,4},{1,5},{2,6},{3,7},{4,0},{5,1},{6,2},{7,3},{8,12},{9,13},{10,... | collective-permute-start | bytes 196616 | tf_op jit(solution)/shard_map/ppermute | solution.py:16
  184.4 3.2 %collective-permute-done.34.refs_7_ = bf16[128,256]{1,0:T(8,128)(2,1)S(1)} collective-permute-done((bf16[128,256]{1,0:T(8,128)(2,1)S(1)}, bf16[128,256]{1,0:T(8,128)(2,1)S(1)}, u32[]{:S(2)}, u32[]{:S(2)}) %collective-permute-start.34) | collective-permute-done | bytes 65568 | tf_op jit(solution)/shard_map/ppermute | solution.py:16
  (125 shorter events, 43.5 us)
Async XLA Ops:
  0.0 8.3 %collective-permute-start = (bf16[64,2048]{1,0:T(8,128)(2,1)}, bf16[64,2048]{1,0:T(8,128)(2,1)S(1)}, u32[]{:S(2)}, u32[]{:S(2)}) collective-permute-start(bf16[64,2048]{1,0:T(8,128)(2,1)} %bitcast.10), channel_id=1, source_target_pairs={{0,1},{1,0},{2,3},{3,2},{4,5},{5,4},{6,7},{7,6},{8,9},{9,8},{10,11... | collective-permute-start | bytes 786440 | tf_op jit(solution)/shard_map/ppermute | solution.py:16
  1.5 21.3 %collective-permute-start.3 = (bf16[64,2048]{1,0:T(8,128)(2,1)}, bf16[64,2048]{1,0:T(8,128)(2,1)S(1)}, u32[]{:S(2)}, u32[]{:S(2)}) collective-permute-start(bf16[64,2048]{1,0:T(8,128)(2,1)} %bitcast.11), channel_id=1, source_target_pairs={{0,4},{1,5},{2,6},{3,7},{4,0},{5,1},{6,2},{7,3},{8,12},{9,13},{10,... | collective-permute-start | bytes 786440 | tf_op jit(solution)/shard_map/ppermute | solution.py:16
  4.1 18.8 %collective-permute-start.4 = (bf16[64,2048]{1,0:T(8,128)(2,1)}, bf16[64,2048]{1,0:T(8,128)(2,1)S(1)}, u32[]{:S(2)}, u32[]{:S(2)}) collective-permute-start(bf16[64,2048]{1,0:T(8,128)(2,1)} %bitcast.12), channel_id=1, source_target_pairs={{0,6},{1,7},{2,4},{3,5},{4,2},{5,3},{6,0},{7,1},{8,14},{9,15},{10,... | collective-permute-start | bytes 786440 | tf_op jit(solution)/shard_map/ppermute | solution.py:16
  5.5 19.6 %collective-permute-start.1 = (bf16[64,2048]{1,0:T(8,128)(2,1)}, bf16[64,2048]{1,0:T(8,128)(2,1)S(1)}, u32[]{:S(2)}, u32[]{:S(2)}) collective-permute-start(bf16[64,2048]{1,0:T(8,128)(2,1)} %bitcast.13), channel_id=1, source_target_pairs={{0,2},{1,3},{2,0},{3,1},{4,6},{5,7},{6,4},{7,5},{8,10},{9,11},{10,... | collective-permute-start | bytes 786440 | tf_op jit(solution)/shard_map/ppermute | solution.py:16
  8.3 20.4 %collective-permute-start.2 = (bf16[64,2048]{1,0:T(8,128)(2,1)S(1)}, bf16[64,2048]{1,0:T(8,128)(2,1)S(1)}, u32[]{:S(2)}, u32[]{:S(2)}) collective-permute-start(bf16[64,2048]{1,0:T(8,128)(2,1)S(1)} %collective-permute-done.refs_1_), channel_id=1, source_target_pairs={{0,2},{1,3},{2,0},{3,1},{4,6},{5,7},{6,4},{7,5},{8,10},{9,11},{10,... | collective-permute-start | bytes 786440 | tf_op jit(solution)/shard_map/ppermute | solution.py:16
  18.0 16.1 %collective-permute-start.6 = (bf16[64,4096]{1,0:T(8,128)(2,1)S(1)}, bf16[64,4096]{1,0:T(8,128)(2,1)S(1)}, u32[]{:S(2)}, u32[]{:S(2)}) collective-permute-start(bf16[64,4096]{1,0:T(8,128)(2,1)S(1)} %get-tuple-element.49), channel_id=1, source_target_pairs={{0,16},{8,24},{1,17},{9,25},{2,18},{10,26},{3,19},{11,27},{4,20},{... | collective-permute-start | bytes 1572872 | tf_op jit(solution)/shard_map/ppermute | solution.py:348
  28.6 11.9 %collective-permute-start.5 = (bf16[128,2048]{1,0:T(8,128)(2,1)S(1)}, bf16[128,2048]{1,0:T(8,128)(2,1)S(1)}, u32[]{:S(2)}, u32[]{:S(2)}) collective-permute-start(bf16[128,2048]{1,0:T(8,128)(2,1)S(1)} %pad_maximum_fusion), channel_id=1, source_target_pairs={{0,1},{1,0},{2,3},{3,2},{4,5},{5,4},{6,7},{7,6},{8,9},{9,8},{10,11... | collective-permute-start | bytes 1572872 | tf_op jit(solution)/shard_map/ppermute | solution.py:16
  29.1 18.4 %collective-permute-start.9 = (bf16[64,4096]{1,0:T(8,128)(2,1)S(1)}, bf16[64,4096]{1,0:T(8,128)(2,1)}, u32[]{:S(2)}, u32[]{:S(2)}) collective-permute-start(bf16[64,4096]{1,0:T(8,128)(2,1)S(1)} %get-tuple-element.51), channel_id=1, source_target_pairs={{0,16},{8,24},{1,17},{9,25},{2,18},{10,26},{3,19},{11,27},{4,20},{... | collective-permute-start | bytes 1572872 | tf_op jit(solution)/shard_map/ppermute | solution.py:348
  47.5 6.4 %collective-permute-start.10 = (bf16[256,4096]{1,0:T(8,128)(2,1)S(1)}, bf16[256,4096]{1,0:T(8,128)(2,1)S(1)}, u32[]{:S(2)}, u32[]{:S(2)}) collective-permute-start(bf16[256,4096]{1,0:T(8,128)(2,1)S(1)} %get-tuple-element.52.refs_2_), channel_id=1, source_target_pairs={{0,8},{16,24},{1,9},{17,25},{2,10},{18,26},{3,11},{19,27},{4,12},{... | collective-permute-start | bytes 6291464 | tf_op jit(solution)/shard_map/ppermute | solution.py:354
  48.9 9.3 %collective-permute-start.7 = (bf16[128,4096]{1,0:T(8,128)(2,1)S(1)}, bf16[128,4096]{1,0:T(8,128)(2,1)S(1)}, u32[]{:S(2)}, u32[]{:S(2)}) collective-permute-start(bf16[128,4096]{1,0:T(8,128)(2,1)S(1)} %get-tuple-element.46.refs_4_.refs_0_), channel_id=1, source_target_pairs={{0,8},{16,24},{1,9},{17,25},{2,10},{18,26},{3,11},{19,27},{4,12},{... | collective-permute-start | bytes 3145736 | tf_op jit(solution)/shard_map/ppermute | solution.py:354
  50.3 9.9 %collective-permute-start.8 = (bf16[128,4096]{1,0:T(8,128)(2,1)S(1)}, bf16[128,4096]{1,0:T(8,128)(2,1)}, u32[]{:S(2)}, u32[]{:S(2)}) collective-permute-start(bf16[128,4096]{1,0:T(8,128)(2,1)S(1)} %encode.4.refs_5_.refs_1_), channel_id=1, source_target_pairs={{0,8},{16,24},{1,9},{17,25},{2,10},{18,26},{3,11},{19,27},{4,12},{... | collective-permute-start | bytes 3145736 | tf_op jit(solution)/shard_map/ppermute | solution.py:354
  52.6 31.7 %collective-permute-start.14 = (bf16[128,4096]{1,0:T(8,128)(2,1)S(1)}, bf16[128,4096]{1,0:T(8,128)(2,1)}, u32[]{:S(2)}, u32[]{:S(2)}) collective-permute-start(bf16[128,4096]{1,0:T(8,128)(2,1)S(1)} %encode.4.refs_5_.refs_1_), channel_id=1, source_target_pairs={{0,16},{8,24},{1,17},{9,25},{2,18},{10,26},{3,19},{11,27},{4,20},{... | collective-permute-start | bytes 3145736 | tf_op jit(solution)/shard_map/ppermute | solution.py:348
  53.9 6.3 %collective-permute-start.12 = (bf16[64,4096]{1,0:T(8,128)(2,1)}, bf16[64,4096]{1,0:T(8,128)(2,1)}, u32[]{:S(2)}, u32[]{:S(2)}) collective-permute-start(bf16[64,4096]{1,0:T(8,128)(2,1)} %collective-permute-done.9.refs_7_), channel_id=1, source_target_pairs={{16,24},{24,16},{17,25},{25,17},{18,26},{26,18},{19,27},{27,19},{2... | collective-permute-start | bytes 1572872 | tf_op jit(solution)/shard_map/ppermute | solution.py:351
  58.3 60.8 %collective-permute-start.23 = (bf16[192,4096]{1,0:T(8,128)(2,1)}, bf16[192,4096]{1,0:T(8,128)(2,1)}, u32[]{:S(2)}, u32[]{:S(2)}) collective-permute-start(bf16[192,4096]{1,0:T(8,128)(2,1)} %get-tuple-element.71), channel_id=1, source_target_pairs={{0,16},{8,24},{1,17},{9,25},{2,18},{10,26},{3,19},{11,27},{4,20},{... | collective-permute-start | bytes 4718600 | tf_op jit(solution)/shard_map/ppermute | solution.py:348
  84.3 13.6 %collective-permute-start.15 = (bf16[128,4096]{1,0:T(8,128)(2,1)}, bf16[128,4096]{1,0:T(8,128)(2,1)S(1)}, u32[]{:S(2)}, u32[]{:S(2)}) collective-permute-start(bf16[128,4096]{1,0:T(8,128)(2,1)} %collective-permute-done.14.refs_0_), channel_id=1, source_target_pairs={{16,24},{24,16},{17,25},{25,17},{18,26},{26,18},{19,27},{27,19},{2... | collective-permute-start | bytes 3145736 | tf_op jit(solution)/shard_map/ppermute | solution.py:351
  95.4 13.1 %collective-permute-start.13 = (bf16[4,128,256]{2,1,0:T(8,128)(2,1)}, bf16[4,128,256]{2,1,0:T(8,128)(2,1)S(1)}, u32[]{:S(2)}, u32[]{:S(2)}) collective-permute-start(bf16[4,128,256]{2,1,0:T(8,128)(2,1)} %get-tuple-element.56.refs_5_), channel_id=1, source_target_pairs={{0,1},{1,0},{2,3},{3,2},{4,5},{5,4},{6,7},{7,6},{8,9},{9,8},{10,11... | collective-permute-start | bytes 786440 | tf_op jit(solution)/shard_map/ppermute | solution.py:16
  107.9 8.9 %collective-permute-start.19 = (bf16[4,128,256]{2,1,0:T(8,128)(2,1)}, bf16[4,128,256]{2,1,0:T(8,128)(2,1)S(1)}, u32[]{:S(2)}, u32[]{:S(2)}) collective-permute-start(bf16[4,128,256]{2,1,0:T(8,128)(2,1)} %get-tuple-element.61.refs_0_), channel_id=1, source_target_pairs={{0,1},{1,0},{2,3},{3,2},{4,5},{5,4},{6,7},{7,6},{8,9},{9,8},{10,11... | collective-permute-start | bytes 786440 | tf_op jit(solution)/shard_map/ppermute | solution.py:16
  119.1 13.5 %collective-permute-start.24 = (bf16[192,4096]{1,0:T(8,128)(2,1)}, bf16[192,4096]{1,0:T(8,128)(2,1)S(1)}, u32[]{:S(2)}, u32[]{:S(2)}) collective-permute-start(bf16[192,4096]{1,0:T(8,128)(2,1)} %collective-permute-done.23.refs_0_), channel_id=1, source_target_pairs={{16,24},{24,16},{17,25},{25,17},{18,26},{26,18},{19,27},{27,19},{2... | collective-permute-start | bytes 4718600 | tf_op jit(solution)/shard_map/ppermute | solution.py:351
  121.0 22.7 %collective-permute-start.26 = (bf16[64,4096]{1,0:T(8,128)(2,1)S(1)}, bf16[64,4096]{1,0:T(8,128)(2,1)}, u32[]{:S(2)}, u32[]{:S(2)}) collective-permute-start(bf16[64,4096]{1,0:T(8,128)(2,1)S(1)} %get-tuple-element.75), channel_id=1, source_target_pairs={{0,16},{8,24},{1,17},{9,25},{2,18},{10,26},{3,19},{11,27},{4,20},{... | collective-permute-start | bytes 1572872 | tf_op jit(solution)/shard_map/ppermute | solution.py:348
  123.9 5.2 %collective-permute-start.17 = (bf16[128,256]{1,0:T(8,128)(2,1)S(1)}, bf16[128,256]{1,0:T(8,128)(2,1)S(1)}, u32[]{:S(2)}, u32[]{:S(2)}) collective-permute-start(bf16[128,256]{1,0:T(8,128)(2,1)S(1)} %get-tuple-element.64), channel_id=1, source_target_pairs={{0,4},{1,5},{2,6},{3,7},{4,0},{5,1},{6,2},{7,3},{8,12},{9,13},{10,... | collective-permute-start | bytes 196616 | tf_op jit(solution)/shard_map/ppermute | solution.py:16
  126.4 6.1 %collective-permute-start.18 = (bf16[128,256]{1,0:T(8,128)(2,1)S(1)}, bf16[128,256]{1,0:T(8,128)(2,1)S(1)}, u32[]{:S(2)}, u32[]{:S(2)}) collective-permute-start(bf16[128,256]{1,0:T(8,128)(2,1)S(1)} %get-tuple-element.65), channel_id=1, source_target_pairs={{0,6},{1,7},{2,4},{3,5},{4,2},{5,3},{6,0},{7,1},{8,14},{9,15},{10,... | collective-permute-start | bytes 196616 | tf_op jit(solution)/shard_map/ppermute | solution.py:16
  143.6 12.1 %collective-permute-start.27 = (bf16[64,4096]{1,0:T(8,128)(2,1)}, bf16[64,4096]{1,0:T(8,128)(2,1)S(1)}, u32[]{:S(2)}, u32[]{:S(2)}) collective-permute-start(bf16[64,4096]{1,0:T(8,128)(2,1)} %collective-permute-done.26.refs_1_), channel_id=1, source_target_pairs={{16,24},{24,16},{17,25},{25,17},{18,26},{26,18},{19,27},{27,19},{2... | collective-permute-start | bytes 1572872 | tf_op jit(solution)/shard_map/ppermute | solution.py:351
  145.8 5.3 %collective-permute-start.20 = (bf16[128,256]{1,0:T(8,128)(2,1)S(1)}, bf16[128,256]{1,0:T(8,128)(2,1)S(1)}, u32[]{:S(2)}, u32[]{:S(2)}) collective-permute-start(bf16[128,256]{1,0:T(8,128)(2,1)S(1)} %get-tuple-element.68), channel_id=1, source_target_pairs={{0,2},{1,3},{2,0},{3,1},{4,6},{5,7},{6,4},{7,5},{8,10},{9,11},{10,... | collective-permute-start | bytes 196616 | tf_op jit(solution)/shard_map/ppermute | solution.py:16
  147.5 5.4 %collective-permute-start.21 = (bf16[128,256]{1,0:T(8,128)(2,1)S(1)}, bf16[128,256]{1,0:T(8,128)(2,1)S(1)}, u32[]{:S(2)}, u32[]{:S(2)}) collective-permute-start(bf16[128,256]{1,0:T(8,128)(2,1)S(1)} %get-tuple-element.69), channel_id=1, source_target_pairs={{0,4},{1,5},{2,6},{3,7},{4,0},{5,1},{6,2},{7,3},{8,12},{9,13},{10,... | collective-permute-start | bytes 196616 | tf_op jit(solution)/shard_map/ppermute | solution.py:16
  149.2 6.5 %collective-permute-start.22 = (bf16[128,256]{1,0:T(8,128)(2,1)S(1)}, bf16[128,256]{1,0:T(8,128)(2,1)S(1)}, u32[]{:S(2)}, u32[]{:S(2)}) collective-permute-start(bf16[128,256]{1,0:T(8,128)(2,1)S(1)} %get-tuple-element.70), channel_id=1, source_target_pairs={{0,6},{1,7},{2,4},{3,5},{4,2},{5,3},{6,0},{7,1},{8,14},{9,15},{10,... | collective-permute-start | bytes 196616 | tf_op jit(solution)/shard_map/ppermute | solution.py:16
  150.5 16.8 %collective-permute-start.25 = (bf16[4,128,256]{2,1,0:T(8,128)(2,1)}, bf16[4,128,256]{2,1,0:T(8,128)(2,1)S(1)}, u32[]{:S(2)}, u32[]{:S(2)}) collective-permute-start(bf16[4,128,256]{2,1,0:T(8,128)(2,1)} %get-tuple-element.74.refs_7_), channel_id=1, source_target_pairs={{0,1},{1,0},{2,3},{3,2},{4,5},{5,4},{6,7},{7,6},{8,9},{9,8},{10,11... | collective-permute-start | bytes 786440 | tf_op jit(solution)/shard_map/ppermute | solution.py:16
  166.7 9.9 %collective-permute-start.31 = (bf16[4,128,256]{2,1,0:T(8,128)(2,1)}, bf16[4,128,256]{2,1,0:T(8,128)(2,1)S(1)}, u32[]{:S(2)}, u32[]{:S(2)}) collective-permute-start(bf16[4,128,256]{2,1,0:T(8,128)(2,1)} %get-tuple-element.77.refs_0_), channel_id=1, source_target_pairs={{0,1},{1,0},{2,3},{3,2},{4,5},{5,4},{6,7},{7,6},{8,9},{9,8},{10,11... | collective-permute-start | bytes 786440 | tf_op jit(solution)/shard_map/ppermute | solution.py:16
  168.9 12.6 %collective-permute-start.28 = (bf16[128,256]{1,0:T(8,128)(2,1)S(1)}, bf16[128,256]{1,0:T(8,128)(2,1)S(1)}, u32[]{:S(2)}, u32[]{:S(2)}) collective-permute-start(bf16[128,256]{1,0:T(8,128)(2,1)S(1)} %get-tuple-element.79), channel_id=1, source_target_pairs={{0,2},{1,3},{2,0},{3,1},{4,6},{5,7},{6,4},{7,5},{8,10},{9,11},{10,... | collective-permute-start | bytes 196616 | tf_op jit(solution)/shard_map/ppermute | solution.py:16
  170.7 12.1 %collective-permute-start.29 = (bf16[128,256]{1,0:T(8,128)(2,1)S(1)}, bf16[128,256]{1,0:T(8,128)(2,1)S(1)}, u32[]{:S(2)}, u32[]{:S(2)}) collective-permute-start(bf16[128,256]{1,0:T(8,128)(2,1)S(1)} %get-tuple-element.80), channel_id=1, source_target_pairs={{0,4},{1,5},{2,6},{3,7},{4,0},{5,1},{6,2},{7,3},{8,12},{9,13},{10,... | collective-permute-start | bytes 196616 | tf_op jit(solution)/shard_map/ppermute | solution.py:16
  172.1 10.7 %collective-permute-start.30 = (bf16[128,256]{1,0:T(8,128)(2,1)S(1)}, bf16[128,256]{1,0:T(8,128)(2,1)S(1)}, u32[]{:S(2)}, u32[]{:S(2)}) collective-permute-start(bf16[128,256]{1,0:T(8,128)(2,1)S(1)} %get-tuple-element.81), channel_id=1, source_target_pairs={{0,6},{1,7},{2,4},{3,5},{4,2},{5,3},{6,0},{7,1},{8,14},{9,15},{10,... | collective-permute-start | bytes 196616 | tf_op jit(solution)/shard_map/ppermute | solution.py:16
  179.1 5.2 %collective-permute-start.33 = (bf16[128,256]{1,0:T(8,128)(2,1)S(1)}, bf16[128,256]{1,0:T(8,128)(2,1)S(1)}, u32[]{:S(2)}, u32[]{:S(2)}) collective-permute-start(bf16[128,256]{1,0:T(8,128)(2,1)S(1)} %get-tuple-element.85), channel_id=1, source_target_pairs={{0,4},{1,5},{2,6},{3,7},{4,0},{5,1},{6,2},{7,3},{8,12},{9,13},{10,... | collective-permute-start | bytes 196616 | tf_op jit(solution)/shard_map/ppermute | solution.py:16
  181.5 6.1 %collective-permute-start.34 = (bf16[128,256]{1,0:T(8,128)(2,1)S(1)}, bf16[128,256]{1,0:T(8,128)(2,1)S(1)}, u32[]{:S(2)}, u32[]{:S(2)}) collective-permute-start(bf16[128,256]{1,0:T(8,128)(2,1)S(1)} %get-tuple-element.86), channel_id=1, source_target_pairs={{0,6},{1,7},{2,4},{3,5},{4,2},{5,3},{6,0},{7,1},{8,14},{9,15},{10,... | collective-permute-start | bytes 196616 | tf_op jit(solution)/shard_map/ppermute | solution.py:16
  (39 other events, 353.8 us)

commit v6 on v5

--- a/solution.py
+++ b/solution.py
@@ -109,8 +109,8 @@
     for count in counts:
         groups.append(refs[:count])
         refs = refs[count:]
-    mine, theirs, direct, swapped = groups
-    weights, out, sent, total, *kept = refs[:6]
+    mine, theirs = groups
+    weights, total, *kept = refs[:4]
     rings, ring_sems, kept_sems = refs[-3:]
     step, steps = pl.program_id(0), pl.num_programs(0)
     slots, block = rings.shape[1], rings.shape[2]
@@ -166,37 +166,26 @@
         fetch(1, step).wait()
         total[...] += product(mine, rings[0, slot]) + product(theirs, rings[1, slot])
 
-    done = out.shape[1]
-
-    @pl.when(upper)
-    def _():
-        keep(0, step).wait()
-        keep(1, step).wait()
-        total[:done, :] += product(direct, kept[0][rows(step), :]) + product(
-            swapped, kept[1][rows(step), :]
-        )
-
-    @pl.when(step == steps - 1)
-    def _():
-        cols = out.shape[2]
-        for j in range(out.shape[0]):
-            split(info, total[:done, 2 * j * cols : 2 * (j + 1) * cols], out, sent, j)
-
-
-def decode_first(info, mine, theirs, direct, swapped, decoder, shards, after):
+    @pl.when((step == steps - 1) & upper)
+    def _():
+        for k in range(kept_sems.shape[1]):
+            keep(0, jnp.int32(k)).wait()
+            keep(1, jnp.int32(k)).wait()
+
+
+def decode_first(info, mine, theirs, decoder, after):
     _, _, features, width = decoder.shape
     block = min(512, features)
     steps = features // block
     rows = sum(part.shape[0] for part in mine)
-    done = sum(part.shape[0] for part in direct)
 
     def acts(part, flag):
         return pl.BlockSpec(
             (part.shape[0], block), lambda k, info: (0, k if flag is None else k * info[flag])
         )
 
-    groups = (mine, theirs, direct, swapped)
-    in_specs = [acts(p, flag) for parts, flag in zip(groups, (None, 0, 1, 1)) for p in parts]
+    groups = (mine, theirs)
+    in_specs = [acts(p, flag) for parts, flag in zip(groups, (None, 0)) for p in parts]
     return pl.pallas_call(
         functools.partial(first_wave_kernel, [len(parts) for parts in groups]),
         grid_spec=pltpu.PrefetchScalarGridSpec(
@@ -204,7 +193,6 @@
             grid=(steps,),
             in_specs=in_specs + [ANYWHERE] * (1 + len(after)),
             out_specs=[
-                *[pl.BlockSpec(h.shape, lambda k, info: (0, 0, 0)) for h in halves(shards, done, width)],
                 pl.BlockSpec((rows, width), lambda k, info: (0, 0)),
                 WHOLE,
                 WHOLE,
@@ -216,7 +204,6 @@
             ],
         ),
         out_shape=[
-            *halves(shards, done, width),
             pltpu.HBM((rows, width), jnp.float32),
             pltpu.VMEM((features, width), decoder.dtype),
             pltpu.VMEM((features, width), decoder.dtype),
@@ -372,7 +359,7 @@
         stream=True,
     )
     d0a, d0b, n0 = up(a0a), up(a0b), beside(a0)
-    rest = exchange(after(jnp.concatenate(far[1:], axis=0), far[0], three), "feat", 1)
+    rest = exchange(after(jnp.concatenate(far[1:], axis=0), far[0], a0a), "feat", 1)
     (a1,) = encode(
         [far[0], three],
         [(0, 0, size), (1, 0, size)],
@@ -396,11 +383,8 @@
     )
     d2, d3, n2 = up(a2a), up(a2b), beside(after(a2, d0b))
 
-    c0a, c0b = across(after(d0a, n2)), across(after(d0b, n2))
-    mine, sent, base, *kept = decode_first(
-        info, [a0, a1, a2], [n0, n1, n2], [d0a, d0b], [c0a, c0b], decoder, shards, []
-    )
-    slots = [[0, 1], [2, 3], list(range(4, shards - 2)), [shards - 2, shards - 1]]
+    base, *kept = decode_first(info, [a0, a1, a2], [n0, n1, n2], decoder, [])
+    slots = [list(range(4)), list(range(4, shards - 2)), [shards - 2, shards - 1]]
 
     def meet(mine, sent, *earlier):
         return add_pair(info, mine, exchange(sent, "feat", 1), size, list(earlier))
@@ -413,24 +397,22 @@
         row = slots[number][0] * size
         return decode_later(info, direct, swapped, order, base, kept, row, shards, list(earlier))
 
-    c1 = across(after(d1, sent))
-    mine1, sent1 = later(1, [d1], [c1], [(0, 0, 2 * size)], sent)
-    met0 = meet(mine, sent, sent1)
+    c0a, c0b, c1 = across(d0a), across(d0b), across(after(d1, base))
+    order = [(0, 0, size), (1, 0, size), (2, 0, 2 * size)]
+    mine0, sent0 = later(0, [d0a, d0b, d1], [c0a, c0b, c1], order)
+    met0 = meet(mine0, sent0)
     where0, parts0 = spread(0, met0)
-    met1 = meet(mine1, sent1, met0[0])
+    c2 = across(after(d2, met0[0]))
+    c3 = across(after(d3, met0[0]))
+    early = (others - 2) * size
+    mine1, sent1 = later(1, [d2], [c2], [(0, 0, early)], met0[0])
+    order = [(0, early, size), (1, 0, size)]
+    mine2, sent2 = later(2, [d2, d3], [c2, c3], order, sent1, *parts0)
+    met1 = meet(mine1, sent1, sent2)
     where1, parts1 = spread(1, met1)
-    c2 = across(after(d2, met1[0]))
-    early = (others - 2) * size
-    mine2, sent2 = later(2, [d2], [c2], [(0, 0, early)], met1[0], *parts0)
-    c3 = across(after(d3, sent2))
-    order = [(0, early, size), (1, 0, size)]
-    mine3, sent3 = later(3, [d2, d3], [c2, c3], order, sent2, *parts1)
-    met2 = meet(mine2, sent2, sent3)
+    met2 = meet(mine2, sent2, *parts1)
     where2, parts2 = spread(2, met2)
-    total = add_up(info, targets[0], -1.0, where0 + where1, parts0 + parts1, [met2[0]])
-    met3 = meet(mine3, sent3, total)
-    where3, parts3 = spread(3, met3)
-    return add_up(info, total, 1.0, where2 + where3, parts2 + parts3, [])[None]
+    return add_up(info, targets[0], -1.0, where0 + where1 + where2, parts0 + parts1 + parts2, [])[None]
 
 
 def grouped(layer_inputs, targets, encoder, encoder_bias, decoder):

time: 190 us -> 209 us (1.10)
  waiting for transfers between devices: 41.5 us -> 54.2 us
  starting transfers between devices: 59.6 us -> 63.5 us
  Pallas kernels: 73.6 us -> 76.3 us
    ppermute x5, waiting for transfers between devices: 0.01 us -> 15 us  [up(): return lax.ppermute(a, 'layer', [(i, i + half) for i in range(half)])]
    pallas_call x3, Pallas kernels: 27.8 us -> 33.5 us  [decode_later(): pl.pallas_call(functools.partial(later_wave_kernel, order, row, len(direc...]
    ppermute x22 -> x18, starting transfers between devices: 28.6 us -> 33.2 us  [exchange(): return lax.ppermute(array, axis, [(i, i ^ flip) for i in range(size)])]
    ppermute x5, starting transfers between devices: 19.5 us -> 16.7 us  [across(): return lax.ppermute(a, 'layer', [(i, i ^ 1) for i in range(half, layers)])]
    ppermute x3, starting transfers between devices: 5.06 us -> 7.21 us  [beside(): return lax.ppermute(a, 'layer', [(i, i + 1) for i in range(0, layers, 2)])]
    ppermute x22 -> x18, waiting for transfers between devices: 39.6 us -> 37.7 us  [exchange(): return lax.ppermute(array, axis, [(i, i ^ flip) for i in range(size)])]
    unnamed x72 -> x58, local copies, waits for them, and re-layouts: 13.1 us -> 13.3 us
  transfers between devices with their start and end apart: 35 -> 31, of which waited for: 13 -> 12; matrix products, arithmetic and copies ran while one was open for 0% -> 0% of each run, Pallas kernels for 38% -> 36%
where the time goes in v6:
time: 209 us; the launch traced here: 208 us
  Pallas kernels  76.3 us (37%)
  starting transfers between devices  63.5 us (30%)
  waiting for transfers between devices  54.2 us (26%)
  local copies, waits for them, and re-layouts  13.9 us (7%)
    ppermute x18, waiting for transfers between devices, exchange(): return lax.ppermute(array, axis, [(i, i ^ flip) for i in range(size)])  37.7 us
    pallas_call x3, Pallas kernels, decode_later(): pl.pallas_call(functools.partial(later_wave_kernel, order, row, len(direc...  33.5 us
    ppermute x18, starting transfers between devices, exchange(): return lax.ppermute(array, axis, [(i, i ^ flip) for i in range(size)])  33.2 us
    pallas_call x1, Pallas kernels, decode_first(): pl.pallas_call(functools.partial(first_wave_kernel, [len(parts) for parts...  22 us
    pallas_call x3, Pallas kernels, encode(): pl.pallas_call(functools.partial(encode_kernel, order, pieces, len(parts)...  17.4 us
    ppermute x5, starting transfers between devices, across(): return lax.ppermute(a, 'layer', [(i, i ^ 1) for i in range(half, layers)])  16.7 us
    ppermute x5, waiting for transfers between devices, up(): return lax.ppermute(a, 'layer', [(i, i + half) for i in range(half)])  15 us
    unnamed x58, local copies, waits for them, and re-layouts  13.3 us
  transfers between devices with their start and end apart: 31, of which 12 were waited for; matrix products, arithmetic and copies ran while one was open for 0% of the time, Pallas kernels for 36%

profile of v6, /device:TPU:2, one launch (start us, length us, event | category | flops | bytes accessed | tf_op | source)
XLA Modules:
  0.0 208.4 jit_solution(15945283254559608729)
XLA Ops:
  1.5 2.6 %collective-permute-start.8 = (bf16[64,2048]{1,0:T(8,128)(2,1)}, bf16[64,2048]{1,0:T(8,128)(2,1)S(1)}, u32[]{:S(2)}, u32[]{:S(2)}) collective-permute-start(bf16[64,2048]{1,0:T(8,128)(2,1)} %bitcast.11), channel_id=1, source_target_pairs={{0,4},{1,5},{2,6},{3,7},{4,0},{5,1},{6,2},{7,3},{8,12},{9,13},{10,... | collective-permute-start | bytes 786440 | tf_op jit(solution)/shard_map/ppermute | solution.py:16
  5.7 2.6 %collective-permute-done.refs_1_ = bf16[64,2048]{1,0:T(8,128)(2,1)S(1)} collective-permute-done((bf16[64,2048]{1,0:T(8,128)(2,1)}, bf16[64,2048]{1,0:T(8,128)(2,1)S(1)}, u32[]{:S(2)}, u32[]{:S(2)}) %collective-permute-start) | collective-permute-done | bytes 262176 | tf_op jit(solution)/shard_map/ppermute | solution.py:16
  9.9 6.5 %encode.3 = (bf16[128,4096]{1,0:T(8,128)(2,1)S(1)}, bf16[64,4096]{1,0:T(8,128)(2,1)S(1)}, bf16[64,4096]{1,0:T(8,128)(2,1)S(1)}, bf16[1,2048,4096]{2,1,0:T(8,128)(2,1)S(1)}) custom-call(bf16[64,2048]{1,0:T(8,128)(2,1)S(1)} %bitcast.14, bf16[64,2048]{1,0:T(8,128)(2,1)S(1)} %collective-permute-done.refs_1_, bf16[1,2048,4096]{2,1,0:T(8,128)(2,1)} %refs_2_.1, ...), custom_call_target="tpu_custom_call" | custom-call | tf_op jit(solution)/shard_map/encode/pallas_call | solution.py:76
  16.5 6.4 %collective-permute-done.8.refs_0_ = bf16[64,2048]{1,0:T(8,128)(2,1)S(1)} collective-permute-done((bf16[64,2048]{1,0:T(8,128)(2,1)}, bf16[64,2048]{1,0:T(8,128)(2,1)S(1)}, u32[]{:S(2)}, u32[]{:S(2)}) %collective-permute-start.8) | collective-permute-done | bytes 262176 | tf_op jit(solution)/shard_map/ppermute | solution.py:16
  26.1 5.3 %collective-permute-start.4 = (bf16[64,2048]{1,0:T(8,128)(2,1)S(1)}, bf16[64,2048]{1,0:T(8,128)(2,1)S(1)}, u32[]{:S(2)}, u32[]{:S(2)}) collective-permute-start(bf16[64,2048]{1,0:T(8,128)(2,1)S(1)} %collective-permute-done.refs_1_), channel_id=1, source_target_pairs={{0,2},{1,3},{2,0},{3,1},{4,6},{5,7},{6,4},{7,5},{8,10},{9,11},{10,... | collective-permute-start | bytes 786440 | tf_op jit(solution)/shard_map/ppermute | solution.py:16
  31.4 6.2 %collective-permute-done.4.refs_1_ = bf16[64,2048]{1,0:T(8,128)(2,1)S(1)} collective-permute-done((bf16[64,2048]{1,0:T(8,128)(2,1)S(1)}, bf16[64,2048]{1,0:T(8,128)(2,1)S(1)}, u32[]{:S(2)}, u32[]{:S(2)}) %collective-permute-start.4) | collective-permute-done | bytes 262176 | tf_op jit(solution)/shard_map/ppermute | solution.py:16
  37.6 3.7 %encode.4.refs_5_.refs_1_ = bf16[128,4096]{1,0:T(8,128)(2,1)S(1)} custom-call(bf16[64,2048]{1,0:T(8,128)(2,1)S(1)} %collective-permute-done.3.refs_0_, bf16[64,2048]{1,0:T(8,128)(2,1)S(1)} %collective-permute-done.4.refs_1_, bf16[1,2048,4096]{2,1,0:T(8,128)(2,1)S(1)} %get-tuple-element.40.refs_2_.refs_3_, f32[1,4096]{1,0:T(1,128)S(1)} %copy-done.17, ...), custom_call_target="tpu_custom_call" | custom-call | tf_op jit(solution)/shard_map/encode/pallas_call | solution.py:76
  41.4 7.2 %encode.5 = (bf16[256,4096]{1,0:T(8,128)(2,1)}, bf16[192,4096]{1,0:T(8,128)(2,1)S(1)}, bf16[64,4096]{1,0:T(8,128)(2,1)S(1)}) custom-call(bf16[64,2048]{1,0:T(8,128)(2,1)S(1)} %collective-permute-done.8.refs_0_, bf16[64,2048]{1,0:T(8,128)(2,1)S(1)} %collective-permute-done.9.refs_1_, bf16[128,2048]{1,0:T(8,128)(2,1)S(1)} %collective-permute-done.10.refs_2_, ...), custom_call_target="tpu_custom_call" | custom-call | tf_op jit(solution)/shard_map/encode/pallas_call | solution.py:76
  49.7 2.7 %collective-permute-start.13 = (bf16[256,4096]{1,0:T(8,128)(2,1)}, bf16[256,4096]{1,0:T(8,128)(2,1)}, u32[]{:S(2)}, u32[]{:S(2)}) collective-permute-start(bf16[256,4096]{1,0:T(8,128)(2,1)} %get-tuple-element.44.refs_2_), channel_id=1, source_target_pairs={{0,8},{16,24},{1,9},{17,25},{2,10},{18,26},{3,11},{19,27},{4,12},{... | collective-permute-start | bytes 6291464 | tf_op jit(solution)/shard_map/ppermute | solution.py:341
  52.4 2.3 %collective-permute-start.11 = (bf16[128,4096]{1,0:T(8,128)(2,1)S(1)}, bf16[128,4096]{1,0:T(8,128)(2,1)}, u32[]{:S(2)}, u32[]{:S(2)}) collective-permute-start(bf16[128,4096]{1,0:T(8,128)(2,1)S(1)} %get-tuple-element.41.refs_4_.refs_0_), channel_id=1, source_target_pairs={{0,8},{16,24},{1,9},{17,25},{2,10},{18,26},{3,11},{19,27},{4,12},{... | collective-permute-start | bytes 3145736 | tf_op jit(solution)/shard_map/ppermute | solution.py:341
  54.6 2.3 %collective-permute-start.12 = (bf16[128,4096]{1,0:T(8,128)(2,1)S(1)}, bf16[128,4096]{1,0:T(8,128)(2,1)}, u32[]{:S(2)}, u32[]{:S(2)}) collective-permute-start(bf16[128,4096]{1,0:T(8,128)(2,1)S(1)} %encode.4.refs_5_.refs_1_), channel_id=1, source_target_pairs={{0,8},{16,24},{1,9},{17,25},{2,10},{18,26},{3,11},{19,27},{4,12},{... | collective-permute-start | bytes 3145736 | tf_op jit(solution)/shard_map/ppermute | solution.py:341
  58.9 22.0 %decode_first.1 = (f32[512,2048]{1,0:T(8,128)}, bf16[4096,2048]{1,0:T(8,128)(2,1)S(1)}, bf16[4096,2048]{1,0:T(8,128)(2,1)S(1)}) custom-call(s32[7]{0:T(128)} %stack.31.info, bf16[128,4096]{1,0:T(8,128)(2,1)} %copy-done.1, bf16[128,4096]{1,0:T(8,128)(2,1)} %copy-done, bf16[256,4096]{1,0:T(8,128)(2,1)} %get-tuple-element.44.refs_2_, ...), custom_call_target="tpu_custom_call" | custom-call | tf_op jit(solution)/shard_map/decode_first/pallas_call | solution.py:189
  80.9 8.3 %collective-permute-start.14 = (bf16[128,4096]{1,0:T(8,128)(2,1)}, bf16[128,4096]{1,0:T(8,128)(2,1)S(1)}, u32[]{:S(2)}, u32[]{:S(2)}) collective-permute-start(bf16[128,4096]{1,0:T(8,128)(2,1)} %collective-permute-done.5.refs_2_), channel_id=1, source_target_pairs={{16,24},{24,16},{17,25},{25,17},{18,26},{26,18},{19,27},{27,19},{2... | collective-permute-start | bytes 3145736 | tf_op jit(solution)/shard_map/ppermute | solution.py:338
  90.5 1.9 collective-permute-start.6
  92.5 2.4 %collective-permute-start.7 = (bf16[64,4096]{1,0:T(8,128)(2,1)S(1)}, bf16[64,4096]{1,0:T(8,128)(2,1)S(1)}, u32[]{:S(2)}, u32[]{:S(2)}) collective-permute-start(bf16[64,4096]{1,0:T(8,128)(2,1)S(1)} %copy-done.25), channel_id=1, source_target_pairs={{16,24},{24,16},{17,25},{25,17},{18,26},{26,18},{19,27},{27,19},{2... | collective-permute-start | bytes 1572872 | tf_op jit(solution)/shard_map/ppermute | solution.py:338
  97.5 14.7 %decode_later.3 = (f32[4,256,256]{2,1,0:T(8,128)}, bf16[4,256,256]{2,1,0:T(8,128)(2,1)}) custom-call(s32[7]{0:T(128)} %stack.31.info, bf16[64,4096]{1,0:T(8,128)(2,1)} %copy-done.4, bf16[64,4096]{1,0:T(8,128)(2,1)} %copy-done.24, bf16[128,4096]{1,0:T(8,128)(2,1)} %collective-permute-done.5.refs_2_, bf16[64,4096]{1,0:T(8,128)(2,1)} %copy-done.27, ...), custom_call_target="tpu_custom_call" | custom-call | tf_op jit(solution)/shard_map/decode_later/pallas_call | solution.py:244
  112.2 1.6 collective-permute-start.15
  113.8 12.9 %collective-permute-done.15.theirs = bf16[4,256,256]{2,1,0:T(8,128)(2,1)S(1)} collective-permute-done((bf16[4,256,256]{2,1,0:T(8,128)(2,1)}, bf16[4,256,256]{2,1,0:T(8,128)(2,1)S(1)}, u32[]{:S(2)}, u32[]{:S(2)}) %collective-permute-start.15) | collective-permute-done | bytes 524320 | tf_op jit(solution)/shard_map/ppermute | solution.py:16
  129.2 1.9 collective-permute-start.20
  132.5 15.0 %collective-permute-done.22.refs_1_ = bf16[64,4096]{1,0:T(8,128)(2,1)} collective-permute-done((bf16[64,4096]{1,0:T(8,128)(2,1)S(1)}, bf16[64,4096]{1,0:T(8,128)(2,1)}, u32[]{:S(2)}, u32[]{:S(2)}) %collective-permute-start.22) | collective-permute-done | bytes 524320 | tf_op jit(solution)/shard_map/ppermute | solution.py:335
  147.5 2.1 %collective-permute-start.23 = (bf16[64,4096]{1,0:T(8,128)(2,1)}, bf16[64,4096]{1,0:T(8,128)(2,1)S(1)}, u32[]{:S(2)}, u32[]{:S(2)}) collective-permute-start(bf16[64,4096]{1,0:T(8,128)(2,1)} %collective-permute-done.22.refs_1_), channel_id=1, source_target_pairs={{16,24},{24,16},{17,25},{25,17},{18,26},{26,18},{19,27},{27,19},{2... | collective-permute-start | bytes 1572872 | tf_op jit(solution)/shard_map/ppermute | solution.py:338
  149.6 5.7 %collective-permute-start.16 = (bf16[256,256]{1,0:T(8,128)(2,1)S(1)}, bf16[256,256]{1,0:T(8,128)(2,1)S(1)}, u32[]{:S(2)}, u32[]{:S(2)}) collective-permute-start(bf16[256,256]{1,0:T(8,128)(2,1)S(1)} %get-tuple-element.52), channel_id=1, source_target_pairs={{0,2},{1,3},{2,0},{3,1},{4,6},{5,7},{6,4},{7,5},{8,10},{9,11},{10,... | collective-permute-start | bytes 393224 | tf_op jit(solution)/shard_map/ppermute | solution.py:16
  155.3 1.9 collective-permute-start.17
  159.8 9.3 %decode_later.4 = (f32[4,128,256]{2,1,0:T(8,128)}, bf16[4,128,256]{2,1,0:T(8,128)(2,1)}) custom-call(s32[7]{0:T(128)} %stack.31.info, bf16[192,4096]{1,0:T(8,128)(2,1)} %collective-permute-done.19.refs_0_, bf16[192,4096]{1,0:T(8,128)(2,1)} %copy-done.22, f32[512,2048]{1,0:T(8,128)} %get-tuple-element.45.refs_6_.refs_2_.refs_4_, ...), custom_call_target="tpu_custom_call" | custom-call | tf_op jit(solution)/shard_map/decode_later/pallas_call | solution.py:244
  169.1 1.6 collective-permute-start.21
  172.2 9.6 %decode_later.5 = (f32[4,128,256]{2,1,0:T(8,128)}, bf16[4,128,256]{2,1,0:T(8,128)(2,1)}) custom-call(s32[7]{0:T(128)} %stack.31.info, bf16[192,4096]{1,0:T(8,128)(2,1)} %collective-permute-done.19.refs_0_, bf16[64,4096]{1,0:T(8,128)(2,1)} %collective-permute-done.22.refs_1_, bf16[192,4096]{1,0:T(8,128)(2,1)} %copy-done.22, bf16[64,4096]{1,0:T(8,128)(2,1)} %copy-done.26, ...), custom_call_target="tpu_custom_call" | custom-call | tf_op jit(solution)/shard_map/decode_later/pallas_call | solution.py:244
  185.2 1.9 collective-permute-start.25
  188.4 1.5 collective-permute-done.27.theirs
  190.0 3.2 %collective-permute-done.25.refs_2_.refs_6_ = bf16[128,256]{1,0:T(8,128)(2,1)S(1)} collective-permute-done((bf16[128,256]{1,0:T(8,128)(2,1)S(1)}, bf16[128,256]{1,0:T(8,128)(2,1)S(1)}, u32[]{:S(2)}, u32[]{:S(2)}) %collective-permute-start.25) | collective-permute-done | bytes 65568 | tf_op jit(solution)/shard_map/ppermute | solution.py:16
  196.2 1.7 collective-permute-start.29
  199.8 3.3 %collective-permute-done.29.refs_10_ = bf16[128,256]{1,0:T(8,128)(2,1)S(1)} collective-permute-done((bf16[128,256]{1,0:T(8,128)(2,1)S(1)}, bf16[128,256]{1,0:T(8,128)(2,1)S(1)}, u32[]{:S(2)}, u32[]{:S(2)}) %collective-permute-start.29) | collective-permute-done | bytes 65568 | tf_op jit(solution)/shard_map/ppermute | solution.py:16
  206.8 1.6 add_up.1
  (101 shorter events, 36.3 us)
Async XLA Ops:
  0.0 8.3 %collective-permute-start = (bf16[64,2048]{1,0:T(8,128)(2,1)}, bf16[64,2048]{1,0:T(8,128)(2,1)S(1)}, u32[]{:S(2)}, u32[]{:S(2)}) collective-permute-start(bf16[64,2048]{1,0:T(8,128)(2,1)} %bitcast.10), channel_id=1, source_target_pairs={{0,1},{1,0},{2,3},{3,2},{4,5},{5,4},{6,7},{7,6},{8,9},{9,8},{10,11... | collective-permute-start | bytes 786440 | tf_op jit(solution)/shard_map/ppermute | solution.py:16
  1.5 21.3 %collective-permute-start.8 = (bf16[64,2048]{1,0:T(8,128)(2,1)}, bf16[64,2048]{1,0:T(8,128)(2,1)S(1)}, u32[]{:S(2)}, u32[]{:S(2)}) collective-permute-start(bf16[64,2048]{1,0:T(8,128)(2,1)} %bitcast.11), channel_id=1, source_target_pairs={{0,4},{1,5},{2,6},{3,7},{4,0},{5,1},{6,2},{7,3},{8,12},{9,13},{10,... | collective-permute-start | bytes 786440 | tf_op jit(solution)/shard_map/ppermute | solution.py:16
  4.1 18.8 %collective-permute-start.9 = (bf16[64,2048]{1,0:T(8,128)(2,1)}, bf16[64,2048]{1,0:T(8,128)(2,1)S(1)}, u32[]{:S(2)}, u32[]{:S(2)}) collective-permute-start(bf16[64,2048]{1,0:T(8,128)(2,1)} %bitcast.12), channel_id=1, source_target_pairs={{0,6},{1,7},{2,4},{3,5},{4,2},{5,3},{6,0},{7,1},{8,14},{9,15},{10,... | collective-permute-start | bytes 786440 | tf_op jit(solution)/shard_map/ppermute | solution.py:16
  5.5 17.5 %collective-permute-start.3 = (bf16[64,2048]{1,0:T(8,128)(2,1)}, bf16[64,2048]{1,0:T(8,128)(2,1)S(1)}, u32[]{:S(2)}, u32[]{:S(2)}) collective-permute-start(bf16[64,2048]{1,0:T(8,128)(2,1)} %bitcast.13), channel_id=1, source_target_pairs={{0,2},{1,3},{2,0},{3,1},{4,6},{5,7},{6,4},{7,5},{8,10},{9,11},{10,... | collective-permute-start | bytes 786440 | tf_op jit(solution)/shard_map/ppermute | solution.py:16
  23.0 18.3 %collective-permute-start.10 = (bf16[128,2048]{1,0:T(8,128)(2,1)S(1)}, bf16[128,2048]{1,0:T(8,128)(2,1)S(1)}, u32[]{:S(2)}, u32[]{:S(2)}) collective-permute-start(bf16[128,2048]{1,0:T(8,128)(2,1)S(1)} %pad_maximum_fusion), channel_id=1, source_target_pairs={{0,1},{1,0},{2,3},{3,2},{4,5},{5,4},{6,7},{7,6},{8,9},{9,8},{10,11... | collective-permute-start | bytes 1572872 | tf_op jit(solution)/shard_map/ppermute | solution.py:16
  23.5 17.8 %collective-permute-start.1 = (bf16[64,4096]{1,0:T(8,128)(2,1)S(1)}, bf16[64,4096]{1,0:T(8,128)(2,1)S(1)}, u32[]{:S(2)}, u32[]{:S(2)}) collective-permute-start(bf16[64,4096]{1,0:T(8,128)(2,1)S(1)} %get-tuple-element.38), channel_id=1, source_target_pairs={{0,16},{8,24},{1,17},{9,25},{2,18},{10,26},{3,19},{11,27},{4,20},{... | collective-permute-start | bytes 1572872 | tf_op jit(solution)/shard_map/ppermute | solution.py:335
  24.8 24.9 %collective-permute-start.2 = (bf16[64,4096]{1,0:T(8,128)(2,1)S(1)}, bf16[64,4096]{1,0:T(8,128)(2,1)S(1)}, u32[]{:S(2)}, u32[]{:S(2)}) collective-permute-start(bf16[64,4096]{1,0:T(8,128)(2,1)S(1)} %get-tuple-element.39), channel_id=1, source_target_pairs={{0,16},{8,24},{1,17},{9,25},{2,18},{10,26},{3,19},{11,27},{4,20},{... | collective-permute-start | bytes 1572872 | tf_op jit(solution)/shard_map/ppermute | solution.py:335
  26.1 11.5 %collective-permute-start.4 = (bf16[64,2048]{1,0:T(8,128)(2,1)S(1)}, bf16[64,2048]{1,0:T(8,128)(2,1)S(1)}, u32[]{:S(2)}, u32[]{:S(2)}) collective-permute-start(bf16[64,2048]{1,0:T(8,128)(2,1)S(1)} %collective-permute-done.refs_1_), channel_id=1, source_target_pairs={{0,2},{1,3},{2,0},{3,1},{4,6},{5,7},{6,4},{7,5},{8,10},{9,11},{10,... | collective-permute-start | bytes 786440 | tf_op jit(solution)/shard_map/ppermute | solution.py:16
  41.3 49.2 %copy-start.4 = (bf16[64,4096]{1,0:T(8,128)(2,1)}, bf16[64,4096]{1,0:T(8,128)(2,1)S(1)}, u32[]{:S(2)}) copy-start(bf16[64,4096]{1,0:T(8,128)(2,1)S(1)} %collective-permute-done.1.refs_6_.refs_0_) | copy-start | bytes 1572868
  49.7 9.2 %collective-permute-start.13 = (bf16[256,4096]{1,0:T(8,128)(2,1)}, bf16[256,4096]{1,0:T(8,128)(2,1)}, u32[]{:S(2)}, u32[]{:S(2)}) collective-permute-start(bf16[256,4096]{1,0:T(8,128)(2,1)} %get-tuple-element.44.refs_2_), channel_id=1, source_target_pairs={{0,8},{16,24},{1,9},{17,25},{2,10},{18,26},{3,11},{19,27},{4,12},{... | collective-permute-start | bytes 6291464 | tf_op jit(solution)/shard_map/ppermute | solution.py:341
  52.4 6.5 %collective-permute-start.11 = (bf16[128,4096]{1,0:T(8,128)(2,1)S(1)}, bf16[128,4096]{1,0:T(8,128)(2,1)}, u32[]{:S(2)}, u32[]{:S(2)}) collective-permute-start(bf16[128,4096]{1,0:T(8,128)(2,1)S(1)} %get-tuple-element.41.refs_4_.refs_0_), channel_id=1, source_target_pairs={{0,8},{16,24},{1,9},{17,25},{2,10},{18,26},{3,11},{19,27},{4,12},{... | collective-permute-start | bytes 3145736 | tf_op jit(solution)/shard_map/ppermute | solution.py:341
  54.6 4.2 %collective-permute-start.12 = (bf16[128,4096]{1,0:T(8,128)(2,1)S(1)}, bf16[128,4096]{1,0:T(8,128)(2,1)}, u32[]{:S(2)}, u32[]{:S(2)}) collective-permute-start(bf16[128,4096]{1,0:T(8,128)(2,1)S(1)} %encode.4.refs_5_.refs_1_), channel_id=1, source_target_pairs={{0,8},{16,24},{1,9},{17,25},{2,10},{18,26},{3,11},{19,27},{4,12},{... | collective-permute-start | bytes 3145736 | tf_op jit(solution)/shard_map/ppermute | solution.py:341
  56.9 23.9 %collective-permute-start.5 = (bf16[128,4096]{1,0:T(8,128)(2,1)S(1)}, bf16[128,4096]{1,0:T(8,128)(2,1)}, u32[]{:S(2)}, u32[]{:S(2)}) collective-permute-start(bf16[128,4096]{1,0:T(8,128)(2,1)S(1)} %encode.4.refs_5_.refs_1_), channel_id=1, source_target_pairs={{0,16},{8,24},{1,17},{9,25},{2,18},{10,26},{3,19},{11,27},{4,20},{... | collective-permute-start | bytes 3145736 | tf_op jit(solution)/shard_map/ppermute | solution.py:335
  80.9 15.5 %collective-permute-start.14 = (bf16[128,4096]{1,0:T(8,128)(2,1)}, bf16[128,4096]{1,0:T(8,128)(2,1)S(1)}, u32[]{:S(2)}, u32[]{:S(2)}) collective-permute-start(bf16[128,4096]{1,0:T(8,128)(2,1)} %collective-permute-done.5.refs_2_), channel_id=1, source_target_pairs={{16,24},{24,16},{17,25},{25,17},{18,26},{26,18},{19,27},{27,19},{2... | collective-permute-start | bytes 3145736 | tf_op jit(solution)/shard_map/ppermute | solution.py:338
  89.2 40.0 %collective-permute-start.19 = (bf16[192,4096]{1,0:T(8,128)(2,1)S(1)}, bf16[192,4096]{1,0:T(8,128)(2,1)}, u32[]{:S(2)}, u32[]{:S(2)}) collective-permute-start(bf16[192,4096]{1,0:T(8,128)(2,1)S(1)} %copy-done.21), channel_id=1, source_target_pairs={{0,16},{8,24},{1,17},{9,25},{2,18},{10,26},{3,19},{11,27},{4,20},{... | collective-permute-start | bytes 4718600 | tf_op jit(solution)/shard_map/ppermute | solution.py:335
  90.5 4.4 %collective-permute-start.6 = (bf16[64,4096]{1,0:T(8,128)(2,1)S(1)}, bf16[64,4096]{1,0:T(8,128)(2,1)S(1)}, u32[]{:S(2)}, u32[]{:S(2)}) collective-permute-start(bf16[64,4096]{1,0:T(8,128)(2,1)S(1)} %collective-permute-done.1.refs_6_.refs_0_), channel_id=1, source_target_pairs={{16,24},{24,16},{17,25},{25,17},{18,26},{26,18},{19,27},{27,19},{2... | collective-permute-start | bytes 1572872 | tf_op jit(solution)/shard_map/ppermute | solution.py:338
  92.5 3.9 %collective-permute-start.7 = (bf16[64,4096]{1,0:T(8,128)(2,1)S(1)}, bf16[64,4096]{1,0:T(8,128)(2,1)S(1)}, u32[]{:S(2)}, u32[]{:S(2)}) collective-permute-start(bf16[64,4096]{1,0:T(8,128)(2,1)S(1)} %copy-done.25), channel_id=1, source_target_pairs={{16,24},{24,16},{17,25},{25,17},{18,26},{26,18},{19,27},{27,19},{2... | collective-permute-start | bytes 1572872 | tf_op jit(solution)/shard_map/ppermute | solution.py:338
  112.2 14.5 %collective-permute-start.15 = (bf16[4,256,256]{2,1,0:T(8,128)(2,1)}, bf16[4,256,256]{2,1,0:T(8,128)(2,1)S(1)}, u32[]{:S(2)}, u32[]{:S(2)}) collective-permute-start(bf16[4,256,256]{2,1,0:T(8,128)(2,1)} %get-tuple-element.50), channel_id=1, source_target_pairs={{0,1},{1,0},{2,3},{3,2},{4,5},{5,4},{6,7},{7,6},{8,9},{9,8},{10,11... | collective-permute-start | bytes 1572872 | tf_op jit(solution)/shard_map/ppermute | solution.py:16
  129.2 29.4 %collective-permute-start.20 = (bf16[192,4096]{1,0:T(8,128)(2,1)}, bf16[192,4096]{1,0:T(8,128)(2,1)S(1)}, u32[]{:S(2)}, u32[]{:S(2)}) collective-permute-start(bf16[192,4096]{1,0:T(8,128)(2,1)} %collective-permute-done.19.refs_0_), channel_id=1, source_target_pairs={{16,24},{24,16},{17,25},{25,17},{18,26},{26,18},{19,27},{27,19},{2... | collective-permute-start | bytes 4718600 | tf_op jit(solution)/shard_map/ppermute | solution.py:338
  131.2 16.3 %collective-permute-start.22 = (bf16[64,4096]{1,0:T(8,128)(2,1)S(1)}, bf16[64,4096]{1,0:T(8,128)(2,1)}, u32[]{:S(2)}, u32[]{:S(2)}) collective-permute-start(bf16[64,4096]{1,0:T(8,128)(2,1)S(1)} %get-tuple-element.59), channel_id=1, source_target_pairs={{0,16},{8,24},{1,17},{9,25},{2,18},{10,26},{3,19},{11,27},{4,20},{... | collective-permute-start | bytes 1572872 | tf_op jit(solution)/shard_map/ppermute | solution.py:335
  147.5 23.2 %collective-permute-start.23 = (bf16[64,4096]{1,0:T(8,128)(2,1)}, bf16[64,4096]{1,0:T(8,128)(2,1)S(1)}, u32[]{:S(2)}, u32[]{:S(2)}) collective-permute-start(bf16[64,4096]{1,0:T(8,128)(2,1)} %collective-permute-done.22.refs_1_), channel_id=1, source_target_pairs={{16,24},{24,16},{17,25},{25,17},{18,26},{26,18},{19,27},{27,19},{2... | collective-permute-start | bytes 1572872 | tf_op jit(solution)/shard_map/ppermute | solution.py:338
  149.6 21.1 %collective-permute-start.16 = (bf16[256,256]{1,0:T(8,128)(2,1)S(1)}, bf16[256,256]{1,0:T(8,128)(2,1)S(1)}, u32[]{:S(2)}, u32[]{:S(2)}) collective-permute-start(bf16[256,256]{1,0:T(8,128)(2,1)S(1)} %get-tuple-element.52), channel_id=1, source_target_pairs={{0,2},{1,3},{2,0},{3,1},{4,6},{5,7},{6,4},{7,5},{8,10},{9,11},{10,... | collective-permute-start | bytes 393224 | tf_op jit(solution)/shard_map/ppermute | solution.py:16
  155.3 15.3 %collective-permute-start.17 = (bf16[256,256]{1,0:T(8,128)(2,1)S(1)}, bf16[256,256]{1,0:T(8,128)(2,1)S(1)}, u32[]{:S(2)}, u32[]{:S(2)}) collective-permute-start(bf16[256,256]{1,0:T(8,128)(2,1)S(1)} %get-tuple-element.53), channel_id=1, source_target_pairs={{0,4},{1,5},{2,6},{3,7},{4,0},{5,1},{6,2},{7,3},{8,12},{9,13},{10,... | collective-permute-start | bytes 393224 | tf_op jit(solution)/shard_map/ppermute | solution.py:16
  157.2 13.5 %collective-permute-start.18 = (bf16[256,256]{1,0:T(8,128)(2,1)S(1)}, bf16[256,256]{1,0:T(8,128)(2,1)S(1)}, u32[]{:S(2)}, u32[]{:S(2)}) collective-permute-start(bf16[256,256]{1,0:T(8,128)(2,1)S(1)} %get-tuple-element.54), channel_id=1, source_target_pairs={{0,6},{1,7},{2,4},{3,5},{4,2},{5,3},{6,0},{7,1},{8,14},{9,15},{10,... | collective-permute-start | bytes 393224 | tf_op jit(solution)/shard_map/ppermute | solution.py:16
  169.1 13.3 %collective-permute-start.21 = (bf16[4,128,256]{2,1,0:T(8,128)(2,1)}, bf16[4,128,256]{2,1,0:T(8,128)(2,1)S(1)}, u32[]{:S(2)}, u32[]{:S(2)}) collective-permute-start(bf16[4,128,256]{2,1,0:T(8,128)(2,1)} %get-tuple-element.58.refs_7_), channel_id=1, source_target_pairs={{0,1},{1,0},{2,3},{3,2},{4,5},{5,4},{6,7},{7,6},{8,9},{9,8},{10,11... | collective-permute-start | bytes 786440 | tf_op jit(solution)/shard_map/ppermute | solution.py:16
  181.8 8.1 %collective-permute-start.27 = (bf16[4,128,256]{2,1,0:T(8,128)(2,1)}, bf16[4,128,256]{2,1,0:T(8,128)(2,1)S(1)}, u32[]{:S(2)}, u32[]{:S(2)}) collective-permute-start(bf16[4,128,256]{2,1,0:T(8,128)(2,1)} %get-tuple-element.61.refs_0_), channel_id=1, source_target_pairs={{0,1},{1,0},{2,3},{3,2},{4,5},{5,4},{6,7},{7,6},{8,9},{9,8},{10,11... | collective-permute-start | bytes 786440 | tf_op jit(solution)/shard_map/ppermute | solution.py:16
  184.0 6.0 %collective-permute-start.24 = (bf16[128,256]{1,0:T(8,128)(2,1)S(1)}, bf16[128,256]{1,0:T(8,128)(2,1)S(1)}, u32[]{:S(2)}, u32[]{:S(2)}) collective-permute-start(bf16[128,256]{1,0:T(8,128)(2,1)S(1)} %get-tuple-element.63), channel_id=1, source_target_pairs={{0,2},{1,3},{2,0},{3,1},{4,6},{5,7},{6,4},{7,5},{8,10},{9,11},{10,... | collective-permute-start | bytes 196616 | tf_op jit(solution)/shard_map/ppermute | solution.py:16
  185.2 8.0 %collective-permute-start.25 = (bf16[128,256]{1,0:T(8,128)(2,1)S(1)}, bf16[128,256]{1,0:T(8,128)(2,1)S(1)}, u32[]{:S(2)}, u32[]{:S(2)}) collective-permute-start(bf16[128,256]{1,0:T(8,128)(2,1)S(1)} %get-tuple-element.64), channel_id=1, source_target_pairs={{0,4},{1,5},{2,6},{3,7},{4,0},{5,1},{6,2},{7,3},{8,12},{9,13},{10,... | collective-permute-start | bytes 196616 | tf_op jit(solution)/shard_map/ppermute | solution.py:16
  187.0 6.1 %collective-permute-start.26 = (bf16[128,256]{1,0:T(8,128)(2,1)S(1)}, bf16[128,256]{1,0:T(8,128)(2,1)S(1)}, u32[]{:S(2)}, u32[]{:S(2)}) collective-permute-start(bf16[128,256]{1,0:T(8,128)(2,1)S(1)} %get-tuple-element.65), channel_id=1, source_target_pairs={{0,6},{1,7},{2,4},{3,5},{4,2},{5,3},{6,0},{7,1},{8,14},{9,15},{10,... | collective-permute-start | bytes 196616 | tf_op jit(solution)/shard_map/ppermute | solution.py:16
  194.8 5.0 %collective-permute-start.28 = (bf16[128,256]{1,0:T(8,128)(2,1)S(1)}, bf16[128,256]{1,0:T(8,128)(2,1)S(1)}, u32[]{:S(2)}, u32[]{:S(2)}) collective-permute-start(bf16[128,256]{1,0:T(8,128)(2,1)S(1)} %get-tuple-element.68), channel_id=1, source_target_pairs={{0,2},{1,3},{2,0},{3,1},{4,6},{5,7},{6,4},{7,5},{8,10},{9,11},{10,... | collective-permute-start | bytes 196616 | tf_op jit(solution)/shard_map/ppermute | solution.py:16
  196.2 6.9 %collective-permute-start.29 = (bf16[128,256]{1,0:T(8,128)(2,1)S(1)}, bf16[128,256]{1,0:T(8,128)(2,1)S(1)}, u32[]{:S(2)}, u32[]{:S(2)}) collective-permute-start(bf16[128,256]{1,0:T(8,128)(2,1)S(1)} %get-tuple-element.69), channel_id=1, source_target_pairs={{0,4},{1,5},{2,6},{3,7},{4,0},{5,1},{6,2},{7,3},{8,12},{9,13},{10,... | collective-permute-start | bytes 196616 | tf_op jit(solution)/shard_map/ppermute | solution.py:16
  197.9 6.2 %collective-permute-start.30 = (bf16[128,256]{1,0:T(8,128)(2,1)S(1)}, bf16[128,256]{1,0:T(8,128)(2,1)S(1)}, u32[]{:S(2)}, u32[]{:S(2)}) collective-permute-start(bf16[128,256]{1,0:T(8,128)(2,1)S(1)} %get-tuple-element.70), channel_id=1, source_target_pairs={{0,6},{1,7},{2,4},{3,5},{4,2},{5,3},{6,0},{7,1},{8,14},{9,15},{10,... | collective-permute-start | bytes 196616 | tf_op jit(solution)/shard_map/ppermute | solution.py:16
  (28 other events, 266.9 us)

commit v7 on v5

--- a/solution.py
+++ b/solution.py
@@ -417,18 +417,18 @@
     mine1, sent1 = later(1, [d1], [c1], [(0, 0, 2 * size)], sent)
     met0 = meet(mine, sent, sent1)
     where0, parts0 = spread(0, met0)
-    met1 = meet(mine1, sent1, met0[0])
+    c2 = across(after(d2, met0[0]))
+    early = (others - 2) * size
+    mine2, sent2 = later(2, [d2], [c2], [(0, 0, early)], met0[0], *parts0)
+    met1 = meet(mine1, sent1, sent2)
     where1, parts1 = spread(1, met1)
-    c2 = across(after(d2, met1[0]))
-    early = (others - 2) * size
-    mine2, sent2 = later(2, [d2], [c2], [(0, 0, early)], met1[0], *parts0)
-    c3 = across(after(d3, sent2))
+    c3 = across(after(d3, met1[0]))
+    total = add_up(info, targets[0], -1.0, where0 + where1, parts0 + parts1, [met1[0]])
     order = [(0, early, size), (1, 0, size)]
-    mine3, sent3 = later(3, [d2, d3], [c2, c3], order, sent2, *parts1)
+    mine3, sent3 = later(3, [d2, d3], [c2, c3], order, sent2, total)
     met2 = meet(mine2, sent2, sent3)
     where2, parts2 = spread(2, met2)
-    total = add_up(info, targets[0], -1.0, where0 + where1, parts0 + parts1, [met2[0]])
-    met3 = meet(mine3, sent3, total)
+    met3 = meet(mine3, sent3, met2[0], parts2[1])
     where3, parts3 = spread(3, met3)
     return add_up(info, total, 1.0, where2 + where3, parts2 + parts3, [])[None]
 

time: 190 us -> 185 us (0.974)
  waiting for transfers between devices: 41.5 us -> 31.6 us
  starting transfers between devices: 59.6 us -> 66.6 us
    ppermute x22, waiting for transfers between devices: 39.6 us -> 29.4 us  [exchange(): return lax.ppermute(array, axis, [(i, i ^ flip) for i in range(size)])]
    ppermute x22, starting transfers between devices: 28.6 us -> 35.5 us  [exchange(): return lax.ppermute(array, axis, [(i, i ^ flip) for i in range(size)])]
    unnamed x72 -> x62, local copies, waits for them, and re-layouts: 13.1 us -> 11.3 us
  transfers between devices with their start and end apart: 35 -> 35, of which waited for: 13 -> 12; matrix products, arithmetic and copies ran while one was open for 0% -> 0% of each run, Pallas kernels for 38% -> 39%
where the time goes in v7:
time: 185 us; the launch traced here: 184 us
  Pallas kernels  73.6 us (40%)
  starting transfers between devices  66.6 us (36%)
  waiting for transfers between devices  31.6 us (17%)
  local copies, waits for them, and re-layouts  12 us (6%)
    ppermute x22, starting transfers between devices, exchange(): return lax.ppermute(array, axis, [(i, i ^ flip) for i in range(size)])  35.5 us
    ppermute x22, waiting for transfers between devices, exchange(): return lax.ppermute(array, axis, [(i, i ^ flip) for i in range(size)])  29.4 us
    pallas_call x3, Pallas kernels, decode_later(): pl.pallas_call(functools.partial(later_wave_kernel, order, row, len(direc...  27.9 us
    pallas_call x1, Pallas kernels, decode_first(): pl.pallas_call(functools.partial(first_wave_kernel, [len(parts) for parts...  24 us
    ppermute x5, starting transfers between devices, across(): return lax.ppermute(a, 'layer', [(i, i ^ 1) for i in range(half, layers)])  19.6 us
    pallas_call x3, Pallas kernels, encode(): pl.pallas_call(functools.partial(encode_kernel, order, pieces, len(parts)...  17.2 us
    unnamed x62, local copies, waits for them, and re-layouts  11.3 us
    ppermute x5, starting transfers between devices, up(): return lax.ppermute(a, 'layer', [(i, i + half) for i in range(half)])  6.44 us
  transfers between devices with their start and end apart: 35, of which 12 were waited for; matrix products, arithmetic and copies ran while one was open for 0% of the time, Pallas kernels for 39%

profile of v7, /device:TPU:2, one launch (start us, length us, event | category | flops | bytes accessed | tf_op | source)
XLA Modules:
  0.0 184.3 jit_solution(85527712330151289)
XLA Ops:
  1.5 2.6 %collective-permute-start.3 = (bf16[64,2048]{1,0:T(8,128)(2,1)}, bf16[64,2048]{1,0:T(8,128)(2,1)S(1)}, u32[]{:S(2)}, u32[]{:S(2)}) collective-permute-start(bf16[64,2048]{1,0:T(8,128)(2,1)} %bitcast.11), channel_id=1, source_target_pairs={{0,4},{1,5},{2,6},{3,7},{4,0},{5,1},{6,2},{7,3},{8,12},{9,13},{10,... | collective-permute-start | bytes 786440 | tf_op jit(solution)/shard_map/ppermute | solution.py:16
  5.7 2.6 %collective-permute-done.refs_1_ = bf16[64,2048]{1,0:T(8,128)(2,1)S(1)} collective-permute-done((bf16[64,2048]{1,0:T(8,128)(2,1)}, bf16[64,2048]{1,0:T(8,128)(2,1)S(1)}, u32[]{:S(2)}, u32[]{:S(2)}) %collective-permute-start) | collective-permute-done | bytes 262176 | tf_op jit(solution)/shard_map/ppermute | solution.py:16
  11.5 6.5 %encode.3 = (bf16[128,4096]{1,0:T(8,128)(2,1)S(1)}, bf16[64,4096]{1,0:T(8,128)(2,1)S(1)}, bf16[64,4096]{1,0:T(8,128)(2,1)S(1)}, bf16[1,2048,4096]{2,1,0:T(8,128)(2,1)S(1)}) custom-call(bf16[64,2048]{1,0:T(8,128)(2,1)S(1)} %bitcast.14, bf16[64,2048]{1,0:T(8,128)(2,1)S(1)} %collective-permute-done.refs_1_, bf16[1,2048,4096]{2,1,0:T(8,128)(2,1)} %refs_2_.1, ...), custom_call_target="tpu_custom_call" | custom-call | tf_op jit(solution)/shard_map/encode/pallas_call | solution.py:76
  19.3 3.5 %collective-permute-done.3.refs_0_ = bf16[64,2048]{1,0:T(8,128)(2,1)S(1)} collective-permute-done((bf16[64,2048]{1,0:T(8,128)(2,1)}, bf16[64,2048]{1,0:T(8,128)(2,1)S(1)}, u32[]{:S(2)}, u32[]{:S(2)}) %collective-permute-start.3) | collective-permute-done | bytes 262176 | tf_op jit(solution)/shard_map/ppermute | solution.py:16
  22.9 2.1 %collective-permute-done.1.refs_0_ = bf16[64,2048]{1,0:T(8,128)(2,1)S(1)} collective-permute-done((bf16[64,2048]{1,0:T(8,128)(2,1)}, bf16[64,2048]{1,0:T(8,128)(2,1)S(1)}, u32[]{:S(2)}, u32[]{:S(2)}) %collective-permute-start.1) | collective-permute-done | bytes 262176 | tf_op jit(solution)/shard_map/ppermute | solution.py:16
  25.0 3.6 %collective-permute-done.2.refs_1_ = bf16[64,2048]{1,0:T(8,128)(2,1)S(1)} collective-permute-done((bf16[64,2048]{1,0:T(8,128)(2,1)S(1)}, bf16[64,2048]{1,0:T(8,128)(2,1)S(1)}, u32[]{:S(2)}, u32[]{:S(2)}) %collective-permute-start.2) | collective-permute-done | bytes 262176 | tf_op jit(solution)/shard_map/ppermute | solution.py:16
  30.4 3.7 %encode.4.refs_5_.refs_1_ = bf16[128,4096]{1,0:T(8,128)(2,1)S(1)} custom-call(bf16[64,2048]{1,0:T(8,128)(2,1)S(1)} %collective-permute-done.1.refs_0_, bf16[64,2048]{1,0:T(8,128)(2,1)S(1)} %collective-permute-done.2.refs_1_, bf16[1,2048,4096]{2,1,0:T(8,128)(2,1)S(1)} %get-tuple-element.47.refs_2_.refs_3_, f32[1,4096]{1,0:T(1,128)S(1)} %copy-done.21, ...), custom_call_target="tpu_custom_call" | custom-call | tf_op jit(solution)/shard_map/encode/pallas_call | solution.py:76
  34.2 6.3 %collective-permute-done.5.refs_2_ = bf16[128,2048]{1,0:T(8,128)(2,1)S(1)} collective-permute-done((bf16[128,2048]{1,0:T(8,128)(2,1)S(1)}, bf16[128,2048]{1,0:T(8,128)(2,1)S(1)}, u32[]{:S(2)}, u32[]{:S(2)}) %collective-permute-start.5) | collective-permute-done | bytes 524320 | tf_op jit(solution)/shard_map/ppermute | solution.py:16
  40.5 7.0 %encode.5 = (bf16[256,4096]{1,0:T(8,128)(2,1)S(1)}, bf16[192,4096]{1,0:T(8,128)(2,1)}, bf16[64,4096]{1,0:T(8,128)(2,1)S(1)}) custom-call(bf16[64,2048]{1,0:T(8,128)(2,1)S(1)} %collective-permute-done.3.refs_0_, bf16[64,2048]{1,0:T(8,128)(2,1)S(1)} %collective-permute-done.4.refs_1_, bf16[128,2048]{1,0:T(8,128)(2,1)S(1)} %collective-permute-done.5.refs_2_, ...), custom_call_target="tpu_custom_call" | custom-call | tf_op jit(solution)/shard_map/encode/pallas_call | solution.py:76
  50.3 2.3 %collective-permute-start.8 = (bf16[128,4096]{1,0:T(8,128)(2,1)S(1)}, bf16[128,4096]{1,0:T(8,128)(2,1)}, u32[]{:S(2)}, u32[]{:S(2)}) collective-permute-start(bf16[128,4096]{1,0:T(8,128)(2,1)S(1)} %encode.4.refs_5_.refs_1_), channel_id=1, source_target_pairs={{0,8},{16,24},{1,9},{17,25},{2,10},{18,26},{3,11},{19,27},{4,12},{... | collective-permute-start | bytes 3145736 | tf_op jit(solution)/shard_map/ppermute | solution.py:354
  53.9 1.9 %collective-permute-start.12 = (bf16[64,4096]{1,0:T(8,128)(2,1)}, bf16[64,4096]{1,0:T(8,128)(2,1)}, u32[]{:S(2)}, u32[]{:S(2)}) collective-permute-start(bf16[64,4096]{1,0:T(8,128)(2,1)} %collective-permute-done.9.refs_7_), channel_id=1, source_target_pairs={{16,24},{24,16},{17,25},{25,17},{18,26},{26,18},{19,27},{27,19},{2... | collective-permute-start | bytes 1572872 | tf_op jit(solution)/shard_map/ppermute | solution.py:351
  55.8 2.4 %collective-permute-start.11 = (bf16[64,4096]{1,0:T(8,128)(2,1)S(1)}, bf16[64,4096]{1,0:T(8,128)(2,1)}, u32[]{:S(2)}, u32[]{:S(2)}) collective-permute-start(bf16[64,4096]{1,0:T(8,128)(2,1)S(1)} %collective-permute-done.6.refs_6_), channel_id=1, source_target_pairs={{16,24},{24,16},{17,25},{25,17},{18,26},{26,18},{19,27},{27,19},{2... | collective-permute-start | bytes 1572872 | tf_op jit(solution)/shard_map/ppermute | solution.py:351
  60.3 24.0 %decode_first.1 = (f32[4,128,256]{2,1,0:T(8,128)}, bf16[4,128,256]{2,1,0:T(8,128)(2,1)}, f32[512,2048]{1,0:T(8,128)}, bf16[4096,2048]{1,0:T(8,128)(2,1)S(1)}, bf16[4096,2048]{1,0:T(8,128)(2,1)S(1)}) custom-call(s32[7]{0:T(128)} %stack.31.info, bf16[128,4096]{1,0:T(8,128)(2,1)} %copy-done.3, bf16[128,4096]{1,0:T(8,128)(2,1)} %copy-done, ...), custom_call_target="tpu_custom_call" | custom-call | tf_op jit(solution)/shard_map/decode_first/pallas_call | solution.py:200
  84.3 11.1 %collective-permute-start.15 = (bf16[128,4096]{1,0:T(8,128)(2,1)}, bf16[128,4096]{1,0:T(8,128)(2,1)S(1)}, u32[]{:S(2)}, u32[]{:S(2)}) collective-permute-start(bf16[128,4096]{1,0:T(8,128)(2,1)} %collective-permute-done.14.refs_0_), channel_id=1, source_target_pairs={{16,24},{24,16},{17,25},{25,17},{18,26},{26,18},{19,27},{27,19},{2... | collective-permute-start | bytes 3145736 | tf_op jit(solution)/shard_map/ppermute | solution.py:351
  96.0 1.9 %collective-permute-done.15.refs_1_ = bf16[128,4096]{1,0:T(8,128)(2,1)S(1)} collective-permute-done((bf16[128,4096]{1,0:T(8,128)(2,1)}, bf16[128,4096]{1,0:T(8,128)(2,1)S(1)}, u32[]{:S(2)}, u32[]{:S(2)}) %collective-permute-start.15) | collective-permute-done | bytes 1048608 | tf_op jit(solution)/shard_map/ppermute | solution.py:351
  98.9 9.0 %decode_later.3 = (f32[4,128,256]{2,1,0:T(8,128)}, bf16[4,128,256]{2,1,0:T(8,128)(2,1)}) custom-call(s32[7]{0:T(128)} %stack.31.info, bf16[128,4096]{1,0:T(8,128)(2,1)} %collective-permute-done.14.refs_0_, bf16[128,4096]{1,0:T(8,128)(2,1)} %copy-done.28, f32[512,2048]{1,0:T(8,128)} %get-tuple-element.58.refs_2_.refs_4_, ...), custom_call_target="tpu_custom_call" | custom-call | tf_op jit(solution)/shard_map/decode_later/pallas_call | solution.py:257
  109.4 2.0 %collective-permute-start.21 = (bf16[192,4096]{1,0:T(8,128)(2,1)}, bf16[192,4096]{1,0:T(8,128)(2,1)S(1)}, u32[]{:S(2)}, u32[]{:S(2)}) collective-permute-start(bf16[192,4096]{1,0:T(8,128)(2,1)} %collective-permute-done.20.refs_0_), channel_id=1, source_target_pairs={{16,24},{24,16},{17,25},{25,17},{18,26},{26,18},{19,27},{27,19},{2... | collective-permute-start | bytes 4718600 | tf_op jit(solution)/shard_map/ppermute | solution.py:351
  113.3 2.6 %collective-permute-start.16 = (bf16[128,256]{1,0:T(8,128)(2,1)S(1)}, bf16[128,256]{1,0:T(8,128)(2,1)S(1)}, u32[]{:S(2)}, u32[]{:S(2)}) collective-permute-start(bf16[128,256]{1,0:T(8,128)(2,1)S(1)} %get-tuple-element.63), channel_id=1, source_target_pairs={{0,2},{1,3},{2,0},{3,1},{4,6},{5,7},{6,4},{7,5},{8,10},{9,11},{10,... | collective-permute-start | bytes 196616 | tf_op jit(solution)/shard_map/ppermute | solution.py:16
  115.9 2.5 %collective-permute-start.17 = (bf16[128,256]{1,0:T(8,128)(2,1)S(1)}, bf16[128,256]{1,0:T(8,128)(2,1)S(1)}, u32[]{:S(2)}, u32[]{:S(2)}) collective-permute-start(bf16[128,256]{1,0:T(8,128)(2,1)S(1)} %get-tuple-element.64), channel_id=1, source_target_pairs={{0,4},{1,5},{2,6},{3,7},{4,0},{5,1},{6,2},{7,3},{8,12},{9,13},{10,... | collective-permute-start | bytes 196616 | tf_op jit(solution)/shard_map/ppermute | solution.py:16
  118.4 4.0 %collective-permute-start.18 = (bf16[128,256]{1,0:T(8,128)(2,1)S(1)}, bf16[128,256]{1,0:T(8,128)(2,1)S(1)}, u32[]{:S(2)}, u32[]{:S(2)}) collective-permute-start(bf16[128,256]{1,0:T(8,128)(2,1)S(1)} %get-tuple-element.65), channel_id=1, source_target_pairs={{0,6},{1,7},{2,4},{3,5},{4,2},{5,3},{6,0},{7,1},{8,14},{9,15},{10,... | collective-permute-start | bytes 196616 | tf_op jit(solution)/shard_map/ppermute | solution.py:16
  122.4 2.5 %collective-permute-done.18.refs_9_.refs_3_ = bf16[128,256]{1,0:T(8,128)(2,1)S(1)} collective-permute-done((bf16[128,256]{1,0:T(8,128)(2,1)S(1)}, bf16[128,256]{1,0:T(8,128)(2,1)S(1)}, u32[]{:S(2)}, u32[]{:S(2)}) %collective-permute-start.18) | collective-permute-done | bytes 65568 | tf_op jit(solution)/shard_map/ppermute | solution.py:16
  126.8 9.3 %decode_later.4 = (f32[4,128,256]{2,1,0:T(8,128)}, bf16[4,128,256]{2,1,0:T(8,128)(2,1)}) custom-call(s32[7]{0:T(128)} %stack.31.info, bf16[192,4096]{1,0:T(8,128)(2,1)} %collective-permute-done.20.refs_0_, bf16[192,4096]{1,0:T(8,128)(2,1)} %copy-done.25, f32[512,2048]{1,0:T(8,128)} %get-tuple-element.58.refs_2_.refs_4_, ...), custom_call_target="tpu_custom_call" | custom-call | tf_op jit(solution)/shard_map/decode_later/pallas_call | solution.py:257
  136.7 2.1 %collective-permute-start.27 = (bf16[64,4096]{1,0:T(8,128)(2,1)S(1)}, bf16[64,4096]{1,0:T(8,128)(2,1)S(1)}, u32[]{:S(2)}, u32[]{:S(2)}) collective-permute-start(bf16[64,4096]{1,0:T(8,128)(2,1)S(1)} %collective-permute-done.26.refs_1_), channel_id=1, source_target_pairs={{16,24},{24,16},{17,25},{25,17},{18,26},{26,18},{19,27},{27,19},{2... | collective-permute-start | bytes 1572872 | tf_op jit(solution)/shard_map/ppermute | solution.py:351
  138.9 1.9 %collective-permute-start.22 = (bf16[128,256]{1,0:T(8,128)(2,1)S(1)}, bf16[128,256]{1,0:T(8,128)(2,1)S(1)}, u32[]{:S(2)}, u32[]{:S(2)}) collective-permute-start(bf16[128,256]{1,0:T(8,128)(2,1)S(1)} %get-tuple-element.71), channel_id=1, source_target_pairs={{0,2},{1,3},{2,0},{3,1},{4,6},{5,7},{6,4},{7,5},{8,10},{9,11},{10,... | collective-permute-start | bytes 196616 | tf_op jit(solution)/shard_map/ppermute | solution.py:16
  140.8 2.3 %collective-permute-start.23 = (bf16[128,256]{1,0:T(8,128)(2,1)S(1)}, bf16[128,256]{1,0:T(8,128)(2,1)S(1)}, u32[]{:S(2)}, u32[]{:S(2)}) collective-permute-start(bf16[128,256]{1,0:T(8,128)(2,1)S(1)} %get-tuple-element.72), channel_id=1, source_target_pairs={{0,4},{1,5},{2,6},{3,7},{4,0},{5,1},{6,2},{7,3},{8,12},{9,13},{10,... | collective-permute-start | bytes 196616 | tf_op jit(solution)/shard_map/ppermute | solution.py:16
  146.1 3.1 %collective-permute-done.24.refs_7_ = bf16[128,256]{1,0:T(8,128)(2,1)S(1)} collective-permute-done((bf16[128,256]{1,0:T(8,128)(2,1)S(1)}, bf16[128,256]{1,0:T(8,128)(2,1)S(1)}, u32[]{:S(2)}, u32[]{:S(2)}) %collective-permute-start.24) | collective-permute-done | bytes 65568 | tf_op jit(solution)/shard_map/ppermute | solution.py:16
  154.1 9.6 %decode_later.5 = (f32[4,128,256]{2,1,0:T(8,128)}, bf16[4,128,256]{2,1,0:T(8,128)(2,1)}) custom-call(s32[7]{0:T(128)} %stack.31.info, bf16[192,4096]{1,0:T(8,128)(2,1)} %collective-permute-done.20.refs_0_, bf16[64,4096]{1,0:T(8,128)(2,1)} %copy-done.29, bf16[192,4096]{1,0:T(8,128)(2,1)} %copy-done.25, bf16[64,4096]{1,0:T(8,128)(2,1)} %copy-done.30, ...), custom_call_target="tpu_custom_call" | custom-call | tf_op jit(solution)/shard_map/decode_later/pallas_call | solution.py:257
  163.7 1.6 collective-permute-start.31
  166.9 1.7 collective-permute-start.28
  168.5 1.7 collective-permute-start.29
  173.0 2.3 %collective-permute-start.32 = (bf16[128,256]{1,0:T(8,128)(2,1)S(1)}, bf16[128,256]{1,0:T(8,128)(2,1)S(1)}, u32[]{:S(2)}, u32[]{:S(2)}) collective-permute-start(bf16[128,256]{1,0:T(8,128)(2,1)S(1)} %get-tuple-element.84), channel_id=1, source_target_pairs={{0,2},{1,3},{2,0},{3,1},{4,6},{5,7},{6,4},{7,5},{8,10},{9,11},{10,... | collective-permute-start | bytes 196616 | tf_op jit(solution)/shard_map/ppermute | solution.py:16
  178.1 3.8 %collective-permute-done.33.refs_6_ = bf16[128,256]{1,0:T(8,128)(2,1)S(1)} collective-permute-done((bf16[128,256]{1,0:T(8,128)(2,1)S(1)}, bf16[128,256]{1,0:T(8,128)(2,1)S(1)}, u32[]{:S(2)}, u32[]{:S(2)}) %collective-permute-start.33) | collective-permute-done | bytes 65568 | tf_op jit(solution)/shard_map/ppermute | solution.py:16
  (115 shorter events, 40.2 us)
Async XLA Ops:
  0.0 8.3 %collective-permute-start = (bf16[64,2048]{1,0:T(8,128)(2,1)}, bf16[64,2048]{1,0:T(8,128)(2,1)S(1)}, u32[]{:S(2)}, u32[]{:S(2)}) collective-permute-start(bf16[64,2048]{1,0:T(8,128)(2,1)} %bitcast.10), channel_id=1, source_target_pairs={{0,1},{1,0},{2,3},{3,2},{4,5},{5,4},{6,7},{7,6},{8,9},{9,8},{10,11... | collective-permute-start | bytes 786440 | tf_op jit(solution)/shard_map/ppermute | solution.py:16
  1.5 21.3 %collective-permute-start.3 = (bf16[64,2048]{1,0:T(8,128)(2,1)}, bf16[64,2048]{1,0:T(8,128)(2,1)S(1)}, u32[]{:S(2)}, u32[]{:S(2)}) collective-permute-start(bf16[64,2048]{1,0:T(8,128)(2,1)} %bitcast.11), channel_id=1, source_target_pairs={{0,4},{1,5},{2,6},{3,7},{4,0},{5,1},{6,2},{7,3},{8,12},{9,13},{10,... | collective-permute-start | bytes 786440 | tf_op jit(solution)/shard_map/ppermute | solution.py:16
  4.1 18.8 %collective-permute-start.4 = (bf16[64,2048]{1,0:T(8,128)(2,1)}, bf16[64,2048]{1,0:T(8,128)(2,1)S(1)}, u32[]{:S(2)}, u32[]{:S(2)}) collective-permute-start(bf16[64,2048]{1,0:T(8,128)(2,1)} %bitcast.12), channel_id=1, source_target_pairs={{0,6},{1,7},{2,4},{3,5},{4,2},{5,3},{6,0},{7,1},{8,14},{9,15},{10,... | collective-permute-start | bytes 786440 | tf_op jit(solution)/shard_map/ppermute | solution.py:16
  5.5 19.6 %collective-permute-start.1 = (bf16[64,2048]{1,0:T(8,128)(2,1)}, bf16[64,2048]{1,0:T(8,128)(2,1)S(1)}, u32[]{:S(2)}, u32[]{:S(2)}) collective-permute-start(bf16[64,2048]{1,0:T(8,128)(2,1)} %bitcast.13), channel_id=1, source_target_pairs={{0,2},{1,3},{2,0},{3,1},{4,6},{5,7},{6,4},{7,5},{8,10},{9,11},{10,... | collective-permute-start | bytes 786440 | tf_op jit(solution)/shard_map/ppermute | solution.py:16
  8.3 20.4 %collective-permute-start.2 = (bf16[64,2048]{1,0:T(8,128)(2,1)S(1)}, bf16[64,2048]{1,0:T(8,128)(2,1)S(1)}, u32[]{:S(2)}, u32[]{:S(2)}) collective-permute-start(bf16[64,2048]{1,0:T(8,128)(2,1)S(1)} %collective-permute-done.refs_1_), channel_id=1, source_target_pairs={{0,2},{1,3},{2,0},{3,1},{4,6},{5,7},{6,4},{7,5},{8,10},{9,11},{10,... | collective-permute-start | bytes 786440 | tf_op jit(solution)/shard_map/ppermute | solution.py:16
  18.0 16.1 %collective-permute-start.6 = (bf16[64,4096]{1,0:T(8,128)(2,1)S(1)}, bf16[64,4096]{1,0:T(8,128)(2,1)S(1)}, u32[]{:S(2)}, u32[]{:S(2)}) collective-permute-start(bf16[64,4096]{1,0:T(8,128)(2,1)S(1)} %get-tuple-element.49), channel_id=1, source_target_pairs={{0,16},{8,24},{1,17},{9,25},{2,18},{10,26},{3,19},{11,27},{4,20},{... | collective-permute-start | bytes 1572872 | tf_op jit(solution)/shard_map/ppermute | solution.py:348
  28.6 11.9 %collective-permute-start.5 = (bf16[128,2048]{1,0:T(8,128)(2,1)S(1)}, bf16[128,2048]{1,0:T(8,128)(2,1)S(1)}, u32[]{:S(2)}, u32[]{:S(2)}) collective-permute-start(bf16[128,2048]{1,0:T(8,128)(2,1)S(1)} %pad_maximum_fusion), channel_id=1, source_target_pairs={{0,1},{1,0},{2,3},{3,2},{4,5},{5,4},{6,7},{7,6},{8,9},{9,8},{10,11... | collective-permute-start | bytes 1572872 | tf_op jit(solution)/shard_map/ppermute | solution.py:16
  29.1 18.4 %collective-permute-start.9 = (bf16[64,4096]{1,0:T(8,128)(2,1)S(1)}, bf16[64,4096]{1,0:T(8,128)(2,1)}, u32[]{:S(2)}, u32[]{:S(2)}) collective-permute-start(bf16[64,4096]{1,0:T(8,128)(2,1)S(1)} %get-tuple-element.51), channel_id=1, source_target_pairs={{0,16},{8,24},{1,17},{9,25},{2,18},{10,26},{3,19},{11,27},{4,20},{... | collective-permute-start | bytes 1572872 | tf_op jit(solution)/shard_map/ppermute | solution.py:348
  47.5 6.4 %collective-permute-start.10 = (bf16[256,4096]{1,0:T(8,128)(2,1)S(1)}, bf16[256,4096]{1,0:T(8,128)(2,1)S(1)}, u32[]{:S(2)}, u32[]{:S(2)}) collective-permute-start(bf16[256,4096]{1,0:T(8,128)(2,1)S(1)} %get-tuple-element.52.refs_2_), channel_id=1, source_target_pairs={{0,8},{16,24},{1,9},{17,25},{2,10},{18,26},{3,11},{19,27},{4,12},{... | collective-permute-start | bytes 6291464 | tf_op jit(solution)/shard_map/ppermute | solution.py:354
  48.9 9.3 %collective-permute-start.7 = (bf16[128,4096]{1,0:T(8,128)(2,1)S(1)}, bf16[128,4096]{1,0:T(8,128)(2,1)S(1)}, u32[]{:S(2)}, u32[]{:S(2)}) collective-permute-start(bf16[128,4096]{1,0:T(8,128)(2,1)S(1)} %get-tuple-element.46.refs_4_.refs_0_), channel_id=1, source_target_pairs={{0,8},{16,24},{1,9},{17,25},{2,10},{18,26},{3,11},{19,27},{4,12},{... | collective-permute-start | bytes 3145736 | tf_op jit(solution)/shard_map/ppermute | solution.py:354
  50.3 10.0 %collective-permute-start.8 = (bf16[128,4096]{1,0:T(8,128)(2,1)S(1)}, bf16[128,4096]{1,0:T(8,128)(2,1)}, u32[]{:S(2)}, u32[]{:S(2)}) collective-permute-start(bf16[128,4096]{1,0:T(8,128)(2,1)S(1)} %encode.4.refs_5_.refs_1_), channel_id=1, source_target_pairs={{0,8},{16,24},{1,9},{17,25},{2,10},{18,26},{3,11},{19,27},{4,12},{... | collective-permute-start | bytes 3145736 | tf_op jit(solution)/shard_map/ppermute | solution.py:354
  52.6 31.7 %collective-permute-start.14 = (bf16[128,4096]{1,0:T(8,128)(2,1)S(1)}, bf16[128,4096]{1,0:T(8,128)(2,1)}, u32[]{:S(2)}, u32[]{:S(2)}) collective-permute-start(bf16[128,4096]{1,0:T(8,128)(2,1)S(1)} %encode.4.refs_5_.refs_1_), channel_id=1, source_target_pairs={{0,16},{8,24},{1,17},{9,25},{2,18},{10,26},{3,19},{11,27},{4,20},{... | collective-permute-start | bytes 3145736 | tf_op jit(solution)/shard_map/ppermute | solution.py:348
  53.9 6.4 %collective-permute-start.12 = (bf16[64,4096]{1,0:T(8,128)(2,1)}, bf16[64,4096]{1,0:T(8,128)(2,1)}, u32[]{:S(2)}, u32[]{:S(2)}) collective-permute-start(bf16[64,4096]{1,0:T(8,128)(2,1)} %collective-permute-done.9.refs_7_), channel_id=1, source_target_pairs={{16,24},{24,16},{17,25},{25,17},{18,26},{26,18},{19,27},{27,19},{2... | collective-permute-start | bytes 1572872 | tf_op jit(solution)/shard_map/ppermute | solution.py:351
  58.3 51.2 %collective-permute-start.20 = (bf16[192,4096]{1,0:T(8,128)(2,1)}, bf16[192,4096]{1,0:T(8,128)(2,1)}, u32[]{:S(2)}, u32[]{:S(2)}) collective-permute-start(bf16[192,4096]{1,0:T(8,128)(2,1)} %get-tuple-element.67), channel_id=1, source_target_pairs={{0,16},{8,24},{1,17},{9,25},{2,18},{10,26},{3,19},{11,27},{4,20},{... | collective-permute-start | bytes 4718600 | tf_op jit(solution)/shard_map/ppermute | solution.py:348
  84.3 13.6 %collective-permute-start.15 = (bf16[128,4096]{1,0:T(8,128)(2,1)}, bf16[128,4096]{1,0:T(8,128)(2,1)S(1)}, u32[]{:S(2)}, u32[]{:S(2)}) collective-permute-start(bf16[128,4096]{1,0:T(8,128)(2,1)} %collective-permute-done.14.refs_0_), channel_id=1, source_target_pairs={{16,24},{24,16},{17,25},{25,17},{18,26},{26,18},{19,27},{27,19},{2... | collective-permute-start | bytes 3145736 | tf_op jit(solution)/shard_map/ppermute | solution.py:351
  95.4 12.5 %collective-permute-start.13 = (bf16[4,128,256]{2,1,0:T(8,128)(2,1)}, bf16[4,128,256]{2,1,0:T(8,128)(2,1)S(1)}, u32[]{:S(2)}, u32[]{:S(2)}) collective-permute-start(bf16[4,128,256]{2,1,0:T(8,128)(2,1)} %get-tuple-element.56.refs_5_), channel_id=1, source_target_pairs={{0,1},{1,0},{2,3},{3,2},{4,5},{5,4},{6,7},{7,6},{8,9},{9,8},{10,11... | collective-permute-start | bytes 786440 | tf_op jit(solution)/shard_map/ppermute | solution.py:16
  109.4 15.5 %collective-permute-start.21 = (bf16[192,4096]{1,0:T(8,128)(2,1)}, bf16[192,4096]{1,0:T(8,128)(2,1)S(1)}, u32[]{:S(2)}, u32[]{:S(2)}) collective-permute-start(bf16[192,4096]{1,0:T(8,128)(2,1)} %collective-permute-done.20.refs_0_), channel_id=1, source_target_pairs={{16,24},{24,16},{17,25},{25,17},{18,26},{26,18},{19,27},{27,19},{2... | collective-permute-start | bytes 4718600 | tf_op jit(solution)/shard_map/ppermute | solution.py:351
  111.4 25.3 %collective-permute-start.26 = (bf16[64,4096]{1,0:T(8,128)(2,1)S(1)}, bf16[64,4096]{1,0:T(8,128)(2,1)S(1)}, u32[]{:S(2)}, u32[]{:S(2)}) collective-permute-start(bf16[64,4096]{1,0:T(8,128)(2,1)S(1)} %get-tuple-element.75), channel_id=1, source_target_pairs={{0,16},{8,24},{1,17},{9,25},{2,18},{10,26},{3,19},{11,27},{4,20},{... | collective-permute-start | bytes 1572872 | tf_op jit(solution)/shard_map/ppermute | solution.py:348
  112.7 23.4 %collective-permute-start.19 = (bf16[4,128,256]{2,1,0:T(8,128)(2,1)}, bf16[4,128,256]{2,1,0:T(8,128)(2,1)S(1)}, u32[]{:S(2)}, u32[]{:S(2)}) collective-permute-start(bf16[4,128,256]{2,1,0:T(8,128)(2,1)} %get-tuple-element.61.refs_0_), channel_id=1, source_target_pairs={{0,1},{1,0},{2,3},{3,2},{4,5},{5,4},{6,7},{7,6},{8,9},{9,8},{10,11... | collective-permute-start | bytes 786440 | tf_op jit(solution)/shard_map/ppermute | solution.py:16
  115.9 6.5 %collective-permute-start.17 = (bf16[128,256]{1,0:T(8,128)(2,1)S(1)}, bf16[128,256]{1,0:T(8,128)(2,1)S(1)}, u32[]{:S(2)}, u32[]{:S(2)}) collective-permute-start(bf16[128,256]{1,0:T(8,128)(2,1)S(1)} %get-tuple-element.64), channel_id=1, source_target_pairs={{0,4},{1,5},{2,6},{3,7},{4,0},{5,1},{6,2},{7,3},{8,12},{9,13},{10,... | collective-permute-start | bytes 196616 | tf_op jit(solution)/shard_map/ppermute | solution.py:16
  118.4 6.5 %collective-permute-start.18 = (bf16[128,256]{1,0:T(8,128)(2,1)S(1)}, bf16[128,256]{1,0:T(8,128)(2,1)S(1)}, u32[]{:S(2)}, u32[]{:S(2)}) collective-permute-start(bf16[128,256]{1,0:T(8,128)(2,1)S(1)} %get-tuple-element.65), channel_id=1, source_target_pairs={{0,6},{1,7},{2,4},{3,5},{4,2},{5,3},{6,0},{7,1},{8,14},{9,15},{10,... | collective-permute-start | bytes 196616 | tf_op jit(solution)/shard_map/ppermute | solution.py:16
  136.7 16.5 %collective-permute-start.27 = (bf16[64,4096]{1,0:T(8,128)(2,1)S(1)}, bf16[64,4096]{1,0:T(8,128)(2,1)S(1)}, u32[]{:S(2)}, u32[]{:S(2)}) collective-permute-start(bf16[64,4096]{1,0:T(8,128)(2,1)S(1)} %collective-permute-done.26.refs_1_), channel_id=1, source_target_pairs={{16,24},{24,16},{17,25},{25,17},{18,26},{26,18},{19,27},{27,19},{2... | collective-permute-start | bytes 1572872 | tf_op jit(solution)/shard_map/ppermute | solution.py:351
  138.9 6.4 %collective-permute-start.22 = (bf16[128,256]{1,0:T(8,128)(2,1)S(1)}, bf16[128,256]{1,0:T(8,128)(2,1)S(1)}, u32[]{:S(2)}, u32[]{:S(2)}) collective-permute-start(bf16[128,256]{1,0:T(8,128)(2,1)S(1)} %get-tuple-element.71), channel_id=1, source_target_pairs={{0,2},{1,3},{2,0},{3,1},{4,6},{5,7},{6,4},{7,5},{8,10},{9,11},{10,... | collective-permute-start | bytes 196616 | tf_op jit(solution)/shard_map/ppermute | solution.py:16
  140.8 5.3 %collective-permute-start.23 = (bf16[128,256]{1,0:T(8,128)(2,1)S(1)}, bf16[128,256]{1,0:T(8,128)(2,1)S(1)}, u32[]{:S(2)}, u32[]{:S(2)}) collective-permute-start(bf16[128,256]{1,0:T(8,128)(2,1)S(1)} %get-tuple-element.72), channel_id=1, source_target_pairs={{0,4},{1,5},{2,6},{3,7},{4,0},{5,1},{6,2},{7,3},{8,12},{9,13},{10,... | collective-permute-start | bytes 196616 | tf_op jit(solution)/shard_map/ppermute | solution.py:16
  143.1 6.1 %collective-permute-start.24 = (bf16[128,256]{1,0:T(8,128)(2,1)S(1)}, bf16[128,256]{1,0:T(8,128)(2,1)S(1)}, u32[]{:S(2)}, u32[]{:S(2)}) collective-permute-start(bf16[128,256]{1,0:T(8,128)(2,1)S(1)} %get-tuple-element.73), channel_id=1, source_target_pairs={{0,6},{1,7},{2,4},{3,5},{4,2},{5,3},{6,0},{7,1},{8,14},{9,15},{10,... | collective-permute-start | bytes 196616 | tf_op jit(solution)/shard_map/ppermute | solution.py:16
  143.7 21.6 %collective-permute-start.25 = (bf16[4,128,256]{2,1,0:T(8,128)(2,1)}, bf16[4,128,256]{2,1,0:T(8,128)(2,1)S(1)}, u32[]{:S(2)}, u32[]{:S(2)}) collective-permute-start(bf16[4,128,256]{2,1,0:T(8,128)(2,1)} %get-tuple-element.69.refs_0_.refs_7_), channel_id=1, source_target_pairs={{0,1},{1,0},{2,3},{3,2},{4,5},{5,4},{6,7},{7,6},{8,9},{9,8},{10,11... | collective-permute-start | bytes 786440 | tf_op jit(solution)/shard_map/ppermute | solution.py:16
  163.7 7.7 %collective-permute-start.31 = (bf16[4,128,256]{2,1,0:T(8,128)(2,1)}, bf16[4,128,256]{2,1,0:T(8,128)(2,1)S(1)}, u32[]{:S(2)}, u32[]{:S(2)}) collective-permute-start(bf16[4,128,256]{2,1,0:T(8,128)(2,1)} %get-tuple-element.77.refs_0_), channel_id=1, source_target_pairs={{0,1},{1,0},{2,3},{3,2},{4,5},{5,4},{6,7},{7,6},{8,9},{9,8},{10,11... | collective-permute-start | bytes 786440 | tf_op jit(solution)/shard_map/ppermute | solution.py:16
  168.5 9.6 %collective-permute-start.29 = (bf16[128,256]{1,0:T(8,128)(2,1)S(1)}, bf16[128,256]{1,0:T(8,128)(2,1)S(1)}, u32[]{:S(2)}, u32[]{:S(2)}) collective-permute-start(bf16[128,256]{1,0:T(8,128)(2,1)S(1)} %get-tuple-element.80), channel_id=1, source_target_pairs={{0,4},{1,5},{2,6},{3,7},{4,0},{5,1},{6,2},{7,3},{8,12},{9,13},{10,... | collective-permute-start | bytes 196616 | tf_op jit(solution)/shard_map/ppermute | solution.py:16
  170.3 7.8 %collective-permute-start.30 = (bf16[128,256]{1,0:T(8,128)(2,1)S(1)}, bf16[128,256]{1,0:T(8,128)(2,1)S(1)}, u32[]{:S(2)}, u32[]{:S(2)}) collective-permute-start(bf16[128,256]{1,0:T(8,128)(2,1)S(1)} %get-tuple-element.81), channel_id=1, source_target_pairs={{0,6},{1,7},{2,4},{3,5},{4,2},{5,3},{6,0},{7,1},{8,14},{9,15},{10,... | collective-permute-start | bytes 196616 | tf_op jit(solution)/shard_map/ppermute | solution.py:16
  173.0 5.1 %collective-permute-start.32 = (bf16[128,256]{1,0:T(8,128)(2,1)S(1)}, bf16[128,256]{1,0:T(8,128)(2,1)S(1)}, u32[]{:S(2)}, u32[]{:S(2)}) collective-permute-start(bf16[128,256]{1,0:T(8,128)(2,1)S(1)} %get-tuple-element.84), channel_id=1, source_target_pairs={{0,2},{1,3},{2,0},{3,1},{4,6},{5,7},{6,4},{7,5},{8,10},{9,11},{10,... | collective-permute-start | bytes 196616 | tf_op jit(solution)/shard_map/ppermute | solution.py:16
  175.3 6.5 %collective-permute-start.33 = (bf16[128,256]{1,0:T(8,128)(2,1)S(1)}, bf16[128,256]{1,0:T(8,128)(2,1)S(1)}, u32[]{:S(2)}, u32[]{:S(2)}) collective-permute-start(bf16[128,256]{1,0:T(8,128)(2,1)S(1)} %get-tuple-element.85), channel_id=1, source_target_pairs={{0,4},{1,5},{2,6},{3,7},{4,0},{5,1},{6,2},{7,3},{8,12},{9,13},{10,... | collective-permute-start | bytes 196616 | tf_op jit(solution)/shard_map/ppermute | solution.py:16
  176.7 6.1 %collective-permute-start.34 = (bf16[128,256]{1,0:T(8,128)(2,1)S(1)}, bf16[128,256]{1,0:T(8,128)(2,1)S(1)}, u32[]{:S(2)}, u32[]{:S(2)}) collective-permute-start(bf16[128,256]{1,0:T(8,128)(2,1)S(1)} %get-tuple-element.86), channel_id=1, source_target_pairs={{0,6},{1,7},{2,4},{3,5},{4,2},{5,3},{6,0},{7,1},{8,14},{9,15},{10,... | collective-permute-start | bytes 196616 | tf_op jit(solution)/shard_map/ppermute | solution.py:16
  (34 other events, 306.3 us)

commit v8 on v7

--- a/solution.py
+++ b/solution.py
@@ -20,8 +20,12 @@
 WHOLE = pl.BlockSpec(memory_space=pltpu.VMEM)
 SLOTS = 3
 ENCODE_MIB = 16
-DECODE_MIB = 27
+DECODE_MIB = 26
 SUM_MIB = 12
+
+
+def landed(array):
+    return pltpu.with_memory_space_constraint(array, pltpu.VMEM)
 
 
 def fill(order, parts, rows_of):
@@ -110,8 +114,8 @@
         groups.append(refs[:count])
         refs = refs[count:]
     mine, theirs, direct, swapped = groups
-    weights, out, sent, total, *kept = refs[:6]
-    rings, ring_sems, kept_sems = refs[-3:]
+    weights, out, sent, base, *kept = refs[:6]
+    total, rings, ring_sems, kept_sems, base_sem = refs[-5:]
     step, steps = pl.program_id(0), pl.num_programs(0)
     slots, block = rings.shape[1], rings.shape[2]
     odd, upper = info[0] == 1, info[1] == 1
@@ -178,9 +182,13 @@
 
     @pl.when(step == steps - 1)
     def _():
+        rest = pl.ds(done, total.shape[0] - done)
+        copy = pltpu.make_async_copy(total.at[rest], base, base_sem)
+        copy.start()
         cols = out.shape[2]
         for j in range(out.shape[0]):
             split(info, total[:done, 2 * j * cols : 2 * (j + 1) * cols], out, sent, j)
+        copy.wait()
 
 
 def decode_first(info, mine, theirs, direct, swapped, decoder, shards, after):
@@ -205,19 +213,21 @@
             in_specs=in_specs + [ANYWHERE] * (1 + len(after)),
             out_specs=[
                 *[pl.BlockSpec(h.shape, lambda k, info: (0, 0, 0)) for h in halves(shards, done, width)],
-                pl.BlockSpec((rows, width), lambda k, info: (0, 0)),
+                ANYWHERE,
                 WHOLE,
                 WHOLE,
             ],
             scratch_shapes=[
+                pltpu.VMEM((rows, width), jnp.float32),
                 pltpu.VMEM((2, SLOTS, block, width), decoder.dtype),
                 pltpu.SemaphoreType.DMA((2, SLOTS)),
                 pltpu.SemaphoreType.DMA((2, steps)),
+                pltpu.SemaphoreType.DMA,
             ],
         ),
         out_shape=[
             *halves(shards, done, width),
-            pltpu.HBM((rows, width), jnp.float32),
+            pltpu.HBM((rows - done, width), jnp.float32),
             pltpu.VMEM((features, width), decoder.dtype),
             pltpu.VMEM((features, width), decoder.dtype),
         ],
@@ -253,7 +263,6 @@
 def decode_later(info, direct, swapped, order, base, kept, row, shards, after):
     rows = sum(size for _, _, size in order)
     features, width = kept[0].shape
-    kept = [pltpu.with_memory_space_constraint(weight, pltpu.VMEM) for weight in kept]
     return pl.pallas_call(
         functools.partial(later_wave_kernel, order, row, len(direct)),
         in_specs=[pl.BlockSpec(memory_space=pltpu.SMEM)]
@@ -270,27 +279,33 @@
         ],
         compiler_params=pltpu.CompilerParams(vmem_limit_bytes=DECODE_MIB * MIB),
         name="decode_later",
-    )(info, *direct, *swapped, base, *kept, *after)
-
-
-def pair_kernel(size, n_after, info, mine, theirs, *refs):
-    outs = refs[n_after:]
+    )(info, *map(landed, direct), *map(landed, swapped), base, *map(landed, kept), *after)
+
+
+def pair_kernel(size, n, n_after, info, *refs):
+    mine, theirs, outs = refs[:n], refs[n : 2 * n], refs[2 * n + n_after :]
     z = info[5]
-    rows = mine.shape[1]
     for q, out in enumerate(outs):
-        for at in range(0, rows, size):
-            partner = at // size ^ 1
-            total = mine[z ^ q, pl.ds(at, size), :] + theirs[
-                z ^ q, pl.ds(partner * size, size), :
-            ].astype(jnp.float32)
-            out[pl.ds(at, size), :] = total.astype(out.dtype)
+        row = 0
+        for kept, met in zip(mine, theirs):
+            rows = kept.shape[1]
+            for at in range(0, rows, size):
+                partner = at // size ^ 1
+                total = kept[z ^ q, pl.ds(at, size), :] + met[
+                    z ^ q, pl.ds(partner * size, size), :
+                ].astype(jnp.float32)
+                out[pl.ds(row + at, size), :] = total.astype(out.dtype)
+            row += rows
 
 
 def add_pair(info, mine, theirs, size, after):
-    count, rows, cols = mine.shape
+    count, _, cols = mine[0].shape
+    rows = sum(kept.shape[1] for kept in mine)
     return pl.pallas_call(
-        functools.partial(pair_kernel, size, len(after)),
-        in_specs=[pl.BlockSpec(memory_space=pltpu.SMEM), WHOLE, WHOLE] + [ANYWHERE] * len(after),
+        functools.partial(pair_kernel, size, len(mine), len(after)),
+        in_specs=[pl.BlockSpec(memory_space=pltpu.SMEM)]
+        + [WHOLE] * (2 * len(mine))
+        + [ANYWHERE] * len(after),
         out_specs=[WHOLE] * count,
         out_shape=[
             jax.ShapeDtypeStruct((rows, cols), jnp.float32 if q == 0 else jnp.bfloat16)
@@ -298,7 +313,7 @@
         ],
         compiler_params=pltpu.CompilerParams(vmem_limit_bytes=SUM_MIB * MIB),
         name="add_pair",
-    )(info, mine, theirs, *after)
+    )(info, *mine, *[landed(array) for array in theirs], *after)
 
 
 def sum_kernel(sign, pieces, info, base, *refs):
@@ -322,7 +337,7 @@
         out_shape=jax.ShapeDtypeStruct(base.shape, base.dtype),
         compiler_params=pltpu.CompilerParams(vmem_limit_bytes=SUM_MIB * MIB),
         name="add_up",
-    )(info, base, *received, *after)
+    )(info, base, *map(landed, received), *after)
 
 
 def pipelined(layer_inputs, targets, encoder, encoder_bias, decoder):
@@ -389,7 +404,7 @@
     a2, a2a, a2b = encode(
         far[1:] + [rest],
         order,
-        [(0, others * size), (0, (others - 1) * size), ((others - 1) * size, size)],
+        [(0, others * size), (0, (others - 2) * size), ((others - 2) * size, 2 * size)],
         encoder_kept,
         encoder_bias,
         [a1, d0a],
@@ -403,33 +418,30 @@
     slots = [[0, 1], [2, 3], list(range(4, shards - 2)), [shards - 2, shards - 1]]
 
     def meet(mine, sent, *earlier):
-        return add_pair(info, mine, exchange(sent, "feat", 1), size, list(earlier))
-
-    def spread(number, sums):
+        theirs = [exchange(array, "feat", 1) for array in sent]
+        return add_pair(info, mine, theirs, size, list(earlier))
+
+    def spread(blocks, sums):
         parts = [part if q == 0 else exchange(part, "feat", 2 * q) for q, part in enumerate(sums)]
-        return [(2 * q, slots[number]) for q in range(len(parts))], parts
-
-    def later(number, direct, swapped, order, *earlier):
-        row = slots[number][0] * size
-        return decode_later(info, direct, swapped, order, base, kept, row, shards, list(earlier))
-
-    c1 = across(after(d1, sent))
-    mine1, sent1 = later(1, [d1], [c1], [(0, 0, 2 * size)], sent)
-    met0 = meet(mine, sent, sent1)
-    where0, parts0 = spread(0, met0)
-    c2 = across(after(d2, met0[0]))
-    early = (others - 2) * size
-    mine2, sent2 = later(2, [d2], [c2], [(0, 0, early)], met0[0], *parts0)
-    met1 = meet(mine1, sent1, sent2)
-    where1, parts1 = spread(1, met1)
+        return [(2 * q, blocks) for q in range(len(parts))], parts
+
+    def later(number, direct, swapped, *earlier):
+        row = (slots[number][0] - slots[1][0]) * size
+        order = [(0, 0, len(slots[number]) * size)]
+        return decode_later(info, [direct], [swapped], order, base, kept, row, shards, list(earlier))
+
+    c1, c2 = across(after(d1, sent)), across(after(d2, sent))
+    mine1, sent1 = later(1, d1, c1, sent, d2)
+    met1 = meet([mine, mine1], [sent, sent1])
+    where1, parts1 = spread(slots[0] + slots[1], met1)
     c3 = across(after(d3, met1[0]))
-    total = add_up(info, targets[0], -1.0, where0 + where1, parts0 + parts1, [met1[0]])
-    order = [(0, early, size), (1, 0, size)]
-    mine3, sent3 = later(3, [d2, d3], [c2, c3], order, sent2, total)
-    met2 = meet(mine2, sent2, sent3)
-    where2, parts2 = spread(2, met2)
-    met3 = meet(mine3, sent3, met2[0], parts2[1])
-    where3, parts3 = spread(3, met3)
+    mine2, sent2 = later(2, d2, c2, met1[0])
+    total = add_up(info, targets[0], -1.0, where1, parts1, [sent2])
+    mine3, sent3 = later(3, d3, c3, sent2, total)
+    met2 = meet([mine2], [sent2], sent3)
+    where2, parts2 = spread(slots[2], met2)
+    met3 = meet([mine3], [sent3], parts2[1])
+    where3, parts3 = spread(slots[3], met3)
     return add_up(info, total, 1.0, where2 + where3, parts2 + parts3, [])[None]
 
 

time: 185 us -> 175 us (0.946)
  starting transfers between devices: 66.6 us -> 58.7 us
  Pallas kernels: 73.6 us -> 70.4 us
  waiting for transfers between devices: 31.6 us -> 33.8 us
    ppermute x22 -> x19, starting transfers between devices: 35.5 us -> 26.9 us  [exchange(): return lax.ppermute(array, axis, [(i, i ^ flip) for i in range(size)])]
    ppermute x5, waiting for transfers between devices: 0.28 us -> 4.8 us  [up(): return lax.ppermute(a, 'layer', [(i, i + half) for i in range(half)])]
    pallas_call x3, Pallas kernels: 27.9 us -> 25.1 us  [decode_later(): pl.pallas_call(functools.partial(later_wave_kernel, order, row, len(direc...]
    unnamed x62 -> x50, local copies, waits for them, and re-layouts: 11.3 us -> 9.78 us
    ppermute x22 -> x19, waiting for transfers between devices: 29.4 us -> 28.4 us  [exchange(): return lax.ppermute(array, axis, [(i, i ^ flip) for i in range(size)])]
  transfers between devices with their start and end apart: 35 -> 32, of which waited for: 12 -> 11; matrix products, arithmetic and copies ran while one was open for 0% -> 0% of each run, Pallas kernels for 39% -> 40%
where the time goes in v8:
time: 175 us; the launch traced here: 174 us
  Pallas kernels  70.4 us (40%)
  starting transfers between devices  58.7 us (34%)
  waiting for transfers between devices  33.8 us (19%)
  local copies, waits for them, and re-layouts  10.4 us (6%)
    ppermute x19, waiting for transfers between devices, exchange(): return lax.ppermute(array, axis, [(i, i ^ flip) for i in range(size)])  28.4 us
    ppermute x19, starting transfers between devices, exchange(): return lax.ppermute(array, axis, [(i, i ^ flip) for i in range(size)])  26.9 us
    pallas_call x3, Pallas kernels, decode_later(): pl.pallas_call(functools.partial(later_wave_kernel, order, row, len(direc...  25.1 us
    pallas_call x1, Pallas kernels, decode_first(): pl.pallas_call(functools.partial(first_wave_kernel, [len(parts) for parts...  24.3 us
    ppermute x5, starting transfers between devices, across(): return lax.ppermute(a, 'layer', [(i, i ^ 1) for i in range(half, layers)])  19.5 us
    pallas_call x3, Pallas kernels, encode(): pl.pallas_call(functools.partial(encode_kernel, order, pieces, len(parts)...  17.1 us
    unnamed x50, local copies, waits for them, and re-layouts  9.78 us
    ppermute x5, starting transfers between devices, up(): return lax.ppermute(a, 'layer', [(i, i + half) for i in range(half)])  6.43 us
  transfers between devices with their start and end apart: 32, of which 11 were waited for; matrix products, arithmetic and copies ran while one was open for 0% of the time, Pallas kernels for 40%

profile of v8, /device:TPU:2, one launch (start us, length us, event | category | flops | bytes accessed | tf_op | source)
XLA Modules:
  0.0 173.8 jit_solution(14743151694440180446)
XLA Ops:
  0.0 1.5 collective-permute-start
  1.5 2.6 %collective-permute-start.3 = (bf16[64,2048]{1,0:T(8,128)(2,1)}, bf16[64,2048]{1,0:T(8,128)(2,1)S(1)}, u32[]{:S(2)}, u32[]{:S(2)}) collective-permute-start(bf16[64,2048]{1,0:T(8,128)(2,1)} %bitcast.11), channel_id=1, source_target_pairs={{0,4},{1,5},{2,6},{3,7},{4,0},{5,1},{6,2},{7,3},{8,12},{9,13},{10,... | collective-permute-start | bytes 786440 | tf_op jit(solution)/shard_map/ppermute | solution.py:16
  5.7 2.6 %collective-permute-done.refs_1_ = bf16[64,2048]{1,0:T(8,128)(2,1)S(1)} collective-permute-done((bf16[64,2048]{1,0:T(8,128)(2,1)}, bf16[64,2048]{1,0:T(8,128)(2,1)S(1)}, u32[]{:S(2)}, u32[]{:S(2)}) %collective-permute-start) | collective-permute-done | bytes 262176 | tf_op jit(solution)/shard_map/ppermute | solution.py:16
  8.3 1.6 collective-permute-start.2
  11.5 6.5 %encode.3 = (bf16[128,4096]{1,0:T(8,128)(2,1)S(1)}, bf16[64,4096]{1,0:T(8,128)(2,1)S(1)}, bf16[64,4096]{1,0:T(8,128)(2,1)S(1)}, bf16[1,2048,4096]{2,1,0:T(8,128)(2,1)S(1)}) custom-call(bf16[64,2048]{1,0:T(8,128)(2,1)S(1)} %bitcast.14, bf16[64,2048]{1,0:T(8,128)(2,1)S(1)} %collective-permute-done.refs_1_, bf16[1,2048,4096]{2,1,0:T(8,128)(2,1)} %refs_2_.1, ...), custom_call_target="tpu_custom_call" | custom-call | tf_op jit(solution)/shard_map/encode/pallas_call | solution.py:80
  19.3 3.5 %collective-permute-done.3.refs_0_ = bf16[64,2048]{1,0:T(8,128)(2,1)S(1)} collective-permute-done((bf16[64,2048]{1,0:T(8,128)(2,1)}, bf16[64,2048]{1,0:T(8,128)(2,1)S(1)}, u32[]{:S(2)}, u32[]{:S(2)}) %collective-permute-start.3) | collective-permute-done | bytes 262176 | tf_op jit(solution)/shard_map/ppermute | solution.py:16
  22.9 2.1 %collective-permute-done.1.refs_0_ = bf16[64,2048]{1,0:T(8,128)(2,1)S(1)} collective-permute-done((bf16[64,2048]{1,0:T(8,128)(2,1)}, bf16[64,2048]{1,0:T(8,128)(2,1)S(1)}, u32[]{:S(2)}, u32[]{:S(2)}) %collective-permute-start.1) | collective-permute-done | bytes 262176 | tf_op jit(solution)/shard_map/ppermute | solution.py:16
  25.0 3.6 %collective-permute-done.2.refs_1_ = bf16[64,2048]{1,0:T(8,128)(2,1)S(1)} collective-permute-done((bf16[64,2048]{1,0:T(8,128)(2,1)S(1)}, bf16[64,2048]{1,0:T(8,128)(2,1)S(1)}, u32[]{:S(2)}, u32[]{:S(2)}) %collective-permute-start.2) | collective-permute-done | bytes 262176 | tf_op jit(solution)/shard_map/ppermute | solution.py:16
  30.4 3.7 %encode.4.refs_5_.refs_1_ = bf16[128,4096]{1,0:T(8,128)(2,1)S(1)} custom-call(bf16[64,2048]{1,0:T(8,128)(2,1)S(1)} %collective-permute-done.1.refs_0_, bf16[64,2048]{1,0:T(8,128)(2,1)S(1)} %collective-permute-done.2.refs_1_, bf16[1,2048,4096]{2,1,0:T(8,128)(2,1)S(1)} %get-tuple-element.43.refs_2_.refs_3_, f32[1,4096]{1,0:T(1,128)S(1)} %copy-done.18, ...), custom_call_target="tpu_custom_call" | custom-call | tf_op jit(solution)/shard_map/encode/pallas_call | solution.py:80
  34.2 6.3 %collective-permute-done.5.refs_2_ = bf16[128,2048]{1,0:T(8,128)(2,1)S(1)} collective-permute-done((bf16[128,2048]{1,0:T(8,128)(2,1)S(1)}, bf16[128,2048]{1,0:T(8,128)(2,1)S(1)}, u32[]{:S(2)}, u32[]{:S(2)}) %collective-permute-start.5) | collective-permute-done | bytes 524320 | tf_op jit(solution)/shard_map/ppermute | solution.py:16
  40.5 6.9 %encode.5 = (bf16[256,4096]{1,0:T(8,128)(2,1)S(1)}, bf16[128,4096]{1,0:T(8,128)(2,1)S(1)}, bf16[128,4096]{1,0:T(8,128)(2,1)}) custom-call(bf16[64,2048]{1,0:T(8,128)(2,1)S(1)} %collective-permute-done.3.refs_0_, bf16[64,2048]{1,0:T(8,128)(2,1)S(1)} %collective-permute-done.4.refs_1_, bf16[128,2048]{1,0:T(8,128)(2,1)S(1)} %collective-permute-done.5.refs_2_, ...), custom_call_target="tpu_custom_call" | custom-call | tf_op jit(solution)/shard_map/encode/pallas_call | solution.py:80
  49.8 2.3 %collective-permute-start.7 = (bf16[128,4096]{1,0:T(8,128)(2,1)S(1)}, bf16[128,4096]{1,0:T(8,128)(2,1)}, u32[]{:S(2)}, u32[]{:S(2)}) collective-permute-start(bf16[128,4096]{1,0:T(8,128)(2,1)S(1)} %get-tuple-element.42.refs_4_.refs_0_), channel_id=1, source_target_pairs={{0,8},{16,24},{1,9},{17,25},{2,10},{18,26},{3,11},{19,27},{4,12},{... | collective-permute-start | bytes 3145736 | tf_op jit(solution)/shard_map/ppermute | solution.py:369
  52.1 2.3 %collective-permute-start.8 = (bf16[128,4096]{1,0:T(8,128)(2,1)S(1)}, bf16[128,4096]{1,0:T(8,128)(2,1)}, u32[]{:S(2)}, u32[]{:S(2)}) collective-permute-start(bf16[128,4096]{1,0:T(8,128)(2,1)S(1)} %encode.4.refs_5_.refs_1_), channel_id=1, source_target_pairs={{0,8},{16,24},{1,9},{17,25},{2,10},{18,26},{3,11},{19,27},{4,12},{... | collective-permute-start | bytes 3145736 | tf_op jit(solution)/shard_map/ppermute | solution.py:369
  55.6 1.9 %collective-permute-start.12 = (bf16[64,4096]{1,0:T(8,128)(2,1)S(1)}, bf16[64,4096]{1,0:T(8,128)(2,1)}, u32[]{:S(2)}, u32[]{:S(2)}) collective-permute-start(bf16[64,4096]{1,0:T(8,128)(2,1)S(1)} %collective-permute-done.9.refs_7_), channel_id=1, source_target_pairs={{16,24},{24,16},{17,25},{25,17},{18,26},{26,18},{19,27},{27,19},{2... | collective-permute-start | bytes 1572872 | tf_op jit(solution)/shard_map/ppermute | solution.py:366
  57.6 2.4 %collective-permute-start.11 = (bf16[64,4096]{1,0:T(8,128)(2,1)S(1)}, bf16[64,4096]{1,0:T(8,128)(2,1)}, u32[]{:S(2)}, u32[]{:S(2)}) collective-permute-start(bf16[64,4096]{1,0:T(8,128)(2,1)S(1)} %collective-permute-done.6.refs_6_), channel_id=1, source_target_pairs={{16,24},{24,16},{17,25},{25,17},{18,26},{26,18},{19,27},{27,19},{2... | collective-permute-start | bytes 1572872 | tf_op jit(solution)/shard_map/ppermute | solution.py:366
  61.9 24.3 %decode_first.1 = (f32[4,128,256]{2,1,0:T(8,128)}, bf16[4,128,256]{2,1,0:T(8,128)(2,1)}, f32[384,2048]{1,0:T(8,128)}, bf16[4096,2048]{1,0:T(8,128)(2,1)S(1)}, bf16[4096,2048]{1,0:T(8,128)(2,1)S(1)}) custom-call(s32[7]{0:T(128)} %stack.31.info, bf16[128,4096]{1,0:T(8,128)(2,1)} %copy-done.3, bf16[128,4096]{1,0:T(8,128)(2,1)} %copy-done, ...), custom_call_target="tpu_custom_call" | custom-call | tf_op jit(solution)/shard_map/decode_first/pallas_call | solution.py:208
  86.2 11.1 %collective-permute-start.14 = (bf16[128,4096]{1,0:T(8,128)(2,1)}, bf16[128,4096]{1,0:T(8,128)(2,1)S(1)}, u32[]{:S(2)}, u32[]{:S(2)}) collective-permute-start(bf16[128,4096]{1,0:T(8,128)(2,1)} %collective-permute-done.13.refs_0_), channel_id=1, source_target_pairs={{16,24},{24,16},{17,25},{25,17},{18,26},{26,18},{19,27},{27,19},{2... | collective-permute-start | bytes 3145736 | tf_op jit(solution)/shard_map/ppermute | solution.py:366
  100.2 8.7 %decode_later.3 = (f32[4,128,256]{2,1,0:T(8,128)}, bf16[4,128,256]{2,1,0:T(8,128)(2,1)}) custom-call(s32[7]{0:T(128)} %stack.31.info, bf16[128,4096]{1,0:T(8,128)(2,1)} %collective-permute-done.13.refs_0_, bf16[128,4096]{1,0:T(8,128)(2,1)S(1)} %collective-permute-done.14.refs_1_, f32[384,2048]{1,0:T(8,128)} %get-tuple-element.54.refs_2_, ...), custom_call_target="tpu_custom_call" | custom-call | tf_op jit(solution)/shard_map/decode_later/pallas_call | solution.py:266
  108.9 1.6 collective-permute-start.17
  110.5 1.9 %collective-permute-start.21 = (bf16[128,4096]{1,0:T(8,128)(2,1)}, bf16[128,4096]{1,0:T(8,128)(2,1)S(1)}, u32[]{:S(2)}, u32[]{:S(2)}) collective-permute-start(bf16[128,4096]{1,0:T(8,128)(2,1)} %copy-done.4), channel_id=1, source_target_pairs={{16,24},{24,16},{17,25},{25,17},{18,26},{26,18},{19,27},{27,19},{2... | collective-permute-start | bytes 3145736 | tf_op jit(solution)/shard_map/ppermute | solution.py:366
  112.4 5.0 %collective-permute-done.17.refs_3_ = bf16[4,128,256]{2,1,0:T(8,128)(2,1)S(1)} collective-permute-done((bf16[4,128,256]{2,1,0:T(8,128)(2,1)}, bf16[4,128,256]{2,1,0:T(8,128)(2,1)S(1)}, u32[]{:S(2)}, u32[]{:S(2)}) %collective-permute-start.17) | collective-permute-done | bytes 262176 | tf_op jit(solution)/shard_map/ppermute | solution.py:16
  119.7 4.8 %collective-permute-done.23.refs_0_ = bf16[128,4096]{1,0:T(8,128)(2,1)S(1)} collective-permute-done((bf16[128,4096]{1,0:T(8,128)(2,1)}, bf16[128,4096]{1,0:T(8,128)(2,1)S(1)}, u32[]{:S(2)}, u32[]{:S(2)}) %collective-permute-start.23) | collective-permute-done | bytes 1048608 | tf_op jit(solution)/shard_map/ppermute | solution.py:363
  124.5 2.1 %collective-permute-start.24 = (bf16[128,4096]{1,0:T(8,128)(2,1)S(1)}, bf16[128,4096]{1,0:T(8,128)(2,1)S(1)}, u32[]{:S(2)}, u32[]{:S(2)}) collective-permute-start(bf16[128,4096]{1,0:T(8,128)(2,1)S(1)} %collective-permute-done.23.refs_0_), channel_id=1, source_target_pairs={{16,24},{24,16},{17,25},{25,17},{18,26},{26,18},{19,27},{27,19},{2... | collective-permute-start | bytes 3145736 | tf_op jit(solution)/shard_map/ppermute | solution.py:366
  126.6 1.6 collective-permute-start.18
  128.2 2.5 %collective-permute-start.19 = (bf16[256,256]{1,0:T(8,128)(2,1)S(1)}, bf16[256,256]{1,0:T(8,128)(2,1)S(1)}, u32[]{:S(2)}, u32[]{:S(2)}) collective-permute-start(bf16[256,256]{1,0:T(8,128)(2,1)S(1)} %get-tuple-element.62), channel_id=1, source_target_pairs={{0,4},{1,5},{2,6},{3,7},{4,0},{5,1},{6,2},{7,3},{8,12},{9,13},{10,... | collective-permute-start | bytes 393224 | tf_op jit(solution)/shard_map/ppermute | solution.py:16
  132.8 8.2 %decode_later.4 = (f32[4,128,256]{2,1,0:T(8,128)}, bf16[4,128,256]{2,1,0:T(8,128)(2,1)}) custom-call(s32[7]{0:T(128)} %stack.31.info, bf16[128,4096]{1,0:T(8,128)(2,1)S(1)} %copy-done.5, bf16[128,4096]{1,0:T(8,128)(2,1)S(1)} %collective-permute-done.21.refs_1_, f32[384,2048]{1,0:T(8,128)} %get-tuple-element.54.refs_2_, ...), custom_call_target="tpu_custom_call" | custom-call | tf_op jit(solution)/shard_map/decode_later/pallas_call | solution.py:266
  144.0 8.3 %decode_later.5 = (f32[4,128,256]{2,1,0:T(8,128)}, bf16[4,128,256]{2,1,0:T(8,128)(2,1)}) custom-call(s32[7]{0:T(128)} %stack.31.info, bf16[128,4096]{1,0:T(8,128)(2,1)S(1)} %collective-permute-done.23.refs_0_, bf16[128,4096]{1,0:T(8,128)(2,1)S(1)} %collective-permute-done.24.refs_1_, f32[384,2048]{1,0:T(8,128)} %get-tuple-element.54.refs_2_, ...), custom_call_target="tpu_custom_call" | custom-call | tf_op jit(solution)/shard_map/decode_later/pallas_call | solution.py:266
  152.3 1.6 collective-permute-start.28
  156.8 2.3 %collective-permute-start.26 = (bf16[128,256]{1,0:T(8,128)(2,1)S(1)}, bf16[128,256]{1,0:T(8,128)(2,1)S(1)}, u32[]{:S(2)}, u32[]{:S(2)}) collective-permute-start(bf16[128,256]{1,0:T(8,128)(2,1)S(1)} %get-tuple-element.72), channel_id=1, source_target_pairs={{0,4},{1,5},{2,6},{3,7},{4,0},{5,1},{6,2},{7,3},{8,12},{9,13},{10,... | collective-permute-start | bytes 196616 | tf_op jit(solution)/shard_map/ppermute | solution.py:16
  162.1 2.0 %collective-permute-start.29 = (bf16[128,256]{1,0:T(8,128)(2,1)S(1)}, bf16[128,256]{1,0:T(8,128)(2,1)S(1)}, u32[]{:S(2)}, u32[]{:S(2)}) collective-permute-start(bf16[128,256]{1,0:T(8,128)(2,1)S(1)} %get-tuple-element.76), channel_id=1, source_target_pairs={{0,2},{1,3},{2,0},{3,1},{4,6},{5,7},{6,4},{7,5},{8,10},{9,11},{10,... | collective-permute-start | bytes 196616 | tf_op jit(solution)/shard_map/ppermute | solution.py:16
  164.2 2.0 %collective-permute-start.30 = (bf16[128,256]{1,0:T(8,128)(2,1)S(1)}, bf16[128,256]{1,0:T(8,128)(2,1)S(1)}, u32[]{:S(2)}, u32[]{:S(2)}) collective-permute-start(bf16[128,256]{1,0:T(8,128)(2,1)S(1)} %get-tuple-element.77), channel_id=1, source_target_pairs={{0,4},{1,5},{2,6},{3,7},{4,0},{5,1},{6,2},{7,3},{8,12},{9,13},{10,... | collective-permute-start | bytes 196616 | tf_op jit(solution)/shard_map/ppermute | solution.py:16
  167.6 3.5 %collective-permute-done.30.refs_6_ = bf16[128,256]{1,0:T(8,128)(2,1)S(1)} collective-permute-done((bf16[128,256]{1,0:T(8,128)(2,1)S(1)}, bf16[128,256]{1,0:T(8,128)(2,1)S(1)}, u32[]{:S(2)}, u32[]{:S(2)}) %collective-permute-start.30) | collective-permute-done | bytes 65568 | tf_op jit(solution)/shard_map/ppermute | solution.py:16
  (96 shorter events, 32.1 us)
Async XLA Ops:
  0.0 8.3 %collective-permute-start = (bf16[64,2048]{1,0:T(8,128)(2,1)}, bf16[64,2048]{1,0:T(8,128)(2,1)S(1)}, u32[]{:S(2)}, u32[]{:S(2)}) collective-permute-start(bf16[64,2048]{1,0:T(8,128)(2,1)} %bitcast.10), channel_id=1, source_target_pairs={{0,1},{1,0},{2,3},{3,2},{4,5},{5,4},{6,7},{7,6},{8,9},{9,8},{10,11... | collective-permute-start | bytes 786440 | tf_op jit(solution)/shard_map/ppermute | solution.py:16
  1.5 21.3 %collective-permute-start.3 = (bf16[64,2048]{1,0:T(8,128)(2,1)}, bf16[64,2048]{1,0:T(8,128)(2,1)S(1)}, u32[]{:S(2)}, u32[]{:S(2)}) collective-permute-start(bf16[64,2048]{1,0:T(8,128)(2,1)} %bitcast.11), channel_id=1, source_target_pairs={{0,4},{1,5},{2,6},{3,7},{4,0},{5,1},{6,2},{7,3},{8,12},{9,13},{10,... | collective-permute-start | bytes 786440 | tf_op jit(solution)/shard_map/ppermute | solution.py:16
  4.1 18.8 %collective-permute-start.4 = (bf16[64,2048]{1,0:T(8,128)(2,1)}, bf16[64,2048]{1,0:T(8,128)(2,1)S(1)}, u32[]{:S(2)}, u32[]{:S(2)}) collective-permute-start(bf16[64,2048]{1,0:T(8,128)(2,1)} %bitcast.12), channel_id=1, source_target_pairs={{0,6},{1,7},{2,4},{3,5},{4,2},{5,3},{6,0},{7,1},{8,14},{9,15},{10,... | collective-permute-start | bytes 786440 | tf_op jit(solution)/shard_map/ppermute | solution.py:16
  5.5 19.6 %collective-permute-start.1 = (bf16[64,2048]{1,0:T(8,128)(2,1)}, bf16[64,2048]{1,0:T(8,128)(2,1)S(1)}, u32[]{:S(2)}, u32[]{:S(2)}) collective-permute-start(bf16[64,2048]{1,0:T(8,128)(2,1)} %bitcast.13), channel_id=1, source_target_pairs={{0,2},{1,3},{2,0},{3,1},{4,6},{5,7},{6,4},{7,5},{8,10},{9,11},{10,... | collective-permute-start | bytes 786440 | tf_op jit(solution)/shard_map/ppermute | solution.py:16
  8.3 20.4 %collective-permute-start.2 = (bf16[64,2048]{1,0:T(8,128)(2,1)S(1)}, bf16[64,2048]{1,0:T(8,128)(2,1)S(1)}, u32[]{:S(2)}, u32[]{:S(2)}) collective-permute-start(bf16[64,2048]{1,0:T(8,128)(2,1)S(1)} %collective-permute-done.refs_1_), channel_id=1, source_target_pairs={{0,2},{1,3},{2,0},{3,1},{4,6},{5,7},{6,4},{7,5},{8,10},{9,11},{10,... | collective-permute-start | bytes 786440 | tf_op jit(solution)/shard_map/ppermute | solution.py:16
  18.0 16.1 %collective-permute-start.6 = (bf16[64,4096]{1,0:T(8,128)(2,1)S(1)}, bf16[64,4096]{1,0:T(8,128)(2,1)S(1)}, u32[]{:S(2)}, u32[]{:S(2)}) collective-permute-start(bf16[64,4096]{1,0:T(8,128)(2,1)S(1)} %get-tuple-element.45), channel_id=1, source_target_pairs={{0,16},{8,24},{1,17},{9,25},{2,18},{10,26},{3,19},{11,27},{4,20},{... | collective-permute-start | bytes 1572872 | tf_op jit(solution)/shard_map/ppermute | solution.py:363
  28.6 11.9 %collective-permute-start.5 = (bf16[128,2048]{1,0:T(8,128)(2,1)S(1)}, bf16[128,2048]{1,0:T(8,128)(2,1)S(1)}, u32[]{:S(2)}, u32[]{:S(2)}) collective-permute-start(bf16[128,2048]{1,0:T(8,128)(2,1)S(1)} %pad_maximum_fusion), channel_id=1, source_target_pairs={{0,1},{1,0},{2,3},{3,2},{4,5},{5,4},{6,7},{7,6},{8,9},{9,8},{10,11... | collective-permute-start | bytes 1572872 | tf_op jit(solution)/shard_map/ppermute | solution.py:16
  29.1 19.2 %collective-permute-start.9 = (bf16[64,4096]{1,0:T(8,128)(2,1)S(1)}, bf16[64,4096]{1,0:T(8,128)(2,1)S(1)}, u32[]{:S(2)}, u32[]{:S(2)}) collective-permute-start(bf16[64,4096]{1,0:T(8,128)(2,1)S(1)} %get-tuple-element.47), channel_id=1, source_target_pairs={{0,16},{8,24},{1,17},{9,25},{2,18},{10,26},{3,19},{11,27},{4,20},{... | collective-permute-start | bytes 1572872 | tf_op jit(solution)/shard_map/ppermute | solution.py:363
  48.4 7.3 %collective-permute-start.10 = (bf16[256,4096]{1,0:T(8,128)(2,1)S(1)}, bf16[256,4096]{1,0:T(8,128)(2,1)S(1)}, u32[]{:S(2)}, u32[]{:S(2)}) collective-permute-start(bf16[256,4096]{1,0:T(8,128)(2,1)S(1)} %get-tuple-element.48.refs_2_), channel_id=1, source_target_pairs={{0,8},{16,24},{1,9},{17,25},{2,10},{18,26},{3,11},{19,27},{4,12},{... | collective-permute-start | bytes 6291464 | tf_op jit(solution)/shard_map/ppermute | solution.py:369
  49.8 10.8 %collective-permute-start.7 = (bf16[128,4096]{1,0:T(8,128)(2,1)S(1)}, bf16[128,4096]{1,0:T(8,128)(2,1)}, u32[]{:S(2)}, u32[]{:S(2)}) collective-permute-start(bf16[128,4096]{1,0:T(8,128)(2,1)S(1)} %get-tuple-element.42.refs_4_.refs_0_), channel_id=1, source_target_pairs={{0,8},{16,24},{1,9},{17,25},{2,10},{18,26},{3,11},{19,27},{4,12},{... | collective-permute-start | bytes 3145736 | tf_op jit(solution)/shard_map/ppermute | solution.py:369
  52.1 9.8 %collective-permute-start.8 = (bf16[128,4096]{1,0:T(8,128)(2,1)S(1)}, bf16[128,4096]{1,0:T(8,128)(2,1)}, u32[]{:S(2)}, u32[]{:S(2)}) collective-permute-start(bf16[128,4096]{1,0:T(8,128)(2,1)S(1)} %encode.4.refs_5_.refs_1_), channel_id=1, source_target_pairs={{0,8},{16,24},{1,9},{17,25},{2,10},{18,26},{3,11},{19,27},{4,12},{... | collective-permute-start | bytes 3145736 | tf_op jit(solution)/shard_map/ppermute | solution.py:369
  54.3 31.9 %collective-permute-start.13 = (bf16[128,4096]{1,0:T(8,128)(2,1)S(1)}, bf16[128,4096]{1,0:T(8,128)(2,1)}, u32[]{:S(2)}, u32[]{:S(2)}) collective-permute-start(bf16[128,4096]{1,0:T(8,128)(2,1)S(1)} %encode.4.refs_5_.refs_1_), channel_id=1, source_target_pairs={{0,16},{8,24},{1,17},{9,25},{2,18},{10,26},{3,19},{11,27},{4,20},{... | collective-permute-start | bytes 3145736 | tf_op jit(solution)/shard_map/ppermute | solution.py:363
  55.6 6.2 %collective-permute-start.12 = (bf16[64,4096]{1,0:T(8,128)(2,1)S(1)}, bf16[64,4096]{1,0:T(8,128)(2,1)}, u32[]{:S(2)}, u32[]{:S(2)}) collective-permute-start(bf16[64,4096]{1,0:T(8,128)(2,1)S(1)} %collective-permute-done.9.refs_7_), channel_id=1, source_target_pairs={{16,24},{24,16},{17,25},{25,17},{18,26},{26,18},{19,27},{27,19},{2... | collective-permute-start | bytes 1572872 | tf_op jit(solution)/shard_map/ppermute | solution.py:366
  57.6 4.3 %collective-permute-start.11 = (bf16[64,4096]{1,0:T(8,128)(2,1)S(1)}, bf16[64,4096]{1,0:T(8,128)(2,1)}, u32[]{:S(2)}, u32[]{:S(2)}) collective-permute-start(bf16[64,4096]{1,0:T(8,128)(2,1)S(1)} %collective-permute-done.6.refs_6_), channel_id=1, source_target_pairs={{16,24},{24,16},{17,25},{25,17},{18,26},{26,18},{19,27},{27,19},{2... | collective-permute-start | bytes 1572872 | tf_op jit(solution)/shard_map/ppermute | solution.py:366
  60.6 38.6 %collective-permute-start.15 = (bf16[128,4096]{1,0:T(8,128)(2,1)}, bf16[128,4096]{1,0:T(8,128)(2,1)S(1)}, u32[]{:S(2)}, u32[]{:S(2)}) collective-permute-start(bf16[128,4096]{1,0:T(8,128)(2,1)} %copy-done.22), channel_id=1, source_target_pairs={{0,16},{8,24},{1,17},{9,25},{2,18},{10,26},{3,19},{11,27},{4,20},{... | collective-permute-start | bytes 3145736 | tf_op jit(solution)/shard_map/ppermute | solution.py:363
  86.2 13.6 %collective-permute-start.14 = (bf16[128,4096]{1,0:T(8,128)(2,1)}, bf16[128,4096]{1,0:T(8,128)(2,1)S(1)}, u32[]{:S(2)}, u32[]{:S(2)}) collective-permute-start(bf16[128,4096]{1,0:T(8,128)(2,1)} %collective-permute-done.13.refs_0_), channel_id=1, source_target_pairs={{16,24},{24,16},{17,25},{25,17},{18,26},{26,18},{19,27},{27,19},{2... | collective-permute-start | bytes 3145736 | tf_op jit(solution)/shard_map/ppermute | solution.py:366
  97.4 27.2 %collective-permute-start.23 = (bf16[128,4096]{1,0:T(8,128)(2,1)}, bf16[128,4096]{1,0:T(8,128)(2,1)S(1)}, u32[]{:S(2)}, u32[]{:S(2)}) collective-permute-start(bf16[128,4096]{1,0:T(8,128)(2,1)} %get-tuple-element.67), channel_id=1, source_target_pairs={{0,16},{8,24},{1,17},{9,25},{2,18},{10,26},{3,19},{11,27},{4,20},{... | collective-permute-start | bytes 3145736 | tf_op jit(solution)/shard_map/ppermute | solution.py:363
  98.7 13.7 %collective-permute-start.16 = (bf16[4,128,256]{2,1,0:T(8,128)(2,1)}, bf16[4,128,256]{2,1,0:T(8,128)(2,1)S(1)}, u32[]{:S(2)}, u32[]{:S(2)}) collective-permute-start(bf16[4,128,256]{2,1,0:T(8,128)(2,1)} %get-tuple-element.52.refs_5_), channel_id=1, source_target_pairs={{0,1},{1,0},{2,3},{3,2},{4,5},{5,4},{6,7},{7,6},{8,9},{9,8},{10,11... | collective-permute-start | bytes 786440 | tf_op jit(solution)/shard_map/ppermute | solution.py:16
  108.9 8.5 %collective-permute-start.17 = (bf16[4,128,256]{2,1,0:T(8,128)(2,1)}, bf16[4,128,256]{2,1,0:T(8,128)(2,1)S(1)}, u32[]{:S(2)}, u32[]{:S(2)}) collective-permute-start(bf16[4,128,256]{2,1,0:T(8,128)(2,1)} %get-tuple-element.59), channel_id=1, source_target_pairs={{0,1},{1,0},{2,3},{3,2},{4,5},{5,4},{6,7},{7,6},{8,9},{9,8},{10,11... | collective-permute-start | bytes 786440 | tf_op jit(solution)/shard_map/ppermute | solution.py:16
  110.5 21.1 %collective-permute-start.21 = (bf16[128,4096]{1,0:T(8,128)(2,1)}, bf16[128,4096]{1,0:T(8,128)(2,1)S(1)}, u32[]{:S(2)}, u32[]{:S(2)}) collective-permute-start(bf16[128,4096]{1,0:T(8,128)(2,1)} %copy-done.4), channel_id=1, source_target_pairs={{16,24},{24,16},{17,25},{25,17},{18,26},{26,18},{19,27},{27,19},{2... | collective-permute-start | bytes 3145736 | tf_op jit(solution)/shard_map/ppermute | solution.py:366
  124.5 19.5 %collective-permute-start.24 = (bf16[128,4096]{1,0:T(8,128)(2,1)S(1)}, bf16[128,4096]{1,0:T(8,128)(2,1)S(1)}, u32[]{:S(2)}, u32[]{:S(2)}) collective-permute-start(bf16[128,4096]{1,0:T(8,128)(2,1)S(1)} %collective-permute-done.23.refs_0_), channel_id=1, source_target_pairs={{16,24},{24,16},{17,25},{25,17},{18,26},{26,18},{19,27},{27,19},{2... | collective-permute-start | bytes 3145736 | tf_op jit(solution)/shard_map/ppermute | solution.py:366
  126.6 14.9 %collective-permute-start.18 = (bf16[256,256]{1,0:T(8,128)(2,1)S(1)}, bf16[256,256]{1,0:T(8,128)(2,1)S(1)}, u32[]{:S(2)}, u32[]{:S(2)}) collective-permute-start(bf16[256,256]{1,0:T(8,128)(2,1)S(1)} %get-tuple-element.61), channel_id=1, source_target_pairs={{0,2},{1,3},{2,0},{3,1},{4,6},{5,7},{6,4},{7,5},{8,10},{9,11},{10,... | collective-permute-start | bytes 393224 | tf_op jit(solution)/shard_map/ppermute | solution.py:16
  128.2 13.3 %collective-permute-start.19 = (bf16[256,256]{1,0:T(8,128)(2,1)S(1)}, bf16[256,256]{1,0:T(8,128)(2,1)S(1)}, u32[]{:S(2)}, u32[]{:S(2)}) collective-permute-start(bf16[256,256]{1,0:T(8,128)(2,1)S(1)} %get-tuple-element.62), channel_id=1, source_target_pairs={{0,4},{1,5},{2,6},{3,7},{4,0},{5,1},{6,2},{7,3},{8,12},{9,13},{10,... | collective-permute-start | bytes 393224 | tf_op jit(solution)/shard_map/ppermute | solution.py:16
  130.8 10.8 %collective-permute-start.20 = (bf16[256,256]{1,0:T(8,128)(2,1)S(1)}, bf16[256,256]{1,0:T(8,128)(2,1)S(1)}, u32[]{:S(2)}, u32[]{:S(2)}) collective-permute-start(bf16[256,256]{1,0:T(8,128)(2,1)S(1)} %get-tuple-element.63), channel_id=1, source_target_pairs={{0,6},{1,7},{2,4},{3,5},{4,2},{5,3},{6,0},{7,1},{8,14},{9,15},{10,... | collective-permute-start | bytes 393224 | tf_op jit(solution)/shard_map/ppermute | solution.py:16
  140.9 12.9 %collective-permute-start.22 = (bf16[4,128,256]{2,1,0:T(8,128)(2,1)}, bf16[4,128,256]{2,1,0:T(8,128)(2,1)S(1)}, u32[]{:S(2)}, u32[]{:S(2)}) collective-permute-start(bf16[4,128,256]{2,1,0:T(8,128)(2,1)} %get-tuple-element.65.refs_4_.refs_5_), channel_id=1, source_target_pairs={{0,1},{1,0},{2,3},{3,2},{4,5},{5,4},{6,7},{7,6},{8,9},{9,8},{10,11... | collective-permute-start | bytes 786440 | tf_op jit(solution)/shard_map/ppermute | solution.py:16
  152.3 8.2 %collective-permute-start.28 = (bf16[4,128,256]{2,1,0:T(8,128)(2,1)}, bf16[4,128,256]{2,1,0:T(8,128)(2,1)S(1)}, u32[]{:S(2)}, u32[]{:S(2)}) collective-permute-start(bf16[4,128,256]{2,1,0:T(8,128)(2,1)} %get-tuple-element.69.refs_2_), channel_id=1, source_target_pairs={{0,1},{1,0},{2,3},{3,2},{4,5},{5,4},{6,7},{7,6},{8,9},{9,8},{10,11... | collective-permute-start | bytes 786440 | tf_op jit(solution)/shard_map/ppermute | solution.py:16
  155.5 5.0 %collective-permute-start.25 = (bf16[128,256]{1,0:T(8,128)(2,1)S(1)}, bf16[128,256]{1,0:T(8,128)(2,1)S(1)}, u32[]{:S(2)}, u32[]{:S(2)}) collective-permute-start(bf16[128,256]{1,0:T(8,128)(2,1)S(1)} %get-tuple-element.71), channel_id=1, source_target_pairs={{0,2},{1,3},{2,0},{3,1},{4,6},{5,7},{6,4},{7,5},{8,10},{9,11},{10,... | collective-permute-start | bytes 196616 | tf_op jit(solution)/shard_map/ppermute | solution.py:16
  156.8 10.7 %collective-permute-start.26 = (bf16[128,256]{1,0:T(8,128)(2,1)S(1)}, bf16[128,256]{1,0:T(8,128)(2,1)S(1)}, u32[]{:S(2)}, u32[]{:S(2)}) collective-permute-start(bf16[128,256]{1,0:T(8,128)(2,1)S(1)} %get-tuple-element.72), channel_id=1, source_target_pairs={{0,4},{1,5},{2,6},{3,7},{4,0},{5,1},{6,2},{7,3},{8,12},{9,13},{10,... | collective-permute-start | bytes 196616 | tf_op jit(solution)/shard_map/ppermute | solution.py:16
  159.1 8.4 %collective-permute-start.27 = (bf16[128,256]{1,0:T(8,128)(2,1)S(1)}, bf16[128,256]{1,0:T(8,128)(2,1)S(1)}, u32[]{:S(2)}, u32[]{:S(2)}) collective-permute-start(bf16[128,256]{1,0:T(8,128)(2,1)S(1)} %get-tuple-element.73), channel_id=1, source_target_pairs={{0,6},{1,7},{2,4},{3,5},{4,2},{5,3},{6,0},{7,1},{8,14},{9,15},{10,... | collective-permute-start | bytes 196616 | tf_op jit(solution)/shard_map/ppermute | solution.py:16
  162.1 5.4 %collective-permute-start.29 = (bf16[128,256]{1,0:T(8,128)(2,1)S(1)}, bf16[128,256]{1,0:T(8,128)(2,1)S(1)}, u32[]{:S(2)}, u32[]{:S(2)}) collective-permute-start(bf16[128,256]{1,0:T(8,128)(2,1)S(1)} %get-tuple-element.76), channel_id=1, source_target_pairs={{0,2},{1,3},{2,0},{3,1},{4,6},{5,7},{6,4},{7,5},{8,10},{9,11},{10,... | collective-permute-start | bytes 196616 | tf_op jit(solution)/shard_map/ppermute | solution.py:16
  164.2 6.9 %collective-permute-start.30 = (bf16[128,256]{1,0:T(8,128)(2,1)S(1)}, bf16[128,256]{1,0:T(8,128)(2,1)S(1)}, u32[]{:S(2)}, u32[]{:S(2)}) collective-permute-start(bf16[128,256]{1,0:T(8,128)(2,1)S(1)} %get-tuple-element.77), channel_id=1, source_target_pairs={{0,4},{1,5},{2,6},{3,7},{4,0},{5,1},{6,2},{7,3},{8,12},{9,13},{10,... | collective-permute-start | bytes 196616 | tf_op jit(solution)/shard_map/ppermute | solution.py:16
  166.2 6.1 %collective-permute-start.31 = (bf16[128,256]{1,0:T(8,128)(2,1)S(1)}, bf16[128,256]{1,0:T(8,128)(2,1)S(1)}, u32[]{:S(2)}, u32[]{:S(2)}) collective-permute-start(bf16[128,256]{1,0:T(8,128)(2,1)S(1)} %get-tuple-element.78), channel_id=1, source_target_pairs={{0,6},{1,7},{2,4},{3,5},{4,2},{5,3},{6,0},{7,1},{8,14},{9,15},{10,... | collective-permute-start | bytes 196616 | tf_op jit(solution)/shard_map/ppermute | solution.py:16
  (25 other events, 231.1 us)

commit v9 on v8

--- a/solution.py
+++ b/solution.py
@@ -28,8 +28,7 @@
     return pltpu.with_memory_space_constraint(array, pltpu.VMEM)
 
 
-def fill(order, parts, rows_of):
-    at = 0
+def fill(order, parts, rows_of, at=0):
     for part, row, size in order:
         rows_of[pl.ds(at, size), :] = parts[part][pl.ds(row, size), :]
         at += size
@@ -40,8 +39,16 @@
     outs, refs = refs[: len(pieces)], refs[len(pieces) :]
     features = weight.shape[2]
     if stream:
-        kept, tokens, sems = refs
+        kept, tokens, sems, bias_here, start_sems = refs
         block = features // sems.shape[0]
+        size = parts[0].shape[0]
+        starts = [
+            pltpu.make_async_copy(parts[0], tokens.at[pl.ds(0, size)], start_sems.at[0]),
+            pltpu.make_async_copy(bias, bias_here, start_sems.at[1]),
+        ]
+        for copy in starts:
+            copy.start()
+        bias = bias_here
     else:
         kept, (tokens,) = weight, refs
         block = min(512, features)
@@ -53,7 +60,11 @@
     if stream:
         for j in range(features // block):
             fetch(jnp.int32(j)).start()
-    fill(order, parts, tokens)
+        fill(order[1:], parts, tokens, size)
+        for copy in starts:
+            copy.wait()
+    else:
+        fill(order, parts, tokens)
 
     @pl.loop(0, features // block)
     def _(j):
@@ -73,13 +84,23 @@
     scratch = [pltpu.VMEM((rows, width), jnp.bfloat16)]
     if stream:
         out_shape.append(pltpu.VMEM(weight.shape, weight.dtype))
-        scratch.append(pltpu.SemaphoreType.DMA((max(1, features // 512),)))
-        weight = pltpu.with_memory_space_constraint(weight, pltpu.HBM)
+        scratch += [
+            pltpu.SemaphoreType.DMA((max(1, features // 512),)),
+            pltpu.VMEM(bias.shape, bias.dtype),
+            pltpu.SemaphoreType.DMA((2,)),
+        ]
+        first, weight, bias = (
+            pltpu.with_memory_space_constraint(array, pltpu.HBM) for array in (parts[0], weight, bias)
+        )
+        parts = [first, *parts[1:]]
     else:
         weight = pltpu.with_memory_space_constraint(weight, pltpu.VMEM)
     return pl.pallas_call(
         functools.partial(encode_kernel, order, pieces, len(parts), len(after), stream),
-        in_specs=[WHOLE] * len(parts) + [ANYWHERE if stream else WHOLE, WHOLE] + [ANYWHERE] * len(after),
+        in_specs=[ANYWHERE if stream else WHOLE]
+        + [WHOLE] * (len(parts) - 1)
+        + [ANYWHERE if stream else WHOLE] * 2
+        + [ANYWHERE] * len(after),
         out_specs=[WHOLE] * len(out_shape),
         out_shape=out_shape,
         scratch_shapes=scratch,
@@ -431,18 +452,18 @@
         return decode_later(info, [direct], [swapped], order, base, kept, row, shards, list(earlier))
 
     c1, c2 = across(after(d1, sent)), across(after(d2, sent))
-    mine1, sent1 = later(1, d1, c1, sent, d2)
-    met1 = meet([mine, mine1], [sent, sent1])
+    mine1, sent1 = later(1, d1, c1, sent, d2, c2)
+    mine2, sent2 = later(2, d2, c2, sent1)
+    met1 = meet([mine, mine1], [sent, sent1], sent2)
     where1, parts1 = spread(slots[0] + slots[1], met1)
     c3 = across(after(d3, met1[0]))
-    mine2, sent2 = later(2, d2, c2, met1[0])
-    total = add_up(info, targets[0], -1.0, where1, parts1, [sent2])
-    mine3, sent3 = later(3, d3, c3, sent2, total)
+    mine3, sent3 = later(3, d3, c3, sent2, *parts1)
     met2 = meet([mine2], [sent2], sent3)
     where2, parts2 = spread(slots[2], met2)
     met3 = meet([mine3], [sent3], parts2[1])
     where3, parts3 = spread(slots[3], met3)
-    return add_up(info, total, 1.0, where2 + where3, parts2 + parts3, [])[None]
+    where, parts = where1 + where2 + where3, parts1 + parts2 + parts3
+    return add_up(info, targets[0], -1.0, where, parts, [])[None]
 
 
 def grouped(layer_inputs, targets, encoder, encoder_bias, decoder):

time: 175 us -> 182 us (1.040)
  waiting for transfers between devices: 33.8 us -> 37.4 us
  starting transfers between devices: 58.7 us -> 61 us
  Pallas kernels: 70.4 us -> 72.3 us
    ppermute x19, waiting for transfers between devices: 28.4 us -> 32 us  [exchange(): return lax.ppermute(array, axis, [(i, i ^ flip) for i in range(size)])]
    ppermute x19, starting transfers between devices: 26.9 us -> 29.7 us  [exchange(): return lax.ppermute(array, axis, [(i, i ^ flip) for i in range(size)])]
    pallas_call x3, Pallas kernels: 17.1 us -> 19.3 us  [encode(): pl.pallas_call(functools.partial(encode_kernel, order, pieces, len(parts)...]
    unnamed x50 -> x54, local copies, waits for them, and re-layouts: 9.78 us -> 9.39 us
  transfers between devices with their start and end apart: 32 -> 32, of which waited for: 11 -> 14; matrix products, arithmetic and copies ran while one was open for 0% -> 0% of each run, Pallas kernels for 40% -> 39%
where the time goes in v9:
time: 182 us; the launch traced here: 181 us
  Pallas kernels  72.3 us (40%)
  starting transfers between devices  61 us (34%)
  waiting for transfers between devices  37.4 us (21%)
  local copies, waits for them, and re-layouts  10.1 us (6%)
    ppermute x19, waiting for transfers between devices, exchange(): return lax.ppermute(array, axis, [(i, i ^ flip) for i in range(size)])  32 us
    ppermute x19, starting transfers between devices, exchange(): return lax.ppermute(array, axis, [(i, i ^ flip) for i in range(size)])  29.7 us
    pallas_call x3, Pallas kernels, decode_later(): pl.pallas_call(functools.partial(later_wave_kernel, order, row, len(direc...  25.4 us
    pallas_call x1, Pallas kernels, decode_first(): pl.pallas_call(functools.partial(first_wave_kernel, [len(parts) for parts...  24.1 us
    ppermute x5, starting transfers between devices, across(): return lax.ppermute(a, 'layer', [(i, i ^ 1) for i in range(half, layers)])  19.8 us
    pallas_call x3, Pallas kernels, encode(): pl.pallas_call(functools.partial(encode_kernel, order, pieces, len(parts)...  19.3 us
    unnamed x54, local copies, waits for them, and re-layouts  9.39 us
    ppermute x5, starting transfers between devices, up(): return lax.ppermute(a, 'layer', [(i, i + half) for i in range(half)])  6.44 us
  transfers between devices with their start and end apart: 32, of which 14 were waited for; matrix products, arithmetic and copies ran while one was open for 0% of the time, Pallas kernels for 39%

profile of v9, /device:TPU:2, one launch (start us, length us, event | category | flops | bytes accessed | tf_op | source)
XLA Modules:
  0.0 181.2 jit_solution(7826389446298808613)
XLA Ops:
  1.5 2.6 %collective-permute-start.3 = (bf16[64,2048]{1,0:T(8,128)(2,1)}, bf16[64,2048]{1,0:T(8,128)(2,1)S(1)}, u32[]{:S(2)}, u32[]{:S(2)}) collective-permute-start(bf16[64,2048]{1,0:T(8,128)(2,1)} %bitcast.11), channel_id=1, source_target_pairs={{0,4},{1,5},{2,6},{3,7},{4,0},{5,1},{6,2},{7,3},{8,12},{9,13},{10,... | collective-permute-start | bytes 786440 | tf_op jit(solution)/shard_map/ppermute | solution.py:16
  5.7 2.6 %collective-permute-done.refs_1_ = bf16[64,2048]{1,0:T(8,128)(2,1)S(1)} collective-permute-done((bf16[64,2048]{1,0:T(8,128)(2,1)}, bf16[64,2048]{1,0:T(8,128)(2,1)S(1)}, u32[]{:S(2)}, u32[]{:S(2)}) %collective-permute-start) | collective-permute-done | bytes 262176 | tf_op jit(solution)/shard_map/ppermute | solution.py:16
  8.3 1.6 collective-permute-start.2
  9.8 8.4 %encode.3 = (bf16[128,4096]{1,0:T(8,128)(2,1)S(1)}, bf16[64,4096]{1,0:T(8,128)(2,1)S(1)}, bf16[64,4096]{1,0:T(8,128)(2,1)S(1)}, bf16[1,2048,4096]{2,1,0:T(8,128)(2,1)S(1)}) custom-call(bf16[64,2048]{1,0:T(8,128)(2,1)} %bitcast.14, bf16[64,2048]{1,0:T(8,128)(2,1)S(1)} %collective-permute-done.refs_1_, bf16[1,2048,4096]{2,1,0:T(8,128)(2,1)} %refs_2_.1, ...), custom_call_target="tpu_custom_call" | custom-call | tf_op jit(solution)/shard_map/encode/pallas_call | solution.py:98
  19.5 3.4 %collective-permute-done.3.refs_0_ = bf16[64,2048]{1,0:T(8,128)(2,1)S(1)} collective-permute-done((bf16[64,2048]{1,0:T(8,128)(2,1)}, bf16[64,2048]{1,0:T(8,128)(2,1)S(1)}, u32[]{:S(2)}, u32[]{:S(2)}) %collective-permute-start.3) | collective-permute-done | bytes 262176 | tf_op jit(solution)/shard_map/ppermute | solution.py:16
  22.9 2.1 %collective-permute-done.1.refs_0_ = bf16[64,2048]{1,0:T(8,128)(2,1)S(1)} collective-permute-done((bf16[64,2048]{1,0:T(8,128)(2,1)}, bf16[64,2048]{1,0:T(8,128)(2,1)S(1)}, u32[]{:S(2)}, u32[]{:S(2)}) %collective-permute-start.1) | collective-permute-done | bytes 262176 | tf_op jit(solution)/shard_map/ppermute | solution.py:16
  25.0 3.6 %collective-permute-done.2.refs_1_ = bf16[64,2048]{1,0:T(8,128)(2,1)S(1)} collective-permute-done((bf16[64,2048]{1,0:T(8,128)(2,1)S(1)}, bf16[64,2048]{1,0:T(8,128)(2,1)S(1)}, u32[]{:S(2)}, u32[]{:S(2)}) %collective-permute-start.2) | collective-permute-done | bytes 262176 | tf_op jit(solution)/shard_map/ppermute | solution.py:16
  30.4 3.8 %encode.4.refs_5_.refs_1_ = bf16[128,4096]{1,0:T(8,128)(2,1)S(1)} custom-call(bf16[64,2048]{1,0:T(8,128)(2,1)S(1)} %collective-permute-done.1.refs_0_, bf16[64,2048]{1,0:T(8,128)(2,1)S(1)} %collective-permute-done.2.refs_1_, bf16[1,2048,4096]{2,1,0:T(8,128)(2,1)S(1)} %get-tuple-element.43.refs_2_.refs_3_, f32[1,4096]{1,0:T(1,128)S(1)} %copy-done.21, ...), custom_call_target="tpu_custom_call" | custom-call | tf_op jit(solution)/shard_map/encode/pallas_call | solution.py:98
  34.2 6.4 %collective-permute-done.5.refs_2_ = bf16[128,2048]{1,0:T(8,128)(2,1)S(1)} collective-permute-done((bf16[128,2048]{1,0:T(8,128)(2,1)S(1)}, bf16[128,2048]{1,0:T(8,128)(2,1)S(1)}, u32[]{:S(2)}, u32[]{:S(2)}) %collective-permute-start.5) | collective-permute-done | bytes 524320 | tf_op jit(solution)/shard_map/ppermute | solution.py:16
  40.6 7.2 %encode.5 = (bf16[256,4096]{1,0:T(8,128)(2,1)S(1)}, bf16[128,4096]{1,0:T(8,128)(2,1)}, bf16[128,4096]{1,0:T(8,128)(2,1)}) custom-call(bf16[64,2048]{1,0:T(8,128)(2,1)S(1)} %collective-permute-done.3.refs_0_, bf16[64,2048]{1,0:T(8,128)(2,1)S(1)} %collective-permute-done.4.refs_1_, bf16[128,2048]{1,0:T(8,128)(2,1)S(1)} %collective-permute-done.5.refs_2_, ...), custom_call_target="tpu_custom_call" | custom-call | tf_op jit(solution)/shard_map/encode/pallas_call | solution.py:98
  50.6 2.3 %collective-permute-start.8 = (bf16[128,4096]{1,0:T(8,128)(2,1)S(1)}, bf16[128,4096]{1,0:T(8,128)(2,1)}, u32[]{:S(2)}, u32[]{:S(2)}) collective-permute-start(bf16[128,4096]{1,0:T(8,128)(2,1)S(1)} %encode.4.refs_5_.refs_1_), channel_id=1, source_target_pairs={{0,8},{16,24},{1,9},{17,25},{2,10},{18,26},{3,11},{19,27},{4,12},{... | collective-permute-start | bytes 3145736 | tf_op jit(solution)/shard_map/ppermute | solution.py:390
  55.5 1.9 %collective-permute-start.12 = (bf16[64,4096]{1,0:T(8,128)(2,1)}, bf16[64,4096]{1,0:T(8,128)(2,1)}, u32[]{:S(2)}, u32[]{:S(2)}) collective-permute-start(bf16[64,4096]{1,0:T(8,128)(2,1)} %collective-permute-done.9.refs_7_), channel_id=1, source_target_pairs={{16,24},{24,16},{17,25},{25,17},{18,26},{26,18},{19,27},{27,19},{2... | collective-permute-start | bytes 1572872 | tf_op jit(solution)/shard_map/ppermute | solution.py:387
  57.4 2.4 %collective-permute-start.11 = (bf16[64,4096]{1,0:T(8,128)(2,1)}, bf16[64,4096]{1,0:T(8,128)(2,1)S(1)}, u32[]{:S(2)}, u32[]{:S(2)}) collective-permute-start(bf16[64,4096]{1,0:T(8,128)(2,1)} %collective-permute-done.6.refs_6_), channel_id=1, source_target_pairs={{16,24},{24,16},{17,25},{25,17},{18,26},{26,18},{19,27},{27,19},{2... | collective-permute-start | bytes 1572872 | tf_op jit(solution)/shard_map/ppermute | solution.py:387
  62.4 24.1 %decode_first.1 = (f32[4,128,256]{2,1,0:T(8,128)}, bf16[4,128,256]{2,1,0:T(8,128)(2,1)}, f32[384,2048]{1,0:T(8,128)}, bf16[4096,2048]{1,0:T(8,128)(2,1)S(1)}, bf16[4096,2048]{1,0:T(8,128)(2,1)S(1)}) custom-call(s32[7]{0:T(128)} %stack.31.info, bf16[128,4096]{1,0:T(8,128)(2,1)} %copy-done.1, bf16[128,4096]{1,0:T(8,128)(2,1)} %copy-done, ...), custom_call_target="tpu_custom_call" | custom-call | tf_op jit(solution)/shard_map/decode_first/pallas_call | solution.py:229
  86.6 11.5 %collective-permute-start.16 = (bf16[128,4096]{1,0:T(8,128)(2,1)S(1)}, bf16[128,4096]{1,0:T(8,128)(2,1)S(1)}, u32[]{:S(2)}, u32[]{:S(2)}) collective-permute-start(bf16[128,4096]{1,0:T(8,128)(2,1)S(1)} %collective-permute-done.15.refs_6_.refs_0_), channel_id=1, source_target_pairs={{16,24},{24,16},{17,25},{25,17},{18,26},{26,18},{19,27},{27,19},{2... | collective-permute-start | bytes 3145736 | tf_op jit(solution)/shard_map/ppermute | solution.py:387
  98.8 1.9 %collective-permute-start.14 = (bf16[128,4096]{1,0:T(8,128)(2,1)}, bf16[128,4096]{1,0:T(8,128)(2,1)S(1)}, u32[]{:S(2)}, u32[]{:S(2)}) collective-permute-start(bf16[128,4096]{1,0:T(8,128)(2,1)} %collective-permute-done.13.refs_0_), channel_id=1, source_target_pairs={{16,24},{24,16},{17,25},{25,17},{18,26},{26,18},{19,27},{27,19},{2... | collective-permute-start | bytes 3145736 | tf_op jit(solution)/shard_map/ppermute | solution.py:387
  103.6 8.6 %decode_later.3 = (f32[4,128,256]{2,1,0:T(8,128)}, bf16[4,128,256]{2,1,0:T(8,128)(2,1)}) custom-call(s32[7]{0:T(128)} %stack.31.info, bf16[128,4096]{1,0:T(8,128)(2,1)} %collective-permute-done.13.refs_0_, bf16[128,4096]{1,0:T(8,128)(2,1)S(1)} %collective-permute-done.14.refs_1_, f32[384,2048]{1,0:T(8,128)} %get-tuple-element.54.refs_2_, ...), custom_call_target="tpu_custom_call" | custom-call | tf_op jit(solution)/shard_map/decode_later/pallas_call | solution.py:287
  112.2 1.6 collective-permute-start.18
  116.3 8.2 %decode_later.4 = (f32[4,128,256]{2,1,0:T(8,128)}, bf16[4,128,256]{2,1,0:T(8,128)(2,1)}) custom-call(s32[7]{0:T(128)} %stack.31.info, bf16[128,4096]{1,0:T(8,128)(2,1)S(1)} %copy-done.3, bf16[128,4096]{1,0:T(8,128)(2,1)S(1)} %copy-done.5, f32[384,2048]{1,0:T(8,128)} %get-tuple-element.54.refs_2_, bf16[4096,2048]{1,0:T(8,128)(2,1)S(1)} %get-tuple-element.55.refs_3_, ...), custom_call_target="tpu_custom_call" | custom-call | tf_op jit(solution)/shard_map/decode_later/pallas_call | solution.py:287
  125.9 2.6 %collective-permute-done.23.refs_0_ = bf16[128,4096]{1,0:T(8,128)(2,1)} collective-permute-done((bf16[128,4096]{1,0:T(8,128)(2,1)}, bf16[128,4096]{1,0:T(8,128)(2,1)}, u32[]{:S(2)}, u32[]{:S(2)}) %collective-permute-start.23) | collective-permute-done | bytes 1048608 | tf_op jit(solution)/shard_map/ppermute | solution.py:384
  128.5 2.1 %collective-permute-start.24 = (bf16[128,4096]{1,0:T(8,128)(2,1)}, bf16[128,4096]{1,0:T(8,128)(2,1)S(1)}, u32[]{:S(2)}, u32[]{:S(2)}) collective-permute-start(bf16[128,4096]{1,0:T(8,128)(2,1)} %collective-permute-done.23.refs_0_), channel_id=1, source_target_pairs={{16,24},{24,16},{17,25},{25,17},{18,26},{26,18},{19,27},{27,19},{2... | collective-permute-start | bytes 3145736 | tf_op jit(solution)/shard_map/ppermute | solution.py:387
  130.6 2.5 %collective-permute-start.19 = (bf16[256,256]{1,0:T(8,128)(2,1)S(1)}, bf16[256,256]{1,0:T(8,128)(2,1)S(1)}, u32[]{:S(2)}, u32[]{:S(2)}) collective-permute-start(bf16[256,256]{1,0:T(8,128)(2,1)S(1)} %get-tuple-element.63), channel_id=1, source_target_pairs={{0,2},{1,3},{2,0},{3,1},{4,6},{5,7},{6,4},{7,5},{8,10},{9,11},{10,... | collective-permute-start | bytes 393224 | tf_op jit(solution)/shard_map/ppermute | solution.py:16
  133.1 2.8 %collective-permute-start.20 = (bf16[256,256]{1,0:T(8,128)(2,1)S(1)}, bf16[256,256]{1,0:T(8,128)(2,1)S(1)}, u32[]{:S(2)}, u32[]{:S(2)}) collective-permute-start(bf16[256,256]{1,0:T(8,128)(2,1)S(1)} %get-tuple-element.64), channel_id=1, source_target_pairs={{0,4},{1,5},{2,6},{3,7},{4,0},{5,1},{6,2},{7,3},{8,12},{9,13},{10,... | collective-permute-start | bytes 393224 | tf_op jit(solution)/shard_map/ppermute | solution.py:16
  137.9 2.3 %collective-permute-done.20.refs_8_.refs_2_ = bf16[256,256]{1,0:T(8,128)(2,1)S(1)} collective-permute-done((bf16[256,256]{1,0:T(8,128)(2,1)S(1)}, bf16[256,256]{1,0:T(8,128)(2,1)S(1)}, u32[]{:S(2)}, u32[]{:S(2)}) %collective-permute-start.20) | collective-permute-done | bytes 131104 | tf_op jit(solution)/shard_map/ppermute | solution.py:16
  140.2 6.7 %collective-permute-done.21.refs_9_.refs_3_ = bf16[256,256]{1,0:T(8,128)(2,1)S(1)} collective-permute-done((bf16[256,256]{1,0:T(8,128)(2,1)S(1)}, bf16[256,256]{1,0:T(8,128)(2,1)S(1)}, u32[]{:S(2)}, u32[]{:S(2)}) %collective-permute-start.21) | collective-permute-done | bytes 131104 | tf_op jit(solution)/shard_map/ppermute | solution.py:16
  147.6 8.6 %decode_later.5 = (f32[4,128,256]{2,1,0:T(8,128)}, bf16[4,128,256]{2,1,0:T(8,128)(2,1)}) custom-call(s32[7]{0:T(128)} %stack.31.info, bf16[128,4096]{1,0:T(8,128)(2,1)} %collective-permute-done.23.refs_0_, bf16[128,4096]{1,0:T(8,128)(2,1)S(1)} %collective-permute-done.24.refs_1_, f32[384,2048]{1,0:T(8,128)} %get-tuple-element.54.refs_2_, ...), custom_call_target="tpu_custom_call" | custom-call | tf_op jit(solution)/shard_map/decode_later/pallas_call | solution.py:287
  158.3 2.4 %collective-permute-start.25 = (bf16[128,256]{1,0:T(8,128)(2,1)S(1)}, bf16[128,256]{1,0:T(8,128)(2,1)S(1)}, u32[]{:S(2)}, u32[]{:S(2)}) collective-permute-start(bf16[128,256]{1,0:T(8,128)(2,1)S(1)} %get-tuple-element.71), channel_id=1, source_target_pairs={{0,2},{1,3},{2,0},{3,1},{4,6},{5,7},{6,4},{7,5},{8,10},{9,11},{10,... | collective-permute-start | bytes 196616 | tf_op jit(solution)/shard_map/ppermute | solution.py:16
  160.7 2.0 %collective-permute-start.26 = (bf16[128,256]{1,0:T(8,128)(2,1)S(1)}, bf16[128,256]{1,0:T(8,128)(2,1)S(1)}, u32[]{:S(2)}, u32[]{:S(2)}) collective-permute-start(bf16[128,256]{1,0:T(8,128)(2,1)S(1)} %get-tuple-element.72), channel_id=1, source_target_pairs={{0,4},{1,5},{2,6},{3,7},{4,0},{5,1},{6,2},{7,3},{8,12},{9,13},{10,... | collective-permute-start | bytes 196616 | tf_op jit(solution)/shard_map/ppermute | solution.py:16
  166.0 2.8 %collective-permute-start.29 = (bf16[128,256]{1,0:T(8,128)(2,1)S(1)}, bf16[128,256]{1,0:T(8,128)(2,1)S(1)}, u32[]{:S(2)}, u32[]{:S(2)}) collective-permute-start(bf16[128,256]{1,0:T(8,128)(2,1)S(1)} %get-tuple-element.76), channel_id=1, source_target_pairs={{0,2},{1,3},{2,0},{3,1},{4,6},{5,7},{6,4},{7,5},{8,10},{9,11},{10,... | collective-permute-start | bytes 196616 | tf_op jit(solution)/shard_map/ppermute | solution.py:16
  168.7 2.0 %collective-permute-start.30 = (bf16[128,256]{1,0:T(8,128)(2,1)S(1)}, bf16[128,256]{1,0:T(8,128)(2,1)S(1)}, u32[]{:S(2)}, u32[]{:S(2)}) collective-permute-start(bf16[128,256]{1,0:T(8,128)(2,1)S(1)} %get-tuple-element.77), channel_id=1, source_target_pairs={{0,4},{1,5},{2,6},{3,7},{4,0},{5,1},{6,2},{7,3},{8,12},{9,13},{10,... | collective-permute-start | bytes 196616 | tf_op jit(solution)/shard_map/ppermute | solution.py:16
  172.1 3.9 %collective-permute-done.30.refs_10_ = bf16[128,256]{1,0:T(8,128)(2,1)S(1)} collective-permute-done((bf16[128,256]{1,0:T(8,128)(2,1)S(1)}, bf16[128,256]{1,0:T(8,128)(2,1)S(1)}, u32[]{:S(2)}, u32[]{:S(2)}) %collective-permute-start.30) | collective-permute-done | bytes 65568 | tf_op jit(solution)/shard_map/ppermute | solution.py:16
  179.6 1.6 add_up.1
  (99 shorter events, 34.4 us)
Async XLA Ops:
  0.0 8.3 %collective-permute-start = (bf16[64,2048]{1,0:T(8,128)(2,1)}, bf16[64,2048]{1,0:T(8,128)(2,1)S(1)}, u32[]{:S(2)}, u32[]{:S(2)}) collective-permute-start(bf16[64,2048]{1,0:T(8,128)(2,1)} %bitcast.10), channel_id=1, source_target_pairs={{0,1},{1,0},{2,3},{3,2},{4,5},{5,4},{6,7},{7,6},{8,9},{9,8},{10,11... | collective-permute-start | bytes 786440 | tf_op jit(solution)/shard_map/ppermute | solution.py:16
  1.5 21.3 %collective-permute-start.3 = (bf16[64,2048]{1,0:T(8,128)(2,1)}, bf16[64,2048]{1,0:T(8,128)(2,1)S(1)}, u32[]{:S(2)}, u32[]{:S(2)}) collective-permute-start(bf16[64,2048]{1,0:T(8,128)(2,1)} %bitcast.11), channel_id=1, source_target_pairs={{0,4},{1,5},{2,6},{3,7},{4,0},{5,1},{6,2},{7,3},{8,12},{9,13},{10,... | collective-permute-start | bytes 786440 | tf_op jit(solution)/shard_map/ppermute | solution.py:16
  4.1 18.8 %collective-permute-start.4 = (bf16[64,2048]{1,0:T(8,128)(2,1)}, bf16[64,2048]{1,0:T(8,128)(2,1)S(1)}, u32[]{:S(2)}, u32[]{:S(2)}) collective-permute-start(bf16[64,2048]{1,0:T(8,128)(2,1)} %bitcast.12), channel_id=1, source_target_pairs={{0,6},{1,7},{2,4},{3,5},{4,2},{5,3},{6,0},{7,1},{8,14},{9,15},{10,... | collective-permute-start | bytes 786440 | tf_op jit(solution)/shard_map/ppermute | solution.py:16
  5.5 19.6 %collective-permute-start.1 = (bf16[64,2048]{1,0:T(8,128)(2,1)}, bf16[64,2048]{1,0:T(8,128)(2,1)S(1)}, u32[]{:S(2)}, u32[]{:S(2)}) collective-permute-start(bf16[64,2048]{1,0:T(8,128)(2,1)} %bitcast.13), channel_id=1, source_target_pairs={{0,2},{1,3},{2,0},{3,1},{4,6},{5,7},{6,4},{7,5},{8,10},{9,11},{10,... | collective-permute-start | bytes 786440 | tf_op jit(solution)/shard_map/ppermute | solution.py:16
  8.3 20.4 %collective-permute-start.2 = (bf16[64,2048]{1,0:T(8,128)(2,1)S(1)}, bf16[64,2048]{1,0:T(8,128)(2,1)S(1)}, u32[]{:S(2)}, u32[]{:S(2)}) collective-permute-start(bf16[64,2048]{1,0:T(8,128)(2,1)S(1)} %collective-permute-done.refs_1_), channel_id=1, source_target_pairs={{0,2},{1,3},{2,0},{3,1},{4,6},{5,7},{6,4},{7,5},{8,10},{9,11},{10,... | collective-permute-start | bytes 786440 | tf_op jit(solution)/shard_map/ppermute | solution.py:16
  18.2 16.0 %collective-permute-start.6 = (bf16[64,4096]{1,0:T(8,128)(2,1)S(1)}, bf16[64,4096]{1,0:T(8,128)(2,1)}, u32[]{:S(2)}, u32[]{:S(2)}) collective-permute-start(bf16[64,4096]{1,0:T(8,128)(2,1)S(1)} %get-tuple-element.45), channel_id=1, source_target_pairs={{0,16},{8,24},{1,17},{9,25},{2,18},{10,26},{3,19},{11,27},{4,20},{... | collective-permute-start | bytes 1572872 | tf_op jit(solution)/shard_map/ppermute | solution.py:384
  28.6 12.0 %collective-permute-start.5 = (bf16[128,2048]{1,0:T(8,128)(2,1)S(1)}, bf16[128,2048]{1,0:T(8,128)(2,1)S(1)}, u32[]{:S(2)}, u32[]{:S(2)}) collective-permute-start(bf16[128,2048]{1,0:T(8,128)(2,1)S(1)} %pad_maximum_fusion), channel_id=1, source_target_pairs={{0,1},{1,0},{2,3},{3,2},{4,5},{5,4},{6,7},{7,6},{8,9},{9,8},{10,11... | collective-permute-start | bytes 1572872 | tf_op jit(solution)/shard_map/ppermute | solution.py:16
  29.1 18.7 %collective-permute-start.9 = (bf16[64,4096]{1,0:T(8,128)(2,1)S(1)}, bf16[64,4096]{1,0:T(8,128)(2,1)}, u32[]{:S(2)}, u32[]{:S(2)}) collective-permute-start(bf16[64,4096]{1,0:T(8,128)(2,1)S(1)} %get-tuple-element.47), channel_id=1, source_target_pairs={{0,16},{8,24},{1,17},{9,25},{2,18},{10,26},{3,19},{11,27},{4,20},{... | collective-permute-start | bytes 1572872 | tf_op jit(solution)/shard_map/ppermute | solution.py:384
  47.8 7.7 %collective-permute-start.10 = (bf16[256,4096]{1,0:T(8,128)(2,1)S(1)}, bf16[256,4096]{1,0:T(8,128)(2,1)S(1)}, u32[]{:S(2)}, u32[]{:S(2)}) collective-permute-start(bf16[256,4096]{1,0:T(8,128)(2,1)S(1)} %get-tuple-element.48.refs_2_), channel_id=1, source_target_pairs={{0,8},{16,24},{1,9},{17,25},{2,10},{18,26},{3,11},{19,27},{4,12},{... | collective-permute-start | bytes 6291464 | tf_op jit(solution)/shard_map/ppermute | solution.py:390
  49.2 8.2 %collective-permute-start.7 = (bf16[128,4096]{1,0:T(8,128)(2,1)S(1)}, bf16[128,4096]{1,0:T(8,128)(2,1)S(1)}, u32[]{:S(2)}, u32[]{:S(2)}) collective-permute-start(bf16[128,4096]{1,0:T(8,128)(2,1)S(1)} %get-tuple-element.42.refs_4_.refs_0_), channel_id=1, source_target_pairs={{0,8},{16,24},{1,9},{17,25},{2,10},{18,26},{3,11},{19,27},{4,12},{... | collective-permute-start | bytes 3145736 | tf_op jit(solution)/shard_map/ppermute | solution.py:390
  50.6 10.0 %collective-permute-start.8 = (bf16[128,4096]{1,0:T(8,128)(2,1)S(1)}, bf16[128,4096]{1,0:T(8,128)(2,1)}, u32[]{:S(2)}, u32[]{:S(2)}) collective-permute-start(bf16[128,4096]{1,0:T(8,128)(2,1)S(1)} %encode.4.refs_5_.refs_1_), channel_id=1, source_target_pairs={{0,8},{16,24},{1,9},{17,25},{2,10},{18,26},{3,11},{19,27},{4,12},{... | collective-permute-start | bytes 3145736 | tf_op jit(solution)/shard_map/ppermute | solution.py:390
  52.9 33.7 %collective-permute-start.15 = (bf16[128,4096]{1,0:T(8,128)(2,1)}, bf16[128,4096]{1,0:T(8,128)(2,1)S(1)}, u32[]{:S(2)}, u32[]{:S(2)}) collective-permute-start(bf16[128,4096]{1,0:T(8,128)(2,1)} %get-tuple-element.57), channel_id=1, source_target_pairs={{0,16},{8,24},{1,17},{9,25},{2,18},{10,26},{3,19},{11,27},{4,20},{... | collective-permute-start | bytes 3145736 | tf_op jit(solution)/shard_map/ppermute | solution.py:384
  54.2 44.6 %collective-permute-start.13 = (bf16[128,4096]{1,0:T(8,128)(2,1)S(1)}, bf16[128,4096]{1,0:T(8,128)(2,1)}, u32[]{:S(2)}, u32[]{:S(2)}) collective-permute-start(bf16[128,4096]{1,0:T(8,128)(2,1)S(1)} %encode.4.refs_5_.refs_1_), channel_id=1, source_target_pairs={{0,16},{8,24},{1,17},{9,25},{2,18},{10,26},{3,19},{11,27},{4,20},{... | collective-permute-start | bytes 3145736 | tf_op jit(solution)/shard_map/ppermute | solution.py:384
  55.5 5.1 %collective-permute-start.12 = (bf16[64,4096]{1,0:T(8,128)(2,1)}, bf16[64,4096]{1,0:T(8,128)(2,1)}, u32[]{:S(2)}, u32[]{:S(2)}) collective-permute-start(bf16[64,4096]{1,0:T(8,128)(2,1)} %collective-permute-done.9.refs_7_), channel_id=1, source_target_pairs={{16,24},{24,16},{17,25},{25,17},{18,26},{26,18},{19,27},{27,19},{2... | collective-permute-start | bytes 1572872 | tf_op jit(solution)/shard_map/ppermute | solution.py:387
  57.4 4.1 %collective-permute-start.11 = (bf16[64,4096]{1,0:T(8,128)(2,1)}, bf16[64,4096]{1,0:T(8,128)(2,1)S(1)}, u32[]{:S(2)}, u32[]{:S(2)}) collective-permute-start(bf16[64,4096]{1,0:T(8,128)(2,1)} %collective-permute-done.6.refs_6_), channel_id=1, source_target_pairs={{16,24},{24,16},{17,25},{25,17},{18,26},{26,18},{19,27},{27,19},{2... | collective-permute-start | bytes 1572872 | tf_op jit(solution)/shard_map/ppermute | solution.py:387
  86.6 16.0 %collective-permute-start.16 = (bf16[128,4096]{1,0:T(8,128)(2,1)S(1)}, bf16[128,4096]{1,0:T(8,128)(2,1)S(1)}, u32[]{:S(2)}, u32[]{:S(2)}) collective-permute-start(bf16[128,4096]{1,0:T(8,128)(2,1)S(1)} %collective-permute-done.15.refs_6_.refs_0_), channel_id=1, source_target_pairs={{16,24},{24,16},{17,25},{25,17},{18,26},{26,18},{19,27},{27,19},{2... | collective-permute-start | bytes 3145736 | tf_op jit(solution)/shard_map/ppermute | solution.py:387
  98.8 4.8 %collective-permute-start.14 = (bf16[128,4096]{1,0:T(8,128)(2,1)}, bf16[128,4096]{1,0:T(8,128)(2,1)S(1)}, u32[]{:S(2)}, u32[]{:S(2)}) collective-permute-start(bf16[128,4096]{1,0:T(8,128)(2,1)} %collective-permute-done.13.refs_0_), channel_id=1, source_target_pairs={{16,24},{24,16},{17,25},{25,17},{18,26},{26,18},{19,27},{27,19},{2... | collective-permute-start | bytes 3145736 | tf_op jit(solution)/shard_map/ppermute | solution.py:387
  100.7 27.8 %collective-permute-start.23 = (bf16[128,4096]{1,0:T(8,128)(2,1)}, bf16[128,4096]{1,0:T(8,128)(2,1)}, u32[]{:S(2)}, u32[]{:S(2)}) collective-permute-start(bf16[128,4096]{1,0:T(8,128)(2,1)} %get-tuple-element.67), channel_id=1, source_target_pairs={{0,16},{8,24},{1,17},{9,25},{2,18},{10,26},{3,19},{11,27},{4,20},{... | collective-permute-start | bytes 3145736 | tf_op jit(solution)/shard_map/ppermute | solution.py:384
  102.0 22.5 %collective-permute-start.17 = (bf16[4,128,256]{2,1,0:T(8,128)(2,1)}, bf16[4,128,256]{2,1,0:T(8,128)(2,1)S(1)}, u32[]{:S(2)}, u32[]{:S(2)}) collective-permute-start(bf16[4,128,256]{2,1,0:T(8,128)(2,1)} %get-tuple-element.52.refs_5_), channel_id=1, source_target_pairs={{0,1},{1,0},{2,3},{3,2},{4,5},{5,4},{6,7},{7,6},{8,9},{9,8},{10,11... | collective-permute-start | bytes 786440 | tf_op jit(solution)/shard_map/ppermute | solution.py:16
  112.2 12.3 %collective-permute-start.18 = (bf16[4,128,256]{2,1,0:T(8,128)(2,1)}, bf16[4,128,256]{2,1,0:T(8,128)(2,1)S(1)}, u32[]{:S(2)}, u32[]{:S(2)}) collective-permute-start(bf16[4,128,256]{2,1,0:T(8,128)(2,1)} %get-tuple-element.60.refs_5_), channel_id=1, source_target_pairs={{0,1},{1,0},{2,3},{3,2},{4,5},{5,4},{6,7},{7,6},{8,9},{9,8},{10,11... | collective-permute-start | bytes 786440 | tf_op jit(solution)/shard_map/ppermute | solution.py:16
  128.5 18.4 %collective-permute-start.24 = (bf16[128,4096]{1,0:T(8,128)(2,1)}, bf16[128,4096]{1,0:T(8,128)(2,1)S(1)}, u32[]{:S(2)}, u32[]{:S(2)}) collective-permute-start(bf16[128,4096]{1,0:T(8,128)(2,1)} %collective-permute-done.23.refs_0_), channel_id=1, source_target_pairs={{16,24},{24,16},{17,25},{25,17},{18,26},{26,18},{19,27},{27,19},{2... | collective-permute-start | bytes 3145736 | tf_op jit(solution)/shard_map/ppermute | solution.py:387
  130.6 7.3 %collective-permute-start.19 = (bf16[256,256]{1,0:T(8,128)(2,1)S(1)}, bf16[256,256]{1,0:T(8,128)(2,1)S(1)}, u32[]{:S(2)}, u32[]{:S(2)}) collective-permute-start(bf16[256,256]{1,0:T(8,128)(2,1)S(1)} %get-tuple-element.63), channel_id=1, source_target_pairs={{0,2},{1,3},{2,0},{3,1},{4,6},{5,7},{6,4},{7,5},{8,10},{9,11},{10,... | collective-permute-start | bytes 393224 | tf_op jit(solution)/shard_map/ppermute | solution.py:16
  133.1 7.1 %collective-permute-start.20 = (bf16[256,256]{1,0:T(8,128)(2,1)S(1)}, bf16[256,256]{1,0:T(8,128)(2,1)S(1)}, u32[]{:S(2)}, u32[]{:S(2)}) collective-permute-start(bf16[256,256]{1,0:T(8,128)(2,1)S(1)} %get-tuple-element.64), channel_id=1, source_target_pairs={{0,4},{1,5},{2,6},{3,7},{4,0},{5,1},{6,2},{7,3},{8,12},{9,13},{10,... | collective-permute-start | bytes 393224 | tf_op jit(solution)/shard_map/ppermute | solution.py:16
  135.9 11.0 %collective-permute-start.21 = (bf16[256,256]{1,0:T(8,128)(2,1)S(1)}, bf16[256,256]{1,0:T(8,128)(2,1)S(1)}, u32[]{:S(2)}, u32[]{:S(2)}) collective-permute-start(bf16[256,256]{1,0:T(8,128)(2,1)S(1)} %get-tuple-element.65), channel_id=1, source_target_pairs={{0,6},{1,7},{2,4},{3,5},{4,2},{5,3},{6,0},{7,1},{8,14},{9,15},{10,... | collective-permute-start | bytes 393224 | tf_op jit(solution)/shard_map/ppermute | solution.py:16
  137.4 19.4 %collective-permute-start.22 = (bf16[4,128,256]{2,1,0:T(8,128)(2,1)}, bf16[4,128,256]{2,1,0:T(8,128)(2,1)S(1)}, u32[]{:S(2)}, u32[]{:S(2)}) collective-permute-start(bf16[4,128,256]{2,1,0:T(8,128)(2,1)} %get-tuple-element.61.refs_4_.refs_5_), channel_id=1, source_target_pairs={{0,1},{1,0},{2,3},{3,2},{4,5},{5,4},{6,7},{7,6},{8,9},{9,8},{10,11... | collective-permute-start | bytes 786440 | tf_op jit(solution)/shard_map/ppermute | solution.py:16
  156.2 8.1 %collective-permute-start.28 = (bf16[4,128,256]{2,1,0:T(8,128)(2,1)}, bf16[4,128,256]{2,1,0:T(8,128)(2,1)S(1)}, u32[]{:S(2)}, u32[]{:S(2)}) collective-permute-start(bf16[4,128,256]{2,1,0:T(8,128)(2,1)} %get-tuple-element.69.refs_2_), channel_id=1, source_target_pairs={{0,1},{1,0},{2,3},{3,2},{4,5},{5,4},{6,7},{7,6},{8,9},{9,8},{10,11... | collective-permute-start | bytes 786440 | tf_op jit(solution)/shard_map/ppermute | solution.py:16
  158.3 5.8 %collective-permute-start.25 = (bf16[128,256]{1,0:T(8,128)(2,1)S(1)}, bf16[128,256]{1,0:T(8,128)(2,1)S(1)}, u32[]{:S(2)}, u32[]{:S(2)}) collective-permute-start(bf16[128,256]{1,0:T(8,128)(2,1)S(1)} %get-tuple-element.71), channel_id=1, source_target_pairs={{0,2},{1,3},{2,0},{3,1},{4,6},{5,7},{6,4},{7,5},{8,10},{9,11},{10,... | collective-permute-start | bytes 196616 | tf_op jit(solution)/shard_map/ppermute | solution.py:16
  160.7 11.4 %collective-permute-start.26 = (bf16[128,256]{1,0:T(8,128)(2,1)S(1)}, bf16[128,256]{1,0:T(8,128)(2,1)S(1)}, u32[]{:S(2)}, u32[]{:S(2)}) collective-permute-start(bf16[128,256]{1,0:T(8,128)(2,1)S(1)} %get-tuple-element.72), channel_id=1, source_target_pairs={{0,4},{1,5},{2,6},{3,7},{4,0},{5,1},{6,2},{7,3},{8,12},{9,13},{10,... | collective-permute-start | bytes 196616 | tf_op jit(solution)/shard_map/ppermute | solution.py:16
  162.7 9.4 %collective-permute-start.27 = (bf16[128,256]{1,0:T(8,128)(2,1)S(1)}, bf16[128,256]{1,0:T(8,128)(2,1)S(1)}, u32[]{:S(2)}, u32[]{:S(2)}) collective-permute-start(bf16[128,256]{1,0:T(8,128)(2,1)S(1)} %get-tuple-element.73), channel_id=1, source_target_pairs={{0,6},{1,7},{2,4},{3,5},{4,2},{5,3},{6,0},{7,1},{8,14},{9,15},{10,... | collective-permute-start | bytes 196616 | tf_op jit(solution)/shard_map/ppermute | solution.py:16
  166.0 6.2 %collective-permute-start.29 = (bf16[128,256]{1,0:T(8,128)(2,1)S(1)}, bf16[128,256]{1,0:T(8,128)(2,1)S(1)}, u32[]{:S(2)}, u32[]{:S(2)}) collective-permute-start(bf16[128,256]{1,0:T(8,128)(2,1)S(1)} %get-tuple-element.76), channel_id=1, source_target_pairs={{0,2},{1,3},{2,0},{3,1},{4,6},{5,7},{6,4},{7,5},{8,10},{9,11},{10,... | collective-permute-start | bytes 196616 | tf_op jit(solution)/shard_map/ppermute | solution.py:16
  168.7 7.3 %collective-permute-start.30 = (bf16[128,256]{1,0:T(8,128)(2,1)S(1)}, bf16[128,256]{1,0:T(8,128)(2,1)S(1)}, u32[]{:S(2)}, u32[]{:S(2)}) collective-permute-start(bf16[128,256]{1,0:T(8,128)(2,1)S(1)} %get-tuple-element.77), channel_id=1, source_target_pairs={{0,4},{1,5},{2,6},{3,7},{4,0},{5,1},{6,2},{7,3},{8,12},{9,13},{10,... | collective-permute-start | bytes 196616 | tf_op jit(solution)/shard_map/ppermute | solution.py:16
  170.7 6.1 %collective-permute-start.31 = (bf16[128,256]{1,0:T(8,128)(2,1)S(1)}, bf16[128,256]{1,0:T(8,128)(2,1)S(1)}, u32[]{:S(2)}, u32[]{:S(2)}) collective-permute-start(bf16[128,256]{1,0:T(8,128)(2,1)S(1)} %get-tuple-element.78), channel_id=1, source_target_pairs={{0,6},{1,7},{2,4},{3,5},{4,2},{5,3},{6,0},{7,1},{8,14},{9,15},{10,... | collective-permute-start | bytes 196616 | tf_op jit(solution)/shard_map/ppermute | solution.py:16
  (27 other events, 296.7 us)

commit v10 on v8

--- a/solution.py
+++ b/solution.py
@@ -117,7 +117,7 @@
     weights, out, sent, base, *kept = refs[:6]
     total, rings, ring_sems, kept_sems, base_sem = refs[-5:]
     step, steps = pl.program_id(0), pl.num_programs(0)
-    slots, block = rings.shape[1], rings.shape[2]
+    slots, block = rings.shape[0], rings.shape[1] // 2
     odd, upper = info[0] == 1, info[1] == 1
 
     def rows(k):
@@ -126,7 +126,9 @@
     def fetch(source, k):
         slot = lax.rem(k, slots)
         return pltpu.make_async_copy(
-            weights.at[0, source, rows(k)], rings.at[source, slot], ring_sems.at[source, slot]
+            weights.at[0, source, rows(k)],
+            rings.at[slot, pl.ds(source * block, block)],
+            ring_sems.at[source, slot],
         )
 
     def keep(source, k):
@@ -153,22 +155,25 @@
 
     pl.when(step + slots - 1 < steps)(lambda: fetch_all(step + slots - 1))
 
+    def stacked(parts):
+        values = [part[...] for part in parts]
+        return values[0] if len(values) == 1 else jnp.concatenate(values, axis=0)
+
     def product(parts, weight):
-        values = [part[...] for part in parts]
-        acts = values[0] if len(values) == 1 else jnp.concatenate(values, axis=0)
-        return jnp.dot(acts, weight, preferred_element_type=jnp.float32)
+        return jnp.dot(stacked(parts), weight, preferred_element_type=jnp.float32)
 
     slot = lax.rem(step, slots)
     fetch(0, step).wait()
 
     @pl.when(jnp.logical_not(odd))
     def _():
-        total[...] += product(mine, rings[0, slot])
+        total[...] += product(mine, rings[slot, pl.ds(0, block), :])
 
     @pl.when(odd)
     def _():
         fetch(1, step).wait()
-        total[...] += product(mine, rings[0, slot]) + product(theirs, rings[1, slot])
+        both = jnp.concatenate([stacked(mine), stacked(theirs)], axis=1)
+        total[...] += jnp.dot(both, rings[slot], preferred_element_type=jnp.float32)
 
     done = out.shape[1]
 
@@ -219,7 +224,7 @@
             ],
             scratch_shapes=[
                 pltpu.VMEM((rows, width), jnp.float32),
-                pltpu.VMEM((2, SLOTS, block, width), decoder.dtype),
+                pltpu.VMEM((SLOTS, 2 * block, width), decoder.dtype),
                 pltpu.SemaphoreType.DMA((2, SLOTS)),
                 pltpu.SemaphoreType.DMA((2, steps)),
                 pltpu.SemaphoreType.DMA,
@@ -401,15 +406,15 @@
     order = []
     for k in range(others // 2):
         order += [(k, 0, size), (others // 2, k * size, size)]
-    a2, a2a, a2b = encode(
+    (a2,) = encode(
         far[1:] + [rest],
         order,
-        [(0, others * size), (0, (others - 2) * size), ((others - 2) * size, 2 * size)],
+        [(0, others * size)],
         encoder_kept,
         encoder_bias,
         [a1, d0a],
     )
-    d2, d3, n2 = up(a2a), up(a2b), beside(after(a2, d0b))
+    d2, n2 = up(a2), beside(after(a2, d0b))
 
     c0a, c0b = across(after(d0a, n2)), across(after(d0b, n2))
     mine, sent, base, *kept = decode_first(
@@ -425,19 +430,19 @@
         parts = [part if q == 0 else exchange(part, "feat", 2 * q) for q, part in enumerate(sums)]
         return [(2 * q, blocks) for q in range(len(parts))], parts
 
-    def later(number, direct, swapped, *earlier):
+    def later(number, direct, swapped, skip, *earlier):
         row = (slots[number][0] - slots[1][0]) * size
-        order = [(0, 0, len(slots[number]) * size)]
+        order = [(0, skip * size, len(slots[number]) * size)]
         return decode_later(info, [direct], [swapped], order, base, kept, row, shards, list(earlier))
 
-    c1, c2 = across(after(d1, sent)), across(after(d2, sent))
-    mine1, sent1 = later(1, d1, c1, sent, d2)
+    c1 = across(after(d1, sent))
+    mine1, sent1 = later(1, d1, c1, 0, sent)
     met1 = meet([mine, mine1], [sent, sent1])
     where1, parts1 = spread(slots[0] + slots[1], met1)
-    c3 = across(after(d3, met1[0]))
-    mine2, sent2 = later(2, d2, c2, met1[0])
+    c2 = across(after(d2, met1[0]))
+    mine2, sent2 = later(2, d2, c2, 0, met1[0])
     total = add_up(info, targets[0], -1.0, where1, parts1, [sent2])
-    mine3, sent3 = later(3, d3, c3, sent2, total)
+    mine3, sent3 = later(3, d2, c2, others - 2, sent2, total)
     met2 = meet([mine2], [sent2], sent3)
     where2, parts2 = spread(slots[2], met2)
     met3 = meet([mine3], [sent3], parts2[1])

time: 175 us -> 177 us (1.011)
  local copies, waits for them, and re-layouts: 10.4 us -> 14.8 us
  starting transfers between devices: 58.7 us -> 54.6 us
    unnamed x50, local copies, waits for them, and re-layouts: 9.78 us -> 14.1 us
    ppermute x5 -> x4, waiting for transfers between devices: 4.8 us -> 0.52 us  [up(): return lax.ppermute(a, 'layer', [(i, i + half) for i in range(half)])]
    ppermute x19, waiting for transfers between devices: 28.4 us -> 31.6 us  [exchange(): return lax.ppermute(array, axis, [(i, i ^ flip) for i in range(size)])]
    ppermute x5 -> x4, waiting for transfers between devices: 0.61 us -> 3.12 us  [across(): return lax.ppermute(a, 'layer', [(i, i ^ 1) for i in range(half, layers)])]
    ppermute x5 -> x4, starting transfers between devices: 19.5 us -> 17.7 us  [across(): return lax.ppermute(a, 'layer', [(i, i ^ 1) for i in range(half, layers)])]
    ppermute x5 -> x4, starting transfers between devices: 6.43 us -> 5.14 us  [up(): return lax.ppermute(a, 'layer', [(i, i + half) for i in range(half)])]
  transfers between devices with their start and end apart: 32 -> 30, of which waited for: 11 -> 12; matrix products, arithmetic and copies ran while one was open for 0% -> 0% of each run, Pallas kernels for 40% -> 40%
where the time goes in v10:
time: 177 us; the launch traced here: 176 us
  Pallas kernels  71.4 us (40%)
  starting transfers between devices  54.6 us (31%)
  waiting for transfers between devices  35.2 us (20%)
  local copies, waits for them, and re-layouts  14.8 us (8%)
    ppermute x19, waiting for transfers between devices, exchange(): return lax.ppermute(array, axis, [(i, i ^ flip) for i in range(size)])  31.6 us
    ppermute x19, starting transfers between devices, exchange(): return lax.ppermute(array, axis, [(i, i ^ flip) for i in range(size)])  26.7 us
    pallas_call x3, Pallas kernels, decode_later(): pl.pallas_call(functools.partial(later_wave_kernel, order, row, len(direc...  25.1 us
    pallas_call x1, Pallas kernels, decode_first(): pl.pallas_call(functools.partial(first_wave_kernel, [len(parts) for parts...  24.2 us
    ppermute x4, starting transfers between devices, across(): return lax.ppermute(a, 'layer', [(i, i ^ 1) for i in range(half, layers)])  17.7 us
    pallas_call x3, Pallas kernels, encode(): pl.pallas_call(functools.partial(encode_kernel, order, pieces, len(parts)...  17.4 us
    unnamed x50, local copies, waits for them, and re-layouts  14.1 us
    ppermute x4, starting transfers between devices, up(): return lax.ppermute(a, 'layer', [(i, i + half) for i in range(half)])  5.14 us
  transfers between devices with their start and end apart: 30, of which 12 were waited for; matrix products, arithmetic and copies ran while one was open for 0% of the time, Pallas kernels for 40%

profile of v10, /device:TPU:2, one launch (start us, length us, event | category | flops | bytes accessed | tf_op | source)
XLA Modules:
  0.0 176.4 jit_solution(4538720711431545839)
XLA Ops:
  0.0 1.5 collective-permute-start
  1.5 2.6 %collective-permute-start.3 = (bf16[64,2048]{1,0:T(8,128)(2,1)}, bf16[64,2048]{1,0:T(8,128)(2,1)S(1)}, u32[]{:S(2)}, u32[]{:S(2)}) collective-permute-start(bf16[64,2048]{1,0:T(8,128)(2,1)} %bitcast.11), channel_id=1, source_target_pairs={{0,4},{1,5},{2,6},{3,7},{4,0},{5,1},{6,2},{7,3},{8,12},{9,13},{10,... | collective-permute-start | bytes 786440 | tf_op jit(solution)/shard_map/ppermute | solution.py:16
  5.7 2.6 %collective-permute-done.refs_1_ = bf16[64,2048]{1,0:T(8,128)(2,1)S(1)} collective-permute-done((bf16[64,2048]{1,0:T(8,128)(2,1)}, bf16[64,2048]{1,0:T(8,128)(2,1)S(1)}, u32[]{:S(2)}, u32[]{:S(2)}) %collective-permute-start) | collective-permute-done | bytes 262176 | tf_op jit(solution)/shard_map/ppermute | solution.py:16
  8.3 1.6 collective-permute-start.2
  11.5 6.5 %encode.3 = (bf16[128,4096]{1,0:T(8,128)(2,1)S(1)}, bf16[64,4096]{1,0:T(8,128)(2,1)S(1)}, bf16[64,4096]{1,0:T(8,128)(2,1)S(1)}, bf16[1,2048,4096]{2,1,0:T(8,128)(2,1)S(1)}) custom-call(bf16[64,2048]{1,0:T(8,128)(2,1)S(1)} %bitcast.14, bf16[64,2048]{1,0:T(8,128)(2,1)S(1)} %collective-permute-done.refs_1_, bf16[1,2048,4096]{2,1,0:T(8,128)(2,1)} %refs_2_.1, ...), custom_call_target="tpu_custom_call" | custom-call | tf_op jit(solution)/shard_map/encode/pallas_call | solution.py:80
  19.3 3.5 %collective-permute-done.3.refs_0_ = bf16[64,2048]{1,0:T(8,128)(2,1)S(1)} collective-permute-done((bf16[64,2048]{1,0:T(8,128)(2,1)}, bf16[64,2048]{1,0:T(8,128)(2,1)S(1)}, u32[]{:S(2)}, u32[]{:S(2)}) %collective-permute-start.3) | collective-permute-done | bytes 262176 | tf_op jit(solution)/shard_map/ppermute | solution.py:16
  22.9 2.1 %collective-permute-done.1.refs_0_ = bf16[64,2048]{1,0:T(8,128)(2,1)S(1)} collective-permute-done((bf16[64,2048]{1,0:T(8,128)(2,1)}, bf16[64,2048]{1,0:T(8,128)(2,1)S(1)}, u32[]{:S(2)}, u32[]{:S(2)}) %collective-permute-start.1) | collective-permute-done | bytes 262176 | tf_op jit(solution)/shard_map/ppermute | solution.py:16
  25.0 3.6 %collective-permute-done.2.refs_1_ = bf16[64,2048]{1,0:T(8,128)(2,1)S(1)} collective-permute-done((bf16[64,2048]{1,0:T(8,128)(2,1)S(1)}, bf16[64,2048]{1,0:T(8,128)(2,1)S(1)}, u32[]{:S(2)}, u32[]{:S(2)}) %collective-permute-start.2) | collective-permute-done | bytes 262176 | tf_op jit(solution)/shard_map/ppermute | solution.py:16
  30.4 3.8 %encode.4.refs_5_.refs_1_ = bf16[128,4096]{1,0:T(8,128)(2,1)S(1)} custom-call(bf16[64,2048]{1,0:T(8,128)(2,1)S(1)} %collective-permute-done.1.refs_0_, bf16[64,2048]{1,0:T(8,128)(2,1)S(1)} %collective-permute-done.2.refs_1_, bf16[1,2048,4096]{2,1,0:T(8,128)(2,1)S(1)} %get-tuple-element.39.refs_2_.refs_3_, f32[1,4096]{1,0:T(1,128)S(1)} %copy-done.19, ...), custom_call_target="tpu_custom_call" | custom-call | tf_op jit(solution)/shard_map/encode/pallas_call | solution.py:80
  34.2 6.4 %collective-permute-done.5.refs_2_ = bf16[128,2048]{1,0:T(8,128)(2,1)S(1)} collective-permute-done((bf16[128,2048]{1,0:T(8,128)(2,1)S(1)}, bf16[128,2048]{1,0:T(8,128)(2,1)S(1)}, u32[]{:S(2)}, u32[]{:S(2)}) %collective-permute-start.5) | collective-permute-done | bytes 524320 | tf_op jit(solution)/shard_map/ppermute | solution.py:16
  40.6 7.1 %encode.5.refs_2_ = bf16[256,4096]{1,0:T(8,128)(2,1)} custom-call(bf16[64,2048]{1,0:T(8,128)(2,1)S(1)} %collective-permute-done.3.refs_0_, bf16[64,2048]{1,0:T(8,128)(2,1)S(1)} %collective-permute-done.4.refs_1_, bf16[128,2048]{1,0:T(8,128)(2,1)S(1)} %collective-permute-done.5.refs_2_, bf16[1,2048,4096]{2,1,0:T(8,128)(2,1)S(1)} %get-tuple-element.39.refs_2_.refs_3_, ...), custom_call_target="tpu_custom_call" | custom-call | tf_op jit(solution)/shard_map/encode/pallas_call | solution.py:80
  50.6 2.3 %collective-permute-start.8 = (bf16[128,4096]{1,0:T(8,128)(2,1)S(1)}, bf16[128,4096]{1,0:T(8,128)(2,1)}, u32[]{:S(2)}, u32[]{:S(2)}) collective-permute-start(bf16[128,4096]{1,0:T(8,128)(2,1)S(1)} %encode.4.refs_5_.refs_1_), channel_id=1, source_target_pairs={{0,8},{16,24},{1,9},{17,25},{2,10},{18,26},{3,11},{19,27},{4,12},{... | collective-permute-start | bytes 3145736 | tf_op jit(solution)/shard_map/ppermute | solution.py:374
  55.4 1.9 %collective-permute-start.12 = (bf16[64,4096]{1,0:T(8,128)(2,1)}, bf16[64,4096]{1,0:T(8,128)(2,1)}, u32[]{:S(2)}, u32[]{:S(2)}) collective-permute-start(bf16[64,4096]{1,0:T(8,128)(2,1)} %collective-permute-done.9.refs_7_), channel_id=1, source_target_pairs={{16,24},{24,16},{17,25},{25,17},{18,26},{26,18},{19,27},{27,19},{2... | collective-permute-start | bytes 1572872 | tf_op jit(solution)/shard_map/ppermute | solution.py:371
  57.4 2.4 %collective-permute-start.11 = (bf16[64,4096]{1,0:T(8,128)(2,1)}, bf16[64,4096]{1,0:T(8,128)(2,1)}, u32[]{:S(2)}, u32[]{:S(2)}) collective-permute-start(bf16[64,4096]{1,0:T(8,128)(2,1)} %collective-permute-done.6.refs_6_), channel_id=1, source_target_pairs={{16,24},{24,16},{17,25},{25,17},{18,26},{26,18},{19,27},{27,19},{2... | collective-permute-start | bytes 1572872 | tf_op jit(solution)/shard_map/ppermute | solution.py:371
  61.7 24.2 %decode_first.1 = (f32[4,128,256]{2,1,0:T(8,128)}, bf16[4,128,256]{2,1,0:T(8,128)(2,1)}, f32[384,2048]{1,0:T(8,128)}, bf16[4096,2048]{1,0:T(8,128)(2,1)S(1)}, bf16[4096,2048]{1,0:T(8,128)(2,1)S(1)}) custom-call(s32[7]{0:T(128)} %stack.31.info, bf16[128,4096]{1,0:T(8,128)(2,1)} %copy-done.7, bf16[128,4096]{1,0:T(8,128)(2,1)} %copy-done, ...), custom_call_target="tpu_custom_call" | custom-call | tf_op jit(solution)/shard_map/decode_first/pallas_call | solution.py:213
  85.9 11.3 %collective-permute-start.14 = (bf16[128,4096]{1,0:T(8,128)(2,1)}, bf16[128,4096]{1,0:T(8,128)(2,1)S(1)}, u32[]{:S(2)}, u32[]{:S(2)}) collective-permute-start(bf16[128,4096]{1,0:T(8,128)(2,1)} %collective-permute-done.13.refs_0_), channel_id=1, source_target_pairs={{16,24},{24,16},{17,25},{25,17},{18,26},{26,18},{19,27},{27,19},{2... | collective-permute-start | bytes 3145736 | tf_op jit(solution)/shard_map/ppermute | solution.py:371
  97.9 1.9 %collective-permute-done.14.refs_1_ = bf16[128,4096]{1,0:T(8,128)(2,1)S(1)} collective-permute-done((bf16[128,4096]{1,0:T(8,128)(2,1)}, bf16[128,4096]{1,0:T(8,128)(2,1)S(1)}, u32[]{:S(2)}, u32[]{:S(2)}) %collective-permute-start.14) | collective-permute-done | bytes 1048608 | tf_op jit(solution)/shard_map/ppermute | solution.py:371
  99.8 8.7 %decode_later.3 = (f32[4,128,256]{2,1,0:T(8,128)}, bf16[4,128,256]{2,1,0:T(8,128)(2,1)}) custom-call(s32[7]{0:T(128)} %stack.31.info, bf16[128,4096]{1,0:T(8,128)(2,1)} %collective-permute-done.13.refs_0_, bf16[128,4096]{1,0:T(8,128)(2,1)S(1)} %collective-permute-done.14.refs_1_, f32[384,2048]{1,0:T(8,128)} %get-tuple-element.49.refs_2_, ...), custom_call_target="tpu_custom_call" | custom-call | tf_op jit(solution)/shard_map/decode_later/pallas_call | solution.py:271
  109.0 8.3 %collective-permute-done.16.refs_3_ = bf16[4,128,256]{2,1,0:T(8,128)(2,1)S(1)} collective-permute-done((bf16[4,128,256]{2,1,0:T(8,128)(2,1)}, bf16[4,128,256]{2,1,0:T(8,128)(2,1)S(1)}, u32[]{:S(2)}, u32[]{:S(2)}) %collective-permute-start.16) | collective-permute-done | bytes 262176 | tf_op jit(solution)/shard_map/ppermute | solution.py:16
  120.9 2.1 %collective-permute-start.21 = (bf16[256,4096]{1,0:T(8,128)(2,1)S(1)}, bf16[256,4096]{1,0:T(8,128)(2,1)S(1)}, u32[]{:S(2)}, u32[]{:S(2)}) collective-permute-start(bf16[256,4096]{1,0:T(8,128)(2,1)S(1)} %collective-permute-done.20.refs_0_), channel_id=1, source_target_pairs={{16,24},{24,16},{17,25},{25,17},{18,26},{26,18},{19,27},{27,19},{2... | collective-permute-start | bytes 6291464 | tf_op jit(solution)/shard_map/ppermute | solution.py:371
  124.3 2.5 %collective-permute-start.17 = (bf16[256,256]{1,0:T(8,128)(2,1)}, bf16[256,256]{1,0:T(8,128)(2,1)S(1)}, u32[]{:S(2)}, u32[]{:S(2)}) collective-permute-start(bf16[256,256]{1,0:T(8,128)(2,1)} %get-tuple-element.55), channel_id=1, source_target_pairs={{0,2},{1,3},{2,0},{3,1},{4,6},{5,7},{6,4},{7,5},{8,10},{9,11},{10,... | collective-permute-start | bytes 393224 | tf_op jit(solution)/shard_map/ppermute | solution.py:16
  126.8 2.7 %collective-permute-start.18 = (bf16[256,256]{1,0:T(8,128)(2,1)}, bf16[256,256]{1,0:T(8,128)(2,1)S(1)}, u32[]{:S(2)}, u32[]{:S(2)}) collective-permute-start(bf16[256,256]{1,0:T(8,128)(2,1)} %get-tuple-element.56), channel_id=1, source_target_pairs={{0,4},{1,5},{2,6},{3,7},{4,0},{5,1},{6,2},{7,3},{8,12},{9,13},{10,... | collective-permute-start | bytes 393224 | tf_op jit(solution)/shard_map/ppermute | solution.py:16
  132.4 1.6 copy-done.2
  134.0 1.6 copy-done.4
  135.5 8.2 %decode_later.4 = (f32[4,128,256]{2,1,0:T(8,128)}, bf16[4,128,256]{2,1,0:T(8,128)(2,1)}) custom-call(s32[7]{0:T(128)} %stack.31.info, bf16[256,4096]{1,0:T(8,128)(2,1)S(1)} %copy-done.2, bf16[256,4096]{1,0:T(8,128)(2,1)S(1)} %copy-done.4, f32[384,2048]{1,0:T(8,128)} %get-tuple-element.49.refs_2_, bf16[4096,2048]{1,0:T(8,128)(2,1)S(1)} %get-tuple-element.50.refs_3_, ...), custom_call_target="tpu_custom_call" | custom-call | tf_op jit(solution)/shard_map/decode_later/pallas_call | solution.py:271
  146.8 8.2 %decode_later.5 = (f32[4,128,256]{2,1,0:T(8,128)}, bf16[4,128,256]{2,1,0:T(8,128)(2,1)}) custom-call(s32[7]{0:T(128)} %stack.31.info, bf16[256,4096]{1,0:T(8,128)(2,1)S(1)} %copy-done.2, bf16[256,4096]{1,0:T(8,128)(2,1)S(1)} %copy-done.4, f32[384,2048]{1,0:T(8,128)} %get-tuple-element.49.refs_2_, bf16[4096,2048]{1,0:T(8,128)(2,1)S(1)} %get-tuple-element.50.refs_3_, ...), custom_call_target="tpu_custom_call" | custom-call | tf_op jit(solution)/shard_map/decode_later/pallas_call | solution.py:271
  155.1 1.6 collective-permute-start.26
  158.8 2.4 %collective-permute-start.24 = (bf16[128,256]{1,0:T(8,128)(2,1)S(1)}, bf16[128,256]{1,0:T(8,128)(2,1)S(1)}, u32[]{:S(2)}, u32[]{:S(2)}) collective-permute-start(bf16[128,256]{1,0:T(8,128)(2,1)S(1)} %get-tuple-element.64), channel_id=1, source_target_pairs={{0,4},{1,5},{2,6},{3,7},{4,0},{5,1},{6,2},{7,3},{8,12},{9,13},{10,... | collective-permute-start | bytes 196616 | tf_op jit(solution)/shard_map/ppermute | solution.py:16
  165.5 2.4 %collective-permute-start.28 = (bf16[128,256]{1,0:T(8,128)(2,1)S(1)}, bf16[128,256]{1,0:T(8,128)(2,1)S(1)}, u32[]{:S(2)}, u32[]{:S(2)}) collective-permute-start(bf16[128,256]{1,0:T(8,128)(2,1)S(1)} %get-tuple-element.69), channel_id=1, source_target_pairs={{0,4},{1,5},{2,6},{3,7},{4,0},{5,1},{6,2},{7,3},{8,12},{9,13},{10,... | collective-permute-start | bytes 196616 | tf_op jit(solution)/shard_map/ppermute | solution.py:16
  169.3 2.7 %collective-permute-done.28.refs_6_ = bf16[128,256]{1,0:T(8,128)(2,1)S(1)} collective-permute-done((bf16[128,256]{1,0:T(8,128)(2,1)S(1)}, bf16[128,256]{1,0:T(8,128)(2,1)S(1)}, u32[]{:S(2)}, u32[]{:S(2)}) %collective-permute-start.28) | collective-permute-done | bytes 65568 | tf_op jit(solution)/shard_map/ppermute | solution.py:16
  172.0 1.9 %collective-permute-done.29.refs_7_ = bf16[128,256]{1,0:T(8,128)(2,1)S(1)} collective-permute-done((bf16[128,256]{1,0:T(8,128)(2,1)S(1)}, bf16[128,256]{1,0:T(8,128)(2,1)S(1)}, u32[]{:S(2)}, u32[]{:S(2)}) %collective-permute-start.29) | collective-permute-done | bytes 65568 | tf_op jit(solution)/shard_map/ppermute | solution.py:16
  174.9 1.5 add_up.3
  (92 shorter events, 34.5 us)
Async XLA Ops:
  0.0 8.3 %collective-permute-start = (bf16[64,2048]{1,0:T(8,128)(2,1)}, bf16[64,2048]{1,0:T(8,128)(2,1)S(1)}, u32[]{:S(2)}, u32[]{:S(2)}) collective-permute-start(bf16[64,2048]{1,0:T(8,128)(2,1)} %bitcast.10), channel_id=1, source_target_pairs={{0,1},{1,0},{2,3},{3,2},{4,5},{5,4},{6,7},{7,6},{8,9},{9,8},{10,11... | collective-permute-start | bytes 786440 | tf_op jit(solution)/shard_map/ppermute | solution.py:16
  1.5 21.3 %collective-permute-start.3 = (bf16[64,2048]{1,0:T(8,128)(2,1)}, bf16[64,2048]{1,0:T(8,128)(2,1)S(1)}, u32[]{:S(2)}, u32[]{:S(2)}) collective-permute-start(bf16[64,2048]{1,0:T(8,128)(2,1)} %bitcast.11), channel_id=1, source_target_pairs={{0,4},{1,5},{2,6},{3,7},{4,0},{5,1},{6,2},{7,3},{8,12},{9,13},{10,... | collective-permute-start | bytes 786440 | tf_op jit(solution)/shard_map/ppermute | solution.py:16
  4.1 18.8 %collective-permute-start.4 = (bf16[64,2048]{1,0:T(8,128)(2,1)}, bf16[64,2048]{1,0:T(8,128)(2,1)S(1)}, u32[]{:S(2)}, u32[]{:S(2)}) collective-permute-start(bf16[64,2048]{1,0:T(8,128)(2,1)} %bitcast.12), channel_id=1, source_target_pairs={{0,6},{1,7},{2,4},{3,5},{4,2},{5,3},{6,0},{7,1},{8,14},{9,15},{10,... | collective-permute-start | bytes 786440 | tf_op jit(solution)/shard_map/ppermute | solution.py:16
  5.5 19.6 %collective-permute-start.1 = (bf16[64,2048]{1,0:T(8,128)(2,1)}, bf16[64,2048]{1,0:T(8,128)(2,1)S(1)}, u32[]{:S(2)}, u32[]{:S(2)}) collective-permute-start(bf16[64,2048]{1,0:T(8,128)(2,1)} %bitcast.13), channel_id=1, source_target_pairs={{0,2},{1,3},{2,0},{3,1},{4,6},{5,7},{6,4},{7,5},{8,10},{9,11},{10,... | collective-permute-start | bytes 786440 | tf_op jit(solution)/shard_map/ppermute | solution.py:16
  8.3 20.4 %collective-permute-start.2 = (bf16[64,2048]{1,0:T(8,128)(2,1)S(1)}, bf16[64,2048]{1,0:T(8,128)(2,1)S(1)}, u32[]{:S(2)}, u32[]{:S(2)}) collective-permute-start(bf16[64,2048]{1,0:T(8,128)(2,1)S(1)} %collective-permute-done.refs_1_), channel_id=1, source_target_pairs={{0,2},{1,3},{2,0},{3,1},{4,6},{5,7},{6,4},{7,5},{8,10},{9,11},{10,... | collective-permute-start | bytes 786440 | tf_op jit(solution)/shard_map/ppermute | solution.py:16
  18.0 31.2 %copy-start.7 = (bf16[128,4096]{1,0:T(8,128)(2,1)}, bf16[128,4096]{1,0:T(8,128)(2,1)S(1)}, u32[]{:S(2)}) copy-start(bf16[128,4096]{1,0:T(8,128)(2,1)S(1)} %get-tuple-element.38.refs_4_.refs_0_) | copy-start | bytes 3145732
  18.0 16.2 %collective-permute-start.6 = (bf16[64,4096]{1,0:T(8,128)(2,1)S(1)}, bf16[64,4096]{1,0:T(8,128)(2,1)}, u32[]{:S(2)}, u32[]{:S(2)}) collective-permute-start(bf16[64,4096]{1,0:T(8,128)(2,1)S(1)} %get-tuple-element.41), channel_id=1, source_target_pairs={{0,16},{8,24},{1,17},{9,25},{2,18},{10,26},{3,19},{11,27},{4,20},{... | collective-permute-start | bytes 1572872 | tf_op jit(solution)/shard_map/ppermute | solution.py:368
  28.6 12.0 %collective-permute-start.5 = (bf16[128,2048]{1,0:T(8,128)(2,1)S(1)}, bf16[128,2048]{1,0:T(8,128)(2,1)S(1)}, u32[]{:S(2)}, u32[]{:S(2)}) collective-permute-start(bf16[128,2048]{1,0:T(8,128)(2,1)S(1)} %pad_maximum_fusion), channel_id=1, source_target_pairs={{0,1},{1,0},{2,3},{3,2},{4,5},{5,4},{6,7},{7,6},{8,9},{9,8},{10,11... | collective-permute-start | bytes 1572872 | tf_op jit(solution)/shard_map/ppermute | solution.py:16
  29.1 18.6 %collective-permute-start.9 = (bf16[64,4096]{1,0:T(8,128)(2,1)S(1)}, bf16[64,4096]{1,0:T(8,128)(2,1)}, u32[]{:S(2)}, u32[]{:S(2)}) collective-permute-start(bf16[64,4096]{1,0:T(8,128)(2,1)S(1)} %get-tuple-element.42), channel_id=1, source_target_pairs={{0,16},{8,24},{1,17},{9,25},{2,18},{10,26},{3,19},{11,27},{4,20},{... | collective-permute-start | bytes 1572872 | tf_op jit(solution)/shard_map/ppermute | solution.py:368
  34.2 27.5 %copy-start = (bf16[128,4096]{1,0:T(8,128)(2,1)}, bf16[128,4096]{1,0:T(8,128)(2,1)S(1)}, u32[]{:S(2)}) copy-start(bf16[128,4096]{1,0:T(8,128)(2,1)S(1)} %encode.4.refs_5_.refs_1_) | copy-start | bytes 3145732
  47.8 7.7 %collective-permute-start.10 = (bf16[256,4096]{1,0:T(8,128)(2,1)}, bf16[256,4096]{1,0:T(8,128)(2,1)S(1)}, u32[]{:S(2)}, u32[]{:S(2)}) collective-permute-start(bf16[256,4096]{1,0:T(8,128)(2,1)} %encode.5.refs_2_), channel_id=1, source_target_pairs={{0,8},{16,24},{1,9},{17,25},{2,10},{18,26},{3,11},{19,27},{4,12},{... | collective-permute-start | bytes 6291464 | tf_op jit(solution)/shard_map/ppermute | solution.py:374
  49.2 8.2 %collective-permute-start.7 = (bf16[128,4096]{1,0:T(8,128)(2,1)S(1)}, bf16[128,4096]{1,0:T(8,128)(2,1)S(1)}, u32[]{:S(2)}, u32[]{:S(2)}) collective-permute-start(bf16[128,4096]{1,0:T(8,128)(2,1)S(1)} %get-tuple-element.38.refs_4_.refs_0_), channel_id=1, source_target_pairs={{0,8},{16,24},{1,9},{17,25},{2,10},{18,26},{3,11},{19,27},{4,12},{... | collective-permute-start | bytes 3145736 | tf_op jit(solution)/shard_map/ppermute | solution.py:374
  50.6 9.9 %collective-permute-start.8 = (bf16[128,4096]{1,0:T(8,128)(2,1)S(1)}, bf16[128,4096]{1,0:T(8,128)(2,1)}, u32[]{:S(2)}, u32[]{:S(2)}) collective-permute-start(bf16[128,4096]{1,0:T(8,128)(2,1)S(1)} %encode.4.refs_5_.refs_1_), channel_id=1, source_target_pairs={{0,8},{16,24},{1,9},{17,25},{2,10},{18,26},{3,11},{19,27},{4,12},{... | collective-permute-start | bytes 3145736 | tf_op jit(solution)/shard_map/ppermute | solution.py:374
  52.8 33.1 %collective-permute-start.13 = (bf16[128,4096]{1,0:T(8,128)(2,1)S(1)}, bf16[128,4096]{1,0:T(8,128)(2,1)}, u32[]{:S(2)}, u32[]{:S(2)}) collective-permute-start(bf16[128,4096]{1,0:T(8,128)(2,1)S(1)} %encode.4.refs_5_.refs_1_), channel_id=1, source_target_pairs={{0,16},{8,24},{1,17},{9,25},{2,18},{10,26},{3,19},{11,27},{4,20},{... | collective-permute-start | bytes 3145736 | tf_op jit(solution)/shard_map/ppermute | solution.py:368
  54.1 66.8 %collective-permute-start.20 = (bf16[256,4096]{1,0:T(8,128)(2,1)}, bf16[256,4096]{1,0:T(8,128)(2,1)S(1)}, u32[]{:S(2)}, u32[]{:S(2)}) collective-permute-start(bf16[256,4096]{1,0:T(8,128)(2,1)} %encode.5.refs_2_), channel_id=1, source_target_pairs={{0,16},{8,24},{1,17},{9,25},{2,18},{10,26},{3,19},{11,27},{4,20},{... | collective-permute-start | bytes 6291464 | tf_op jit(solution)/shard_map/ppermute | solution.py:368
  55.4 5.0 %collective-permute-start.12 = (bf16[64,4096]{1,0:T(8,128)(2,1)}, bf16[64,4096]{1,0:T(8,128)(2,1)}, u32[]{:S(2)}, u32[]{:S(2)}) collective-permute-start(bf16[64,4096]{1,0:T(8,128)(2,1)} %collective-permute-done.9.refs_7_), channel_id=1, source_target_pairs={{16,24},{24,16},{17,25},{25,17},{18,26},{26,18},{19,27},{27,19},{2... | collective-permute-start | bytes 1572872 | tf_op jit(solution)/shard_map/ppermute | solution.py:371
  57.4 4.3 %collective-permute-start.11 = (bf16[64,4096]{1,0:T(8,128)(2,1)}, bf16[64,4096]{1,0:T(8,128)(2,1)}, u32[]{:S(2)}, u32[]{:S(2)}) collective-permute-start(bf16[64,4096]{1,0:T(8,128)(2,1)} %collective-permute-done.6.refs_6_), channel_id=1, source_target_pairs={{16,24},{24,16},{17,25},{25,17},{18,26},{26,18},{19,27},{27,19},{2... | collective-permute-start | bytes 1572872 | tf_op jit(solution)/shard_map/ppermute | solution.py:371
  85.9 13.8 %collective-permute-start.14 = (bf16[128,4096]{1,0:T(8,128)(2,1)}, bf16[128,4096]{1,0:T(8,128)(2,1)S(1)}, u32[]{:S(2)}, u32[]{:S(2)}) collective-permute-start(bf16[128,4096]{1,0:T(8,128)(2,1)} %collective-permute-done.13.refs_0_), channel_id=1, source_target_pairs={{16,24},{24,16},{17,25},{25,17},{18,26},{26,18},{19,27},{27,19},{2... | collective-permute-start | bytes 3145736 | tf_op jit(solution)/shard_map/ppermute | solution.py:371
  97.3 11.7 %collective-permute-start.15 = (bf16[4,128,256]{2,1,0:T(8,128)(2,1)}, bf16[4,128,256]{2,1,0:T(8,128)(2,1)S(1)}, u32[]{:S(2)}, u32[]{:S(2)}) collective-permute-start(bf16[4,128,256]{2,1,0:T(8,128)(2,1)} %get-tuple-element.47.refs_5_), channel_id=1, source_target_pairs={{0,1},{1,0},{2,3},{3,2},{4,5},{5,4},{6,7},{7,6},{8,9},{9,8},{10,11... | collective-permute-start | bytes 786440 | tf_op jit(solution)/shard_map/ppermute | solution.py:16
  108.4 8.9 %collective-permute-start.16 = (bf16[4,128,256]{2,1,0:T(8,128)(2,1)}, bf16[4,128,256]{2,1,0:T(8,128)(2,1)S(1)}, u32[]{:S(2)}, u32[]{:S(2)}) collective-permute-start(bf16[4,128,256]{2,1,0:T(8,128)(2,1)} %get-tuple-element.53), channel_id=1, source_target_pairs={{0,1},{1,0},{2,3},{3,2},{4,5},{5,4},{6,7},{7,6},{8,9},{9,8},{10,11... | collective-permute-start | bytes 786440 | tf_op jit(solution)/shard_map/ppermute | solution.py:16
  120.9 10.1 %collective-permute-start.21 = (bf16[256,4096]{1,0:T(8,128)(2,1)S(1)}, bf16[256,4096]{1,0:T(8,128)(2,1)S(1)}, u32[]{:S(2)}, u32[]{:S(2)}) collective-permute-start(bf16[256,4096]{1,0:T(8,128)(2,1)S(1)} %collective-permute-done.20.refs_0_), channel_id=1, source_target_pairs={{16,24},{24,16},{17,25},{25,17},{18,26},{26,18},{19,27},{27,19},{2... | collective-permute-start | bytes 6291464 | tf_op jit(solution)/shard_map/ppermute | solution.py:371
  124.3 20.0 %collective-permute-start.17 = (bf16[256,256]{1,0:T(8,128)(2,1)}, bf16[256,256]{1,0:T(8,128)(2,1)S(1)}, u32[]{:S(2)}, u32[]{:S(2)}) collective-permute-start(bf16[256,256]{1,0:T(8,128)(2,1)} %get-tuple-element.55), channel_id=1, source_target_pairs={{0,2},{1,3},{2,0},{3,1},{4,6},{5,7},{6,4},{7,5},{8,10},{9,11},{10,... | collective-permute-start | bytes 393224 | tf_op jit(solution)/shard_map/ppermute | solution.py:16
  126.8 17.5 %collective-permute-start.18 = (bf16[256,256]{1,0:T(8,128)(2,1)}, bf16[256,256]{1,0:T(8,128)(2,1)S(1)}, u32[]{:S(2)}, u32[]{:S(2)}) collective-permute-start(bf16[256,256]{1,0:T(8,128)(2,1)} %get-tuple-element.56), channel_id=1, source_target_pairs={{0,4},{1,5},{2,6},{3,7},{4,0},{5,1},{6,2},{7,3},{8,12},{9,13},{10,... | collective-permute-start | bytes 393224 | tf_op jit(solution)/shard_map/ppermute | solution.py:16
  129.5 14.8 %collective-permute-start.19 = (bf16[256,256]{1,0:T(8,128)(2,1)}, bf16[256,256]{1,0:T(8,128)(2,1)S(1)}, u32[]{:S(2)}, u32[]{:S(2)}) collective-permute-start(bf16[256,256]{1,0:T(8,128)(2,1)} %get-tuple-element.57), channel_id=1, source_target_pairs={{0,6},{1,7},{2,4},{3,5},{4,2},{5,3},{6,0},{7,1},{8,14},{9,15},{10,... | collective-permute-start | bytes 393224 | tf_op jit(solution)/shard_map/ppermute | solution.py:16
  143.7 12.9 %collective-permute-start.22 = (bf16[4,128,256]{2,1,0:T(8,128)(2,1)}, bf16[4,128,256]{2,1,0:T(8,128)(2,1)S(1)}, u32[]{:S(2)}, u32[]{:S(2)}) collective-permute-start(bf16[4,128,256]{2,1,0:T(8,128)(2,1)} %get-tuple-element.59.refs_4_.refs_5_), channel_id=1, source_target_pairs={{0,1},{1,0},{2,3},{3,2},{4,5},{5,4},{6,7},{7,6},{8,9},{9,8},{10,11... | collective-permute-start | bytes 786440 | tf_op jit(solution)/shard_map/ppermute | solution.py:16
  155.1 8.2 %collective-permute-start.26 = (bf16[4,128,256]{2,1,0:T(8,128)(2,1)}, bf16[4,128,256]{2,1,0:T(8,128)(2,1)S(1)}, u32[]{:S(2)}, u32[]{:S(2)}) collective-permute-start(bf16[4,128,256]{2,1,0:T(8,128)(2,1)} %get-tuple-element.61.refs_2_), channel_id=1, source_target_pairs={{0,1},{1,0},{2,3},{3,2},{4,5},{5,4},{6,7},{7,6},{8,9},{9,8},{10,11... | collective-permute-start | bytes 786440 | tf_op jit(solution)/shard_map/ppermute | solution.py:16
  158.2 5.0 %collective-permute-start.23 = (bf16[128,256]{1,0:T(8,128)(2,1)S(1)}, bf16[128,256]{1,0:T(8,128)(2,1)S(1)}, u32[]{:S(2)}, u32[]{:S(2)}) collective-permute-start(bf16[128,256]{1,0:T(8,128)(2,1)S(1)} %get-tuple-element.63), channel_id=1, source_target_pairs={{0,2},{1,3},{2,0},{3,1},{4,6},{5,7},{6,4},{7,5},{8,10},{9,11},{10,... | collective-permute-start | bytes 196616 | tf_op jit(solution)/shard_map/ppermute | solution.py:16
  158.8 10.5 %collective-permute-start.24 = (bf16[128,256]{1,0:T(8,128)(2,1)S(1)}, bf16[128,256]{1,0:T(8,128)(2,1)S(1)}, u32[]{:S(2)}, u32[]{:S(2)}) collective-permute-start(bf16[128,256]{1,0:T(8,128)(2,1)S(1)} %get-tuple-element.64), channel_id=1, source_target_pairs={{0,4},{1,5},{2,6},{3,7},{4,0},{5,1},{6,2},{7,3},{8,12},{9,13},{10,... | collective-permute-start | bytes 196616 | tf_op jit(solution)/shard_map/ppermute | solution.py:16
  161.2 8.1 %collective-permute-start.25 = (bf16[128,256]{1,0:T(8,128)(2,1)S(1)}, bf16[128,256]{1,0:T(8,128)(2,1)S(1)}, u32[]{:S(2)}, u32[]{:S(2)}) collective-permute-start(bf16[128,256]{1,0:T(8,128)(2,1)S(1)} %get-tuple-element.65), channel_id=1, source_target_pairs={{0,6},{1,7},{2,4},{3,5},{4,2},{5,3},{6,0},{7,1},{8,14},{9,15},{10,... | collective-permute-start | bytes 196616 | tf_op jit(solution)/shard_map/ppermute | solution.py:16
  164.9 4.5 %collective-permute-start.27 = (bf16[128,256]{1,0:T(8,128)(2,1)S(1)}, bf16[128,256]{1,0:T(8,128)(2,1)S(1)}, u32[]{:S(2)}, u32[]{:S(2)}) collective-permute-start(bf16[128,256]{1,0:T(8,128)(2,1)S(1)} %get-tuple-element.68), channel_id=1, source_target_pairs={{0,2},{1,3},{2,0},{3,1},{4,6},{5,7},{6,4},{7,5},{8,10},{9,11},{10,... | collective-permute-start | bytes 196616 | tf_op jit(solution)/shard_map/ppermute | solution.py:16
  165.5 6.6 %collective-permute-start.28 = (bf16[128,256]{1,0:T(8,128)(2,1)S(1)}, bf16[128,256]{1,0:T(8,128)(2,1)S(1)}, u32[]{:S(2)}, u32[]{:S(2)}) collective-permute-start(bf16[128,256]{1,0:T(8,128)(2,1)S(1)} %get-tuple-element.69), channel_id=1, source_target_pairs={{0,4},{1,5},{2,6},{3,7},{4,0},{5,1},{6,2},{7,3},{8,12},{9,13},{10,... | collective-permute-start | bytes 196616 | tf_op jit(solution)/shard_map/ppermute | solution.py:16
  167.8 6.1 %collective-permute-start.29 = (bf16[128,256]{1,0:T(8,128)(2,1)S(1)}, bf16[128,256]{1,0:T(8,128)(2,1)S(1)}, u32[]{:S(2)}, u32[]{:S(2)}) collective-permute-start(bf16[128,256]{1,0:T(8,128)(2,1)S(1)} %get-tuple-element.70), channel_id=1, source_target_pairs={{0,6},{1,7},{2,4},{3,5},{4,2},{5,3},{6,0},{7,1},{8,14},{9,15},{10,... | collective-permute-start | bytes 196616 | tf_op jit(solution)/shard_map/ppermute | solution.py:16
  (23 other events, 124.5 us)

commit v11 on v10

--- a/solution.py
+++ b/solution.py
@@ -26,6 +26,10 @@
 
 def landed(array):
     return pltpu.with_memory_space_constraint(array, pltpu.VMEM)
+
+
+def fetched(array):
+    return pltpu.with_memory_space_constraint(array, pltpu.HBM)
 
 
 def fill(order, parts, rows_of):
@@ -241,16 +245,20 @@
     )(info, *sum(groups, []), decoder, *after)
 
 
-def later_wave_kernel(order, row, n, info, *refs):
-    direct, swapped, (base, *kept) = refs[:n], refs[n : 2 * n], refs[2 * n : 2 * n + 3]
-    out, sent, first, second, start, sem = refs[-6:]
+def later_wave_kernel(row, skip, info, direct, swapped, base, kept_direct, kept_swapped, *refs):
+    kept = kept_direct, kept_swapped
+    out, sent, first, second, start, sems = refs[-6:]
     rows = out.shape[1]
     pairs, cols = out.shape[0], out.shape[2]
-    copy = pltpu.make_async_copy(base.at[pl.ds(row, rows)], start, sem)
-    copy.start()
-    fill(order, direct, first)
-    fill(order, swapped, second)
-    copy.wait()
+    copies = [
+        pltpu.make_async_copy(direct.at[pl.ds(skip, rows)], first, sems.at[0]),
+        pltpu.make_async_copy(swapped.at[pl.ds(skip, rows)], second, sems.at[1]),
+        pltpu.make_async_copy(base.at[pl.ds(row, rows)], start, sems.at[2]),
+    ]
+    for copy in copies:
+        copy.start()
+    for copy in copies:
+        copy.wait()
 
     @pl.loop(0, pairs)
     def _(j):
@@ -265,14 +273,13 @@
         split(info, start[:, at], out, sent, j)
 
 
-def decode_later(info, direct, swapped, order, base, kept, row, shards, after):
-    rows = sum(size for _, _, size in order)
+def decode_later(info, direct, swapped, skip, rows, base, kept, row, shards, after):
     features, width = kept[0].shape
     return pl.pallas_call(
-        functools.partial(later_wave_kernel, order, row, len(direct)),
+        functools.partial(later_wave_kernel, row, skip),
         in_specs=[pl.BlockSpec(memory_space=pltpu.SMEM)]
-        + [WHOLE] * (2 * len(direct))
-        + [ANYWHERE, WHOLE, WHOLE]
+        + [ANYWHERE] * 3
+        + [WHOLE] * 2
         + [ANYWHERE] * len(after),
         out_specs=[WHOLE, WHOLE],
         out_shape=halves(shards, rows, width),
@@ -280,15 +287,21 @@
             pltpu.VMEM((rows, features), jnp.bfloat16),
             pltpu.VMEM((rows, features), jnp.bfloat16),
             pltpu.VMEM((rows, width), jnp.float32),
-            pltpu.SemaphoreType.DMA,
+            pltpu.SemaphoreType.DMA((3,)),
         ],
         compiler_params=pltpu.CompilerParams(vmem_limit_bytes=DECODE_MIB * MIB),
         name="decode_later",
-    )(info, *map(landed, direct), *map(landed, swapped), base, *map(landed, kept), *after)
+    )(info, fetched(direct), landed(swapped), fetched(base), *map(landed, kept), *after)
 
 
 def pair_kernel(size, n, n_after, info, *refs):
-    mine, theirs, outs = refs[:n], refs[n : 2 * n], refs[2 * n + n_after :]
+    theirs, outs, sems = refs[n : 2 * n], refs[2 * n + n_after : -1 - n], refs[-1]
+    mine = refs[-1 - n : -1]
+    copies = [pltpu.make_async_copy(refs[i], mine[i], sems.at[i]) for i in range(n)]
+    for copy in copies:
+        copy.start()
+    for copy in copies:
+        copy.wait()
     z = info[5]
     for q, out in enumerate(outs):
         row = 0
@@ -309,40 +322,52 @@
     return pl.pallas_call(
         functools.partial(pair_kernel, size, len(mine), len(after)),
         in_specs=[pl.BlockSpec(memory_space=pltpu.SMEM)]
-        + [WHOLE] * (2 * len(mine))
+        + [ANYWHERE] * len(mine)
+        + [WHOLE] * len(theirs)
         + [ANYWHERE] * len(after),
         out_specs=[WHOLE] * count,
+        scratch_shapes=[pltpu.VMEM(array.shape, array.dtype) for array in mine]
+        + [pltpu.SemaphoreType.DMA((len(mine),))],
         out_shape=[
             jax.ShapeDtypeStruct((rows, cols), jnp.float32 if q == 0 else jnp.bfloat16)
             for q in range(count)
         ],
         compiler_params=pltpu.CompilerParams(vmem_limit_bytes=SUM_MIB * MIB),
         name="add_pair",
-    )(info, *mine, *[landed(array) for array in theirs], *after)
+    )(info, *map(fetched, mine), *map(landed, theirs), *after)
 
 
 def sum_kernel(sign, pieces, info, base, *refs):
-    received, out = refs[: len(pieces)], refs[-1]
+    received, (out, total, sems) = refs[: len(pieces)], refs[-3:]
     me = info[6]
-    out[...] = sign * base[...]
+    copy = pltpu.make_async_copy(base, total, sems.at[0])
+    copy.start()
+    copy.wait()
+    if sign != 1.0:
+        total[...] = sign * total[...]
     for ref, (source, blocks) in zip(received, pieces):
         size = ref.shape[0] // len(blocks)
         for k, s in enumerate(blocks):
             at = pl.ds(pl.multiple_of((me ^ (source ^ s)) * size, size), size)
-            out[at, :] += ref[pl.ds(k * size, size), :].astype(jnp.float32)
+            total[at, :] += ref[pl.ds(k * size, size), :].astype(jnp.float32)
+    copy = pltpu.make_async_copy(total, out, sems.at[1])
+    copy.start()
+    copy.wait()
 
 
 def add_up(info, base, sign, pieces, received, after):
     return pl.pallas_call(
         functools.partial(sum_kernel, sign, pieces),
         in_specs=[pl.BlockSpec(memory_space=pltpu.SMEM)]
-        + [WHOLE] * (1 + len(received))
+        + [ANYWHERE]
+        + [WHOLE] * len(received)
         + [ANYWHERE] * len(after),
-        out_specs=WHOLE,
-        out_shape=jax.ShapeDtypeStruct(base.shape, base.dtype),
+        out_specs=ANYWHERE,
+        out_shape=pltpu.HBM(base.shape, base.dtype),
+        scratch_shapes=[pltpu.VMEM(base.shape, base.dtype), pltpu.SemaphoreType.DMA((2,))],
         compiler_params=pltpu.CompilerParams(vmem_limit_bytes=SUM_MIB * MIB),
         name="add_up",
-    )(info, base, *map(landed, received), *after)
+    )(info, fetched(base), *map(landed, received), *after)
 
 
 def pipelined(layer_inputs, targets, encoder, encoder_bias, decoder):
@@ -432,8 +457,10 @@
 
     def later(number, direct, swapped, skip, *earlier):
         row = (slots[number][0] - slots[1][0]) * size
-        order = [(0, skip * size, len(slots[number]) * size)]
-        return decode_later(info, [direct], [swapped], order, base, kept, row, shards, list(earlier))
+        rows = len(slots[number]) * size
+        return decode_later(
+            info, direct, swapped, skip * size, rows, base, kept, row, shards, list(earlier)
+        )
 
     c1 = across(after(d1, sent))
     mine1, sent1 = later(1, d1, c1, 0, sent)

time: 177 us -> 174 us (0.983)
  local copies, waits for them, and re-layouts: 14.8 us -> 4.93 us
  Pallas kernels: 71.4 us -> 75.8 us
    unnamed x50 -> x30, local copies, waits for them, and re-layouts: 14.1 us -> 4.33 us
    pallas_call x2, Pallas kernels: 2.16 us -> 5.04 us  [add_up(): pl.pallas_call(functools.partial(sum_kernel, sign, pieces), in_specs=[pl....]
    pallas_call x3, Pallas kernels: 2.53 us -> 5.15 us  [add_pair(): pl.pallas_call(functools.partial(pair_kernel, size, len(mine), len(after)...]
  transfers between devices with their start and end apart: 30 -> 30, of which waited for: 12 -> 12; matrix products, arithmetic and copies ran while one was open for 0% -> 0% of each run, Pallas kernels for 40% -> 42%
where the time goes in v11:
time: 174 us
  Pallas kernels  75.8 us (44%)
  starting transfers between devices  56 us (32%)
  waiting for transfers between devices  36.3 us (21%)
  local copies, waits for them, and re-layouts  4.93 us (3%)
    ppermute x19, waiting for transfers between devices, exchange(): return lax.ppermute(array, axis, [(i, i ^ flip) for i in range(size)])  31.9 us
    ppermute x19, starting transfers between devices, exchange(): return lax.ppermute(array, axis, [(i, i ^ flip) for i in range(size)])  27.9 us
    pallas_call x3, Pallas kernels, decode_later(): pl.pallas_call(functools.partial(later_wave_kernel, row, skip), in_specs=...  25.4 us
    pallas_call x1, Pallas kernels, decode_first(): pl.pallas_call(functools.partial(first_wave_kernel, [len(parts) for parts...  24.1 us
    ppermute x4, starting transfers between devices, across(): return lax.ppermute(a, 'layer', [(i, i ^ 1) for i in range(half, layers)])  17.9 us
    pallas_call x3, Pallas kernels, encode(): pl.pallas_call(functools.partial(encode_kernel, order, pieces, len(parts)...  16.1 us
    pallas_call x3, Pallas kernels, add_pair(): pl.pallas_call(functools.partial(pair_kernel, size, len(mine), len(after)...  5.15 us
    ppermute x4, starting transfers between devices, up(): return lax.ppermute(a, 'layer', [(i, i + half) for i in range(half)])  5.14 us
  transfers between devices with their start and end apart: 30, of which 12 were waited for; matrix products, arithmetic and copies ran while one was open for 0% of the time, Pallas kernels for 42%

profile of v11, /device:TPU:2, one launch (start us, length us, event | category | flops | bytes accessed | tf_op | source)
XLA Modules:
  0.0 173.5 jit_solution(15586230101302240139)
XLA Ops:
  1.5 2.6 %collective-permute-start.3 = (bf16[64,2048]{1,0:T(8,128)(2,1)}, bf16[64,2048]{1,0:T(8,128)(2,1)S(1)}, u32[]{:S(2)}, u32[]{:S(2)}) collective-permute-start(bf16[64,2048]{1,0:T(8,128)(2,1)} %bitcast.10), channel_id=1, source_target_pairs={{0,4},{1,5},{2,6},{3,7},{4,0},{5,1},{6,2},{7,3},{8,12},{9,13},{10,... | collective-permute-start | bytes 786440 | tf_op jit(solution)/shard_map/ppermute | solution.py:16
  5.7 2.6 %collective-permute-done.refs_1_ = bf16[64,2048]{1,0:T(8,128)(2,1)S(1)} collective-permute-done((bf16[64,2048]{1,0:T(8,128)(2,1)}, bf16[64,2048]{1,0:T(8,128)(2,1)S(1)}, u32[]{:S(2)}, u32[]{:S(2)}) %collective-permute-start) | collective-permute-done | bytes 262176 | tf_op jit(solution)/shard_map/ppermute | solution.py:16
  11.5 6.5 %encode.3 = (bf16[128,4096]{1,0:T(8,128)(2,1)S(1)}, bf16[64,4096]{1,0:T(8,128)(2,1)S(1)}, bf16[64,4096]{1,0:T(8,128)(2,1)S(1)}, bf16[1,2048,4096]{2,1,0:T(8,128)(2,1)S(1)}) custom-call(bf16[64,2048]{1,0:T(8,128)(2,1)S(1)} %bitcast.13, bf16[64,2048]{1,0:T(8,128)(2,1)S(1)} %collective-permute-done.refs_1_, bf16[1,2048,4096]{2,1,0:T(8,128)(2,1)} %refs_2_.1, ...), custom_call_target="tpu_custom_call" | custom-call | tf_op jit(solution)/shard_map/encode/pallas_call | solution.py:84
  19.3 3.5 %collective-permute-done.3.refs_0_ = bf16[64,2048]{1,0:T(8,128)(2,1)S(1)} collective-permute-done((bf16[64,2048]{1,0:T(8,128)(2,1)}, bf16[64,2048]{1,0:T(8,128)(2,1)S(1)}, u32[]{:S(2)}, u32[]{:S(2)}) %collective-permute-start.3) | collective-permute-done | bytes 262176 | tf_op jit(solution)/shard_map/ppermute | solution.py:16
  22.9 2.1 %collective-permute-done.1.refs_0_ = bf16[64,2048]{1,0:T(8,128)(2,1)S(1)} collective-permute-done((bf16[64,2048]{1,0:T(8,128)(2,1)}, bf16[64,2048]{1,0:T(8,128)(2,1)S(1)}, u32[]{:S(2)}, u32[]{:S(2)}) %collective-permute-start.1) | collective-permute-done | bytes 262176 | tf_op jit(solution)/shard_map/ppermute | solution.py:16
  25.0 3.6 %collective-permute-done.2.refs_1_ = bf16[64,2048]{1,0:T(8,128)(2,1)S(1)} collective-permute-done((bf16[64,2048]{1,0:T(8,128)(2,1)S(1)}, bf16[64,2048]{1,0:T(8,128)(2,1)S(1)}, u32[]{:S(2)}, u32[]{:S(2)}) %collective-permute-start.2) | collective-permute-done | bytes 262176 | tf_op jit(solution)/shard_map/ppermute | solution.py:16
  30.4 3.7 %encode.4.refs_5_.refs_1_ = bf16[128,4096]{1,0:T(8,128)(2,1)S(1)} custom-call(bf16[64,2048]{1,0:T(8,128)(2,1)S(1)} %collective-permute-done.1.refs_0_, bf16[64,2048]{1,0:T(8,128)(2,1)S(1)} %collective-permute-done.2.refs_1_, bf16[1,2048,4096]{2,1,0:T(8,128)(2,1)S(1)} %get-tuple-element.39.refs_2_.refs_3_, f32[1,4096]{1,0:T(1,128)S(1)} %copy-done.8, ...), custom_call_target="tpu_custom_call" | custom-call | tf_op jit(solution)/shard_map/encode/pallas_call | solution.py:84
  34.2 6.4 %collective-permute-done.5.refs_2_ = bf16[128,2048]{1,0:T(8,128)(2,1)S(1)} collective-permute-done((bf16[128,2048]{1,0:T(8,128)(2,1)S(1)}, bf16[128,2048]{1,0:T(8,128)(2,1)S(1)}, u32[]{:S(2)}, u32[]{:S(2)}) %collective-permute-start.5) | collective-permute-done | bytes 524320 | tf_op jit(solution)/shard_map/ppermute | solution.py:16
  40.6 5.8 %encode.5.refs_2_ = bf16[256,4096]{1,0:T(8,128)(2,1)S(1)} custom-call(bf16[64,2048]{1,0:T(8,128)(2,1)S(1)} %collective-permute-done.3.refs_0_, bf16[64,2048]{1,0:T(8,128)(2,1)S(1)} %collective-permute-done.4.refs_1_, bf16[128,2048]{1,0:T(8,128)(2,1)S(1)} %collective-permute-done.5.refs_2_, bf16[1,2048,4096]{2,1,0:T(8,128)(2,1)S(1)} %get-tuple-element.39.refs_2_.refs_3_, ...), custom_call_target="tpu_custom_call" | custom-call | tf_op jit(solution)/shard_map/encode/pallas_call | solution.py:84
  49.3 2.3 %collective-permute-start.8 = (bf16[128,4096]{1,0:T(8,128)(2,1)S(1)}, bf16[128,4096]{1,0:T(8,128)(2,1)}, u32[]{:S(2)}, u32[]{:S(2)}) collective-permute-start(bf16[128,4096]{1,0:T(8,128)(2,1)S(1)} %encode.4.refs_5_.refs_1_), channel_id=1, source_target_pairs={{0,8},{16,24},{1,9},{17,25},{2,10},{18,26},{3,11},{19,27},{4,12},{... | collective-permute-start | bytes 3145736 | tf_op jit(solution)/shard_map/ppermute | solution.py:399
  54.2 1.9 %collective-permute-start.12 = (bf16[64,4096]{1,0:T(8,128)(2,1)}, bf16[64,4096]{1,0:T(8,128)(2,1)}, u32[]{:S(2)}, u32[]{:S(2)}) collective-permute-start(bf16[64,4096]{1,0:T(8,128)(2,1)} %collective-permute-done.9.refs_7_), channel_id=1, source_target_pairs={{16,24},{24,16},{17,25},{25,17},{18,26},{26,18},{19,27},{27,19},{2... | collective-permute-start | bytes 1572872 | tf_op jit(solution)/shard_map/ppermute | solution.py:396
  56.1 2.4 %collective-permute-start.11 = (bf16[64,4096]{1,0:T(8,128)(2,1)}, bf16[64,4096]{1,0:T(8,128)(2,1)}, u32[]{:S(2)}, u32[]{:S(2)}) collective-permute-start(bf16[64,4096]{1,0:T(8,128)(2,1)} %collective-permute-done.6.refs_6_), channel_id=1, source_target_pairs={{16,24},{24,16},{17,25},{25,17},{18,26},{26,18},{19,27},{27,19},{2... | collective-permute-start | bytes 1572872 | tf_op jit(solution)/shard_map/ppermute | solution.py:396
  60.4 24.1 %decode_first.1 = (f32[4,128,256]{2,1,0:T(8,128)}, bf16[4,128,256]{2,1,0:T(8,128)(2,1)}, f32[384,2048]{1,0:T(8,128)}, bf16[4096,2048]{1,0:T(8,128)(2,1)S(1)}, bf16[4096,2048]{1,0:T(8,128)(2,1)S(1)}) custom-call(s32[7]{0:T(128)} %stack.31.info, bf16[128,4096]{1,0:T(8,128)(2,1)} %copy-done.2, bf16[128,4096]{1,0:T(8,128)(2,1)} %copy-done, ...), custom_call_target="tpu_custom_call" | custom-call | tf_op jit(solution)/shard_map/decode_first/pallas_call | solution.py:217
  84.5 11.4 %collective-permute-start.14 = (bf16[128,4096]{1,0:T(8,128)(2,1)}, bf16[128,4096]{1,0:T(8,128)(2,1)S(1)}, u32[]{:S(2)}, u32[]{:S(2)}) collective-permute-start(bf16[128,4096]{1,0:T(8,128)(2,1)} %collective-permute-done.13.direct), channel_id=1, source_target_pairs={{16,24},{24,16},{17,25},{25,17},{18,26},{26,18},{19,27},{27,19},{2... | collective-permute-start | bytes 3145736 | tf_op jit(solution)/shard_map/ppermute | solution.py:396
  96.5 1.9 %collective-permute-done.14.swapped = bf16[128,4096]{1,0:T(8,128)(2,1)S(1)} collective-permute-done((bf16[128,4096]{1,0:T(8,128)(2,1)}, bf16[128,4096]{1,0:T(8,128)(2,1)S(1)}, u32[]{:S(2)}, u32[]{:S(2)}) %collective-permute-start.14) | collective-permute-done | bytes 1048608 | tf_op jit(solution)/shard_map/ppermute | solution.py:396
  98.5 8.5 %decode_later.3 = (f32[4,128,256]{2,1,0:T(8,128)}, bf16[4,128,256]{2,1,0:T(8,128)(2,1)}) custom-call(s32[7]{0:T(128)} %stack.31.info, bf16[128,4096]{1,0:T(8,128)(2,1)} %collective-permute-done.13.direct, bf16[128,4096]{1,0:T(8,128)(2,1)S(1)} %collective-permute-done.14.swapped, f32[384,2048]{1,0:T(8,128)} %get-tuple-element.49.base, ...), custom_call_target="tpu_custom_call" | custom-call | tf_op jit(solution)/shard_map/decode_later/pallas_call | solution.py:278
  107.6 8.3 %collective-permute-done.16.refs_3_ = bf16[4,128,256]{2,1,0:T(8,128)(2,1)S(1)} collective-permute-done((bf16[4,128,256]{2,1,0:T(8,128)(2,1)}, bf16[4,128,256]{2,1,0:T(8,128)(2,1)S(1)}, u32[]{:S(2)}, u32[]{:S(2)}) %collective-permute-start.16) | collective-permute-done | bytes 262176 | tf_op jit(solution)/shard_map/ppermute | solution.py:16
  115.9 1.9 %add_pair.3 = (f32[256,256]{1,0:T(8,128)S(1)}, bf16[256,256]{1,0:T(8,128)(2,1)S(1)}, bf16[256,256]{1,0:T(8,128)(2,1)S(1)}, bf16[256,256]{1,0:T(8,128)(2,1)S(1)}) custom-call(s32[7]{0:T(128)S(1)} %copy-done.10, f32[4,128,256]{2,1,0:T(8,128)} %get-tuple-element.46.refs_0_, f32[4,128,256]{2,1,0:T(8,128)} %get-tuple-element.52.refs_1_, ...), custom_call_target="tpu_custom_call" | custom-call | tf_op jit(solution)/shard_map/add_pair/pallas_call | solution.py:322
  119.7 2.1 %collective-permute-start.21 = (bf16[256,4096]{1,0:T(8,128)(2,1)}, bf16[256,4096]{1,0:T(8,128)(2,1)S(1)}, u32[]{:S(2)}, u32[]{:S(2)}) collective-permute-start(bf16[256,4096]{1,0:T(8,128)(2,1)} %collective-permute-done.20.direct), channel_id=1, source_target_pairs={{16,24},{24,16},{17,25},{25,17},{18,26},{26,18},{19,27},{27,19},{2... | collective-permute-start | bytes 6291464 | tf_op jit(solution)/shard_map/ppermute | solution.py:396
  121.8 2.5 %collective-permute-start.17 = (bf16[256,256]{1,0:T(8,128)(2,1)S(1)}, bf16[256,256]{1,0:T(8,128)(2,1)S(1)}, u32[]{:S(2)}, u32[]{:S(2)}) collective-permute-start(bf16[256,256]{1,0:T(8,128)(2,1)S(1)} %get-tuple-element.55), channel_id=1, source_target_pairs={{0,2},{1,3},{2,0},{3,1},{4,6},{5,7},{6,4},{7,5},{8,10},{9,11},{10,... | collective-permute-start | bytes 393224 | tf_op jit(solution)/shard_map/ppermute | solution.py:16
  124.4 2.8 %collective-permute-start.18 = (bf16[256,256]{1,0:T(8,128)(2,1)S(1)}, bf16[256,256]{1,0:T(8,128)(2,1)S(1)}, u32[]{:S(2)}, u32[]{:S(2)}) collective-permute-start(bf16[256,256]{1,0:T(8,128)(2,1)S(1)} %get-tuple-element.56), channel_id=1, source_target_pairs={{0,4},{1,5},{2,6},{3,7},{4,0},{5,1},{6,2},{7,3},{8,12},{9,13},{10,... | collective-permute-start | bytes 393224 | tf_op jit(solution)/shard_map/ppermute | solution.py:16
  128.6 8.4 %decode_later.4 = (f32[4,128,256]{2,1,0:T(8,128)}, bf16[4,128,256]{2,1,0:T(8,128)(2,1)}) custom-call(s32[7]{0:T(128)} %stack.31.info, bf16[256,4096]{1,0:T(8,128)(2,1)} %collective-permute-done.20.direct, bf16[256,4096]{1,0:T(8,128)(2,1)S(1)} %collective-permute-done.21.swapped, f32[384,2048]{1,0:T(8,128)} %get-tuple-element.49.base, ...), custom_call_target="tpu_custom_call" | custom-call | tf_op jit(solution)/shard_map/decode_later/pallas_call | solution.py:278
  139.1 2.5 %add_up.2.refs_1_.base = f32[512,256]{1,0:T(8,128)} custom-call(s32[7]{0:T(128)S(1)} %copy-done.11, f32[512,256]{1,0:T(8,128)} %bitcast.14, f32[256,256]{1,0:T(8,128)S(1)} %copy-done.4, bf16[256,256]{1,0:T(8,128)(2,1)S(1)} %collective-permute-done.17.refs_1_, bf16[256,256]{1,0:T(8,128)(2,1)S(1)} %collective-permute-done.18.refs_2_, ...), custom_call_target="tpu_custom_call" | custom-call | tf_op jit(solution)/shard_map/add_up/pallas_call | solution.py:359
  141.7 8.5 %decode_later.5 = (f32[4,128,256]{2,1,0:T(8,128)}, bf16[4,128,256]{2,1,0:T(8,128)(2,1)}) custom-call(s32[7]{0:T(128)} %stack.31.info, bf16[256,4096]{1,0:T(8,128)(2,1)} %collective-permute-done.20.direct, bf16[256,4096]{1,0:T(8,128)(2,1)S(1)} %collective-permute-done.21.swapped, f32[384,2048]{1,0:T(8,128)} %get-tuple-element.49.base, ...), custom_call_target="tpu_custom_call" | custom-call | tf_op jit(solution)/shard_map/decode_later/pallas_call | solution.py:278
  152.1 1.6 add_pair.4
  153.8 2.0 %collective-permute-start.23 = (bf16[128,256]{1,0:T(8,128)(2,1)S(1)}, bf16[128,256]{1,0:T(8,128)(2,1)S(1)}, u32[]{:S(2)}, u32[]{:S(2)}) collective-permute-start(bf16[128,256]{1,0:T(8,128)(2,1)S(1)} %get-tuple-element.63), channel_id=1, source_target_pairs={{0,2},{1,3},{2,0},{3,1},{4,6},{5,7},{6,4},{7,5},{8,10},{9,11},{10,... | collective-permute-start | bytes 196616 | tf_op jit(solution)/shard_map/ppermute | solution.py:16
  155.8 2.0 %collective-permute-start.24 = (bf16[128,256]{1,0:T(8,128)(2,1)S(1)}, bf16[128,256]{1,0:T(8,128)(2,1)S(1)}, u32[]{:S(2)}, u32[]{:S(2)}) collective-permute-start(bf16[128,256]{1,0:T(8,128)(2,1)S(1)} %get-tuple-element.64), channel_id=1, source_target_pairs={{0,4},{1,5},{2,6},{3,7},{4,0},{5,1},{6,2},{7,3},{8,12},{9,13},{10,... | collective-permute-start | bytes 196616 | tf_op jit(solution)/shard_map/ppermute | solution.py:16
  159.2 1.7 add_pair.5
  160.8 1.9 %collective-permute-start.27 = (bf16[128,256]{1,0:T(8,128)(2,1)S(1)}, bf16[128,256]{1,0:T(8,128)(2,1)S(1)}, u32[]{:S(2)}, u32[]{:S(2)}) collective-permute-start(bf16[128,256]{1,0:T(8,128)(2,1)S(1)} %get-tuple-element.68), channel_id=1, source_target_pairs={{0,2},{1,3},{2,0},{3,1},{4,6},{5,7},{6,4},{7,5},{8,10},{9,11},{10,... | collective-permute-start | bytes 196616 | tf_op jit(solution)/shard_map/ppermute | solution.py:16
  162.8 2.0 %collective-permute-start.28 = (bf16[128,256]{1,0:T(8,128)(2,1)S(1)}, bf16[128,256]{1,0:T(8,128)(2,1)S(1)}, u32[]{:S(2)}, u32[]{:S(2)}) collective-permute-start(bf16[128,256]{1,0:T(8,128)(2,1)S(1)} %get-tuple-element.69), channel_id=1, source_target_pairs={{0,4},{1,5},{2,6},{3,7},{4,0},{5,1},{6,2},{7,3},{8,12},{9,13},{10,... | collective-permute-start | bytes 196616 | tf_op jit(solution)/shard_map/ppermute | solution.py:16
  166.1 3.9 %collective-permute-done.28.refs_6_ = bf16[128,256]{1,0:T(8,128)(2,1)S(1)} collective-permute-done((bf16[128,256]{1,0:T(8,128)(2,1)S(1)}, bf16[128,256]{1,0:T(8,128)(2,1)S(1)}, u32[]{:S(2)}, u32[]{:S(2)}) %collective-permute-start.28) | collective-permute-done | bytes 65568 | tf_op jit(solution)/shard_map/ppermute | solution.py:16
  170.9 2.5 %add_up.3 = f32[512,256]{1,0:T(8,128)} custom-call(s32[7]{0:T(128)S(1)} %copy-done.12, f32[512,256]{1,0:T(8,128)} %add_up.2.refs_1_.base, f32[128,256]{1,0:T(8,128)S(1)} %get-tuple-element.62.refs_0_, bf16[128,256]{1,0:T(8,128)(2,1)S(1)} %collective-permute-done.23.refs_2_.refs_1_, bf16[128,256]{1,0:T(8,128)(2,1)S(1)} %collective-permute-done.24.refs_2_, ...), custom_call_target="tpu_custom_call" | custom-call | tf_op jit(solution)/shard_map/add_up/pallas_call | solution.py:359
  (72 shorter events, 29.0 us)
Async XLA Ops:
  0.0 8.3 %collective-permute-start = (bf16[64,2048]{1,0:T(8,128)(2,1)}, bf16[64,2048]{1,0:T(8,128)(2,1)S(1)}, u32[]{:S(2)}, u32[]{:S(2)}) collective-permute-start(bf16[64,2048]{1,0:T(8,128)(2,1)} %bitcast.9), channel_id=1, source_target_pairs={{0,1},{1,0},{2,3},{3,2},{4,5},{5,4},{6,7},{7,6},{8,9},{9,8},{10,11... | collective-permute-start | bytes 786440 | tf_op jit(solution)/shard_map/ppermute | solution.py:16
  1.5 21.3 %collective-permute-start.3 = (bf16[64,2048]{1,0:T(8,128)(2,1)}, bf16[64,2048]{1,0:T(8,128)(2,1)S(1)}, u32[]{:S(2)}, u32[]{:S(2)}) collective-permute-start(bf16[64,2048]{1,0:T(8,128)(2,1)} %bitcast.10), channel_id=1, source_target_pairs={{0,4},{1,5},{2,6},{3,7},{4,0},{5,1},{6,2},{7,3},{8,12},{9,13},{10,... | collective-permute-start | bytes 786440 | tf_op jit(solution)/shard_map/ppermute | solution.py:16
  4.1 18.8 %collective-permute-start.4 = (bf16[64,2048]{1,0:T(8,128)(2,1)}, bf16[64,2048]{1,0:T(8,128)(2,1)S(1)}, u32[]{:S(2)}, u32[]{:S(2)}) collective-permute-start(bf16[64,2048]{1,0:T(8,128)(2,1)} %bitcast.11), channel_id=1, source_target_pairs={{0,6},{1,7},{2,4},{3,5},{4,2},{5,3},{6,0},{7,1},{8,14},{9,15},{10,... | collective-permute-start | bytes 786440 | tf_op jit(solution)/shard_map/ppermute | solution.py:16
  5.5 19.6 %collective-permute-start.1 = (bf16[64,2048]{1,0:T(8,128)(2,1)}, bf16[64,2048]{1,0:T(8,128)(2,1)S(1)}, u32[]{:S(2)}, u32[]{:S(2)}) collective-permute-start(bf16[64,2048]{1,0:T(8,128)(2,1)} %bitcast.12), channel_id=1, source_target_pairs={{0,2},{1,3},{2,0},{3,1},{4,6},{5,7},{6,4},{7,5},{8,10},{9,11},{10,... | collective-permute-start | bytes 786440 | tf_op jit(solution)/shard_map/ppermute | solution.py:16
  8.3 20.4 %collective-permute-start.2 = (bf16[64,2048]{1,0:T(8,128)(2,1)S(1)}, bf16[64,2048]{1,0:T(8,128)(2,1)S(1)}, u32[]{:S(2)}, u32[]{:S(2)}) collective-permute-start(bf16[64,2048]{1,0:T(8,128)(2,1)S(1)} %collective-permute-done.refs_1_), channel_id=1, source_target_pairs={{0,2},{1,3},{2,0},{3,1},{4,6},{5,7},{6,4},{7,5},{8,10},{9,11},{10,... | collective-permute-start | bytes 786440 | tf_op jit(solution)/shard_map/ppermute | solution.py:16
  11.5 29.1 %copy-start.9 = (f32[1,4096]{1,0:T(1,128)S(1)}, f32[1,4096]{1,0:T(1,128)}, u32[]{:S(2)}) copy-start(f32[1,4096]{1,0:T(1,128)} %refs_4_.1) | copy-start | bytes 49156
  18.0 29.9 %copy-start.2 = (bf16[128,4096]{1,0:T(8,128)(2,1)}, bf16[128,4096]{1,0:T(8,128)(2,1)S(1)}, u32[]{:S(2)}) copy-start(bf16[128,4096]{1,0:T(8,128)(2,1)S(1)} %get-tuple-element.38.refs_4_.refs_0_) | copy-start | bytes 3145732
  18.0 16.1 %collective-permute-start.6 = (bf16[64,4096]{1,0:T(8,128)(2,1)S(1)}, bf16[64,4096]{1,0:T(8,128)(2,1)}, u32[]{:S(2)}, u32[]{:S(2)}) collective-permute-start(bf16[64,4096]{1,0:T(8,128)(2,1)S(1)} %get-tuple-element.41), channel_id=1, source_target_pairs={{0,16},{8,24},{1,17},{9,25},{2,18},{10,26},{3,19},{11,27},{4,20},{... | collective-permute-start | bytes 1572872 | tf_op jit(solution)/shard_map/ppermute | solution.py:393
  28.6 12.0 %collective-permute-start.5 = (bf16[128,2048]{1,0:T(8,128)(2,1)S(1)}, bf16[128,2048]{1,0:T(8,128)(2,1)S(1)}, u32[]{:S(2)}, u32[]{:S(2)}) collective-permute-start(bf16[128,2048]{1,0:T(8,128)(2,1)S(1)} %pad_maximum_fusion), channel_id=1, source_target_pairs={{0,1},{1,0},{2,3},{3,2},{4,5},{5,4},{6,7},{7,6},{8,9},{9,8},{10,11... | collective-permute-start | bytes 1572872 | tf_op jit(solution)/shard_map/ppermute | solution.py:16
  29.1 17.3 %collective-permute-start.9 = (bf16[64,4096]{1,0:T(8,128)(2,1)S(1)}, bf16[64,4096]{1,0:T(8,128)(2,1)}, u32[]{:S(2)}, u32[]{:S(2)}) collective-permute-start(bf16[64,4096]{1,0:T(8,128)(2,1)S(1)} %get-tuple-element.42), channel_id=1, source_target_pairs={{0,16},{8,24},{1,17},{9,25},{2,18},{10,26},{3,19},{11,27},{4,20},{... | collective-permute-start | bytes 1572872 | tf_op jit(solution)/shard_map/ppermute | solution.py:393
  46.5 7.7 %collective-permute-start.10 = (bf16[256,4096]{1,0:T(8,128)(2,1)S(1)}, bf16[256,4096]{1,0:T(8,128)(2,1)S(1)}, u32[]{:S(2)}, u32[]{:S(2)}) collective-permute-start(bf16[256,4096]{1,0:T(8,128)(2,1)S(1)} %encode.5.refs_2_), channel_id=1, source_target_pairs={{0,8},{16,24},{1,9},{17,25},{2,10},{18,26},{3,11},{19,27},{4,12},{... | collective-permute-start | bytes 6291464 | tf_op jit(solution)/shard_map/ppermute | solution.py:399
  47.9 8.2 %collective-permute-start.7 = (bf16[128,4096]{1,0:T(8,128)(2,1)S(1)}, bf16[128,4096]{1,0:T(8,128)(2,1)S(1)}, u32[]{:S(2)}, u32[]{:S(2)}) collective-permute-start(bf16[128,4096]{1,0:T(8,128)(2,1)S(1)} %get-tuple-element.38.refs_4_.refs_0_), channel_id=1, source_target_pairs={{0,8},{16,24},{1,9},{17,25},{2,10},{18,26},{3,11},{19,27},{4,12},{... | collective-permute-start | bytes 3145736 | tf_op jit(solution)/shard_map/ppermute | solution.py:399
  49.3 9.9 %collective-permute-start.8 = (bf16[128,4096]{1,0:T(8,128)(2,1)S(1)}, bf16[128,4096]{1,0:T(8,128)(2,1)}, u32[]{:S(2)}, u32[]{:S(2)}) collective-permute-start(bf16[128,4096]{1,0:T(8,128)(2,1)S(1)} %encode.4.refs_5_.refs_1_), channel_id=1, source_target_pairs={{0,8},{16,24},{1,9},{17,25},{2,10},{18,26},{3,11},{19,27},{4,12},{... | collective-permute-start | bytes 3145736 | tf_op jit(solution)/shard_map/ppermute | solution.py:399
  51.5 33.0 %collective-permute-start.13 = (bf16[128,4096]{1,0:T(8,128)(2,1)S(1)}, bf16[128,4096]{1,0:T(8,128)(2,1)}, u32[]{:S(2)}, u32[]{:S(2)}) collective-permute-start(bf16[128,4096]{1,0:T(8,128)(2,1)S(1)} %encode.4.refs_5_.refs_1_), channel_id=1, source_target_pairs={{0,16},{8,24},{1,17},{9,25},{2,18},{10,26},{3,19},{11,27},{4,20},{... | collective-permute-start | bytes 3145736 | tf_op jit(solution)/shard_map/ppermute | solution.py:393
  52.8 66.9 %collective-permute-start.20 = (bf16[256,4096]{1,0:T(8,128)(2,1)S(1)}, bf16[256,4096]{1,0:T(8,128)(2,1)}, u32[]{:S(2)}, u32[]{:S(2)}) collective-permute-start(bf16[256,4096]{1,0:T(8,128)(2,1)S(1)} %encode.5.refs_2_), channel_id=1, source_target_pairs={{0,16},{8,24},{1,17},{9,25},{2,18},{10,26},{3,19},{11,27},{4,20},{... | collective-permute-start | bytes 6291464 | tf_op jit(solution)/shard_map/ppermute | solution.py:393
  54.2 5.0 %collective-permute-start.12 = (bf16[64,4096]{1,0:T(8,128)(2,1)}, bf16[64,4096]{1,0:T(8,128)(2,1)}, u32[]{:S(2)}, u32[]{:S(2)}) collective-permute-start(bf16[64,4096]{1,0:T(8,128)(2,1)} %collective-permute-done.9.refs_7_), channel_id=1, source_target_pairs={{16,24},{24,16},{17,25},{25,17},{18,26},{26,18},{19,27},{27,19},{2... | collective-permute-start | bytes 1572872 | tf_op jit(solution)/shard_map/ppermute | solution.py:396
  56.1 4.3 %collective-permute-start.11 = (bf16[64,4096]{1,0:T(8,128)(2,1)}, bf16[64,4096]{1,0:T(8,128)(2,1)}, u32[]{:S(2)}, u32[]{:S(2)}) collective-permute-start(bf16[64,4096]{1,0:T(8,128)(2,1)} %collective-permute-done.6.refs_6_), channel_id=1, source_target_pairs={{16,24},{24,16},{17,25},{25,17},{18,26},{26,18},{19,27},{27,19},{2... | collective-permute-start | bytes 1572872 | tf_op jit(solution)/shard_map/ppermute | solution.py:396
  84.5 13.9 %collective-permute-start.14 = (bf16[128,4096]{1,0:T(8,128)(2,1)}, bf16[128,4096]{1,0:T(8,128)(2,1)S(1)}, u32[]{:S(2)}, u32[]{:S(2)}) collective-permute-start(bf16[128,4096]{1,0:T(8,128)(2,1)} %collective-permute-done.13.direct), channel_id=1, source_target_pairs={{16,24},{24,16},{17,25},{25,17},{18,26},{26,18},{19,27},{27,19},{2... | collective-permute-start | bytes 3145736 | tf_op jit(solution)/shard_map/ppermute | solution.py:396
  96.0 11.6 %collective-permute-start.15 = (bf16[4,128,256]{2,1,0:T(8,128)(2,1)}, bf16[4,128,256]{2,1,0:T(8,128)(2,1)S(1)}, u32[]{:S(2)}, u32[]{:S(2)}) collective-permute-start(bf16[4,128,256]{2,1,0:T(8,128)(2,1)} %get-tuple-element.47.refs_0_), channel_id=1, source_target_pairs={{0,1},{1,0},{2,3},{3,2},{4,5},{5,4},{6,7},{7,6},{8,9},{9,8},{10,11... | collective-permute-start | bytes 786440 | tf_op jit(solution)/shard_map/ppermute | solution.py:16
  107.0 8.9 %collective-permute-start.16 = (bf16[4,128,256]{2,1,0:T(8,128)(2,1)}, bf16[4,128,256]{2,1,0:T(8,128)(2,1)S(1)}, u32[]{:S(2)}, u32[]{:S(2)}) collective-permute-start(bf16[4,128,256]{2,1,0:T(8,128)(2,1)} %get-tuple-element.53), channel_id=1, source_target_pairs={{0,1},{1,0},{2,3},{3,2},{4,5},{5,4},{6,7},{7,6},{8,9},{9,8},{10,11... | collective-permute-start | bytes 786440 | tf_op jit(solution)/shard_map/ppermute | solution.py:16
  119.7 8.8 %collective-permute-start.21 = (bf16[256,4096]{1,0:T(8,128)(2,1)}, bf16[256,4096]{1,0:T(8,128)(2,1)S(1)}, u32[]{:S(2)}, u32[]{:S(2)}) collective-permute-start(bf16[256,4096]{1,0:T(8,128)(2,1)} %collective-permute-done.20.direct), channel_id=1, source_target_pairs={{16,24},{24,16},{17,25},{25,17},{18,26},{26,18},{19,27},{27,19},{2... | collective-permute-start | bytes 6291464 | tf_op jit(solution)/shard_map/ppermute | solution.py:396
  121.8 15.7 %collective-permute-start.17 = (bf16[256,256]{1,0:T(8,128)(2,1)S(1)}, bf16[256,256]{1,0:T(8,128)(2,1)S(1)}, u32[]{:S(2)}, u32[]{:S(2)}) collective-permute-start(bf16[256,256]{1,0:T(8,128)(2,1)S(1)} %get-tuple-element.55), channel_id=1, source_target_pairs={{0,2},{1,3},{2,0},{3,1},{4,6},{5,7},{6,4},{7,5},{8,10},{9,11},{10,... | collective-permute-start | bytes 393224 | tf_op jit(solution)/shard_map/ppermute | solution.py:16
  124.4 13.2 %collective-permute-start.18 = (bf16[256,256]{1,0:T(8,128)(2,1)S(1)}, bf16[256,256]{1,0:T(8,128)(2,1)S(1)}, u32[]{:S(2)}, u32[]{:S(2)}) collective-permute-start(bf16[256,256]{1,0:T(8,128)(2,1)S(1)} %get-tuple-element.56), channel_id=1, source_target_pairs={{0,4},{1,5},{2,6},{3,7},{4,0},{5,1},{6,2},{7,3},{8,12},{9,13},{10,... | collective-permute-start | bytes 393224 | tf_op jit(solution)/shard_map/ppermute | solution.py:16
  127.2 11.0 %collective-permute-start.19 = (bf16[256,256]{1,0:T(8,128)(2,1)S(1)}, bf16[256,256]{1,0:T(8,128)(2,1)S(1)}, u32[]{:S(2)}, u32[]{:S(2)}) collective-permute-start(bf16[256,256]{1,0:T(8,128)(2,1)S(1)} %get-tuple-element.57), channel_id=1, source_target_pairs={{0,6},{1,7},{2,4},{3,5},{4,2},{5,3},{6,0},{7,1},{8,14},{9,15},{10,... | collective-permute-start | bytes 393224 | tf_op jit(solution)/shard_map/ppermute | solution.py:16
  137.0 14.2 %collective-permute-start.22 = (bf16[4,128,256]{2,1,0:T(8,128)(2,1)}, bf16[4,128,256]{2,1,0:T(8,128)(2,1)S(1)}, u32[]{:S(2)}, u32[]{:S(2)}) collective-permute-start(bf16[4,128,256]{2,1,0:T(8,128)(2,1)} %get-tuple-element.59.refs_4_.refs_0_), channel_id=1, source_target_pairs={{0,1},{1,0},{2,3},{3,2},{4,5},{5,4},{6,7},{7,6},{8,9},{9,8},{10,11... | collective-permute-start | bytes 786440 | tf_op jit(solution)/shard_map/ppermute | solution.py:16
  150.2 9.0 %collective-permute-start.26 = (bf16[4,128,256]{2,1,0:T(8,128)(2,1)}, bf16[4,128,256]{2,1,0:T(8,128)(2,1)S(1)}, u32[]{:S(2)}, u32[]{:S(2)}) collective-permute-start(bf16[4,128,256]{2,1,0:T(8,128)(2,1)} %get-tuple-element.61.refs_2_), channel_id=1, source_target_pairs={{0,1},{1,0},{2,3},{3,2},{4,5},{5,4},{6,7},{7,6},{8,9},{9,8},{10,11... | collective-permute-start | bytes 786440 | tf_op jit(solution)/shard_map/ppermute | solution.py:16
  153.8 5.4 %collective-permute-start.23 = (bf16[128,256]{1,0:T(8,128)(2,1)S(1)}, bf16[128,256]{1,0:T(8,128)(2,1)S(1)}, u32[]{:S(2)}, u32[]{:S(2)}) collective-permute-start(bf16[128,256]{1,0:T(8,128)(2,1)S(1)} %get-tuple-element.63), channel_id=1, source_target_pairs={{0,2},{1,3},{2,0},{3,1},{4,6},{5,7},{6,4},{7,5},{8,10},{9,11},{10,... | collective-permute-start | bytes 196616 | tf_op jit(solution)/shard_map/ppermute | solution.py:16
  155.8 10.4 %collective-permute-start.24 = (bf16[128,256]{1,0:T(8,128)(2,1)S(1)}, bf16[128,256]{1,0:T(8,128)(2,1)S(1)}, u32[]{:S(2)}, u32[]{:S(2)}) collective-permute-start(bf16[128,256]{1,0:T(8,128)(2,1)S(1)} %get-tuple-element.64), channel_id=1, source_target_pairs={{0,4},{1,5},{2,6},{3,7},{4,0},{5,1},{6,2},{7,3},{8,12},{9,13},{10,... | collective-permute-start | bytes 196616 | tf_op jit(solution)/shard_map/ppermute | solution.py:16
  157.8 8.4 %collective-permute-start.25 = (bf16[128,256]{1,0:T(8,128)(2,1)S(1)}, bf16[128,256]{1,0:T(8,128)(2,1)S(1)}, u32[]{:S(2)}, u32[]{:S(2)}) collective-permute-start(bf16[128,256]{1,0:T(8,128)(2,1)S(1)} %get-tuple-element.65), channel_id=1, source_target_pairs={{0,6},{1,7},{2,4},{3,5},{4,2},{5,3},{6,0},{7,1},{8,14},{9,15},{10,... | collective-permute-start | bytes 196616 | tf_op jit(solution)/shard_map/ppermute | solution.py:16
  160.8 5.3 %collective-permute-start.27 = (bf16[128,256]{1,0:T(8,128)(2,1)S(1)}, bf16[128,256]{1,0:T(8,128)(2,1)S(1)}, u32[]{:S(2)}, u32[]{:S(2)}) collective-permute-start(bf16[128,256]{1,0:T(8,128)(2,1)S(1)} %get-tuple-element.68), channel_id=1, source_target_pairs={{0,2},{1,3},{2,0},{3,1},{4,6},{5,7},{6,4},{7,5},{8,10},{9,11},{10,... | collective-permute-start | bytes 196616 | tf_op jit(solution)/shard_map/ppermute | solution.py:16
  162.8 7.3 %collective-permute-start.28 = (bf16[128,256]{1,0:T(8,128)(2,1)S(1)}, bf16[128,256]{1,0:T(8,128)(2,1)S(1)}, u32[]{:S(2)}, u32[]{:S(2)}) collective-permute-start(bf16[128,256]{1,0:T(8,128)(2,1)S(1)} %get-tuple-element.69), channel_id=1, source_target_pairs={{0,4},{1,5},{2,6},{3,7},{4,0},{5,1},{6,2},{7,3},{8,12},{9,13},{10,... | collective-permute-start | bytes 196616 | tf_op jit(solution)/shard_map/ppermute | solution.py:16
  164.7 6.1 %collective-permute-start.29 = (bf16[128,256]{1,0:T(8,128)(2,1)S(1)}, bf16[128,256]{1,0:T(8,128)(2,1)S(1)}, u32[]{:S(2)}, u32[]{:S(2)}) collective-permute-start(bf16[128,256]{1,0:T(8,128)(2,1)S(1)} %get-tuple-element.70), channel_id=1, source_target_pairs={{0,6},{1,7},{2,4},{3,5},{4,2},{5,3},{6,0},{7,1},{8,14},{9,15},{10,... | collective-permute-start | bytes 196616 | tf_op jit(solution)/shard_map/ppermute | solution.py:16
  (13 other events, 97.8 us)

commit v12 on v11

--- a/solution.py
+++ b/solution.py
@@ -40,7 +40,8 @@
 
 
 def encode_kernel(order, pieces, n_in, n_after, stream, *refs):
-    parts, weight, bias, refs = refs[:n_in], refs[n_in], refs[n_in + 1], refs[n_in + 2 + n_after :]
+    parts, weight, bias, refs = refs[:n_in], refs[n_in], refs[n_in + 1], refs[n_in + 2 :]
+    earlier, refs = refs[:n_after], refs[n_after:]
     outs, refs = refs[: len(pieces)], refs[len(pieces) :]
     features = weight.shape[2]
     if stream:
@@ -67,13 +68,19 @@
         preact = jnp.dot(tokens[...], kept[0, :, cols], preferred_element_type=jnp.float32)
         acts = jnp.maximum(preact + bias[:, cols], 0.0).astype(jnp.bfloat16)
         for out, (row, size) in zip(outs, pieces):
-            out[:, cols] = acts[row : row + size]
-
-
-def encode(parts, order, pieces, weight, bias, after, stream=False):
+            before = out.shape[0] - size
+            out[pl.ds(before, size), cols] = acts[row : row + size]
+            if before:
+                out[pl.ds(0, before), cols] = earlier[0][:, cols]
+
+
+def encode(parts, order, pieces, weight, bias, after, stream=False, join=False):
     rows = sum(size for _, _, size in order)
     _, width, features = weight.shape
     out_shape = [jax.ShapeDtypeStruct((size, features), jnp.bfloat16) for _, size in pieces]
+    if join:
+        joined = (after[0].shape[0] + pieces[0][1], features)
+        out_shape[0] = jax.ShapeDtypeStruct(joined, jnp.bfloat16)
     scratch = [pltpu.VMEM((rows, width), jnp.bfloat16)]
     if stream:
         out_shape.append(pltpu.VMEM(weight.shape, weight.dtype))
@@ -83,7 +90,7 @@
         weight = pltpu.with_memory_space_constraint(weight, pltpu.VMEM)
     return pl.pallas_call(
         functools.partial(encode_kernel, order, pieces, len(parts), len(after), stream),
-        in_specs=[WHOLE] * len(parts) + [ANYWHERE if stream else WHOLE, WHOLE] + [ANYWHERE] * len(after),
+        in_specs=[WHOLE] * len(parts) + [ANYWHERE if stream else WHOLE, WHOLE] + [WHOLE if join and i == 0 else ANYWHERE for i in range(len(after))],
         out_specs=[WHOLE] * len(out_shape),
         out_shape=out_shape,
         scratch_shapes=scratch,
@@ -338,36 +345,27 @@
 
 
 def sum_kernel(sign, pieces, info, base, *refs):
-    received, (out, total, sems) = refs[: len(pieces)], refs[-3:]
+    received, out = refs[: len(pieces)], refs[-1]
     me = info[6]
-    copy = pltpu.make_async_copy(base, total, sems.at[0])
-    copy.start()
-    copy.wait()
-    if sign != 1.0:
-        total[...] = sign * total[...]
+    out[...] = sign * base[...]
     for ref, (source, blocks) in zip(received, pieces):
         size = ref.shape[0] // len(blocks)
         for k, s in enumerate(blocks):
             at = pl.ds(pl.multiple_of((me ^ (source ^ s)) * size, size), size)
-            total[at, :] += ref[pl.ds(k * size, size), :].astype(jnp.float32)
-    copy = pltpu.make_async_copy(total, out, sems.at[1])
-    copy.start()
-    copy.wait()
+            out[at, :] += ref[pl.ds(k * size, size), :].astype(jnp.float32)
 
 
 def add_up(info, base, sign, pieces, received, after):
     return pl.pallas_call(
         functools.partial(sum_kernel, sign, pieces),
         in_specs=[pl.BlockSpec(memory_space=pltpu.SMEM)]
-        + [ANYWHERE]
-        + [WHOLE] * len(received)
+        + [WHOLE] * (1 + len(received))
         + [ANYWHERE] * len(after),
-        out_specs=ANYWHERE,
+        out_specs=WHOLE,
         out_shape=pltpu.HBM(base.shape, base.dtype),
-        scratch_shapes=[pltpu.VMEM(base.shape, base.dtype), pltpu.SemaphoreType.DMA((2,))],
         compiler_params=pltpu.CompilerParams(vmem_limit_bytes=SUM_MIB * MIB),
         name="add_up",
-    )(info, fetched(base), *map(landed, received), *after)
+    )(info, base, *map(landed, received), *after)
 
 
 def pipelined(layer_inputs, targets, encoder, encoder_bias, decoder):
@@ -416,17 +414,18 @@
         [],
         stream=True,
     )
-    d0a, d0b, n0 = up(a0a), up(a0b), beside(a0)
+    d0a, d0b = up(a0a), up(a0b)
     rest = exchange(after(jnp.concatenate(far[1:], axis=0), far[0], three), "feat", 1)
-    (a1,) = encode(
+    a01, a1 = encode(
         [far[0], three],
         [(0, 0, size), (1, 0, size)],
-        [(0, 2 * size)],
+        [(0, 2 * size), (0, 2 * size)],
         encoder_kept,
         encoder_bias,
         [a0],
-    )
-    d1, n1 = up(a1), beside(a1)
+        join=True,
+    )
+    d1, n01 = up(a1), beside(a01)
     others = shards - 4
     order = []
     for k in range(others // 2):
@@ -443,7 +442,7 @@
 
     c0a, c0b = across(after(d0a, n2)), across(after(d0b, n2))
     mine, sent, base, *kept = decode_first(
-        info, [a0, a1, a2], [n0, n1, n2], [d0a, d0b], [c0a, c0b], decoder, shards, []
+        info, [a01, a2], [n01, n2], [d0a, d0b], [c0a, c0b], decoder, shards, []
     )
     slots = [[0, 1], [2, 3], list(range(4, shards - 2)), [shards - 2, shards - 1]]
 

time: 174 us -> 171 us (0.983)
  waiting for transfers between devices: 36.3 us -> 34.3 us
    pallas_call x2, Pallas kernels: 5.04 us -> 2.97 us  [add_up(): pl.pallas_call(functools.partial(sum_kernel, sign, pieces), in_specs=[pl....]
    ppermute x19, waiting for transfers between devices: 31.9 us -> 30 us  [exchange(): return lax.ppermute(array, axis, [(i, i ^ flip) for i in range(size)])]
    ppermute x3 -> x2, starting transfers between devices: 5.05 us -> 4.01 us  [beside(): return lax.ppermute(a, 'layer', [(i, i + 1) for i in range(0, layers, 2)])]
    unnamed x30 -> x32, local copies, waits for them, and re-layouts: 4.33 us -> 4.31 us
  transfers between devices with their start and end apart: 30 -> 29, of which waited for: 12 -> 12; matrix products, arithmetic and copies ran while one was open for 0% -> 0% of each run, Pallas kernels for 42% -> 44%
where the time goes in v12:
time: 171 us; the launch traced here: 170 us
  Pallas kernels  75.4 us (44%)
  starting transfers between devices  54.9 us (32%)
  waiting for transfers between devices  34.3 us (20%)
  local copies, waits for them, and re-layouts  4.99 us (3%)
    ppermute x19, waiting for transfers between devices, exchange(): return lax.ppermute(array, axis, [(i, i ^ flip) for i in range(size)])  30 us
    ppermute x19, starting transfers between devices, exchange(): return lax.ppermute(array, axis, [(i, i ^ flip) for i in range(size)])  28 us
    pallas_call x3, Pallas kernels, decode_later(): pl.pallas_call(functools.partial(later_wave_kernel, row, skip), in_specs=...  25.4 us
    pallas_call x1, Pallas kernels, decode_first(): pl.pallas_call(functools.partial(first_wave_kernel, [len(parts) for parts...  24.1 us
    ppermute x4, starting transfers between devices, across(): return lax.ppermute(a, 'layer', [(i, i ^ 1) for i in range(half, layers)])  17.8 us
    pallas_call x3, Pallas kernels, encode(): pl.pallas_call(functools.partial(encode_kernel, order, pieces, len(parts)...  17.7 us
    pallas_call x3, Pallas kernels, add_pair(): pl.pallas_call(functools.partial(pair_kernel, size, len(mine), len(after)...  5.15 us
    ppermute x4, starting transfers between devices, up(): return lax.ppermute(a, 'layer', [(i, i + half) for i in range(half)])  5.14 us
  transfers between devices with their start and end apart: 29, of which 12 were waited for; matrix products, arithmetic and copies ran while one was open for 0% of the time, Pallas kernels for 44%

profile of v12, /device:TPU:2, one launch (start us, length us, event | category | flops | bytes accessed | tf_op | source)
XLA Modules:
  0.0 169.9 jit_solution(963824317093333442)
XLA Ops:
  0.0 1.5 collective-permute-start.1
  1.5 2.6 %collective-permute-start.3 = (bf16[64,2048]{1,0:T(8,128)(2,1)}, bf16[64,2048]{1,0:T(8,128)(2,1)S(1)}, u32[]{:S(2)}, u32[]{:S(2)}) collective-permute-start(bf16[64,2048]{1,0:T(8,128)(2,1)} %bitcast.11), channel_id=1, source_target_pairs={{0,4},{1,5},{2,6},{3,7},{4,0},{5,1},{6,2},{7,3},{8,12},{9,13},{10,... | collective-permute-start | bytes 786440 | tf_op jit(solution)/shard_map/ppermute | solution.py:16
  5.7 2.6 %collective-permute-done.1.refs_1_ = bf16[64,2048]{1,0:T(8,128)(2,1)S(1)} collective-permute-done((bf16[64,2048]{1,0:T(8,128)(2,1)}, bf16[64,2048]{1,0:T(8,128)(2,1)S(1)}, u32[]{:S(2)}, u32[]{:S(2)}) %collective-permute-start.1) | collective-permute-done | bytes 262176 | tf_op jit(solution)/shard_map/ppermute | solution.py:16
  8.3 1.6 collective-permute-start.2
  11.5 6.5 %encode.3 = (bf16[128,4096]{1,0:T(8,128)(2,1)S(1)}, bf16[64,4096]{1,0:T(8,128)(2,1)S(1)}, bf16[64,4096]{1,0:T(8,128)(2,1)S(1)}, bf16[1,2048,4096]{2,1,0:T(8,128)(2,1)S(1)}) custom-call(bf16[64,2048]{1,0:T(8,128)(2,1)S(1)} %bitcast.14, bf16[64,2048]{1,0:T(8,128)(2,1)S(1)} %collective-permute-done.1.refs_1_, bf16[1,2048,4096]{2,1,0:T(8,128)(2,1)} %refs_2_.1, ...), custom_call_target="tpu_custom_call" | custom-call | tf_op jit(solution)/shard_map/encode/pallas_call | solution.py:91
  19.3 3.5 %collective-permute-done.3.refs_0_ = bf16[64,2048]{1,0:T(8,128)(2,1)S(1)} collective-permute-done((bf16[64,2048]{1,0:T(8,128)(2,1)}, bf16[64,2048]{1,0:T(8,128)(2,1)S(1)}, u32[]{:S(2)}, u32[]{:S(2)}) %collective-permute-start.3) | collective-permute-done | bytes 262176 | tf_op jit(solution)/shard_map/ppermute | solution.py:16
  22.9 2.1 %collective-permute-done.refs_0_ = bf16[64,2048]{1,0:T(8,128)(2,1)S(1)} collective-permute-done((bf16[64,2048]{1,0:T(8,128)(2,1)}, bf16[64,2048]{1,0:T(8,128)(2,1)S(1)}, u32[]{:S(2)}, u32[]{:S(2)}) %collective-permute-start) | collective-permute-done | bytes 262176 | tf_op jit(solution)/shard_map/ppermute | solution.py:16
  25.0 3.6 %collective-permute-done.2.refs_1_ = bf16[64,2048]{1,0:T(8,128)(2,1)S(1)} collective-permute-done((bf16[64,2048]{1,0:T(8,128)(2,1)S(1)}, bf16[64,2048]{1,0:T(8,128)(2,1)S(1)}, u32[]{:S(2)}, u32[]{:S(2)}) %collective-permute-start.2) | collective-permute-done | bytes 262176 | tf_op jit(solution)/shard_map/ppermute | solution.py:16
  30.4 5.4 %encode.4 = (bf16[256,4096]{1,0:T(8,128)(2,1)}, bf16[128,4096]{1,0:T(8,128)(2,1)}) custom-call(bf16[64,2048]{1,0:T(8,128)(2,1)S(1)} %collective-permute-done.refs_0_, bf16[64,2048]{1,0:T(8,128)(2,1)S(1)} %collective-permute-done.2.refs_1_, bf16[1,2048,4096]{2,1,0:T(8,128)(2,1)S(1)} %get-tuple-element.40.refs_2_.refs_3_, f32[1,4096]{1,0:T(1,128)S(1)} %copy-done.10, ...), custom_call_target="tpu_custom_call" | custom-call | tf_op jit(solution)/shard_map/encode/pallas_call | solution.py:91
  35.8 4.7 %collective-permute-done.5.refs_2_ = bf16[128,2048]{1,0:T(8,128)(2,1)S(1)} collective-permute-done((bf16[128,2048]{1,0:T(8,128)(2,1)S(1)}, bf16[128,2048]{1,0:T(8,128)(2,1)S(1)}, u32[]{:S(2)}, u32[]{:S(2)}) %collective-permute-start.5) | collective-permute-done | bytes 524320 | tf_op jit(solution)/shard_map/ppermute | solution.py:16
  40.5 5.8 %encode.5.refs_1_ = bf16[256,4096]{1,0:T(8,128)(2,1)S(1)} custom-call(bf16[64,2048]{1,0:T(8,128)(2,1)S(1)} %collective-permute-done.3.refs_0_, bf16[64,2048]{1,0:T(8,128)(2,1)S(1)} %collective-permute-done.4.refs_1_, bf16[128,2048]{1,0:T(8,128)(2,1)S(1)} %collective-permute-done.5.refs_2_, bf16[1,2048,4096]{2,1,0:T(8,128)(2,1)S(1)} %get-tuple-element.40.refs_2_.refs_3_, ...), custom_call_target="tpu_custom_call" | custom-call | tf_op jit(solution)/shard_map/encode/pallas_call | solution.py:91
  47.8 2.6 %collective-permute-start.7 = (bf16[256,4096]{1,0:T(8,128)(2,1)}, bf16[256,4096]{1,0:T(8,128)(2,1)}, u32[]{:S(2)}, u32[]{:S(2)}) collective-permute-start(bf16[256,4096]{1,0:T(8,128)(2,1)} %get-tuple-element.42.refs_0_), channel_id=1, source_target_pairs={{0,8},{16,24},{1,9},{17,25},{2,10},{18,26},{3,11},{19,27},{4,12},{... | collective-permute-start | bytes 6291464 | tf_op jit(solution)/shard_map/ppermute | solution.py:397
  53.0 1.9 %collective-permute-start.11 = (bf16[64,4096]{1,0:T(8,128)(2,1)S(1)}, bf16[64,4096]{1,0:T(8,128)(2,1)}, u32[]{:S(2)}, u32[]{:S(2)}) collective-permute-start(bf16[64,4096]{1,0:T(8,128)(2,1)S(1)} %collective-permute-done.8.refs_5_), channel_id=1, source_target_pairs={{16,24},{24,16},{17,25},{25,17},{18,26},{26,18},{19,27},{27,19},{2... | collective-permute-start | bytes 1572872 | tf_op jit(solution)/shard_map/ppermute | solution.py:394
  54.9 2.4 %collective-permute-start.10 = (bf16[64,4096]{1,0:T(8,128)(2,1)S(1)}, bf16[64,4096]{1,0:T(8,128)(2,1)}, u32[]{:S(2)}, u32[]{:S(2)}) collective-permute-start(bf16[64,4096]{1,0:T(8,128)(2,1)S(1)} %collective-permute-done.6.refs_6_.refs_4_), channel_id=1, source_target_pairs={{16,24},{24,16},{17,25},{25,17},{18,26},{26,18},{19,27},{27,19},{2... | collective-permute-start | bytes 1572872 | tf_op jit(solution)/shard_map/ppermute | solution.py:394
  59.0 24.1 %decode_first.1 = (f32[4,128,256]{2,1,0:T(8,128)}, bf16[4,128,256]{2,1,0:T(8,128)(2,1)}, f32[384,2048]{1,0:T(8,128)}, bf16[4096,2048]{1,0:T(8,128)(2,1)S(1)}, bf16[4096,2048]{1,0:T(8,128)(2,1)S(1)}) custom-call(s32[7]{0:T(128)} %stack.31.info, bf16[256,4096]{1,0:T(8,128)(2,1)} %get-tuple-element.42.refs_0_, bf16[256,4096]{1,0:T(8,128)(2,1)} %copy-done, ...), custom_call_target="tpu_custom_call" | custom-call | tf_op jit(solution)/shard_map/decode_first/pallas_call | solution.py:224
  83.1 11.3 %collective-permute-start.13 = (bf16[128,4096]{1,0:T(8,128)(2,1)}, bf16[128,4096]{1,0:T(8,128)(2,1)S(1)}, u32[]{:S(2)}, u32[]{:S(2)}) collective-permute-start(bf16[128,4096]{1,0:T(8,128)(2,1)} %collective-permute-done.12.direct), channel_id=1, source_target_pairs={{16,24},{24,16},{17,25},{25,17},{18,26},{26,18},{19,27},{27,19},{2... | collective-permute-start | bytes 3145736 | tf_op jit(solution)/shard_map/ppermute | solution.py:394
  95.0 1.9 %collective-permute-done.13.swapped = bf16[128,4096]{1,0:T(8,128)(2,1)S(1)} collective-permute-done((bf16[128,4096]{1,0:T(8,128)(2,1)}, bf16[128,4096]{1,0:T(8,128)(2,1)S(1)}, u32[]{:S(2)}, u32[]{:S(2)}) %collective-permute-start.13) | collective-permute-done | bytes 1048608 | tf_op jit(solution)/shard_map/ppermute | solution.py:394
  96.9 8.5 %decode_later.3 = (f32[4,128,256]{2,1,0:T(8,128)}, bf16[4,128,256]{2,1,0:T(8,128)(2,1)}) custom-call(s32[7]{0:T(128)} %stack.31.info, bf16[128,4096]{1,0:T(8,128)(2,1)} %collective-permute-done.12.direct, bf16[128,4096]{1,0:T(8,128)(2,1)S(1)} %collective-permute-done.13.swapped, f32[384,2048]{1,0:T(8,128)} %get-tuple-element.53.base, ...), custom_call_target="tpu_custom_call" | custom-call | tf_op jit(solution)/shard_map/decode_later/pallas_call | solution.py:285
  106.1 8.3 %collective-permute-done.15.refs_3_ = bf16[4,128,256]{2,1,0:T(8,128)(2,1)S(1)} collective-permute-done((bf16[4,128,256]{2,1,0:T(8,128)(2,1)}, bf16[4,128,256]{2,1,0:T(8,128)(2,1)S(1)}, u32[]{:S(2)}, u32[]{:S(2)}) %collective-permute-start.15) | collective-permute-done | bytes 262176 | tf_op jit(solution)/shard_map/ppermute | solution.py:16
  114.3 1.9 %add_pair.3 = (f32[256,256]{1,0:T(8,128)S(1)}, bf16[256,256]{1,0:T(8,128)(2,1)S(1)}, bf16[256,256]{1,0:T(8,128)(2,1)S(1)}, bf16[256,256]{1,0:T(8,128)(2,1)S(1)}) custom-call(s32[7]{0:T(128)S(1)} %copy-done.11, f32[4,128,256]{2,1,0:T(8,128)} %get-tuple-element.50.refs_0_, f32[4,128,256]{2,1,0:T(8,128)} %get-tuple-element.56.refs_1_, ...), custom_call_target="tpu_custom_call" | custom-call | tf_op jit(solution)/shard_map/add_pair/pallas_call | solution.py:329
  118.3 2.1 %collective-permute-start.20 = (bf16[256,4096]{1,0:T(8,128)(2,1)}, bf16[256,4096]{1,0:T(8,128)(2,1)S(1)}, u32[]{:S(2)}, u32[]{:S(2)}) collective-permute-start(bf16[256,4096]{1,0:T(8,128)(2,1)} %collective-permute-done.19.direct), channel_id=1, source_target_pairs={{16,24},{24,16},{17,25},{25,17},{18,26},{26,18},{19,27},{27,19},{2... | collective-permute-start | bytes 6291464 | tf_op jit(solution)/shard_map/ppermute | solution.py:394
  120.4 2.7 %collective-permute-start.16 = (bf16[256,256]{1,0:T(8,128)(2,1)S(1)}, bf16[256,256]{1,0:T(8,128)(2,1)S(1)}, u32[]{:S(2)}, u32[]{:S(2)}) collective-permute-start(bf16[256,256]{1,0:T(8,128)(2,1)S(1)} %get-tuple-element.59), channel_id=1, source_target_pairs={{0,2},{1,3},{2,0},{3,1},{4,6},{5,7},{6,4},{7,5},{8,10},{9,11},{10,... | collective-permute-start | bytes 393224 | tf_op jit(solution)/shard_map/ppermute | solution.py:16
  123.2 2.6 %collective-permute-start.17 = (bf16[256,256]{1,0:T(8,128)(2,1)S(1)}, bf16[256,256]{1,0:T(8,128)(2,1)S(1)}, u32[]{:S(2)}, u32[]{:S(2)}) collective-permute-start(bf16[256,256]{1,0:T(8,128)(2,1)S(1)} %get-tuple-element.60), channel_id=1, source_target_pairs={{0,4},{1,5},{2,6},{3,7},{4,0},{5,1},{6,2},{7,3},{8,12},{9,13},{10,... | collective-permute-start | bytes 393224 | tf_op jit(solution)/shard_map/ppermute | solution.py:16
  127.2 8.4 %decode_later.4 = (f32[4,128,256]{2,1,0:T(8,128)}, bf16[4,128,256]{2,1,0:T(8,128)(2,1)}) custom-call(s32[7]{0:T(128)} %stack.31.info, bf16[256,4096]{1,0:T(8,128)(2,1)} %collective-permute-done.19.direct, bf16[256,4096]{1,0:T(8,128)(2,1)S(1)} %collective-permute-done.20.swapped, f32[384,2048]{1,0:T(8,128)} %get-tuple-element.53.base, ...), custom_call_target="tpu_custom_call" | custom-call | tf_op jit(solution)/shard_map/decode_later/pallas_call | solution.py:285
  139.2 8.5 %decode_later.5 = (f32[4,128,256]{2,1,0:T(8,128)}, bf16[4,128,256]{2,1,0:T(8,128)(2,1)}) custom-call(s32[7]{0:T(128)} %stack.31.info, bf16[256,4096]{1,0:T(8,128)(2,1)} %collective-permute-done.19.direct, bf16[256,4096]{1,0:T(8,128)(2,1)S(1)} %collective-permute-done.20.swapped, f32[384,2048]{1,0:T(8,128)} %get-tuple-element.53.base, ...), custom_call_target="tpu_custom_call" | custom-call | tf_op jit(solution)/shard_map/decode_later/pallas_call | solution.py:285
  149.8 1.6 add_pair.4
  151.5 2.0 %collective-permute-start.22 = (bf16[128,256]{1,0:T(8,128)(2,1)S(1)}, bf16[128,256]{1,0:T(8,128)(2,1)S(1)}, u32[]{:S(2)}, u32[]{:S(2)}) collective-permute-start(bf16[128,256]{1,0:T(8,128)(2,1)S(1)} %get-tuple-element.67), channel_id=1, source_target_pairs={{0,2},{1,3},{2,0},{3,1},{4,6},{5,7},{6,4},{7,5},{8,10},{9,11},{10,... | collective-permute-start | bytes 196616 | tf_op jit(solution)/shard_map/ppermute | solution.py:16
  153.5 2.0 %collective-permute-start.23 = (bf16[128,256]{1,0:T(8,128)(2,1)S(1)}, bf16[128,256]{1,0:T(8,128)(2,1)S(1)}, u32[]{:S(2)}, u32[]{:S(2)}) collective-permute-start(bf16[128,256]{1,0:T(8,128)(2,1)S(1)} %get-tuple-element.68), channel_id=1, source_target_pairs={{0,4},{1,5},{2,6},{3,7},{4,0},{5,1},{6,2},{7,3},{8,12},{9,13},{10,... | collective-permute-start | bytes 196616 | tf_op jit(solution)/shard_map/ppermute | solution.py:16
  156.9 1.7 add_pair.5
  158.5 1.8 %collective-permute-start.26 = (bf16[128,256]{1,0:T(8,128)(2,1)S(1)}, bf16[128,256]{1,0:T(8,128)(2,1)S(1)}, u32[]{:S(2)}, u32[]{:S(2)}) collective-permute-start(bf16[128,256]{1,0:T(8,128)(2,1)S(1)} %get-tuple-element.72), channel_id=1, source_target_pairs={{0,2},{1,3},{2,0},{3,1},{4,6},{5,7},{6,4},{7,5},{8,10},{9,11},{10,... | collective-permute-start | bytes 196616 | tf_op jit(solution)/shard_map/ppermute | solution.py:16
  160.3 2.0 %collective-permute-start.27 = (bf16[128,256]{1,0:T(8,128)(2,1)S(1)}, bf16[128,256]{1,0:T(8,128)(2,1)S(1)}, u32[]{:S(2)}, u32[]{:S(2)}) collective-permute-start(bf16[128,256]{1,0:T(8,128)(2,1)S(1)} %get-tuple-element.73), channel_id=1, source_target_pairs={{0,4},{1,5},{2,6},{3,7},{4,0},{5,1},{6,2},{7,3},{8,12},{9,13},{10,... | collective-permute-start | bytes 196616 | tf_op jit(solution)/shard_map/ppermute | solution.py:16
  163.7 3.8 %collective-permute-done.27.refs_6_ = bf16[128,256]{1,0:T(8,128)(2,1)S(1)} collective-permute-done((bf16[128,256]{1,0:T(8,128)(2,1)S(1)}, bf16[128,256]{1,0:T(8,128)(2,1)S(1)}, u32[]{:S(2)}, u32[]{:S(2)}) %collective-permute-start.27) | collective-permute-done | bytes 65568 | tf_op jit(solution)/shard_map/ppermute | solution.py:16
  (72 shorter events, 27.6 us)
Async XLA Ops:
  0.0 8.3 %collective-permute-start.1 = (bf16[64,2048]{1,0:T(8,128)(2,1)}, bf16[64,2048]{1,0:T(8,128)(2,1)S(1)}, u32[]{:S(2)}, u32[]{:S(2)}) collective-permute-start(bf16[64,2048]{1,0:T(8,128)(2,1)} %bitcast.10), channel_id=1, source_target_pairs={{0,1},{1,0},{2,3},{3,2},{4,5},{5,4},{6,7},{7,6},{8,9},{9,8},{10,11... | collective-permute-start | bytes 786440 | tf_op jit(solution)/shard_map/ppermute | solution.py:16
  1.5 21.3 %collective-permute-start.3 = (bf16[64,2048]{1,0:T(8,128)(2,1)}, bf16[64,2048]{1,0:T(8,128)(2,1)S(1)}, u32[]{:S(2)}, u32[]{:S(2)}) collective-permute-start(bf16[64,2048]{1,0:T(8,128)(2,1)} %bitcast.11), channel_id=1, source_target_pairs={{0,4},{1,5},{2,6},{3,7},{4,0},{5,1},{6,2},{7,3},{8,12},{9,13},{10,... | collective-permute-start | bytes 786440 | tf_op jit(solution)/shard_map/ppermute | solution.py:16
  4.1 18.8 %collective-permute-start.4 = (bf16[64,2048]{1,0:T(8,128)(2,1)}, bf16[64,2048]{1,0:T(8,128)(2,1)S(1)}, u32[]{:S(2)}, u32[]{:S(2)}) collective-permute-start(bf16[64,2048]{1,0:T(8,128)(2,1)} %bitcast.12), channel_id=1, source_target_pairs={{0,6},{1,7},{2,4},{3,5},{4,2},{5,3},{6,0},{7,1},{8,14},{9,15},{10,... | collective-permute-start | bytes 786440 | tf_op jit(solution)/shard_map/ppermute | solution.py:16
  5.5 19.6 %collective-permute-start = (bf16[64,2048]{1,0:T(8,128)(2,1)}, bf16[64,2048]{1,0:T(8,128)(2,1)S(1)}, u32[]{:S(2)}, u32[]{:S(2)}) collective-permute-start(bf16[64,2048]{1,0:T(8,128)(2,1)} %bitcast.13), channel_id=1, source_target_pairs={{0,2},{1,3},{2,0},{3,1},{4,6},{5,7},{6,4},{7,5},{8,10},{9,11},{10,... | collective-permute-start | bytes 786440 | tf_op jit(solution)/shard_map/ppermute | solution.py:16
  8.3 20.4 %collective-permute-start.2 = (bf16[64,2048]{1,0:T(8,128)(2,1)S(1)}, bf16[64,2048]{1,0:T(8,128)(2,1)S(1)}, u32[]{:S(2)}, u32[]{:S(2)}) collective-permute-start(bf16[64,2048]{1,0:T(8,128)(2,1)S(1)} %collective-permute-done.1.refs_1_), channel_id=1, source_target_pairs={{0,2},{1,3},{2,0},{3,1},{4,6},{5,7},{6,4},{7,5},{8,10},{9,11},{10,... | collective-permute-start | bytes 786440 | tf_op jit(solution)/shard_map/ppermute | solution.py:16
  11.5 18.9 %copy-start.10 = (f32[1,4096]{1,0:T(1,128)S(1)}, f32[1,4096]{1,0:T(1,128)}, u32[]{:S(2)}) copy-start(f32[1,4096]{1,0:T(1,128)} %refs_4_.1) | copy-start | bytes 49156
  18.0 17.8 %collective-permute-start.6 = (bf16[64,4096]{1,0:T(8,128)(2,1)S(1)}, bf16[64,4096]{1,0:T(8,128)(2,1)S(1)}, u32[]{:S(2)}, u32[]{:S(2)}) collective-permute-start(bf16[64,4096]{1,0:T(8,128)(2,1)S(1)} %get-tuple-element.45), channel_id=1, source_target_pairs={{0,16},{8,24},{1,17},{9,25},{2,18},{10,26},{3,19},{11,27},{4,20},{... | collective-permute-start | bytes 1572872 | tf_op jit(solution)/shard_map/ppermute | solution.py:391
  28.6 11.9 %collective-permute-start.5 = (bf16[128,2048]{1,0:T(8,128)(2,1)S(1)}, bf16[128,2048]{1,0:T(8,128)(2,1)S(1)}, u32[]{:S(2)}, u32[]{:S(2)}) collective-permute-start(bf16[128,2048]{1,0:T(8,128)(2,1)S(1)} %pad_maximum_fusion), channel_id=1, source_target_pairs={{0,1},{1,0},{2,3},{3,2},{4,5},{5,4},{6,7},{7,6},{8,9},{9,8},{10,11... | collective-permute-start | bytes 1572872 | tf_op jit(solution)/shard_map/ppermute | solution.py:16
  29.1 17.2 %collective-permute-start.8 = (bf16[64,4096]{1,0:T(8,128)(2,1)S(1)}, bf16[64,4096]{1,0:T(8,128)(2,1)S(1)}, u32[]{:S(2)}, u32[]{:S(2)}) collective-permute-start(bf16[64,4096]{1,0:T(8,128)(2,1)S(1)} %get-tuple-element.46), channel_id=1, source_target_pairs={{0,16},{8,24},{1,17},{9,25},{2,18},{10,26},{3,19},{11,27},{4,20},{... | collective-permute-start | bytes 1572872 | tf_op jit(solution)/shard_map/ppermute | solution.py:391
  35.8 19.1 %copy-start.2 = (bf16[64,4096]{1,0:T(8,128)(2,1)}, bf16[64,4096]{1,0:T(8,128)(2,1)S(1)}, u32[]{:S(2)}) copy-start(bf16[64,4096]{1,0:T(8,128)(2,1)S(1)} %collective-permute-done.6.refs_6_.refs_4_) | copy-start | bytes 1572868
  46.4 6.6 %collective-permute-start.9 = (bf16[256,4096]{1,0:T(8,128)(2,1)S(1)}, bf16[256,4096]{1,0:T(8,128)(2,1)S(1)}, u32[]{:S(2)}, u32[]{:S(2)}) collective-permute-start(bf16[256,4096]{1,0:T(8,128)(2,1)S(1)} %encode.5.refs_1_), channel_id=1, source_target_pairs={{0,8},{16,24},{1,9},{17,25},{2,10},{18,26},{3,11},{19,27},{4,12},{... | collective-permute-start | bytes 6291464 | tf_op jit(solution)/shard_map/ppermute | solution.py:397
  47.8 10.3 %collective-permute-start.7 = (bf16[256,4096]{1,0:T(8,128)(2,1)}, bf16[256,4096]{1,0:T(8,128)(2,1)}, u32[]{:S(2)}, u32[]{:S(2)}) collective-permute-start(bf16[256,4096]{1,0:T(8,128)(2,1)} %get-tuple-element.42.refs_0_), channel_id=1, source_target_pairs={{0,8},{16,24},{1,9},{17,25},{2,10},{18,26},{3,11},{19,27},{4,12},{... | collective-permute-start | bytes 6291464 | tf_op jit(solution)/shard_map/ppermute | solution.py:397
  50.4 32.7 %collective-permute-start.12 = (bf16[128,4096]{1,0:T(8,128)(2,1)}, bf16[128,4096]{1,0:T(8,128)(2,1)}, u32[]{:S(2)}, u32[]{:S(2)}) collective-permute-start(bf16[128,4096]{1,0:T(8,128)(2,1)} %get-tuple-element.44.refs_5_), channel_id=1, source_target_pairs={{0,16},{8,24},{1,17},{9,25},{2,18},{10,26},{3,19},{11,27},{4,20},{... | collective-permute-start | bytes 3145736 | tf_op jit(solution)/shard_map/ppermute | solution.py:391
  51.7 66.7 %collective-permute-start.19 = (bf16[256,4096]{1,0:T(8,128)(2,1)S(1)}, bf16[256,4096]{1,0:T(8,128)(2,1)}, u32[]{:S(2)}, u32[]{:S(2)}) collective-permute-start(bf16[256,4096]{1,0:T(8,128)(2,1)S(1)} %encode.5.refs_1_), channel_id=1, source_target_pairs={{0,16},{8,24},{1,17},{9,25},{2,18},{10,26},{3,19},{11,27},{4,20},{... | collective-permute-start | bytes 6291464 | tf_op jit(solution)/shard_map/ppermute | solution.py:391
  53.0 5.1 %collective-permute-start.11 = (bf16[64,4096]{1,0:T(8,128)(2,1)S(1)}, bf16[64,4096]{1,0:T(8,128)(2,1)}, u32[]{:S(2)}, u32[]{:S(2)}) collective-permute-start(bf16[64,4096]{1,0:T(8,128)(2,1)S(1)} %collective-permute-done.8.refs_5_), channel_id=1, source_target_pairs={{16,24},{24,16},{17,25},{25,17},{18,26},{26,18},{19,27},{27,19},{2... | collective-permute-start | bytes 1572872 | tf_op jit(solution)/shard_map/ppermute | solution.py:394
  54.9 4.1 %collective-permute-start.10 = (bf16[64,4096]{1,0:T(8,128)(2,1)S(1)}, bf16[64,4096]{1,0:T(8,128)(2,1)}, u32[]{:S(2)}, u32[]{:S(2)}) collective-permute-start(bf16[64,4096]{1,0:T(8,128)(2,1)S(1)} %collective-permute-done.6.refs_6_.refs_4_), channel_id=1, source_target_pairs={{16,24},{24,16},{17,25},{25,17},{18,26},{26,18},{19,27},{27,19},{2... | collective-permute-start | bytes 1572872 | tf_op jit(solution)/shard_map/ppermute | solution.py:394
  83.1 13.8 %collective-permute-start.13 = (bf16[128,4096]{1,0:T(8,128)(2,1)}, bf16[128,4096]{1,0:T(8,128)(2,1)S(1)}, u32[]{:S(2)}, u32[]{:S(2)}) collective-permute-start(bf16[128,4096]{1,0:T(8,128)(2,1)} %collective-permute-done.12.direct), channel_id=1, source_target_pairs={{16,24},{24,16},{17,25},{25,17},{18,26},{26,18},{19,27},{27,19},{2... | collective-permute-start | bytes 3145736 | tf_op jit(solution)/shard_map/ppermute | solution.py:394
  94.5 11.6 %collective-permute-start.14 = (bf16[4,128,256]{2,1,0:T(8,128)(2,1)}, bf16[4,128,256]{2,1,0:T(8,128)(2,1)S(1)}, u32[]{:S(2)}, u32[]{:S(2)}) collective-permute-start(bf16[4,128,256]{2,1,0:T(8,128)(2,1)} %get-tuple-element.51.refs_0_), channel_id=1, source_target_pairs={{0,1},{1,0},{2,3},{3,2},{4,5},{5,4},{6,7},{7,6},{8,9},{9,8},{10,11... | collective-permute-start | bytes 786440 | tf_op jit(solution)/shard_map/ppermute | solution.py:16
  105.5 8.9 %collective-permute-start.15 = (bf16[4,128,256]{2,1,0:T(8,128)(2,1)}, bf16[4,128,256]{2,1,0:T(8,128)(2,1)S(1)}, u32[]{:S(2)}, u32[]{:S(2)}) collective-permute-start(bf16[4,128,256]{2,1,0:T(8,128)(2,1)} %get-tuple-element.57), channel_id=1, source_target_pairs={{0,1},{1,0},{2,3},{3,2},{4,5},{5,4},{6,7},{7,6},{8,9},{9,8},{10,11... | collective-permute-start | bytes 786440 | tf_op jit(solution)/shard_map/ppermute | solution.py:16
  118.3 8.9 %collective-permute-start.20 = (bf16[256,4096]{1,0:T(8,128)(2,1)}, bf16[256,4096]{1,0:T(8,128)(2,1)S(1)}, u32[]{:S(2)}, u32[]{:S(2)}) collective-permute-start(bf16[256,4096]{1,0:T(8,128)(2,1)} %collective-permute-done.19.direct), channel_id=1, source_target_pairs={{16,24},{24,16},{17,25},{25,17},{18,26},{26,18},{19,27},{27,19},{2... | collective-permute-start | bytes 6291464 | tf_op jit(solution)/shard_map/ppermute | solution.py:394
  120.4 15.8 %collective-permute-start.16 = (bf16[256,256]{1,0:T(8,128)(2,1)S(1)}, bf16[256,256]{1,0:T(8,128)(2,1)S(1)}, u32[]{:S(2)}, u32[]{:S(2)}) collective-permute-start(bf16[256,256]{1,0:T(8,128)(2,1)S(1)} %get-tuple-element.59), channel_id=1, source_target_pairs={{0,2},{1,3},{2,0},{3,1},{4,6},{5,7},{6,4},{7,5},{8,10},{9,11},{10,... | collective-permute-start | bytes 393224 | tf_op jit(solution)/shard_map/ppermute | solution.py:16
  123.2 13.1 %collective-permute-start.17 = (bf16[256,256]{1,0:T(8,128)(2,1)S(1)}, bf16[256,256]{1,0:T(8,128)(2,1)S(1)}, u32[]{:S(2)}, u32[]{:S(2)}) collective-permute-start(bf16[256,256]{1,0:T(8,128)(2,1)S(1)} %get-tuple-element.60), channel_id=1, source_target_pairs={{0,4},{1,5},{2,6},{3,7},{4,0},{5,1},{6,2},{7,3},{8,12},{9,13},{10,... | collective-permute-start | bytes 393224 | tf_op jit(solution)/shard_map/ppermute | solution.py:16
  125.8 11.0 %collective-permute-start.18 = (bf16[256,256]{1,0:T(8,128)(2,1)S(1)}, bf16[256,256]{1,0:T(8,128)(2,1)S(1)}, u32[]{:S(2)}, u32[]{:S(2)}) collective-permute-start(bf16[256,256]{1,0:T(8,128)(2,1)S(1)} %get-tuple-element.61), channel_id=1, source_target_pairs={{0,6},{1,7},{2,4},{3,5},{4,2},{5,3},{6,0},{7,1},{8,14},{9,15},{10,... | collective-permute-start | bytes 393224 | tf_op jit(solution)/shard_map/ppermute | solution.py:16
  135.6 13.2 %collective-permute-start.21 = (bf16[4,128,256]{2,1,0:T(8,128)(2,1)}, bf16[4,128,256]{2,1,0:T(8,128)(2,1)S(1)}, u32[]{:S(2)}, u32[]{:S(2)}) collective-permute-start(bf16[4,128,256]{2,1,0:T(8,128)(2,1)} %get-tuple-element.63.refs_4_.refs_0_), channel_id=1, source_target_pairs={{0,1},{1,0},{2,3},{3,2},{4,5},{5,4},{6,7},{7,6},{8,9},{9,8},{10,11... | collective-permute-start | bytes 786440 | tf_op jit(solution)/shard_map/ppermute | solution.py:16
  139.2 29.3 %copy-start.1 = (f32[512,256]{1,0:T(8,128)S(1)}, f32[512,256]{1,0:T(8,128)}, u32[]{:S(2)}) copy-start(f32[512,256]{1,0:T(8,128)} %add_up.2.refs_1_.base) | copy-start | bytes 1572868
  147.7 9.1 %collective-permute-start.25 = (bf16[4,128,256]{2,1,0:T(8,128)(2,1)}, bf16[4,128,256]{2,1,0:T(8,128)(2,1)S(1)}, u32[]{:S(2)}, u32[]{:S(2)}) collective-permute-start(bf16[4,128,256]{2,1,0:T(8,128)(2,1)} %get-tuple-element.65.refs_2_), channel_id=1, source_target_pairs={{0,1},{1,0},{2,3},{3,2},{4,5},{5,4},{6,7},{7,6},{8,9},{9,8},{10,11... | collective-permute-start | bytes 786440 | tf_op jit(solution)/shard_map/ppermute | solution.py:16
  151.5 5.4 %collective-permute-start.22 = (bf16[128,256]{1,0:T(8,128)(2,1)S(1)}, bf16[128,256]{1,0:T(8,128)(2,1)S(1)}, u32[]{:S(2)}, u32[]{:S(2)}) collective-permute-start(bf16[128,256]{1,0:T(8,128)(2,1)S(1)} %get-tuple-element.67), channel_id=1, source_target_pairs={{0,2},{1,3},{2,0},{3,1},{4,6},{5,7},{6,4},{7,5},{8,10},{9,11},{10,... | collective-permute-start | bytes 196616 | tf_op jit(solution)/shard_map/ppermute | solution.py:16
  153.5 10.3 %collective-permute-start.23 = (bf16[128,256]{1,0:T(8,128)(2,1)S(1)}, bf16[128,256]{1,0:T(8,128)(2,1)S(1)}, u32[]{:S(2)}, u32[]{:S(2)}) collective-permute-start(bf16[128,256]{1,0:T(8,128)(2,1)S(1)} %get-tuple-element.68), channel_id=1, source_target_pairs={{0,4},{1,5},{2,6},{3,7},{4,0},{5,1},{6,2},{7,3},{8,12},{9,13},{10,... | collective-permute-start | bytes 196616 | tf_op jit(solution)/shard_map/ppermute | solution.py:16
  155.5 8.3 %collective-permute-start.24 = (bf16[128,256]{1,0:T(8,128)(2,1)S(1)}, bf16[128,256]{1,0:T(8,128)(2,1)S(1)}, u32[]{:S(2)}, u32[]{:S(2)}) collective-permute-start(bf16[128,256]{1,0:T(8,128)(2,1)S(1)} %get-tuple-element.69), channel_id=1, source_target_pairs={{0,6},{1,7},{2,4},{3,5},{4,2},{5,3},{6,0},{7,1},{8,14},{9,15},{10,... | collective-permute-start | bytes 196616 | tf_op jit(solution)/shard_map/ppermute | solution.py:16
  158.5 5.2 %collective-permute-start.26 = (bf16[128,256]{1,0:T(8,128)(2,1)S(1)}, bf16[128,256]{1,0:T(8,128)(2,1)S(1)}, u32[]{:S(2)}, u32[]{:S(2)}) collective-permute-start(bf16[128,256]{1,0:T(8,128)(2,1)S(1)} %get-tuple-element.72), channel_id=1, source_target_pairs={{0,2},{1,3},{2,0},{3,1},{4,6},{5,7},{6,4},{7,5},{8,10},{9,11},{10,... | collective-permute-start | bytes 196616 | tf_op jit(solution)/shard_map/ppermute | solution.py:16
  160.3 7.2 %collective-permute-start.27 = (bf16[128,256]{1,0:T(8,128)(2,1)S(1)}, bf16[128,256]{1,0:T(8,128)(2,1)S(1)}, u32[]{:S(2)}, u32[]{:S(2)}) collective-permute-start(bf16[128,256]{1,0:T(8,128)(2,1)S(1)} %get-tuple-element.73), channel_id=1, source_target_pairs={{0,4},{1,5},{2,6},{3,7},{4,0},{5,1},{6,2},{7,3},{8,12},{9,13},{10,... | collective-permute-start | bytes 196616 | tf_op jit(solution)/shard_map/ppermute | solution.py:16
  162.3 6.1 %collective-permute-start.28 = (bf16[128,256]{1,0:T(8,128)(2,1)S(1)}, bf16[128,256]{1,0:T(8,128)(2,1)S(1)}, u32[]{:S(2)}, u32[]{:S(2)}) collective-permute-start(bf16[128,256]{1,0:T(8,128)(2,1)S(1)} %get-tuple-element.74), channel_id=1, source_target_pairs={{0,6},{1,7},{2,4},{3,5},{4,2},{5,3},{6,0},{7,1},{8,14},{9,15},{10,... | collective-permute-start | bytes 196616 | tf_op jit(solution)/shard_map/ppermute | solution.py:16
  (13 other events, 94.0 us)

commit v13 on v12

--- a/solution.py
+++ b/solution.py
@@ -440,7 +440,7 @@
     )
     d2, n2 = up(a2), beside(after(a2, d0b))
 
-    c0a, c0b = across(after(d0a, n2)), across(after(d0b, n2))
+    c0a, c0b = across(after(d0a, n2, n01)), across(after(d0b, n2, n01))
     mine, sent, base, *kept = decode_first(
         info, [a01, a2], [n01, n2], [d0a, d0b], [c0a, c0b], decoder, shards, []
     )

time: 171 us -> 169 us (0.988)
    unnamed x32 -> x36, local copies, waits for them, and re-layouts: 4.31 us -> 4.32 us
  transfers between devices with their start and end apart: 29 -> 29, of which waited for: 12 -> 13; matrix products, arithmetic and copies ran while one was open for 0% -> 0% of each run, Pallas kernels for 44% -> 43%
where the time goes in v13:
time: 169 us
  Pallas kernels  74.7 us (44%)
  starting transfers between devices  53.5 us (32%)
  waiting for transfers between devices  35.1 us (21%)
  local copies, waits for them, and re-layouts  4.99 us (3%)
    ppermute x19, waiting for transfers between devices, exchange(): return lax.ppermute(array, axis, [(i, i ^ flip) for i in range(size)])  29.3 us
    ppermute x19, starting transfers between devices, exchange(): return lax.ppermute(array, axis, [(i, i ^ flip) for i in range(size)])  28 us
    pallas_call x3, Pallas kernels, decode_later(): pl.pallas_call(functools.partial(later_wave_kernel, row, skip), in_specs=...  25.4 us
    pallas_call x1, Pallas kernels, decode_first(): pl.pallas_call(functools.partial(first_wave_kernel, [len(parts) for parts...  24.1 us
    ppermute x4, starting transfers between devices, across(): return lax.ppermute(a, 'layer', [(i, i ^ 1) for i in range(half, layers)])  17.6 us
    pallas_call x3, Pallas kernels, encode(): pl.pallas_call(functools.partial(encode_kernel, order, pieces, len(parts)...  17.1 us
    ppermute x4, starting transfers between devices, up(): return lax.ppermute(a, 'layer', [(i, i + half) for i in range(half)])  5.16 us
    pallas_call x3, Pallas kernels, add_pair(): pl.pallas_call(functools.partial(pair_kernel, size, len(mine), len(after)...  5.15 us
  transfers between devices with their start and end apart: 29, of which 13 were waited for; matrix products, arithmetic and copies ran while one was open for 0% of the time, Pallas kernels for 43%

profile of v13, /device:TPU:2, one launch (start us, length us, event | category | flops | bytes accessed | tf_op | source)
XLA Modules:
  0.0 168.7 jit_solution(17956910634251336702)
XLA Ops:
  0.0 1.5 collective-permute-start.1
  1.5 2.6 %collective-permute-start.3 = (bf16[64,2048]{1,0:T(8,128)(2,1)}, bf16[64,2048]{1,0:T(8,128)(2,1)S(1)}, u32[]{:S(2)}, u32[]{:S(2)}) collective-permute-start(bf16[64,2048]{1,0:T(8,128)(2,1)} %bitcast.11), channel_id=1, source_target_pairs={{0,4},{1,5},{2,6},{3,7},{4,0},{5,1},{6,2},{7,3},{8,12},{9,13},{10,... | collective-permute-start | bytes 786440 | tf_op jit(solution)/shard_map/ppermute | solution.py:16
  5.7 2.6 %collective-permute-done.1.refs_1_ = bf16[64,2048]{1,0:T(8,128)(2,1)S(1)} collective-permute-done((bf16[64,2048]{1,0:T(8,128)(2,1)}, bf16[64,2048]{1,0:T(8,128)(2,1)S(1)}, u32[]{:S(2)}, u32[]{:S(2)}) %collective-permute-start.1) | collective-permute-done | bytes 262176 | tf_op jit(solution)/shard_map/ppermute | solution.py:16
  8.3 1.6 collective-permute-start.2
  11.5 6.5 %encode.3 = (bf16[128,4096]{1,0:T(8,128)(2,1)S(1)}, bf16[64,4096]{1,0:T(8,128)(2,1)S(1)}, bf16[64,4096]{1,0:T(8,128)(2,1)S(1)}, bf16[1,2048,4096]{2,1,0:T(8,128)(2,1)S(1)}) custom-call(bf16[64,2048]{1,0:T(8,128)(2,1)S(1)} %bitcast.14, bf16[64,2048]{1,0:T(8,128)(2,1)S(1)} %collective-permute-done.1.refs_1_, bf16[1,2048,4096]{2,1,0:T(8,128)(2,1)} %refs_2_.1, ...), custom_call_target="tpu_custom_call" | custom-call | tf_op jit(solution)/shard_map/encode/pallas_call | solution.py:91
  19.3 3.5 %collective-permute-done.3.refs_0_ = bf16[64,2048]{1,0:T(8,128)(2,1)S(1)} collective-permute-done((bf16[64,2048]{1,0:T(8,128)(2,1)}, bf16[64,2048]{1,0:T(8,128)(2,1)S(1)}, u32[]{:S(2)}, u32[]{:S(2)}) %collective-permute-start.3) | collective-permute-done | bytes 262176 | tf_op jit(solution)/shard_map/ppermute | solution.py:16
  22.9 2.1 %collective-permute-done.refs_0_ = bf16[64,2048]{1,0:T(8,128)(2,1)S(1)} collective-permute-done((bf16[64,2048]{1,0:T(8,128)(2,1)}, bf16[64,2048]{1,0:T(8,128)(2,1)S(1)}, u32[]{:S(2)}, u32[]{:S(2)}) %collective-permute-start) | collective-permute-done | bytes 262176 | tf_op jit(solution)/shard_map/ppermute | solution.py:16
  25.0 3.6 %collective-permute-done.2.refs_1_ = bf16[64,2048]{1,0:T(8,128)(2,1)S(1)} collective-permute-done((bf16[64,2048]{1,0:T(8,128)(2,1)S(1)}, bf16[64,2048]{1,0:T(8,128)(2,1)S(1)}, u32[]{:S(2)}, u32[]{:S(2)}) %collective-permute-start.2) | collective-permute-done | bytes 262176 | tf_op jit(solution)/shard_map/ppermute | solution.py:16
  30.4 4.7 %encode.4 = (bf16[256,4096]{1,0:T(8,128)(2,1)S(1)}, bf16[128,4096]{1,0:T(8,128)(2,1)}) custom-call(bf16[64,2048]{1,0:T(8,128)(2,1)S(1)} %collective-permute-done.refs_0_, bf16[64,2048]{1,0:T(8,128)(2,1)S(1)} %collective-permute-done.2.refs_1_, bf16[1,2048,4096]{2,1,0:T(8,128)(2,1)S(1)} %get-tuple-element.40.refs_2_.refs_3_, f32[1,4096]{1,0:T(1,128)S(1)} %copy-done.11, ...), custom_call_target="tpu_custom_call" | custom-call | tf_op jit(solution)/shard_map/encode/pallas_call | solution.py:91
  36.6 3.9 %collective-permute-done.5.refs_2_ = bf16[128,2048]{1,0:T(8,128)(2,1)S(1)} collective-permute-done((bf16[128,2048]{1,0:T(8,128)(2,1)S(1)}, bf16[128,2048]{1,0:T(8,128)(2,1)S(1)}, u32[]{:S(2)}, u32[]{:S(2)}) %collective-permute-start.5) | collective-permute-done | bytes 524320 | tf_op jit(solution)/shard_map/ppermute | solution.py:16
  40.5 5.8 %encode.5.refs_1_ = bf16[256,4096]{1,0:T(8,128)(2,1)S(1)} custom-call(bf16[64,2048]{1,0:T(8,128)(2,1)S(1)} %collective-permute-done.3.refs_0_, bf16[64,2048]{1,0:T(8,128)(2,1)S(1)} %collective-permute-done.4.refs_1_, bf16[128,2048]{1,0:T(8,128)(2,1)S(1)} %collective-permute-done.5.refs_2_, bf16[1,2048,4096]{2,1,0:T(8,128)(2,1)S(1)} %get-tuple-element.40.refs_2_.refs_3_, ...), custom_call_target="tpu_custom_call" | custom-call | tf_op jit(solution)/shard_map/encode/pallas_call | solution.py:91
  51.4 2.3 %collective-permute-start.11 = (bf16[64,4096]{1,0:T(8,128)(2,1)S(1)}, bf16[64,4096]{1,0:T(8,128)(2,1)}, u32[]{:S(2)}, u32[]{:S(2)}) collective-permute-start(bf16[64,4096]{1,0:T(8,128)(2,1)S(1)} %collective-permute-done.8.refs_5_), channel_id=1, source_target_pairs={{16,24},{24,16},{17,25},{25,17},{18,26},{26,18},{19,27},{27,19},{2... | collective-permute-start | bytes 1572872 | tf_op jit(solution)/shard_map/ppermute | solution.py:394
  53.7 2.0 %collective-permute-start.10 = (bf16[64,4096]{1,0:T(8,128)(2,1)S(1)}, bf16[64,4096]{1,0:T(8,128)(2,1)}, u32[]{:S(2)}, u32[]{:S(2)}) collective-permute-start(bf16[64,4096]{1,0:T(8,128)(2,1)S(1)} %collective-permute-done.6.refs_6_.refs_4_), channel_id=1, source_target_pairs={{16,24},{24,16},{17,25},{25,17},{18,26},{26,18},{19,27},{27,19},{2... | collective-permute-start | bytes 1572872 | tf_op jit(solution)/shard_map/ppermute | solution.py:394
  57.7 24.1 %decode_first.1 = (f32[4,128,256]{2,1,0:T(8,128)}, bf16[4,128,256]{2,1,0:T(8,128)(2,1)}, f32[384,2048]{1,0:T(8,128)}, bf16[4096,2048]{1,0:T(8,128)(2,1)S(1)}, bf16[4096,2048]{1,0:T(8,128)(2,1)S(1)}) custom-call(s32[7]{0:T(128)} %stack.31.info, bf16[256,4096]{1,0:T(8,128)(2,1)} %copy-done.3, bf16[256,4096]{1,0:T(8,128)(2,1)} %copy-done, ...), custom_call_target="tpu_custom_call" | custom-call | tf_op jit(solution)/shard_map/decode_first/pallas_call | solution.py:224
  81.7 11.2 %collective-permute-start.13 = (bf16[128,4096]{1,0:T(8,128)(2,1)}, bf16[128,4096]{1,0:T(8,128)(2,1)S(1)}, u32[]{:S(2)}, u32[]{:S(2)}) collective-permute-start(bf16[128,4096]{1,0:T(8,128)(2,1)} %collective-permute-done.12.direct), channel_id=1, source_target_pairs={{16,24},{24,16},{17,25},{25,17},{18,26},{26,18},{19,27},{27,19},{2... | collective-permute-start | bytes 3145736 | tf_op jit(solution)/shard_map/ppermute | solution.py:394
  93.5 1.9 %collective-permute-done.13.swapped = bf16[128,4096]{1,0:T(8,128)(2,1)S(1)} collective-permute-done((bf16[128,4096]{1,0:T(8,128)(2,1)}, bf16[128,4096]{1,0:T(8,128)(2,1)S(1)}, u32[]{:S(2)}, u32[]{:S(2)}) %collective-permute-start.13) | collective-permute-done | bytes 1048608 | tf_op jit(solution)/shard_map/ppermute | solution.py:394
  95.4 8.5 %decode_later.3 = (f32[4,128,256]{2,1,0:T(8,128)}, bf16[4,128,256]{2,1,0:T(8,128)(2,1)}) custom-call(s32[7]{0:T(128)} %stack.31.info, bf16[128,4096]{1,0:T(8,128)(2,1)} %collective-permute-done.12.direct, bf16[128,4096]{1,0:T(8,128)(2,1)S(1)} %collective-permute-done.13.swapped, f32[384,2048]{1,0:T(8,128)} %get-tuple-element.53.base, ...), custom_call_target="tpu_custom_call" | custom-call | tf_op jit(solution)/shard_map/decode_later/pallas_call | solution.py:285
  104.5 8.3 %collective-permute-done.15.refs_3_ = bf16[4,128,256]{2,1,0:T(8,128)(2,1)S(1)} collective-permute-done((bf16[4,128,256]{2,1,0:T(8,128)(2,1)}, bf16[4,128,256]{2,1,0:T(8,128)(2,1)S(1)}, u32[]{:S(2)}, u32[]{:S(2)}) %collective-permute-start.15) | collective-permute-done | bytes 262176 | tf_op jit(solution)/shard_map/ppermute | solution.py:16
  112.8 1.9 %add_pair.3 = (f32[256,256]{1,0:T(8,128)S(1)}, bf16[256,256]{1,0:T(8,128)(2,1)S(1)}, bf16[256,256]{1,0:T(8,128)(2,1)S(1)}, bf16[256,256]{1,0:T(8,128)(2,1)S(1)}) custom-call(s32[7]{0:T(128)S(1)} %copy-done.12, f32[4,128,256]{2,1,0:T(8,128)} %get-tuple-element.50.refs_0_, f32[4,128,256]{2,1,0:T(8,128)} %get-tuple-element.56.refs_1_, ...), custom_call_target="tpu_custom_call" | custom-call | tf_op jit(solution)/shard_map/add_pair/pallas_call | solution.py:329
  115.4 1.7 collective-permute-done.19.direct
  117.0 2.1 %collective-permute-start.20 = (bf16[256,4096]{1,0:T(8,128)(2,1)}, bf16[256,4096]{1,0:T(8,128)(2,1)S(1)}, u32[]{:S(2)}, u32[]{:S(2)}) collective-permute-start(bf16[256,4096]{1,0:T(8,128)(2,1)} %collective-permute-done.19.direct), channel_id=1, source_target_pairs={{16,24},{24,16},{17,25},{25,17},{18,26},{26,18},{19,27},{27,19},{2... | collective-permute-start | bytes 6291464 | tf_op jit(solution)/shard_map/ppermute | solution.py:394
  119.1 2.7 %collective-permute-start.16 = (bf16[256,256]{1,0:T(8,128)(2,1)S(1)}, bf16[256,256]{1,0:T(8,128)(2,1)S(1)}, u32[]{:S(2)}, u32[]{:S(2)}) collective-permute-start(bf16[256,256]{1,0:T(8,128)(2,1)S(1)} %get-tuple-element.59), channel_id=1, source_target_pairs={{0,2},{1,3},{2,0},{3,1},{4,6},{5,7},{6,4},{7,5},{8,10},{9,11},{10,... | collective-permute-start | bytes 393224 | tf_op jit(solution)/shard_map/ppermute | solution.py:16
  121.9 2.6 %collective-permute-start.17 = (bf16[256,256]{1,0:T(8,128)(2,1)S(1)}, bf16[256,256]{1,0:T(8,128)(2,1)S(1)}, u32[]{:S(2)}, u32[]{:S(2)}) collective-permute-start(bf16[256,256]{1,0:T(8,128)(2,1)S(1)} %get-tuple-element.60), channel_id=1, source_target_pairs={{0,4},{1,5},{2,6},{3,7},{4,0},{5,1},{6,2},{7,3},{8,12},{9,13},{10,... | collective-permute-start | bytes 393224 | tf_op jit(solution)/shard_map/ppermute | solution.py:16
  125.9 8.4 %decode_later.4 = (f32[4,128,256]{2,1,0:T(8,128)}, bf16[4,128,256]{2,1,0:T(8,128)(2,1)}) custom-call(s32[7]{0:T(128)} %stack.31.info, bf16[256,4096]{1,0:T(8,128)(2,1)} %collective-permute-done.19.direct, bf16[256,4096]{1,0:T(8,128)(2,1)S(1)} %collective-permute-done.20.swapped, f32[384,2048]{1,0:T(8,128)} %get-tuple-element.53.base, ...), custom_call_target="tpu_custom_call" | custom-call | tf_op jit(solution)/shard_map/decode_later/pallas_call | solution.py:285
  137.9 8.5 %decode_later.5 = (f32[4,128,256]{2,1,0:T(8,128)}, bf16[4,128,256]{2,1,0:T(8,128)(2,1)}) custom-call(s32[7]{0:T(128)} %stack.31.info, bf16[256,4096]{1,0:T(8,128)(2,1)} %collective-permute-done.19.direct, bf16[256,4096]{1,0:T(8,128)(2,1)S(1)} %collective-permute-done.20.swapped, f32[384,2048]{1,0:T(8,128)} %get-tuple-element.53.base, ...), custom_call_target="tpu_custom_call" | custom-call | tf_op jit(solution)/shard_map/decode_later/pallas_call | solution.py:285
  148.5 1.6 add_pair.4
  150.2 2.0 %collective-permute-start.22 = (bf16[128,256]{1,0:T(8,128)(2,1)S(1)}, bf16[128,256]{1,0:T(8,128)(2,1)S(1)}, u32[]{:S(2)}, u32[]{:S(2)}) collective-permute-start(bf16[128,256]{1,0:T(8,128)(2,1)S(1)} %get-tuple-element.67), channel_id=1, source_target_pairs={{0,2},{1,3},{2,0},{3,1},{4,6},{5,7},{6,4},{7,5},{8,10},{9,11},{10,... | collective-permute-start | bytes 196616 | tf_op jit(solution)/shard_map/ppermute | solution.py:16
  152.2 2.0 %collective-permute-start.23 = (bf16[128,256]{1,0:T(8,128)(2,1)S(1)}, bf16[128,256]{1,0:T(8,128)(2,1)S(1)}, u32[]{:S(2)}, u32[]{:S(2)}) collective-permute-start(bf16[128,256]{1,0:T(8,128)(2,1)S(1)} %get-tuple-element.68), channel_id=1, source_target_pairs={{0,4},{1,5},{2,6},{3,7},{4,0},{5,1},{6,2},{7,3},{8,12},{9,13},{10,... | collective-permute-start | bytes 196616 | tf_op jit(solution)/shard_map/ppermute | solution.py:16
  155.6 1.7 add_pair.5
  157.2 1.8 %collective-permute-start.26 = (bf16[128,256]{1,0:T(8,128)(2,1)S(1)}, bf16[128,256]{1,0:T(8,128)(2,1)S(1)}, u32[]{:S(2)}, u32[]{:S(2)}) collective-permute-start(bf16[128,256]{1,0:T(8,128)(2,1)S(1)} %get-tuple-element.72), channel_id=1, source_target_pairs={{0,2},{1,3},{2,0},{3,1},{4,6},{5,7},{6,4},{7,5},{8,10},{9,11},{10,... | collective-permute-start | bytes 196616 | tf_op jit(solution)/shard_map/ppermute | solution.py:16
  159.1 2.0 %collective-permute-start.27 = (bf16[128,256]{1,0:T(8,128)(2,1)S(1)}, bf16[128,256]{1,0:T(8,128)(2,1)S(1)}, u32[]{:S(2)}, u32[]{:S(2)}) collective-permute-start(bf16[128,256]{1,0:T(8,128)(2,1)S(1)} %get-tuple-element.73), channel_id=1, source_target_pairs={{0,4},{1,5},{2,6},{3,7},{4,0},{5,1},{6,2},{7,3},{8,12},{9,13},{10,... | collective-permute-start | bytes 196616 | tf_op jit(solution)/shard_map/ppermute | solution.py:16
  162.5 3.9 %collective-permute-done.27.refs_6_ = bf16[128,256]{1,0:T(8,128)(2,1)S(1)} collective-permute-done((bf16[128,256]{1,0:T(8,128)(2,1)S(1)}, bf16[128,256]{1,0:T(8,128)(2,1)S(1)}, u32[]{:S(2)}, u32[]{:S(2)}) %collective-permute-start.27) | collective-permute-done | bytes 65568 | tf_op jit(solution)/shard_map/ppermute | solution.py:16
  (76 shorter events, 28.8 us)
Async XLA Ops:
  0.0 8.3 %collective-permute-start.1 = (bf16[64,2048]{1,0:T(8,128)(2,1)}, bf16[64,2048]{1,0:T(8,128)(2,1)S(1)}, u32[]{:S(2)}, u32[]{:S(2)}) collective-permute-start(bf16[64,2048]{1,0:T(8,128)(2,1)} %bitcast.10), channel_id=1, source_target_pairs={{0,1},{1,0},{2,3},{3,2},{4,5},{5,4},{6,7},{7,6},{8,9},{9,8},{10,11... | collective-permute-start | bytes 786440 | tf_op jit(solution)/shard_map/ppermute | solution.py:16
  1.5 21.3 %collective-permute-start.3 = (bf16[64,2048]{1,0:T(8,128)(2,1)}, bf16[64,2048]{1,0:T(8,128)(2,1)S(1)}, u32[]{:S(2)}, u32[]{:S(2)}) collective-permute-start(bf16[64,2048]{1,0:T(8,128)(2,1)} %bitcast.11), channel_id=1, source_target_pairs={{0,4},{1,5},{2,6},{3,7},{4,0},{5,1},{6,2},{7,3},{8,12},{9,13},{10,... | collective-permute-start | bytes 786440 | tf_op jit(solution)/shard_map/ppermute | solution.py:16
  4.1 18.8 %collective-permute-start.4 = (bf16[64,2048]{1,0:T(8,128)(2,1)}, bf16[64,2048]{1,0:T(8,128)(2,1)S(1)}, u32[]{:S(2)}, u32[]{:S(2)}) collective-permute-start(bf16[64,2048]{1,0:T(8,128)(2,1)} %bitcast.12), channel_id=1, source_target_pairs={{0,6},{1,7},{2,4},{3,5},{4,2},{5,3},{6,0},{7,1},{8,14},{9,15},{10,... | collective-permute-start | bytes 786440 | tf_op jit(solution)/shard_map/ppermute | solution.py:16
  5.5 19.6 %collective-permute-start = (bf16[64,2048]{1,0:T(8,128)(2,1)}, bf16[64,2048]{1,0:T(8,128)(2,1)S(1)}, u32[]{:S(2)}, u32[]{:S(2)}) collective-permute-start(bf16[64,2048]{1,0:T(8,128)(2,1)} %bitcast.13), channel_id=1, source_target_pairs={{0,2},{1,3},{2,0},{3,1},{4,6},{5,7},{6,4},{7,5},{8,10},{9,11},{10,... | collective-permute-start | bytes 786440 | tf_op jit(solution)/shard_map/ppermute | solution.py:16
  8.3 20.4 %collective-permute-start.2 = (bf16[64,2048]{1,0:T(8,128)(2,1)S(1)}, bf16[64,2048]{1,0:T(8,128)(2,1)S(1)}, u32[]{:S(2)}, u32[]{:S(2)}) collective-permute-start(bf16[64,2048]{1,0:T(8,128)(2,1)S(1)} %collective-permute-done.1.refs_1_), channel_id=1, source_target_pairs={{0,2},{1,3},{2,0},{3,1},{4,6},{5,7},{6,4},{7,5},{8,10},{9,11},{10,... | collective-permute-start | bytes 786440 | tf_op jit(solution)/shard_map/ppermute | solution.py:16
  11.5 18.9 %copy-start.11 = (f32[1,4096]{1,0:T(1,128)S(1)}, f32[1,4096]{1,0:T(1,128)}, u32[]{:S(2)}) copy-start(f32[1,4096]{1,0:T(1,128)} %refs_4_.1) | copy-start | bytes 49156
  18.0 18.6 %collective-permute-start.6 = (bf16[64,4096]{1,0:T(8,128)(2,1)S(1)}, bf16[64,4096]{1,0:T(8,128)(2,1)S(1)}, u32[]{:S(2)}, u32[]{:S(2)}) collective-permute-start(bf16[64,4096]{1,0:T(8,128)(2,1)S(1)} %get-tuple-element.45), channel_id=1, source_target_pairs={{0,16},{8,24},{1,17},{9,25},{2,18},{10,26},{3,19},{11,27},{4,20},{... | collective-permute-start | bytes 1572872 | tf_op jit(solution)/shard_map/ppermute | solution.py:391
  28.6 11.9 %collective-permute-start.5 = (bf16[128,2048]{1,0:T(8,128)(2,1)S(1)}, bf16[128,2048]{1,0:T(8,128)(2,1)S(1)}, u32[]{:S(2)}, u32[]{:S(2)}) collective-permute-start(bf16[128,2048]{1,0:T(8,128)(2,1)S(1)} %pad_maximum_fusion), channel_id=1, source_target_pairs={{0,1},{1,0},{2,3},{3,2},{4,5},{5,4},{6,7},{7,6},{8,9},{9,8},{10,11... | collective-permute-start | bytes 1572872 | tf_op jit(solution)/shard_map/ppermute | solution.py:16
  29.1 17.2 %collective-permute-start.8 = (bf16[64,4096]{1,0:T(8,128)(2,1)S(1)}, bf16[64,4096]{1,0:T(8,128)(2,1)S(1)}, u32[]{:S(2)}, u32[]{:S(2)}) collective-permute-start(bf16[64,4096]{1,0:T(8,128)(2,1)S(1)} %get-tuple-element.46), channel_id=1, source_target_pairs={{0,16},{8,24},{1,17},{9,25},{2,18},{10,26},{3,19},{11,27},{4,20},{... | collective-permute-start | bytes 1572872 | tf_op jit(solution)/shard_map/ppermute | solution.py:391
  35.2 15.3 %collective-permute-start.7 = (bf16[256,4096]{1,0:T(8,128)(2,1)S(1)}, bf16[256,4096]{1,0:T(8,128)(2,1)S(1)}, u32[]{:S(2)}, u32[]{:S(2)}) collective-permute-start(bf16[256,4096]{1,0:T(8,128)(2,1)S(1)} %get-tuple-element.42.refs_0_), channel_id=1, source_target_pairs={{0,8},{16,24},{1,9},{17,25},{2,10},{18,26},{3,11},{19,27},{4,12},{... | collective-permute-start | bytes 6291464 | tf_op jit(solution)/shard_map/ppermute | solution.py:397
  46.4 5.1 %collective-permute-start.9 = (bf16[256,4096]{1,0:T(8,128)(2,1)S(1)}, bf16[256,4096]{1,0:T(8,128)(2,1)S(1)}, u32[]{:S(2)}, u32[]{:S(2)}) collective-permute-start(bf16[256,4096]{1,0:T(8,128)(2,1)S(1)} %encode.5.refs_1_), channel_id=1, source_target_pairs={{0,8},{16,24},{1,9},{17,25},{2,10},{18,26},{3,11},{19,27},{4,12},{... | collective-permute-start | bytes 6291464 | tf_op jit(solution)/shard_map/ppermute | solution.py:397
  47.8 33.9 %collective-permute-start.12 = (bf16[128,4096]{1,0:T(8,128)(2,1)}, bf16[128,4096]{1,0:T(8,128)(2,1)}, u32[]{:S(2)}, u32[]{:S(2)}) collective-permute-start(bf16[128,4096]{1,0:T(8,128)(2,1)} %get-tuple-element.44.refs_5_), channel_id=1, source_target_pairs={{0,16},{8,24},{1,17},{9,25},{2,18},{10,26},{3,19},{11,27},{4,20},{... | collective-permute-start | bytes 3145736 | tf_op jit(solution)/shard_map/ppermute | solution.py:391
  49.1 67.9 %collective-permute-start.19 = (bf16[256,4096]{1,0:T(8,128)(2,1)S(1)}, bf16[256,4096]{1,0:T(8,128)(2,1)}, u32[]{:S(2)}, u32[]{:S(2)}) collective-permute-start(bf16[256,4096]{1,0:T(8,128)(2,1)S(1)} %encode.5.refs_1_), channel_id=1, source_target_pairs={{0,16},{8,24},{1,17},{9,25},{2,18},{10,26},{3,19},{11,27},{4,20},{... | collective-permute-start | bytes 6291464 | tf_op jit(solution)/shard_map/ppermute | solution.py:391
  51.4 5.0 %collective-permute-start.11 = (bf16[64,4096]{1,0:T(8,128)(2,1)S(1)}, bf16[64,4096]{1,0:T(8,128)(2,1)}, u32[]{:S(2)}, u32[]{:S(2)}) collective-permute-start(bf16[64,4096]{1,0:T(8,128)(2,1)S(1)} %collective-permute-done.8.refs_5_), channel_id=1, source_target_pairs={{16,24},{24,16},{17,25},{25,17},{18,26},{26,18},{19,27},{27,19},{2... | collective-permute-start | bytes 1572872 | tf_op jit(solution)/shard_map/ppermute | solution.py:394
  53.7 3.9 %collective-permute-start.10 = (bf16[64,4096]{1,0:T(8,128)(2,1)S(1)}, bf16[64,4096]{1,0:T(8,128)(2,1)}, u32[]{:S(2)}, u32[]{:S(2)}) collective-permute-start(bf16[64,4096]{1,0:T(8,128)(2,1)S(1)} %collective-permute-done.6.refs_6_.refs_4_), channel_id=1, source_target_pairs={{16,24},{24,16},{17,25},{25,17},{18,26},{26,18},{19,27},{27,19},{2... | collective-permute-start | bytes 1572872 | tf_op jit(solution)/shard_map/ppermute | solution.py:394
  81.7 13.7 %collective-permute-start.13 = (bf16[128,4096]{1,0:T(8,128)(2,1)}, bf16[128,4096]{1,0:T(8,128)(2,1)S(1)}, u32[]{:S(2)}, u32[]{:S(2)}) collective-permute-start(bf16[128,4096]{1,0:T(8,128)(2,1)} %collective-permute-done.12.direct), channel_id=1, source_target_pairs={{16,24},{24,16},{17,25},{25,17},{18,26},{26,18},{19,27},{27,19},{2... | collective-permute-start | bytes 3145736 | tf_op jit(solution)/shard_map/ppermute | solution.py:394
  92.9 11.6 %collective-permute-start.14 = (bf16[4,128,256]{2,1,0:T(8,128)(2,1)}, bf16[4,128,256]{2,1,0:T(8,128)(2,1)S(1)}, u32[]{:S(2)}, u32[]{:S(2)}) collective-permute-start(bf16[4,128,256]{2,1,0:T(8,128)(2,1)} %get-tuple-element.51.refs_0_), channel_id=1, source_target_pairs={{0,1},{1,0},{2,3},{3,2},{4,5},{5,4},{6,7},{7,6},{8,9},{9,8},{10,11... | collective-permute-start | bytes 786440 | tf_op jit(solution)/shard_map/ppermute | solution.py:16
  95.4 17.4 %copy-start.12 = (s32[7]{0:T(128)S(1)}, s32[7]{0:T(128)}, u32[]{:S(2)}) copy-start(s32[7]{0:T(128)} %stack.31.info) | copy-start | bytes 88
  103.9 8.9 %collective-permute-start.15 = (bf16[4,128,256]{2,1,0:T(8,128)(2,1)}, bf16[4,128,256]{2,1,0:T(8,128)(2,1)S(1)}, u32[]{:S(2)}, u32[]{:S(2)}) collective-permute-start(bf16[4,128,256]{2,1,0:T(8,128)(2,1)} %get-tuple-element.57), channel_id=1, source_target_pairs={{0,1},{1,0},{2,3},{3,2},{4,5},{5,4},{6,7},{7,6},{8,9},{9,8},{10,11... | collective-permute-start | bytes 786440 | tf_op jit(solution)/shard_map/ppermute | solution.py:16
  117.0 8.9 %collective-permute-start.20 = (bf16[256,4096]{1,0:T(8,128)(2,1)}, bf16[256,4096]{1,0:T(8,128)(2,1)S(1)}, u32[]{:S(2)}, u32[]{:S(2)}) collective-permute-start(bf16[256,4096]{1,0:T(8,128)(2,1)} %collective-permute-done.19.direct), channel_id=1, source_target_pairs={{16,24},{24,16},{17,25},{25,17},{18,26},{26,18},{19,27},{27,19},{2... | collective-permute-start | bytes 6291464 | tf_op jit(solution)/shard_map/ppermute | solution.py:394
  119.1 15.8 %collective-permute-start.16 = (bf16[256,256]{1,0:T(8,128)(2,1)S(1)}, bf16[256,256]{1,0:T(8,128)(2,1)S(1)}, u32[]{:S(2)}, u32[]{:S(2)}) collective-permute-start(bf16[256,256]{1,0:T(8,128)(2,1)S(1)} %get-tuple-element.59), channel_id=1, source_target_pairs={{0,2},{1,3},{2,0},{3,1},{4,6},{5,7},{6,4},{7,5},{8,10},{9,11},{10,... | collective-permute-start | bytes 393224 | tf_op jit(solution)/shard_map/ppermute | solution.py:16
  121.9 13.0 %collective-permute-start.17 = (bf16[256,256]{1,0:T(8,128)(2,1)S(1)}, bf16[256,256]{1,0:T(8,128)(2,1)S(1)}, u32[]{:S(2)}, u32[]{:S(2)}) collective-permute-start(bf16[256,256]{1,0:T(8,128)(2,1)S(1)} %get-tuple-element.60), channel_id=1, source_target_pairs={{0,4},{1,5},{2,6},{3,7},{4,0},{5,1},{6,2},{7,3},{8,12},{9,13},{10,... | collective-permute-start | bytes 393224 | tf_op jit(solution)/shard_map/ppermute | solution.py:16
  124.5 11.0 %collective-permute-start.18 = (bf16[256,256]{1,0:T(8,128)(2,1)S(1)}, bf16[256,256]{1,0:T(8,128)(2,1)S(1)}, u32[]{:S(2)}, u32[]{:S(2)}) collective-permute-start(bf16[256,256]{1,0:T(8,128)(2,1)S(1)} %get-tuple-element.61), channel_id=1, source_target_pairs={{0,6},{1,7},{2,4},{3,5},{4,2},{5,3},{6,0},{7,1},{8,14},{9,15},{10,... | collective-permute-start | bytes 393224 | tf_op jit(solution)/shard_map/ppermute | solution.py:16
  134.3 13.2 %collective-permute-start.21 = (bf16[4,128,256]{2,1,0:T(8,128)(2,1)}, bf16[4,128,256]{2,1,0:T(8,128)(2,1)S(1)}, u32[]{:S(2)}, u32[]{:S(2)}) collective-permute-start(bf16[4,128,256]{2,1,0:T(8,128)(2,1)} %get-tuple-element.63.refs_4_.refs_0_), channel_id=1, source_target_pairs={{0,1},{1,0},{2,3},{3,2},{4,5},{5,4},{6,7},{7,6},{8,9},{9,8},{10,11... | collective-permute-start | bytes 786440 | tf_op jit(solution)/shard_map/ppermute | solution.py:16
  137.9 29.3 %copy-start.1 = (f32[512,256]{1,0:T(8,128)S(1)}, f32[512,256]{1,0:T(8,128)}, u32[]{:S(2)}) copy-start(f32[512,256]{1,0:T(8,128)} %add_up.2.refs_1_.base) | copy-start | bytes 1572868
  146.5 9.1 %collective-permute-start.25 = (bf16[4,128,256]{2,1,0:T(8,128)(2,1)}, bf16[4,128,256]{2,1,0:T(8,128)(2,1)S(1)}, u32[]{:S(2)}, u32[]{:S(2)}) collective-permute-start(bf16[4,128,256]{2,1,0:T(8,128)(2,1)} %get-tuple-element.65.refs_2_), channel_id=1, source_target_pairs={{0,1},{1,0},{2,3},{3,2},{4,5},{5,4},{6,7},{7,6},{8,9},{9,8},{10,11... | collective-permute-start | bytes 786440 | tf_op jit(solution)/shard_map/ppermute | solution.py:16
  150.2 5.4 %collective-permute-start.22 = (bf16[128,256]{1,0:T(8,128)(2,1)S(1)}, bf16[128,256]{1,0:T(8,128)(2,1)S(1)}, u32[]{:S(2)}, u32[]{:S(2)}) collective-permute-start(bf16[128,256]{1,0:T(8,128)(2,1)S(1)} %get-tuple-element.67), channel_id=1, source_target_pairs={{0,2},{1,3},{2,0},{3,1},{4,6},{5,7},{6,4},{7,5},{8,10},{9,11},{10,... | collective-permute-start | bytes 196616 | tf_op jit(solution)/shard_map/ppermute | solution.py:16
  152.2 10.3 %collective-permute-start.23 = (bf16[128,256]{1,0:T(8,128)(2,1)S(1)}, bf16[128,256]{1,0:T(8,128)(2,1)S(1)}, u32[]{:S(2)}, u32[]{:S(2)}) collective-permute-start(bf16[128,256]{1,0:T(8,128)(2,1)S(1)} %get-tuple-element.68), channel_id=1, source_target_pairs={{0,4},{1,5},{2,6},{3,7},{4,0},{5,1},{6,2},{7,3},{8,12},{9,13},{10,... | collective-permute-start | bytes 196616 | tf_op jit(solution)/shard_map/ppermute | solution.py:16
  154.2 8.3 %collective-permute-start.24 = (bf16[128,256]{1,0:T(8,128)(2,1)S(1)}, bf16[128,256]{1,0:T(8,128)(2,1)S(1)}, u32[]{:S(2)}, u32[]{:S(2)}) collective-permute-start(bf16[128,256]{1,0:T(8,128)(2,1)S(1)} %get-tuple-element.69), channel_id=1, source_target_pairs={{0,6},{1,7},{2,4},{3,5},{4,2},{5,3},{6,0},{7,1},{8,14},{9,15},{10,... | collective-permute-start | bytes 196616 | tf_op jit(solution)/shard_map/ppermute | solution.py:16
  157.2 5.2 %collective-permute-start.26 = (bf16[128,256]{1,0:T(8,128)(2,1)S(1)}, bf16[128,256]{1,0:T(8,128)(2,1)S(1)}, u32[]{:S(2)}, u32[]{:S(2)}) collective-permute-start(bf16[128,256]{1,0:T(8,128)(2,1)S(1)} %get-tuple-element.72), channel_id=1, source_target_pairs={{0,2},{1,3},{2,0},{3,1},{4,6},{5,7},{6,4},{7,5},{8,10},{9,11},{10,... | collective-permute-start | bytes 196616 | tf_op jit(solution)/shard_map/ppermute | solution.py:16
  159.1 7.2 %collective-permute-start.27 = (bf16[128,256]{1,0:T(8,128)(2,1)S(1)}, bf16[128,256]{1,0:T(8,128)(2,1)S(1)}, u32[]{:S(2)}, u32[]{:S(2)}) collective-permute-start(bf16[128,256]{1,0:T(8,128)(2,1)S(1)} %get-tuple-element.73), channel_id=1, source_target_pairs={{0,4},{1,5},{2,6},{3,7},{4,0},{5,1},{6,2},{7,3},{8,12},{9,13},{10,... | collective-permute-start | bytes 196616 | tf_op jit(solution)/shard_map/ppermute | solution.py:16
  161.1 6.1 %collective-permute-start.28 = (bf16[128,256]{1,0:T(8,128)(2,1)S(1)}, bf16[128,256]{1,0:T(8,128)(2,1)S(1)}, u32[]{:S(2)}, u32[]{:S(2)}) collective-permute-start(bf16[128,256]{1,0:T(8,128)(2,1)S(1)} %get-tuple-element.74), channel_id=1, source_target_pairs={{0,6},{1,7},{2,4},{3,5},{4,2},{5,3},{6,0},{7,1},{8,14},{9,15},{10,... | collective-permute-start | bytes 196616 | tf_op jit(solution)/shard_map/ppermute | solution.py:16
  (15 other events, 107.6 us)

commit v14 on v13

--- a/solution.py
+++ b/solution.py
@@ -149,10 +149,11 @@
             kept_sems.at[source, k],
         )
 
-    def fetch_all(k):
+    def fetch_own(k):
         fetch(0, k).start()
         pl.when(odd)(lambda: fetch(1, k).start())
 
+    def fetch_kept(k):
         @pl.when(upper)
         def _():
             keep(0, k).start()
@@ -161,10 +162,15 @@
     @pl.when(step == 0)
     def _():
         for k in range(slots - 1):
-            fetch_all(jnp.int32(k))
+            fetch_own(jnp.int32(k))
+        for k in range(slots - 1):
+            fetch_kept(jnp.int32(k))
         total[...] = jnp.zeros_like(total)
 
-    pl.when(step + slots - 1 < steps)(lambda: fetch_all(step + slots - 1))
+    @pl.when(step + slots - 1 < steps)
+    def _():
+        fetch_own(step + slots - 1)
+        fetch_kept(step + slots - 1)
 
     def stacked(parts):
         values = [part[...] for part in parts]

time: 169 us -> 169 us (level)
  no operation moved by 1% of the time
where the time goes in v14:
time: 169 us
  Pallas kernels  74.7 us (44%)
  starting transfers between devices  53.5 us (32%)
  waiting for transfers between devices  35.1 us (21%)
  local copies, waits for them, and re-layouts  4.99 us (3%)
    ppermute x19, waiting for transfers between devices, exchange(): return lax.ppermute(array, axis, [(i, i ^ flip) for i in range(size)])  29.3 us
    ppermute x19, starting transfers between devices, exchange(): return lax.ppermute(array, axis, [(i, i ^ flip) for i in range(size)])  28 us
    pallas_call x3, Pallas kernels, decode_later(): pl.pallas_call(functools.partial(later_wave_kernel, row, skip), in_specs=...  25.4 us
    pallas_call x1, Pallas kernels, decode_first(): pl.pallas_call(functools.partial(first_wave_kernel, [len(parts) for parts...  24.1 us
    ppermute x4, starting transfers between devices, across(): return lax.ppermute(a, 'layer', [(i, i ^ 1) for i in range(half, layers)])  17.6 us
    pallas_call x3, Pallas kernels, encode(): pl.pallas_call(functools.partial(encode_kernel, order, pieces, len(parts)...  17.1 us
    ppermute x4, starting transfers between devices, up(): return lax.ppermute(a, 'layer', [(i, i + half) for i in range(half)])  5.16 us
    pallas_call x3, Pallas kernels, add_pair(): pl.pallas_call(functools.partial(pair_kernel, size, len(mine), len(after)...  5.15 us
  transfers between devices with their start and end apart: 29, of which 13 were waited for; matrix products, arithmetic and copies ran while one was open for 0% of the time, Pallas kernels for 43%

profile of v14, /device:TPU:2, one launch (start us, length us, event | category | flops | bytes accessed | tf_op | source)
XLA Modules:
  0.0 168.7 jit_solution(17956910634251336702)
XLA Ops:
  0.0 1.5 collective-permute-start.1
  1.5 2.6 %collective-permute-start.3 = (bf16[64,2048]{1,0:T(8,128)(2,1)}, bf16[64,2048]{1,0:T(8,128)(2,1)S(1)}, u32[]{:S(2)}, u32[]{:S(2)}) collective-permute-start(bf16[64,2048]{1,0:T(8,128)(2,1)} %bitcast.11), channel_id=1, source_target_pairs={{0,4},{1,5},{2,6},{3,7},{4,0},{5,1},{6,2},{7,3},{8,12},{9,13},{10,... | collective-permute-start | bytes 786440 | tf_op jit(solution)/shard_map/ppermute | solution.py:16
  5.7 2.6 %collective-permute-done.1.refs_1_ = bf16[64,2048]{1,0:T(8,128)(2,1)S(1)} collective-permute-done((bf16[64,2048]{1,0:T(8,128)(2,1)}, bf16[64,2048]{1,0:T(8,128)(2,1)S(1)}, u32[]{:S(2)}, u32[]{:S(2)}) %collective-permute-start.1) | collective-permute-done | bytes 262176 | tf_op jit(solution)/shard_map/ppermute | solution.py:16
  8.3 1.6 collective-permute-start.2
  11.5 6.5 %encode.3 = (bf16[128,4096]{1,0:T(8,128)(2,1)S(1)}, bf16[64,4096]{1,0:T(8,128)(2,1)S(1)}, bf16[64,4096]{1,0:T(8,128)(2,1)S(1)}, bf16[1,2048,4096]{2,1,0:T(8,128)(2,1)S(1)}) custom-call(bf16[64,2048]{1,0:T(8,128)(2,1)S(1)} %bitcast.14, bf16[64,2048]{1,0:T(8,128)(2,1)S(1)} %collective-permute-done.1.refs_1_, bf16[1,2048,4096]{2,1,0:T(8,128)(2,1)} %refs_2_.1, ...), custom_call_target="tpu_custom_call" | custom-call | tf_op jit(solution)/shard_map/encode/pallas_call | solution.py:91
  19.3 3.5 %collective-permute-done.3.refs_0_ = bf16[64,2048]{1,0:T(8,128)(2,1)S(1)} collective-permute-done((bf16[64,2048]{1,0:T(8,128)(2,1)}, bf16[64,2048]{1,0:T(8,128)(2,1)S(1)}, u32[]{:S(2)}, u32[]{:S(2)}) %collective-permute-start.3) | collective-permute-done | bytes 262176 | tf_op jit(solution)/shard_map/ppermute | solution.py:16
  22.9 2.1 %collective-permute-done.refs_0_ = bf16[64,2048]{1,0:T(8,128)(2,1)S(1)} collective-permute-done((bf16[64,2048]{1,0:T(8,128)(2,1)}, bf16[64,2048]{1,0:T(8,128)(2,1)S(1)}, u32[]{:S(2)}, u32[]{:S(2)}) %collective-permute-start) | collective-permute-done | bytes 262176 | tf_op jit(solution)/shard_map/ppermute | solution.py:16
  25.0 3.6 %collective-permute-done.2.refs_1_ = bf16[64,2048]{1,0:T(8,128)(2,1)S(1)} collective-permute-done((bf16[64,2048]{1,0:T(8,128)(2,1)S(1)}, bf16[64,2048]{1,0:T(8,128)(2,1)S(1)}, u32[]{:S(2)}, u32[]{:S(2)}) %collective-permute-start.2) | collective-permute-done | bytes 262176 | tf_op jit(solution)/shard_map/ppermute | solution.py:16
  30.4 4.7 %encode.4 = (bf16[256,4096]{1,0:T(8,128)(2,1)S(1)}, bf16[128,4096]{1,0:T(8,128)(2,1)}) custom-call(bf16[64,2048]{1,0:T(8,128)(2,1)S(1)} %collective-permute-done.refs_0_, bf16[64,2048]{1,0:T(8,128)(2,1)S(1)} %collective-permute-done.2.refs_1_, bf16[1,2048,4096]{2,1,0:T(8,128)(2,1)S(1)} %get-tuple-element.40.refs_2_.refs_3_, f32[1,4096]{1,0:T(1,128)S(1)} %copy-done.11, ...), custom_call_target="tpu_custom_call" | custom-call | tf_op jit(solution)/shard_map/encode/pallas_call | solution.py:91
  36.6 3.9 %collective-permute-done.5.refs_2_ = bf16[128,2048]{1,0:T(8,128)(2,1)S(1)} collective-permute-done((bf16[128,2048]{1,0:T(8,128)(2,1)S(1)}, bf16[128,2048]{1,0:T(8,128)(2,1)S(1)}, u32[]{:S(2)}, u32[]{:S(2)}) %collective-permute-start.5) | collective-permute-done | bytes 524320 | tf_op jit(solution)/shard_map/ppermute | solution.py:16
  40.5 5.8 %encode.5.refs_1_ = bf16[256,4096]{1,0:T(8,128)(2,1)S(1)} custom-call(bf16[64,2048]{1,0:T(8,128)(2,1)S(1)} %collective-permute-done.3.refs_0_, bf16[64,2048]{1,0:T(8,128)(2,1)S(1)} %collective-permute-done.4.refs_1_, bf16[128,2048]{1,0:T(8,128)(2,1)S(1)} %collective-permute-done.5.refs_2_, bf16[1,2048,4096]{2,1,0:T(8,128)(2,1)S(1)} %get-tuple-element.40.refs_2_.refs_3_, ...), custom_call_target="tpu_custom_call" | custom-call | tf_op jit(solution)/shard_map/encode/pallas_call | solution.py:91
  51.4 2.3 %collective-permute-start.11 = (bf16[64,4096]{1,0:T(8,128)(2,1)S(1)}, bf16[64,4096]{1,0:T(8,128)(2,1)}, u32[]{:S(2)}, u32[]{:S(2)}) collective-permute-start(bf16[64,4096]{1,0:T(8,128)(2,1)S(1)} %collective-permute-done.8.refs_5_), channel_id=1, source_target_pairs={{16,24},{24,16},{17,25},{25,17},{18,26},{26,18},{19,27},{27,19},{2... | collective-permute-start | bytes 1572872 | tf_op jit(solution)/shard_map/ppermute | solution.py:400
  53.7 2.0 %collective-permute-start.10 = (bf16[64,4096]{1,0:T(8,128)(2,1)S(1)}, bf16[64,4096]{1,0:T(8,128)(2,1)}, u32[]{:S(2)}, u32[]{:S(2)}) collective-permute-start(bf16[64,4096]{1,0:T(8,128)(2,1)S(1)} %collective-permute-done.6.refs_6_.refs_4_), channel_id=1, source_target_pairs={{16,24},{24,16},{17,25},{25,17},{18,26},{26,18},{19,27},{27,19},{2... | collective-permute-start | bytes 1572872 | tf_op jit(solution)/shard_map/ppermute | solution.py:400
  57.7 24.1 %decode_first.1 = (f32[4,128,256]{2,1,0:T(8,128)}, bf16[4,128,256]{2,1,0:T(8,128)(2,1)}, f32[384,2048]{1,0:T(8,128)}, bf16[4096,2048]{1,0:T(8,128)(2,1)S(1)}, bf16[4096,2048]{1,0:T(8,128)(2,1)S(1)}) custom-call(s32[7]{0:T(128)} %stack.31.info, bf16[256,4096]{1,0:T(8,128)(2,1)} %copy-done.3, bf16[256,4096]{1,0:T(8,128)(2,1)} %copy-done, ...), custom_call_target="tpu_custom_call" | custom-call | tf_op jit(solution)/shard_map/decode_first/pallas_call | solution.py:230
  81.7 11.2 %collective-permute-start.13 = (bf16[128,4096]{1,0:T(8,128)(2,1)}, bf16[128,4096]{1,0:T(8,128)(2,1)S(1)}, u32[]{:S(2)}, u32[]{:S(2)}) collective-permute-start(bf16[128,4096]{1,0:T(8,128)(2,1)} %collective-permute-done.12.direct), channel_id=1, source_target_pairs={{16,24},{24,16},{17,25},{25,17},{18,26},{26,18},{19,27},{27,19},{2... | collective-permute-start | bytes 3145736 | tf_op jit(solution)/shard_map/ppermute | solution.py:400
  93.5 1.9 %collective-permute-done.13.swapped = bf16[128,4096]{1,0:T(8,128)(2,1)S(1)} collective-permute-done((bf16[128,4096]{1,0:T(8,128)(2,1)}, bf16[128,4096]{1,0:T(8,128)(2,1)S(1)}, u32[]{:S(2)}, u32[]{:S(2)}) %collective-permute-start.13) | collective-permute-done | bytes 1048608 | tf_op jit(solution)/shard_map/ppermute | solution.py:400
  95.4 8.5 %decode_later.3 = (f32[4,128,256]{2,1,0:T(8,128)}, bf16[4,128,256]{2,1,0:T(8,128)(2,1)}) custom-call(s32[7]{0:T(128)} %stack.31.info, bf16[128,4096]{1,0:T(8,128)(2,1)} %collective-permute-done.12.direct, bf16[128,4096]{1,0:T(8,128)(2,1)S(1)} %collective-permute-done.13.swapped, f32[384,2048]{1,0:T(8,128)} %get-tuple-element.53.base, ...), custom_call_target="tpu_custom_call" | custom-call | tf_op jit(solution)/shard_map/decode_later/pallas_call | solution.py:291
  104.5 8.3 %collective-permute-done.15.refs_3_ = bf16[4,128,256]{2,1,0:T(8,128)(2,1)S(1)} collective-permute-done((bf16[4,128,256]{2,1,0:T(8,128)(2,1)}, bf16[4,128,256]{2,1,0:T(8,128)(2,1)S(1)}, u32[]{:S(2)}, u32[]{:S(2)}) %collective-permute-start.15) | collective-permute-done | bytes 262176 | tf_op jit(solution)/shard_map/ppermute | solution.py:16
  112.8 1.9 %add_pair.3 = (f32[256,256]{1,0:T(8,128)S(1)}, bf16[256,256]{1,0:T(8,128)(2,1)S(1)}, bf16[256,256]{1,0:T(8,128)(2,1)S(1)}, bf16[256,256]{1,0:T(8,128)(2,1)S(1)}) custom-call(s32[7]{0:T(128)S(1)} %copy-done.12, f32[4,128,256]{2,1,0:T(8,128)} %get-tuple-element.50.refs_0_, f32[4,128,256]{2,1,0:T(8,128)} %get-tuple-element.56.refs_1_, ...), custom_call_target="tpu_custom_call" | custom-call | tf_op jit(solution)/shard_map/add_pair/pallas_call | solution.py:335
  115.4 1.7 collective-permute-done.19.direct
  117.0 2.1 %collective-permute-start.20 = (bf16[256,4096]{1,0:T(8,128)(2,1)}, bf16[256,4096]{1,0:T(8,128)(2,1)S(1)}, u32[]{:S(2)}, u32[]{:S(2)}) collective-permute-start(bf16[256,4096]{1,0:T(8,128)(2,1)} %collective-permute-done.19.direct), channel_id=1, source_target_pairs={{16,24},{24,16},{17,25},{25,17},{18,26},{26,18},{19,27},{27,19},{2... | collective-permute-start | bytes 6291464 | tf_op jit(solution)/shard_map/ppermute | solution.py:400
  119.1 2.7 %collective-permute-start.16 = (bf16[256,256]{1,0:T(8,128)(2,1)S(1)}, bf16[256,256]{1,0:T(8,128)(2,1)S(1)}, u32[]{:S(2)}, u32[]{:S(2)}) collective-permute-start(bf16[256,256]{1,0:T(8,128)(2,1)S(1)} %get-tuple-element.59), channel_id=1, source_target_pairs={{0,2},{1,3},{2,0},{3,1},{4,6},{5,7},{6,4},{7,5},{8,10},{9,11},{10,... | collective-permute-start | bytes 393224 | tf_op jit(solution)/shard_map/ppermute | solution.py:16
  121.9 2.6 %collective-permute-start.17 = (bf16[256,256]{1,0:T(8,128)(2,1)S(1)}, bf16[256,256]{1,0:T(8,128)(2,1)S(1)}, u32[]{:S(2)}, u32[]{:S(2)}) collective-permute-start(bf16[256,256]{1,0:T(8,128)(2,1)S(1)} %get-tuple-element.60), channel_id=1, source_target_pairs={{0,4},{1,5},{2,6},{3,7},{4,0},{5,1},{6,2},{7,3},{8,12},{9,13},{10,... | collective-permute-start | bytes 393224 | tf_op jit(solution)/shard_map/ppermute | solution.py:16
  125.9 8.4 %decode_later.4 = (f32[4,128,256]{2,1,0:T(8,128)}, bf16[4,128,256]{2,1,0:T(8,128)(2,1)}) custom-call(s32[7]{0:T(128)} %stack.31.info, bf16[256,4096]{1,0:T(8,128)(2,1)} %collective-permute-done.19.direct, bf16[256,4096]{1,0:T(8,128)(2,1)S(1)} %collective-permute-done.20.swapped, f32[384,2048]{1,0:T(8,128)} %get-tuple-element.53.base, ...), custom_call_target="tpu_custom_call" | custom-call | tf_op jit(solution)/shard_map/decode_later/pallas_call | solution.py:291
  137.9 8.5 %decode_later.5 = (f32[4,128,256]{2,1,0:T(8,128)}, bf16[4,128,256]{2,1,0:T(8,128)(2,1)}) custom-call(s32[7]{0:T(128)} %stack.31.info, bf16[256,4096]{1,0:T(8,128)(2,1)} %collective-permute-done.19.direct, bf16[256,4096]{1,0:T(8,128)(2,1)S(1)} %collective-permute-done.20.swapped, f32[384,2048]{1,0:T(8,128)} %get-tuple-element.53.base, ...), custom_call_target="tpu_custom_call" | custom-call | tf_op jit(solution)/shard_map/decode_later/pallas_call | solution.py:291
  148.5 1.6 add_pair.4
  150.2 2.0 %collective-permute-start.22 = (bf16[128,256]{1,0:T(8,128)(2,1)S(1)}, bf16[128,256]{1,0:T(8,128)(2,1)S(1)}, u32[]{:S(2)}, u32[]{:S(2)}) collective-permute-start(bf16[128,256]{1,0:T(8,128)(2,1)S(1)} %get-tuple-element.67), channel_id=1, source_target_pairs={{0,2},{1,3},{2,0},{3,1},{4,6},{5,7},{6,4},{7,5},{8,10},{9,11},{10,... | collective-permute-start | bytes 196616 | tf_op jit(solution)/shard_map/ppermute | solution.py:16
  152.2 2.0 %collective-permute-start.23 = (bf16[128,256]{1,0:T(8,128)(2,1)S(1)}, bf16[128,256]{1,0:T(8,128)(2,1)S(1)}, u32[]{:S(2)}, u32[]{:S(2)}) collective-permute-start(bf16[128,256]{1,0:T(8,128)(2,1)S(1)} %get-tuple-element.68), channel_id=1, source_target_pairs={{0,4},{1,5},{2,6},{3,7},{4,0},{5,1},{6,2},{7,3},{8,12},{9,13},{10,... | collective-permute-start | bytes 196616 | tf_op jit(solution)/shard_map/ppermute | solution.py:16
  155.6 1.7 add_pair.5
  157.2 1.8 %collective-permute-start.26 = (bf16[128,256]{1,0:T(8,128)(2,1)S(1)}, bf16[128,256]{1,0:T(8,128)(2,1)S(1)}, u32[]{:S(2)}, u32[]{:S(2)}) collective-permute-start(bf16[128,256]{1,0:T(8,128)(2,1)S(1)} %get-tuple-element.72), channel_id=1, source_target_pairs={{0,2},{1,3},{2,0},{3,1},{4,6},{5,7},{6,4},{7,5},{8,10},{9,11},{10,... | collective-permute-start | bytes 196616 | tf_op jit(solution)/shard_map/ppermute | solution.py:16
  159.1 2.0 %collective-permute-start.27 = (bf16[128,256]{1,0:T(8,128)(2,1)S(1)}, bf16[128,256]{1,0:T(8,128)(2,1)S(1)}, u32[]{:S(2)}, u32[]{:S(2)}) collective-permute-start(bf16[128,256]{1,0:T(8,128)(2,1)S(1)} %get-tuple-element.73), channel_id=1, source_target_pairs={{0,4},{1,5},{2,6},{3,7},{4,0},{5,1},{6,2},{7,3},{8,12},{9,13},{10,... | collective-permute-start | bytes 196616 | tf_op jit(solution)/shard_map/ppermute | solution.py:16
  162.5 3.9 %collective-permute-done.27.refs_6_ = bf16[128,256]{1,0:T(8,128)(2,1)S(1)} collective-permute-done((bf16[128,256]{1,0:T(8,128)(2,1)S(1)}, bf16[128,256]{1,0:T(8,128)(2,1)S(1)}, u32[]{:S(2)}, u32[]{:S(2)}) %collective-permute-start.27) | collective-permute-done | bytes 65568 | tf_op jit(solution)/shard_map/ppermute | solution.py:16
  (76 shorter events, 28.8 us)
Async XLA Ops:
  0.0 8.3 %collective-permute-start.1 = (bf16[64,2048]{1,0:T(8,128)(2,1)}, bf16[64,2048]{1,0:T(8,128)(2,1)S(1)}, u32[]{:S(2)}, u32[]{:S(2)}) collective-permute-start(bf16[64,2048]{1,0:T(8,128)(2,1)} %bitcast.10), channel_id=1, source_target_pairs={{0,1},{1,0},{2,3},{3,2},{4,5},{5,4},{6,7},{7,6},{8,9},{9,8},{10,11... | collective-permute-start | bytes 786440 | tf_op jit(solution)/shard_map/ppermute | solution.py:16
  1.5 21.3 %collective-permute-start.3 = (bf16[64,2048]{1,0:T(8,128)(2,1)}, bf16[64,2048]{1,0:T(8,128)(2,1)S(1)}, u32[]{:S(2)}, u32[]{:S(2)}) collective-permute-start(bf16[64,2048]{1,0:T(8,128)(2,1)} %bitcast.11), channel_id=1, source_target_pairs={{0,4},{1,5},{2,6},{3,7},{4,0},{5,1},{6,2},{7,3},{8,12},{9,13},{10,... | collective-permute-start | bytes 786440 | tf_op jit(solution)/shard_map/ppermute | solution.py:16
  4.1 18.8 %collective-permute-start.4 = (bf16[64,2048]{1,0:T(8,128)(2,1)}, bf16[64,2048]{1,0:T(8,128)(2,1)S(1)}, u32[]{:S(2)}, u32[]{:S(2)}) collective-permute-start(bf16[64,2048]{1,0:T(8,128)(2,1)} %bitcast.12), channel_id=1, source_target_pairs={{0,6},{1,7},{2,4},{3,5},{4,2},{5,3},{6,0},{7,1},{8,14},{9,15},{10,... | collective-permute-start | bytes 786440 | tf_op jit(solution)/shard_map/ppermute | solution.py:16
  5.5 19.6 %collective-permute-start = (bf16[64,2048]{1,0:T(8,128)(2,1)}, bf16[64,2048]{1,0:T(8,128)(2,1)S(1)}, u32[]{:S(2)}, u32[]{:S(2)}) collective-permute-start(bf16[64,2048]{1,0:T(8,128)(2,1)} %bitcast.13), channel_id=1, source_target_pairs={{0,2},{1,3},{2,0},{3,1},{4,6},{5,7},{6,4},{7,5},{8,10},{9,11},{10,... | collective-permute-start | bytes 786440 | tf_op jit(solution)/shard_map/ppermute | solution.py:16
  8.3 20.4 %collective-permute-start.2 = (bf16[64,2048]{1,0:T(8,128)(2,1)S(1)}, bf16[64,2048]{1,0:T(8,128)(2,1)S(1)}, u32[]{:S(2)}, u32[]{:S(2)}) collective-permute-start(bf16[64,2048]{1,0:T(8,128)(2,1)S(1)} %collective-permute-done.1.refs_1_), channel_id=1, source_target_pairs={{0,2},{1,3},{2,0},{3,1},{4,6},{5,7},{6,4},{7,5},{8,10},{9,11},{10,... | collective-permute-start | bytes 786440 | tf_op jit(solution)/shard_map/ppermute | solution.py:16
  11.5 18.9 %copy-start.11 = (f32[1,4096]{1,0:T(1,128)S(1)}, f32[1,4096]{1,0:T(1,128)}, u32[]{:S(2)}) copy-start(f32[1,4096]{1,0:T(1,128)} %refs_4_.1) | copy-start | bytes 49156
  18.0 18.6 %collective-permute-start.6 = (bf16[64,4096]{1,0:T(8,128)(2,1)S(1)}, bf16[64,4096]{1,0:T(8,128)(2,1)S(1)}, u32[]{:S(2)}, u32[]{:S(2)}) collective-permute-start(bf16[64,4096]{1,0:T(8,128)(2,1)S(1)} %get-tuple-element.45), channel_id=1, source_target_pairs={{0,16},{8,24},{1,17},{9,25},{2,18},{10,26},{3,19},{11,27},{4,20},{... | collective-permute-start | bytes 1572872 | tf_op jit(solution)/shard_map/ppermute | solution.py:397
  28.6 11.9 %collective-permute-start.5 = (bf16[128,2048]{1,0:T(8,128)(2,1)S(1)}, bf16[128,2048]{1,0:T(8,128)(2,1)S(1)}, u32[]{:S(2)}, u32[]{:S(2)}) collective-permute-start(bf16[128,2048]{1,0:T(8,128)(2,1)S(1)} %pad_maximum_fusion), channel_id=1, source_target_pairs={{0,1},{1,0},{2,3},{3,2},{4,5},{5,4},{6,7},{7,6},{8,9},{9,8},{10,11... | collective-permute-start | bytes 1572872 | tf_op jit(solution)/shard_map/ppermute | solution.py:16
  29.1 17.2 %collective-permute-start.8 = (bf16[64,4096]{1,0:T(8,128)(2,1)S(1)}, bf16[64,4096]{1,0:T(8,128)(2,1)S(1)}, u32[]{:S(2)}, u32[]{:S(2)}) collective-permute-start(bf16[64,4096]{1,0:T(8,128)(2,1)S(1)} %get-tuple-element.46), channel_id=1, source_target_pairs={{0,16},{8,24},{1,17},{9,25},{2,18},{10,26},{3,19},{11,27},{4,20},{... | collective-permute-start | bytes 1572872 | tf_op jit(solution)/shard_map/ppermute | solution.py:397
  35.2 15.3 %collective-permute-start.7 = (bf16[256,4096]{1,0:T(8,128)(2,1)S(1)}, bf16[256,4096]{1,0:T(8,128)(2,1)S(1)}, u32[]{:S(2)}, u32[]{:S(2)}) collective-permute-start(bf16[256,4096]{1,0:T(8,128)(2,1)S(1)} %get-tuple-element.42.refs_0_), channel_id=1, source_target_pairs={{0,8},{16,24},{1,9},{17,25},{2,10},{18,26},{3,11},{19,27},{4,12},{... | collective-permute-start | bytes 6291464 | tf_op jit(solution)/shard_map/ppermute | solution.py:403
  46.4 5.1 %collective-permute-start.9 = (bf16[256,4096]{1,0:T(8,128)(2,1)S(1)}, bf16[256,4096]{1,0:T(8,128)(2,1)S(1)}, u32[]{:S(2)}, u32[]{:S(2)}) collective-permute-start(bf16[256,4096]{1,0:T(8,128)(2,1)S(1)} %encode.5.refs_1_), channel_id=1, source_target_pairs={{0,8},{16,24},{1,9},{17,25},{2,10},{18,26},{3,11},{19,27},{4,12},{... | collective-permute-start | bytes 6291464 | tf_op jit(solution)/shard_map/ppermute | solution.py:403
  47.8 33.9 %collective-permute-start.12 = (bf16[128,4096]{1,0:T(8,128)(2,1)}, bf16[128,4096]{1,0:T(8,128)(2,1)}, u32[]{:S(2)}, u32[]{:S(2)}) collective-permute-start(bf16[128,4096]{1,0:T(8,128)(2,1)} %get-tuple-element.44.refs_5_), channel_id=1, source_target_pairs={{0,16},{8,24},{1,17},{9,25},{2,18},{10,26},{3,19},{11,27},{4,20},{... | collective-permute-start | bytes 3145736 | tf_op jit(solution)/shard_map/ppermute | solution.py:397
  49.1 67.9 %collective-permute-start.19 = (bf16[256,4096]{1,0:T(8,128)(2,1)S(1)}, bf16[256,4096]{1,0:T(8,128)(2,1)}, u32[]{:S(2)}, u32[]{:S(2)}) collective-permute-start(bf16[256,4096]{1,0:T(8,128)(2,1)S(1)} %encode.5.refs_1_), channel_id=1, source_target_pairs={{0,16},{8,24},{1,17},{9,25},{2,18},{10,26},{3,19},{11,27},{4,20},{... | collective-permute-start | bytes 6291464 | tf_op jit(solution)/shard_map/ppermute | solution.py:397
  51.4 5.0 %collective-permute-start.11 = (bf16[64,4096]{1,0:T(8,128)(2,1)S(1)}, bf16[64,4096]{1,0:T(8,128)(2,1)}, u32[]{:S(2)}, u32[]{:S(2)}) collective-permute-start(bf16[64,4096]{1,0:T(8,128)(2,1)S(1)} %collective-permute-done.8.refs_5_), channel_id=1, source_target_pairs={{16,24},{24,16},{17,25},{25,17},{18,26},{26,18},{19,27},{27,19},{2... | collective-permute-start | bytes 1572872 | tf_op jit(solution)/shard_map/ppermute | solution.py:400
  53.7 3.9 %collective-permute-start.10 = (bf16[64,4096]{1,0:T(8,128)(2,1)S(1)}, bf16[64,4096]{1,0:T(8,128)(2,1)}, u32[]{:S(2)}, u32[]{:S(2)}) collective-permute-start(bf16[64,4096]{1,0:T(8,128)(2,1)S(1)} %collective-permute-done.6.refs_6_.refs_4_), channel_id=1, source_target_pairs={{16,24},{24,16},{17,25},{25,17},{18,26},{26,18},{19,27},{27,19},{2... | collective-permute-start | bytes 1572872 | tf_op jit(solution)/shard_map/ppermute | solution.py:400
  81.7 13.7 %collective-permute-start.13 = (bf16[128,4096]{1,0:T(8,128)(2,1)}, bf16[128,4096]{1,0:T(8,128)(2,1)S(1)}, u32[]{:S(2)}, u32[]{:S(2)}) collective-permute-start(bf16[128,4096]{1,0:T(8,128)(2,1)} %collective-permute-done.12.direct), channel_id=1, source_target_pairs={{16,24},{24,16},{17,25},{25,17},{18,26},{26,18},{19,27},{27,19},{2... | collective-permute-start | bytes 3145736 | tf_op jit(solution)/shard_map/ppermute | solution.py:400
  92.9 11.6 %collective-permute-start.14 = (bf16[4,128,256]{2,1,0:T(8,128)(2,1)}, bf16[4,128,256]{2,1,0:T(8,128)(2,1)S(1)}, u32[]{:S(2)}, u32[]{:S(2)}) collective-permute-start(bf16[4,128,256]{2,1,0:T(8,128)(2,1)} %get-tuple-element.51.refs_0_), channel_id=1, source_target_pairs={{0,1},{1,0},{2,3},{3,2},{4,5},{5,4},{6,7},{7,6},{8,9},{9,8},{10,11... | collective-permute-start | bytes 786440 | tf_op jit(solution)/shard_map/ppermute | solution.py:16
  95.4 17.4 %copy-start.12 = (s32[7]{0:T(128)S(1)}, s32[7]{0:T(128)}, u32[]{:S(2)}) copy-start(s32[7]{0:T(128)} %stack.31.info) | copy-start | bytes 88
  103.9 8.9 %collective-permute-start.15 = (bf16[4,128,256]{2,1,0:T(8,128)(2,1)}, bf16[4,128,256]{2,1,0:T(8,128)(2,1)S(1)}, u32[]{:S(2)}, u32[]{:S(2)}) collective-permute-start(bf16[4,128,256]{2,1,0:T(8,128)(2,1)} %get-tuple-element.57), channel_id=1, source_target_pairs={{0,1},{1,0},{2,3},{3,2},{4,5},{5,4},{6,7},{7,6},{8,9},{9,8},{10,11... | collective-permute-start | bytes 786440 | tf_op jit(solution)/shard_map/ppermute | solution.py:16
  117.0 8.9 %collective-permute-start.20 = (bf16[256,4096]{1,0:T(8,128)(2,1)}, bf16[256,4096]{1,0:T(8,128)(2,1)S(1)}, u32[]{:S(2)}, u32[]{:S(2)}) collective-permute-start(bf16[256,4096]{1,0:T(8,128)(2,1)} %collective-permute-done.19.direct), channel_id=1, source_target_pairs={{16,24},{24,16},{17,25},{25,17},{18,26},{26,18},{19,27},{27,19},{2... | collective-permute-start | bytes 6291464 | tf_op jit(solution)/shard_map/ppermute | solution.py:400
  119.1 15.8 %collective-permute-start.16 = (bf16[256,256]{1,0:T(8,128)(2,1)S(1)}, bf16[256,256]{1,0:T(8,128)(2,1)S(1)}, u32[]{:S(2)}, u32[]{:S(2)}) collective-permute-start(bf16[256,256]{1,0:T(8,128)(2,1)S(1)} %get-tuple-element.59), channel_id=1, source_target_pairs={{0,2},{1,3},{2,0},{3,1},{4,6},{5,7},{6,4},{7,5},{8,10},{9,11},{10,... | collective-permute-start | bytes 393224 | tf_op jit(solution)/shard_map/ppermute | solution.py:16
  121.9 13.0 %collective-permute-start.17 = (bf16[256,256]{1,0:T(8,128)(2,1)S(1)}, bf16[256,256]{1,0:T(8,128)(2,1)S(1)}, u32[]{:S(2)}, u32[]{:S(2)}) collective-permute-start(bf16[256,256]{1,0:T(8,128)(2,1)S(1)} %get-tuple-element.60), channel_id=1, source_target_pairs={{0,4},{1,5},{2,6},{3,7},{4,0},{5,1},{6,2},{7,3},{8,12},{9,13},{10,... | collective-permute-start | bytes 393224 | tf_op jit(solution)/shard_map/ppermute | solution.py:16
  124.5 11.0 %collective-permute-start.18 = (bf16[256,256]{1,0:T(8,128)(2,1)S(1)}, bf16[256,256]{1,0:T(8,128)(2,1)S(1)}, u32[]{:S(2)}, u32[]{:S(2)}) collective-permute-start(bf16[256,256]{1,0:T(8,128)(2,1)S(1)} %get-tuple-element.61), channel_id=1, source_target_pairs={{0,6},{1,7},{2,4},{3,5},{4,2},{5,3},{6,0},{7,1},{8,14},{9,15},{10,... | collective-permute-start | bytes 393224 | tf_op jit(solution)/shard_map/ppermute | solution.py:16
  134.3 13.2 %collective-permute-start.21 = (bf16[4,128,256]{2,1,0:T(8,128)(2,1)}, bf16[4,128,256]{2,1,0:T(8,128)(2,1)S(1)}, u32[]{:S(2)}, u32[]{:S(2)}) collective-permute-start(bf16[4,128,256]{2,1,0:T(8,128)(2,1)} %get-tuple-element.63.refs_4_.refs_0_), channel_id=1, source_target_pairs={{0,1},{1,0},{2,3},{3,2},{4,5},{5,4},{6,7},{7,6},{8,9},{9,8},{10,11... | collective-permute-start | bytes 786440 | tf_op jit(solution)/shard_map/ppermute | solution.py:16
  137.9 29.3 %copy-start.1 = (f32[512,256]{1,0:T(8,128)S(1)}, f32[512,256]{1,0:T(8,128)}, u32[]{:S(2)}) copy-start(f32[512,256]{1,0:T(8,128)} %add_up.2.refs_1_.base) | copy-start | bytes 1572868
  146.5 9.1 %collective-permute-start.25 = (bf16[4,128,256]{2,1,0:T(8,128)(2,1)}, bf16[4,128,256]{2,1,0:T(8,128)(2,1)S(1)}, u32[]{:S(2)}, u32[]{:S(2)}) collective-permute-start(bf16[4,128,256]{2,1,0:T(8,128)(2,1)} %get-tuple-element.65.refs_2_), channel_id=1, source_target_pairs={{0,1},{1,0},{2,3},{3,2},{4,5},{5,4},{6,7},{7,6},{8,9},{9,8},{10,11... | collective-permute-start | bytes 786440 | tf_op jit(solution)/shard_map/ppermute | solution.py:16
  150.2 5.4 %collective-permute-start.22 = (bf16[128,256]{1,0:T(8,128)(2,1)S(1)}, bf16[128,256]{1,0:T(8,128)(2,1)S(1)}, u32[]{:S(2)}, u32[]{:S(2)}) collective-permute-start(bf16[128,256]{1,0:T(8,128)(2,1)S(1)} %get-tuple-element.67), channel_id=1, source_target_pairs={{0,2},{1,3},{2,0},{3,1},{4,6},{5,7},{6,4},{7,5},{8,10},{9,11},{10,... | collective-permute-start | bytes 196616 | tf_op jit(solution)/shard_map/ppermute | solution.py:16
  152.2 10.3 %collective-permute-start.23 = (bf16[128,256]{1,0:T(8,128)(2,1)S(1)}, bf16[128,256]{1,0:T(8,128)(2,1)S(1)}, u32[]{:S(2)}, u32[]{:S(2)}) collective-permute-start(bf16[128,256]{1,0:T(8,128)(2,1)S(1)} %get-tuple-element.68), channel_id=1, source_target_pairs={{0,4},{1,5},{2,6},{3,7},{4,0},{5,1},{6,2},{7,3},{8,12},{9,13},{10,... | collective-permute-start | bytes 196616 | tf_op jit(solution)/shard_map/ppermute | solution.py:16
  154.2 8.3 %collective-permute-start.24 = (bf16[128,256]{1,0:T(8,128)(2,1)S(1)}, bf16[128,256]{1,0:T(8,128)(2,1)S(1)}, u32[]{:S(2)}, u32[]{:S(2)}) collective-permute-start(bf16[128,256]{1,0:T(8,128)(2,1)S(1)} %get-tuple-element.69), channel_id=1, source_target_pairs={{0,6},{1,7},{2,4},{3,5},{4,2},{5,3},{6,0},{7,1},{8,14},{9,15},{10,... | collective-permute-start | bytes 196616 | tf_op jit(solution)/shard_map/ppermute | solution.py:16
  157.2 5.2 %collective-permute-start.26 = (bf16[128,256]{1,0:T(8,128)(2,1)S(1)}, bf16[128,256]{1,0:T(8,128)(2,1)S(1)}, u32[]{:S(2)}, u32[]{:S(2)}) collective-permute-start(bf16[128,256]{1,0:T(8,128)(2,1)S(1)} %get-tuple-element.72), channel_id=1, source_target_pairs={{0,2},{1,3},{2,0},{3,1},{4,6},{5,7},{6,4},{7,5},{8,10},{9,11},{10,... | collective-permute-start | bytes 196616 | tf_op jit(solution)/shard_map/ppermute | solution.py:16
  159.1 7.2 %collective-permute-start.27 = (bf16[128,256]{1,0:T(8,128)(2,1)S(1)}, bf16[128,256]{1,0:T(8,128)(2,1)S(1)}, u32[]{:S(2)}, u32[]{:S(2)}) collective-permute-start(bf16[128,256]{1,0:T(8,128)(2,1)S(1)} %get-tuple-element.73), channel_id=1, source_target_pairs={{0,4},{1,5},{2,6},{3,7},{4,0},{5,1},{6,2},{7,3},{8,12},{9,13},{10,... | collective-permute-start | bytes 196616 | tf_op jit(solution)/shard_map/ppermute | solution.py:16
  161.1 6.1 %collective-permute-start.28 = (bf16[128,256]{1,0:T(8,128)(2,1)S(1)}, bf16[128,256]{1,0:T(8,128)(2,1)S(1)}, u32[]{:S(2)}, u32[]{:S(2)}) collective-permute-start(bf16[128,256]{1,0:T(8,128)(2,1)S(1)} %get-tuple-element.74), channel_id=1, source_target_pairs={{0,6},{1,7},{2,4},{3,5},{4,2},{5,3},{6,0},{7,1},{8,14},{9,15},{10,... | collective-permute-start | bytes 196616 | tf_op jit(solution)/shard_map/ppermute | solution.py:16
  (15 other events, 107.6 us)
